TPU v7x, 32 devices: a whole 2x2x4 slice. The times are simulated.
32 devices in a mesh: len: 8 (over y, x, core), mem: 4 (over z).
Axes of the slice: x: 2, y: 2, z: 4, core: 2. Of those that a mesh axis runs over, the one named last changes fastest.
Arguments:
- phase_left: float32 [32, 1048576], P('mem', 'len'), may hold values from -3.140625 to 3.140625
- phase_right: float32 [32, 1048576], P('mem', 'len'), may hold values from -3.140625 to 3.140625
- roughness: float32 [32], P('mem'), may hold values from 0.1 to 10
- waviness: float32 [32], P('mem'), may hold values from 1.5 to 2.5
- coherence: float32 [32], P('mem'), may hold values from 32 to 512
Outputs:
- profile: float32 [2, 32, 1048576], P(None, 'mem', 'len')
- r_factor: float32 [32, 32], replicated
All inputs are finite; a program needn't handle non-finite values.
Results may differ from a plain program's by a relative error of at most 0.0003.
Values sent between devices are 32-bit elements; how exact they have to be, the bound alone decides.
No kernel may reach another device: no remote copies, remote signals or barrier semaphores. Data moves between devices by JAX's collectives and lax.ppermute only.
A program may use at most 128 MiB of HBM per device.

v0:
```python
import math

import jax
import jax.numpy as jnp
from jax import lax
from jax.sharding import PartitionSpec as P

OUTER = 1024
INNER = 1024
ANCHOR = 64


highest = lax.Precision.HIGHEST


def merged(shard, axis, combine):
    everything = lax.all_gather(shard, axis)
    leading = everything[0]

    def step(k, so_far):
        return combine(so_far, everything[k])

    return lax.fori_loop(1, lax.axis_size(axis), step, leading)


def dft_tables(length):
    index = lax.iota(jnp.int32, length)
    product = index[:, None] * index[None, :] % length
    phase_angle = product.astype(jnp.float32) * (2.0 * math.pi / length)
    return (jnp.cos(phase_angle), jnp.sin(phase_angle))


def spectra_of(phase_left, phase_right, roughness, waviness, coherence, freq):
    amplitude = jnp.sqrt(2.0 * roughness * (waviness - 1.0) / ANCHOR)[:, None] * (
        (freq + ANCHOR) / ANCHOR
    ) ** (-0.5 * waviness[:, None])
    freq_ratio = freq / coherence[:, None]
    coherent = 1.0 / (1.0 + freq_ratio * freq_ratio)
    incoherent = freq_ratio * jnp.sqrt(2.0 + freq_ratio * freq_ratio) * coherent
    cos_left = jnp.cos(phase_left)
    sin_left = jnp.sin(phase_left)
    cos_right = jnp.cos(phase_right)
    sin_right = jnp.sin(phase_right)
    real_part = jnp.stack(
        [amplitude * cos_left, amplitude * (coherent * cos_left + incoherent * cos_right)]
    )
    imag_part = jnp.stack(
        [amplitude * sin_left, amplitude * (coherent * sin_left + incoherent * sin_right)]
    )
    return (real_part, imag_part)


def upper_of(gram_matrix):
    return jnp.linalg.cholesky(gram_matrix).T


def combine_factors(upper_a, upper_b):
    gram_matrix = jnp.dot(upper_a.T, upper_a, precision=highest) + jnp.dot(
        upper_b.T, upper_b, precision=highest
    )
    return upper_of(gram_matrix)


def gram_of(snapshot):
    return jnp.einsum("tmr,tnr->mn", snapshot, snapshot, precision=highest)


def per_device(phase_left, phase_right, roughness, waviness, coherence):
    shards = lax.axis_size("len")
    my_index = lax.axis_index("len")
    local_members, local_len = phase_left.shape
    columns = 2 * local_members
    outer_block = OUTER // shards
    inner_block = INNER // shards

    def to_rows(part):
        shaped = part.reshape(2, local_members, inner_block, OUTER)
        return jnp.transpose(shaped, (2, 3, 0, 1)).reshape(
            inner_block, shards, outer_block * columns
        )

    inner_cos, inner_sin = dft_tables(INNER)
    freq = (my_index * local_len + lax.iota(jnp.int32, local_len)).astype(jnp.float32)[None, :]
    real_part, imag_part = spectra_of(phase_left, phase_right, roughness, waviness, coherence, freq)
    pieces = (
        lax.all_to_all(to_rows(real_part), "len", split_axis=1, concat_axis=0, tiled=True),
        lax.all_to_all(to_rows(imag_part), "len", split_axis=1, concat_axis=0, tiled=True),
    )
    real_in = pieces[0].reshape(INNER, -1)
    imag_in = pieces[1].reshape(INNER, -1)
    real_out = jnp.dot(inner_cos, real_in, precision=highest) - jnp.dot(
        inner_sin, imag_in, precision=highest
    )
    imag_out = jnp.dot(inner_cos, imag_in, precision=highest) + jnp.dot(
        inner_sin, real_in, precision=highest
    )
    row_index = lax.iota(jnp.int32, INNER)[:, None]
    outer_index = (my_index * outer_block + lax.iota(jnp.int32, outer_block))[None, :]
    twist = (row_index * outer_index % (OUTER * INNER)).astype(jnp.float32) * (
        2.0 * math.pi / (OUTER * INNER)
    )
    twist_cos = jnp.repeat(jnp.cos(twist), columns, axis=1)
    twist_sin = jnp.repeat(jnp.sin(twist), columns, axis=1)
    rot_real = (real_out * twist_cos - imag_out * twist_sin).reshape(
        shards, inner_block, outer_block * columns
    )
    rot_imag = (real_out * twist_sin + imag_out * twist_cos).reshape(
        shards, inner_block, outer_block * columns
    )
    outer_cos, outer_sin = dft_tables(OUTER)
    outer_cos = outer_cos.reshape(OUTER, shards, outer_block)
    outer_sin = outer_sin.reshape(OUTER, shards, outer_block)
    pieces = (
        lax.all_to_all(rot_real, "len", split_axis=0, concat_axis=0, tiled=True),
        lax.all_to_all(rot_imag, "len", split_axis=0, concat_axis=0, tiled=True),
    )
    item_count = pieces[0].shape[1]
    real_in = pieces[0].reshape(shards, item_count, outer_block, columns)
    imag_in = pieces[1].reshape(shards, item_count, outer_block, columns)
    first = jnp.einsum("jqa,qiac->cij", outer_cos, real_in, precision=highest)
    second = jnp.einsum("jqa,qiac->cij", outer_sin, imag_in, precision=highest)
    profile_block = first - second
    outgoing = jnp.transpose(
        profile_block.reshape(columns, inner_block, shards, outer_block), (2, 0, 1, 3)
    ).reshape(shards, -1)
    arrived = lax.all_to_all(outgoing, "len", split_axis=0, concat_axis=0, tiled=True)
    profile = jnp.transpose(
        arrived.reshape(shards, columns, inner_block, outer_block), (1, 3, 0, 2)
    ).reshape(2, local_members, local_len)
    scale = 1.0 / math.sqrt(2.0 * OUTER * INNER)
    snapshot = profile_block.reshape(2, local_members, inner_block * OUTER) * scale
    gathered = lax.all_gather(snapshot, "mem", axis=1, tiled=True)
    gram_local = gram_of(gathered)
    r_factor = merged(upper_of(gram_local), "len", combine_factors)
    return (profile, r_factor)


def solution(mesh):
    placed = (P("mem", "len"), P("mem", "len"), P("mem"), P("mem"), P("mem"))
    return jax.shard_map(
        per_device,
        mesh=mesh,
        in_specs=placed,
        out_specs=(P(None, "mem", "len"), P()),
        check_vma=False,
    )
```

profile of v0, /device:TPU:0, one launch (start us, length us, event | category | flops | bytes accessed | tf_op | source)
XLA Modules:
  0.0 1350.4 jit_solution(6611854208396604374)
XLA Ops:
  7.4 15.9 %fusion.70 = (f32[8,131072]{1,0:T(8,128)S(1)}, f32[8,131072]{1,0:T(8,128)S(1)}) fusion(f32[8,131072]{1,0:T(8,128)} %param.8), kind=kLoop, calls=%fused_computation.111 | loop fusion | bytes 12582912 | tf_op jit(solution)/shard_map/cos | solution.py:40
  23.3 23.4 %add_multiply_fusion.1 = (f32[8,131072]{1,0:T(8,128)S(1)}, f32[8,131072]{1,0:T(8,128)}, f32[8,131072]{1,0:T(8,128)}, f32[8,131072]{1,0:T(8,128)S(1)}) fusion(f32[8,131072]{1,0:T(8,128)S(1)} %copy-done, f32[8,131072]{1,0:T(8,128)S(1)} %get-tuple-element.124, f32[8]{0:T(128)S(1)} %copy-done.1, f32[131072]{0:T(1024)S(1)} %add_convert_fusion, ...), kind=kLoop, calls=%fused_computation.45 | loop fusion | flops 18874368 | bytes 30408800 | tf_op jit(solution)/shard_map/mul | solution.py:45
  46.7 4.9 copy_bitcast_fusion.3
  51.6 4.2 maximum_bitcast_fusion
  55.8 9.2 copy.53
  65.0 5.4 all-to-all-start
  70.4 8.3 copy_bitcast_fusion.1
  78.7 4.2 maximum_bitcast_fusion.1
  83.0 9.2 copy.55
  92.2 72.7 %all-to-all-done = f32[128,8,2048]{0,2,1:T(8,128)} async-done(((f32[128,8,2048]{0,2,1:T(8,128)}), f32[128,8,2048]{0,2,1:T(8,128)}, u32[]{:S(2)}, u32[]{:S(2)}) %all-to-all-start) | async-done | bytes 8388640 | tf_op jit(solution)/shard_map/all_to_all | solution.py:86
  164.9 5.4 all-to-all-start.1
  170.4 2.1 fusion.43
  172.5 4.5 broadcast_in_dim.5
  177.0 9.2 copy.58
  186.2 4.5 broadcast_in_dim.4
  190.6 9.2 copy.57
  199.9 9.1 copy.54
  209.0 49.5 %fusion.33 = f32[1024,2048]{1,0:T(8,128)} fusion(f32[1024,2048]{1,0:T(8,128)} %bitcast.124), kind=kOutput, calls=%fused_computation.61 | convolution fusion | flops 25784483840 | bytes 16777216 | tf_op jit(solution)/shard_map/dot_general | solution.py:91
  258.5 5.9 all-to-all-done.1
  264.4 9.2 copy.56
  273.6 49.7 %fusion.31 = f32[1024,2048]{1,0:T(8,128)} fusion(f32[1024,2048]{1,0:T(8,128)} %bitcast.137), kind=kOutput, calls=%fused_computation.60 | convolution fusion | flops 25784483840 | bytes 16777216 | tf_op jit(solution)/shard_map/dot_general | solution.py:94
  323.3 49.4 %convolution_subtract_fusion = f32[1024,2048]{1,0:T(8,128)} fusion(f32[1024,2048]{1,0:T(8,128)} %fusion.33, f32[1024,2048]{1,0:T(8,128)} %bitcast.138), kind=kOutput, calls=%fused_computation.56 | convolution fusion | flops 25786580992 | bytes 25165824 | tf_op jit(solution)/shard_map/dot_general | solution.py:91
  372.8 54.4 %multiply_subtract_fusion = (f32[1024,2048]{1,0:T(8,128)}, f32[1024,2048]{1,0:T(8,128)}) fusion(f32[1024,2048]{1,0:T(8,128)S(1)} %bitcast.123, f32[1024,2048]{1,0:T(8,128)} %convolution_subtract_fusion, f32[1024,2048]{1,0:T(8,128)} %copy.57, f32[1024,2048]{1,0:T(8,128)} %fusion.31, f32[1024,2048]{1,0:T(8,128)} %bitcast.125), kind=kOutput, calls=%fused_computation.21 | convolution fusion | flops 25799163904 | bytes 58720256 | tf_op jit(solution)/shard_map/dot_general | solution.py:94
  427.2 9.1 copy.59
  436.3 5.0 all-to-all-start.2
  441.3 9.2 copy.63
  450.5 84.9 %all-to-all-done.2 = f32[8,128,2048]{1,2,0:T(8,128)} async-done(((f32[8,128,2048]{1,2,0:T(8,128)}), f32[8,128,2048]{1,2,0:T(8,128)}, u32[]{:S(2)}, u32[]{:S(2)}) %all-to-all-start.2) | async-done | bytes 8388640 | tf_op jit(solution)/shard_map/all_to_all | solution.py:114
  535.4 5.0 all-to-all-start.3
  540.6 17.2 %fusion.85 = f32[1024,8,128,1]{2,0,1,3:T(8,128)S(1)} fusion(s32[8,128]{1,0:T(8,128)S(1)} %multiply_add_fusion.1), kind=kLoop, calls=%fused_computation.39.clone.1 | loop fusion | flops 14680064 | bytes 4198400 | tf_op jit(solution)/shard_map/jqa,qiac->cij/dot_general | solution.py:120
  557.8 16.3 %fusion.14.clone.4 = f32[1024,8,128,1]{2,0,1,3:T(8,128)} fusion(s32[8,128]{1,0:T(8,128)S(1)} %multiply_add_fusion.1), kind=kLoop, calls=%fused_computation.38.clone.clone.clone.1 | loop fusion | flops 14680064 | bytes 4198400 | tf_op jit(solution)/shard_map/mul | solution.py:131
  574.1 58.4 %fusion.6 = f32[128,16,1024,1]{2,0,3,1:T(8,128)} fusion(f32[8,128,128,16]{1,3,2,0:T(8,128)} %bitcast.16, f32[1024,8,128,1]{2,0,1,3:T(8,128)S(1)} %fusion.85), kind=kOutput, calls=%fused_computation.18 | convolution fusion | flops 25769803776 | bytes 20971520 | tf_op jit(solution)/shard_map/jqa,qiac->cij/dot_general | solution.py:120
  632.5 2.0 all-to-all-done.3
  634.4 60.8 %bitcast_multiply_fusion = (f32[16,128,1024]{2,1,0:T(8,128)}, f32[128,16,1024,1]{2,0,3,1:T(8,128)}) fusion(f32[128,16,1024,1]{2,0,3,1:T(8,128)} %fusion.6, f32[8,128,128,16]{1,3,2,0:T(8,128)} %bitcast.21, f32[1024,8,128,1]{2,0,1,3:T(8,128)} %fusion.14.clone.4), kind=kOutput, calls=%fused_computation.14 | convolution fusion | flops 25773998080 | bytes 37748736 | tf_op jit(solution)/shard_map/jqa,qiac->cij/dot_general | solution.py:121
  695.2 6.2 mul.216
  701.4 12.7 copy_bitcast_fusion
  714.1 5.1 all-to-all-start.4
  719.2 94.1 %all-to-all-done.4 = f32[8,1,262144]{2,1,0:T(1,128)} async-done(((f32[8,1,262144]{2,1,0:T(1,128)}), f32[8,1,262144]{2,1,0:T(1,128)}, u32[]{:S(2)}, u32[]{:S(2)}) %all-to-all-start.4) | async-done | bytes 8388640 | tf_op jit(solution)/shard_map/all_to_all | solution.py:126
  813.3 9.3 copy.67
  822.6 6.4 reshape.119
  829.0 434.4 %all-gather.3.cloned.1.call-done = f32[2,32,131072]{2,1,0:T(8,128)} async-done(((f32[2,8,131072]{2,1,0:T(8,128)}), f32[2,32,131072]{2,1,0:T(8,128)}) %all-gather.3.cloned.1.call-update) | async-done | bytes 33554448 | tf_op jit(solution)/shard_map/all_gather | solution.py:132
  1263.4 31.5 %convolution_bitcast_fusion = f32[32,32]{1,0:T(8,128)S(1)} fusion(f32[2,32,131072]{2,1,0:T(8,128)} %all-gather.3.cloned.1.call-done), kind=kOutput, calls=%fused_computation.62 | convolution fusion | flops 3221225472 | bytes 33558528 | tf_op jit(solution)/shard_map/tmr,tnr->mn/dot_general | solution.py:65
  1295.0 2.9 cholesky.55
  1298.0 0.7 compare_reduce_fusion.1
  1298.7 0.7 select_bitcast_fusion.1
  1299.5 9.2 all-gather
  1308.7 34.0 %while.15 = (s32[]{:T(128)}, f32[32,32]{0,1:T(8,128)S(1)}, f32[8,32,32]{2,1,0:T(8,128)S(1)}, s32[]{:T(128)}, s32[]{:T(128)}, /*index=5*/s32[]{:T(128)}) while((s32[]{:T(128)}, f32[32,32]{0,1:T(8,128)S(1)}, f32[8,32,32]{2,1,0:T(8,128)S(1)}, s32[]{:T(128)}, s32[]{:T(128)}, /*index=5*/s32[]{:T(128)}) %tuple.65), condition=%wide.region_3.5_spmd, body=%wide.region_2.4_spmd.sunk | while | flops 795684 | bytes 78197 | solution.py:23
  1309.2 2.9 cholesky.117
  1312.1 0.7 compare_reduce_fusion.3
  1312.8 0.7 select_bitcast_fusion.3
  1314.0 2.9 cholesky.117
  1317.0 0.7 compare_reduce_fusion.3
  1317.7 0.7 select_bitcast_fusion.3
  1318.9 2.9 cholesky.117
  1321.8 0.7 compare_reduce_fusion.3
  1322.5 0.7 select_bitcast_fusion.3
  1323.7 2.9 cholesky.117
  1326.7 0.7 compare_reduce_fusion.3
  1327.4 0.7 select_bitcast_fusion.3
  1328.6 2.9 cholesky.117
  1331.5 0.7 compare_reduce_fusion.3
  1333.4 2.9 cholesky.117
  1336.4 0.7 compare_reduce_fusion.3
  1338.3 2.9 cholesky.117
  1341.2 0.7 compare_reduce_fusion.3
  (65 shorter events, 6.7 us)
Async XLA Ops:
  7.3 16.0 %copy-start.2 = (f32[8]{0:T(128)S(1)}, f32[8]{0:T(128)}, u32[]{:S(2)}) copy-start(f32[8]{0:T(128)} %param.11) | copy-start | bytes 100
  7.3 16.0 %copy-start.3 = (f32[8]{0:T(128)S(1)}, f32[8]{0:T(128)}, u32[]{:S(2)}) copy-start(f32[8]{0:T(128)} %param.10) | copy-start | bytes 100
  7.4 16.0 %copy-start = (f32[8,131072]{1,0:T(8,128)S(1)}, f32[8,131072]{1,0:T(8,128)}, u32[]{:S(2)}) copy-start(f32[8,131072]{1,0:T(8,128)} %param.9) | copy-start | bytes 12582916
  7.4 16.0 %copy-start.1 = (f32[8]{0:T(128)S(1)}, f32[8]{0:T(128)}, u32[]{:S(2)}) copy-start(f32[8]{0:T(128)} %param.12) | copy-start | bytes 100
  65.0 99.9 %all-to-all-start = ((f32[128,8,2048]{0,2,1:T(8,128)}), f32[128,8,2048]{0,2,1:T(8,128)}, u32[]{:S(2)}, u32[]{:S(2)}) async-start(f32[128,8,2048]{0,2,1:T(8,128)} %bitcast.130), calls=%async_computation | async-start | bytes 16777216 | tf_op jit(solution)/shard_map/all_to_all | solution.py:86
  164.9 99.5 %all-to-all-start.1 = ((f32[128,8,2048]{0,2,1:T(8,128)}), f32[128,8,2048]{0,2,1:T(8,128)}, u32[]{:S(2)}, u32[]{:S(2)}) async-start(f32[128,8,2048]{0,2,1:T(8,128)} %bitcast.129), calls=%async_computation.1 | async-start | bytes 16777216 | tf_op jit(solution)/shard_map/all_to_all | solution.py:87
  273.6 99.1 %slice-start = ((s8[8388608]{0:T(1024)(128)(4,1)}), s8[4194304]{0:T(1024)(128)(4,1)S(1)}, s32[]{:S(2)}) async-start(s8[8388608]{0:T(1024)(128)(4,1)} %bitcast.122), calls=%async_computation.6 | async-start | bytes 8388608
  323.3 49.4 %slice-start.1 = ((s8[8388608]{0:T(1024)(128)(4,1)}), s8[4194304]{0:T(1024)(128)(4,1)S(1)}, s32[]{:S(2)}) async-start(s8[8388608]{0:T(1024)(128)(4,1)} %bitcast.122), calls=%async_computation.7 | async-start | bytes 8388608
  436.3 99.1 %all-to-all-start.2 = ((f32[8,128,2048]{1,2,0:T(8,128)}), f32[8,128,2048]{1,2,0:T(8,128)}, u32[]{:S(2)}, u32[]{:S(2)}) async-start(f32[8,128,2048]{1,2,0:T(8,128)} %copy.59), calls=%async_computation.2 | async-start | bytes 16777216 | tf_op jit(solution)/shard_map/all_to_all | solution.py:114
  535.4 99.0 %all-to-all-start.3 = ((f32[8,128,2048]{1,2,0:T(8,128)}), f32[8,128,2048]{1,2,0:T(8,128)}, u32[]{:S(2)}, u32[]{:S(2)}) async-start(f32[8,128,2048]{1,2,0:T(8,128)} %copy.63), calls=%async_computation.3 | async-start | bytes 16777216 | tf_op jit(solution)/shard_map/all_to_all | solution.py:115
  540.4 723.0 %all-gather.3.cloned.1.call-start = ((), (), s32[]{:S(2)}) async-start(), calls=%async_computation.5 | async-start | bytes 41943040 | tf_op jit(solution)/shard_map/all_gather | solution.py:132
  714.1 99.2 %all-to-all-start.4 = ((f32[8,1,262144]{2,1,0:T(1,128)}), f32[8,1,262144]{2,1,0:T(1,128)}, u32[]{:S(2)}, u32[]{:S(2)}) async-start(f32[8,1,262144]{2,1,0:T(1,128)} %bitcast.128), calls=%async_computation.4 | async-start | bytes 16777216 | tf_op jit(solution)/shard_map/all_to_all | solution.py:126
Sparse Core Ops, SparseCore 0:
  701.6 561.7 all-gather.2
where the time goes:
time: 1360 us; the launch traced here: 1350 us
  waiting for transfers between devices  694 us (51%)
  matrix products  356 us (26%)
  local copies, waits for them, and re-layouts  135 us (10%)
  other arithmetic  115 us (8%)
  starting transfers between devices  26.1 us (2%)
  between operations  14.5 us (1%)
    all_gather x1, waiting for transfers between devices, per_device(): gathered = lax.all_gather(snapshot, 'mem', axis=1, tiled=True)  434 us
    all_to_all x1, waiting for transfers between devices, per_device(): lax.all_to_all(outgoing, 'len', split_axis=0, concat_axis=0, tiled=True)  94.1 us
    all_to_all x1, waiting for transfers between devices, per_device(): lax.all_to_all(rot_real, 'len', split_axis=0, concat_axis=0, tiled=True)  84.9 us
    all_to_all x1, waiting for transfers between devices, per_device(): lax.all_to_all(to_rows(real_part), 'len', split_axis=1, concat_axis=0, ti...  72.7 us
    dot_general x1, matrix products, per_device(): second = jnp.einsum('jqa,qiac->cij', outer_sin, imag_in, precision=highest)  60.8 us
    dot_general x1, matrix products, per_device(): first = jnp.einsum('jqa,qiac->cij', outer_cos, real_in, precision=highest)  58.4 us
    dot_general x1, matrix products, per_device(): jnp.dot(inner_sin, real_in, precision=highest)  54.4 us
    dot_general x1, matrix products, per_device(): jnp.dot(inner_cos, imag_in, precision=highest)  49.7 us
  transfers between devices with their start and end apart: 6, of which 6 were waited for; matrix products, arithmetic and copies ran while one was open for 18% of the time, Pallas kernels for 0%

commit v1 on v0

--- a/solution.py
+++ b/solution.py
@@ -1,13 +1,35 @@
+import functools
 import math
 
 import jax
 import jax.numpy as jnp
+import numpy as np
 from jax import lax
+from jax.experimental import pallas as pl
+from jax.experimental.pallas import tpu as pltpu
 from jax.sharding import PartitionSpec as P
 
 OUTER = 1024
 INNER = 1024
 ANCHOR = 64
+RADIX = 4
+QUARTER = 256
+LANES = 128
+STEP = 16
+WIDE = 256
+BLOCK_ROWS = 16
+IN_PARTS = 2
+OUT_PARTS = 2
+VMEM_LIMIT = 48 * 1024 * 1024
+SIN_HALF = (0.49999999785787, -0.02083332246218, 2.604078316692e-4, -1.547581723527e-6, 5.088214043e-9)
+COS_HALF = (
+    0.99999999977982,
+    -0.12499999839235,
+    2.604164763023e-3,
+    -2.170056380508e-5,
+    9.67192778775e-8,
+    -2.5440497557e-10,
+)
 
 
 highest = lax.Precision.HIGHEST
@@ -65,7 +87,7 @@
     return jnp.einsum("tmr,tnr->mn", snapshot, snapshot, precision=highest)
 
 
-def per_device(phase_left, phase_right, roughness, waviness, coherence):
+def per_device_spread(phase_left, phase_right, roughness, waviness, coherence):
     shards = lax.axis_size("len")
     my_index = lax.axis_index("len")
     local_members, local_len = phase_left.shape
@@ -135,6 +157,327 @@
     return (profile, r_factor)
 
 
+def host_cis(product, period):
+    angle = product % period * (2.0 * np.pi / period)
+    return np.cos(angle), np.sin(angle)
+
+
+def split_host(table):
+    coarse = table.astype(np.float32).astype(jnp.bfloat16)
+    fine = (table - coarse.astype(np.float64)).astype(np.float32).astype(jnp.bfloat16)
+    return np.stack([coarse, fine])
+
+
+def outer_matrices():
+    c, e, b = np.arange(QUARTER), np.arange(RADIX), np.arange(QUARTER)
+    cos_part, sin_part = host_cis((RADIX * c[None, :, None] + e[:, None, None]) * b[None, None, :], OUTER)
+    upper = np.concatenate([cos_part, -sin_part], axis=2)
+    lower = np.concatenate([sin_part, cos_part], axis=2)
+    return split_host(np.concatenate([upper, lower], axis=1))
+
+
+def inner_matrices():
+    c, e, b = np.arange(QUARTER), np.arange(RADIX), np.arange(QUARTER)
+    cos_part, sin_part = host_cis((RADIX * c[None, :, None] + e[:, None, None]) * b[None, None, :], INNER)
+    return split_host(np.concatenate([cos_part, -sin_part], axis=2))
+
+
+def twist_tables():
+    j1 = RADIX * np.arange(QUARTER)[None, :, None] + np.arange(RADIX)[:, None, None]
+    cos_part, sin_part = host_cis(j1 * np.arange(INNER)[None, None, :], OUTER * INNER)
+    return np.stack([cos_part, sin_part]).astype(np.float32)
+
+
+def sin_cos(angle):
+    square = angle * angle
+
+    def series(coefficients):
+        total = jnp.float32(coefficients[-1])
+        for coefficient in coefficients[-2::-1]:
+            total = total * square + jnp.float32(coefficient)
+        return total
+
+    half_sin = angle * series(SIN_HALF)
+    half_cos = series(COS_HALF)
+    twice = half_sin + half_sin
+    return twice * half_cos, 1.0 - twice * half_sin
+
+
+def line_spectra(left, right, freq, scale, exponent, inverse_coherence):
+    amplitude = scale * jnp.exp2(exponent * jnp.log2((freq + ANCHOR) * (1.0 / ANCHOR)))
+    freq_ratio = freq * inverse_coherence
+    ratio_square = freq_ratio * freq_ratio
+    coherent = 1.0 / (1.0 + ratio_square)
+    incoherent = freq_ratio * jnp.sqrt(2.0 + ratio_square) * coherent
+    sin_left, cos_left = sin_cos(left)
+    sin_right, cos_right = sin_cos(right)
+    independent = amplitude * incoherent
+    first = (amplitude * cos_left, amplitude * sin_left)
+    second = (
+        coherent * first[0] + independent * cos_right,
+        coherent * first[1] + independent * sin_right,
+    )
+    return first, second
+
+
+def radix_four(parts):
+    (r0, i0), (r1, i1), (r2, i2), (r3, i3) = parts
+    even_sum, even_gap = (r0 + r2, i0 + i2), (r0 - r2, i0 - i2)
+    odd_sum, odd_gap = (r1 + r3, i1 + i3), (r1 - r3, i1 - i3)
+    return (
+        (even_sum[0] + odd_sum[0], even_sum[1] + odd_sum[1]),
+        (even_gap[0] - odd_gap[1], even_gap[1] + odd_gap[0]),
+        (even_sum[0] - odd_sum[0], even_sum[1] - odd_sum[1]),
+        (even_gap[0] + odd_gap[1], even_gap[1] - odd_gap[0]),
+    )
+
+
+def store_split(coarse_ref, fine_ref, where, value):
+    coarse = value.astype(jnp.bfloat16)
+    coarse_ref[where] = coarse
+    fine_ref[where] = (value - coarse.astype(jnp.float32)).astype(jnp.bfloat16)
+
+
+def triple_dot(matrix_ref, e, coarse, fine, dims):
+    def product(a, b):
+        return lax.dot_general(a, b, (dims, ((), ())), preferred_element_type=jnp.float32)
+
+    return product(matrix_ref[0, e], coarse) + (
+        product(matrix_ref[0, e], fine) + product(matrix_ref[1, e], coarse)
+    )
+
+
+def outer_kernel(base, params_ref, phase_ref, matrix_ref, twist_ref, out_ref, coarse_ref, fine_ref):
+    scale, exponent, inverse_coherence = params_ref[0], params_ref[1], params_ref[2]
+    rows = phase_ref.shape[3]
+    first_lane = base + pl.program_id(0) * LANES
+    lane = lax.broadcasted_iota(jnp.int32, (STEP, LANES), 1) + first_lane
+    row = lax.broadcasted_iota(jnp.int32, (STEP, LANES), 0)
+    place = row * INNER + lane
+
+    def some_rows(step, carry):
+        b = step * STEP
+        tracks = []
+        for a in range(RADIX):
+            k1 = a * QUARTER + b
+            source, inside = k1 // rows, pl.multiple_of(k1 % rows, STEP)
+            freq = (place + k1 * INNER).astype(jnp.float32)
+            left = phase_ref[source, 0, 0, pl.ds(inside, STEP), :]
+            right = phase_ref[source, 1, 0, pl.ds(inside, STEP), :]
+            tracks.append(line_spectra(left, right, freq, scale, exponent, inverse_coherence))
+        for t in range(2):
+            mixed = radix_four([track[t] for track in tracks])
+            for e in range(RADIX):
+                for ri in range(2):
+                    at = pl.ds(pl.multiple_of(ri * QUARTER + b, STEP), STEP)
+                    store_split(coarse_ref, fine_ref, (e, at, pl.ds(t * LANES, LANES)), mixed[e][ri])
+        return carry
+
+    lax.fori_loop(0, QUARTER // STEP, some_rows, 0)
+    for e in range(RADIX):
+        mid = triple_dot(matrix_ref, e, coarse_ref[e], fine_ref[e], ((1,), (0,)))
+        cos_part, sin_part = twist_ref[0, e], twist_ref[1, e]
+        for t in range(2):
+            real = mid[:QUARTER, t * LANES : (t + 1) * LANES]
+            imag = mid[QUARTER:, t * LANES : (t + 1) * LANES]
+            out_ref[t, 0, pl.ds(e, QUARTER, stride=RADIX), :] = real * cos_part - imag * sin_part
+            out_ref[t, 1, pl.ds(e, QUARTER, stride=RADIX), :] = real * sin_part + imag * cos_part
+
+
+def inner_kernel(*refs):
+    mid_refs, (matrix_ref, out_ref, coarse_ref, fine_ref) = refs[:-4], refs[-4:]
+    wide, columns = mid_refs[0].shape[2:]
+    shards, _, _, rows, _ = out_ref.shape
+
+    def some_rows(step, carry):
+        at = pl.multiple_of(step * STEP, STEP)
+        for t in range(2):
+            for half in range(0, QUARTER, 128):
+                parts = [
+                    tuple(
+                        mid_refs[(a * QUARTER + half) // columns][
+                            t, ri, pl.ds(at, STEP), pl.ds((a * QUARTER + half) % columns, 128)
+                        ]
+                        for ri in range(2)
+                    )
+                    for a in range(RADIX)
+                ]
+                mixed = radix_four(parts)
+                for e in range(RADIX):
+                    for ri in range(2):
+                        where = (
+                            e,
+                            pl.ds(pl.multiple_of(t * wide + at, STEP), STEP),
+                            pl.ds(ri * QUARTER + half, 128),
+                        )
+                        store_split(coarse_ref, fine_ref, where, mixed[e][ri])
+        return carry
+
+    lax.fori_loop(0, wide // STEP, some_rows, 0)
+    some = rows // RADIX
+    for e in range(RADIX):
+        value = triple_dot(matrix_ref, e, coarse_ref[e], fine_ref[e], ((1,), (1,)))
+        for t in range(2):
+            for f in range(shards):
+                for tile in range(wide // LANES):
+                    lanes = t * wide + tile * LANES
+                    out_ref[f, t, tile, pl.ds(e, some, stride=RADIX), :] = value[
+                        f * some : (f + 1) * some, lanes : lanes + LANES
+                    ]
+
+
+def part_kernel(left_ref, right_ref, *out_refs):
+    members, _, tiles, rows, _ = out_refs[0].shape
+    flat_refs = [ref.reshape(members * 2 * tiles * rows, LANES) for ref in out_refs]
+    for t, ref in enumerate((left_ref, right_ref)):
+        for r in range(rows):
+            for part, flat_ref in enumerate(flat_refs):
+                for tile in range(tiles):
+                    at = r * INNER + (part * tiles + tile) * LANES
+                    start = (t * tiles + tile) * rows + r
+                    flat_ref[pl.ds(start, members, stride=2 * tiles * rows), :] = ref[:, at : at + LANES]
+
+
+def join_kernel(*refs):
+    out_ref = refs[-1]
+    members, _, tiles, rows, _ = refs[0].shape
+    flat_refs = [ref.reshape(members * 2 * tiles * rows, LANES) for ref in refs[:-1]]
+    for t in range(2):
+        for r in range(rows):
+            for part, flat_ref in enumerate(flat_refs):
+                for tile in range(tiles):
+                    at = r * INNER + (part * tiles + tile) * LANES
+                    start = (t * tiles + tile) * rows + r
+                    out_ref[t, :, at : at + LANES] = flat_ref[
+                        pl.ds(start, members, stride=2 * tiles * rows), :
+                    ]
+
+
+def limits():
+    return pltpu.CompilerParams(vmem_limit_bytes=VMEM_LIMIT)
+
+
+def part_call(phase_left, phase_right, parts):
+    members, length = phase_left.shape
+    rows = length // INNER
+    tiles = INNER // parts // LANES
+    return pl.pallas_call(
+        part_kernel,
+        grid=(rows // BLOCK_ROWS,),
+        in_specs=[pl.BlockSpec((members, BLOCK_ROWS * INNER), lambda g: (0, g))] * 2,
+        out_specs=[pl.BlockSpec((members, 2, tiles, BLOCK_ROWS, LANES), lambda g: (0, 0, 0, g, 0))] * parts,
+        out_shape=[jax.ShapeDtypeStruct((members, 2, tiles, rows, LANES), jnp.float32)] * parts,
+        compiler_params=limits(),
+        cost_estimate=pl.CostEstimate(flops=0, bytes_accessed=16 * members * length, transcendentals=0),
+    )(phase_left, phase_right)
+
+
+def join_call(pieces):
+    members, _, tiles, rows, _ = pieces[0].shape
+    return pl.pallas_call(
+        join_kernel,
+        grid=(rows // BLOCK_ROWS,),
+        in_specs=[pl.BlockSpec((members, 2, tiles, BLOCK_ROWS, LANES), lambda g: (0, 0, 0, g, 0))]
+        * len(pieces),
+        out_specs=pl.BlockSpec((2, members, BLOCK_ROWS * INNER), lambda g: (0, 0, g)),
+        out_shape=jax.ShapeDtypeStruct((2, members, rows * INNER), jnp.float32),
+        compiler_params=limits(),
+        cost_estimate=pl.CostEstimate(flops=0, bytes_accessed=16 * members * rows * INNER, transcendentals=0),
+    )(*pieces)
+
+
+def outer_call(params, phases, matrices, twists, part):
+    sources, _, tiles, rows, _ = phases.shape
+    columns = tiles * LANES
+    return pl.pallas_call(
+        functools.partial(outer_kernel, part * columns),
+        grid=(columns // LANES,),
+        in_specs=[
+            pl.BlockSpec(memory_space=pltpu.SMEM),
+            pl.BlockSpec((sources, 2, 1, rows, LANES), lambda g: (0, 0, g, 0, 0)),
+            pl.BlockSpec(matrices.shape, lambda g: (0, 0, 0, 0)),
+            pl.BlockSpec(
+                (2, RADIX, QUARTER, LANES), lambda g: (0, 0, 0, part * (columns // LANES) + g)
+            ),
+        ],
+        out_specs=pl.BlockSpec((2, 2, OUTER, LANES), lambda g: (0, 0, 0, g)),
+        out_shape=jax.ShapeDtypeStruct((2, 2, OUTER, columns), jnp.float32),
+        scratch_shapes=[pltpu.VMEM((RADIX, 2 * QUARTER, 2 * LANES), jnp.bfloat16)] * 2,
+        compiler_params=limits(),
+        cost_estimate=pl.CostEstimate(
+            flops=48 * OUTER * QUARTER * columns, bytes_accessed=32 * OUTER * columns, transcendentals=0
+        ),
+    )(params, phases, matrices, twists)
+
+
+def inner_call(mids, matrices, shards, part, parts):
+    wide = WIDE
+    rows = INNER // shards
+    columns = OUTER // parts
+    blocks = columns // wide
+
+    return pl.pallas_call(
+        inner_kernel,
+        grid=(blocks,),
+        in_specs=[
+            pl.BlockSpec((2, 2, wide, mid.shape[-1]), lambda g: (0, 0, part * blocks + g, 0)) for mid in mids
+        ]
+        + [pl.BlockSpec(matrices.shape, lambda g: (0, 0, 0, 0))],
+        out_specs=pl.BlockSpec((shards, 2, wide // LANES, rows, LANES), lambda g: (0, 0, g, 0, 0)),
+        out_shape=jax.ShapeDtypeStruct((shards, 2, columns // LANES, rows, LANES), jnp.float32),
+        scratch_shapes=[pltpu.VMEM((RADIX, 2 * wide, 2 * QUARTER), jnp.bfloat16)] * 2,
+        compiler_params=limits(),
+        cost_estimate=pl.CostEstimate(
+            flops=24 * OUTER * QUARTER * columns, bytes_accessed=24 * OUTER * columns, transcendentals=0
+        ),
+    )(*mids, matrices)
+
+
+def per_device_whole(phase_left, phase_right, roughness, waviness, coherence):
+    local_members, local_len = phase_left.shape
+    shards = lax.axis_size("len")
+    my_index = lax.axis_index("len")
+    points = OUTER * INNER
+
+    def own(values):
+        return lax.dynamic_index_in_dim(values, my_index, 0, keepdims=False)
+
+    def swap(piece):
+        return lax.all_to_all(piece, "len", split_axis=0, concat_axis=0, tiled=True)
+
+    params = jnp.stack(
+        [
+            own(jnp.sqrt(2.0 * roughness * (waviness - 1.0) / ANCHOR)),
+            own(-0.5 * waviness),
+            own(1.0 / coherence),
+        ]
+    )
+    outer_tables = jnp.asarray(outer_matrices())
+    inner_tables = jnp.asarray(inner_matrices())
+    twists = jnp.asarray(twist_tables())
+    mids = [
+        outer_call(params, swap(piece), outer_tables, twists, part)
+        for part, piece in enumerate(part_call(phase_left, phase_right, IN_PARTS))
+    ]
+    pieces = [swap(inner_call(mids, inner_tables, shards, part, OUT_PARTS)) for part in range(OUT_PARTS)]
+    profile = join_call(pieces)
+    groups = lax.axis_size("mem")
+    stretch = local_len // groups
+    stretches = jnp.stack([profile[:, :, q * stretch : (q + 1) * stretch] for q in range(groups)])
+    together = lax.all_to_all(stretches, "mem", split_axis=0, concat_axis=0, tiled=True)
+    gram_matrix = sum(
+        gram_of(together[:, t].reshape(1, groups * local_members, stretch)) for t in range(2)
+    )
+    gram_matrix = lax.psum(gram_matrix, ("len", "mem")) * (0.5 / points)
+    return (profile, upper_of(gram_matrix))
+
+
+def per_device(phase_left, phase_right, roughness, waviness, coherence):
+    whole_members = phase_left.shape[0] == lax.axis_size("len")
+    form = per_device_whole if whole_members else per_device_spread
+    return form(phase_left, phase_right, roughness, waviness, coherence)
+
+
 def solution(mesh):
     placed = (P("mem", "len"), P("mem", "len"), P("mem"), P("mem"), P("mem"))
     return jax.shard_map(

time: 1360 us -> 510 us (0.38)
  waiting for transfers between devices: 694 us -> 62.5 us
  matrix products: 356 us -> 6.9 us
  blocking collectives: 9.17 us -> 334 us
  local copies, waits for them, and re-layouts: 135 us -> 8.86 us
  other arithmetic: 115 us -> 6.9 us
  Pallas kernels: 0 us -> 80.1 us
  starting transfers between devices: 26.1 us -> 9.31 us
  between operations: 14.5 us -> 0.73 us
    all_gather x1 -> x0, waiting for transfers between devices: 434 us -> none  [per_device(): gathered = lax.all_gather(snapshot, 'mem', axis=1, tiled=True)]
    dot_general x20 -> x0, matrix products: 325 us -> none  [the longest x1 60.8 us: per_device(): second = jnp.einsum('jqa,qiac->cij', outer_sin, imag_in, precision=highest)]
    all_to_all x0 -> x3, blocking collectives: none -> 296 us  [the longest x1 188 us: per_device_whole(): lax.all_to_all(stretches, 'mem', split_axis=0, concat_axis=0, tiled=True)]
    all_to_all x5 -> x2, waiting for transfers between devices: 260 us -> 62.5 us  [swap(): return lax.all_to_all(piece, 'len', split_axis=0, concat_axis=0, tiled=True)]
    pallas_call x0 -> x6, Pallas kernels: none -> 80.1 us  [the longest x2 40.4 us: outer_call(): pl.pallas_call(functools.partial(outer_kernel, part * columns), grid=(col...]
    reshape x5 -> x0, local copies, waits for them, and re-layouts: 43.1 us -> none  [the longest x1 9.24 us: per_device(): twist_cos = jnp.repeat(jnp.cos(twist), columns, axis=1)]
    mul x3 -> x1, other arithmetic: 39.7 us -> 0.01 us  [per_device_whole(): gram_matrix = lax.psum(gram_matrix, ('len', 'mem')) * (0.5 / points)]
    psum x0 -> x1, blocking collectives: none -> 38 us  [per_device_whole(): gram_matrix = lax.psum(gram_matrix, ('len', 'mem')) * (0.5 / points)]
  transfers between devices with their start and end apart: 6 -> 2, of which waited for: 6 -> 2; matrix products, arithmetic and copies ran while one was open for 18% -> 1% of each run, Pallas kernels for 0% -> 6%
where the time goes in v1:
time: 510 us; the launch traced here: 509 us
  blocking collectives  334 us (65%)
  Pallas kernels  80.1 us (16%)
  waiting for transfers between devices  62.5 us (12%)
  starting transfers between devices  9.31 us (2%)
  local copies, waits for them, and re-layouts  8.86 us (2%)
  other arithmetic  6.9 us (1%)
  matrix products  6.9 us (1%)
    all_to_all x1, blocking collectives, per_device_whole(): lax.all_to_all(stretches, 'mem', split_axis=0, concat_axis=0, tiled=True)  188 us
    all_to_all x2, blocking collectives, swap(): return lax.all_to_all(piece, 'len', split_axis=0, concat_axis=0, tiled=True)  108 us
    all_to_all x2, waiting for transfers between devices, swap(): return lax.all_to_all(piece, 'len', split_axis=0, concat_axis=0, tiled=True)  62.5 us
    pallas_call x2, Pallas kernels, outer_call(): pl.pallas_call(functools.partial(outer_kernel, part * columns), grid=(col...  40.4 us
    psum x1, blocking collectives, per_device_whole(): gram_matrix = lax.psum(gram_matrix, ('len', 'mem')) * (0.5 / points)  38 us
    pallas_call x2, Pallas kernels, inner_call(): pl.pallas_call(inner_kernel, grid=(blocks,), in_specs=[pl.BlockSpec((2, 2...  18.9 us
    pallas_call x1, Pallas kernels, join_call(): pl.pallas_call(join_kernel, grid=(rows // BLOCK_ROWS,), in_specs=[pl.Bloc...  10.5 us
    pallas_call x1, Pallas kernels, part_call(): pl.pallas_call(part_kernel, grid=(rows // BLOCK_ROWS,), in_specs=[pl.Bloc...  10.2 us
  transfers between devices with their start and end apart: 2, of which 2 were waited for; matrix products, arithmetic and copies ran while one was open for 1% of the time, Pallas kernels for 6%

profile of v1, /device:TPU:0, one launch (start us, length us, event | category | flops | bytes accessed | tf_op | source)
XLA Modules:
  0.0 509.3 jit_solution(13565381326589357921)
XLA Ops:
  0.6 10.2 %shard_map.95 = (f32[8,2,4,128,128]{4,3,2,1,0:T(8,128)S(1)}, f32[8,2,4,128,128]{4,3,2,1,0:T(8,128)}) custom-call(f32[8,131072]{1,0:T(8,128)} %left_ref.1, f32[8,131072]{1,0:T(8,128)} %right_ref.1), custom_call_target="tpu_custom_call" | custom-call | bytes 16777216 | tf_op jit(solution)/shard_map/pallas_call | solution.py:364
  10.9 0.0 copy-start.2
  10.9 54.3 %all_to_all.25.phase_ref = f32[8,2,4,128,128]{4,3,2,1,0:T(8,128)} all-to-all(f32[8,2,4,128,128]{4,3,2,1,0:T(8,128)} %get-tuple-element.5), channel_id=1, replica_groups=mesh['len'=8,'mem'=4] {'len'}, dimensions={0} | all-to-all | bytes 8388608 | tf_op jit(solution)/shard_map/all_to_all | solution.py:446
  65.2 0.0 copy-done.2
  65.2 0.0 copy-start.5
  65.2 0.0 copy-start.3
  65.2 0.0 copy-start.4
  65.2 4.7 all-to-all-start
  69.9 0.0 copy-done.5
  70.0 0.6 dynamic_slice.12
  70.5 0.0 copy-done.3
  70.5 0.0 copy-done.4
  70.6 0.6 dynamic_slice.11
  71.1 0.6 dynamic_slice.10
  71.8 2.0 pad_maximum_fusion.1.params_ref
  73.8 0.0 copy-start
  73.8 2.2 copy-done
  76.0 20.2 %shard_map.97.refs_1_ = f32[2,2,1024,512]{3,2,1,0:T(8,128)} custom-call(f32[3]{0:T(128)S(1)} %pad_maximum_fusion.1.params_ref, f32[8,2,4,128,128]{4,3,2,1,0:T(8,128)S(1)} %copy-done, bf16[2,4,512,512]{3,2,1,0:T(8,128)(2,1)} %constant.72.clone.matrix_ref, f32[2,4,256,1024]{3,2,1,0:T(8,128)} %constant.74.clone.twist_ref), custom_call_target="tpu_custom_call" | custom-call | flops 6442450944 | bytes 16777216 | tf_op jit(solution)/shard_map/pallas_call | solution.py:392
  96.3 0.0 copy-start.1
  96.3 22.8 %all-to-all-done.phase_ref = f32[8,2,4,128,128]{4,3,2,1,0:T(8,128)} async-done(((f32[8,2,4,128,128]{4,3,2,1,0:T(8,128)}), f32[8,2,4,128,128]{4,3,2,1,0:T(8,128)}, u32[]{:S(2)}, u32[]{:S(2)}) %all-to-all-start) | async-done | bytes 4194336 | tf_op jit(solution)/shard_map/all_to_all | solution.py:446
  119.1 20.2 %shard_map.96.refs_0_ = f32[2,2,1024,512]{3,2,1,0:T(8,128)} custom-call(f32[3]{0:T(128)S(1)} %pad_maximum_fusion.1.params_ref, f32[8,2,4,128,128]{4,3,2,1,0:T(8,128)} %all-to-all-done.phase_ref, bf16[2,4,512,512]{3,2,1,0:T(8,128)(2,1)} %constant.72.clone.matrix_ref, f32[2,4,256,1024]{3,2,1,0:T(8,128)} %constant.74.clone.twist_ref), custom_call_target="tpu_custom_call" | custom-call | flops 6442450944 | bytes 16777216 | tf_op jit(solution)/shard_map/pallas_call | solution.py:392
  139.3 0.0 copy-done.1
  139.3 9.5 %shard_map.98 = f32[8,2,4,128,128]{4,3,2,1,0:T(8,128)} custom-call(f32[2,2,1024,512]{3,2,1,0:T(8,128)} %shard_map.96.refs_0_, f32[2,2,1024,512]{3,2,1,0:T(8,128)} %shard_map.97.refs_1_, bf16[2,4,256,512]{3,2,1,0:T(8,128)(2,1)S(1)} %copy-done.1), custom_call_target="tpu_custom_call" | custom-call | flops 3221225472 | bytes 12582912 | tf_op jit(solution)/shard_map/pallas_call | solution.py:419
  148.7 4.6 all-to-all-start.2
  153.3 9.4 %shard_map.99 = f32[8,2,4,128,128]{4,3,2,1,0:T(8,128)} custom-call(f32[2,2,1024,512]{3,2,1,0:T(8,128)} %shard_map.96.refs_0_, f32[2,2,1024,512]{3,2,1,0:T(8,128)} %shard_map.97.refs_1_, bf16[2,4,256,512]{3,2,1,0:T(8,128)(2,1)S(1)} %copy-done.1), custom_call_target="tpu_custom_call" | custom-call | flops 3221225472 | bytes 12582912 | tf_op jit(solution)/shard_map/pallas_call | solution.py:419
  162.8 39.7 %all-to-all-done.2.refs_0_ = f32[8,2,4,128,128]{4,3,2,1,0:T(8,128)} async-done(((f32[8,2,4,128,128]{4,3,2,1,0:T(8,128)}), f32[8,2,4,128,128]{4,3,2,1,0:T(8,128)}, u32[]{:S(2)}, u32[]{:S(2)}) %all-to-all-start.2) | async-done | bytes 4194336 | tf_op jit(solution)/shard_map/all_to_all | solution.py:446
  202.5 53.6 %all_to_all.26.refs_1_ = f32[8,2,4,128,128]{4,3,2,1,0:T(8,128)} all-to-all(f32[8,2,4,128,128]{4,3,2,1,0:T(8,128)} %shard_map.99), channel_id=1, replica_groups=mesh['len'=8,'mem'=4] {'len'}, dimensions={0} | all-to-all | bytes 8388608 | tf_op jit(solution)/shard_map/all_to_all | solution.py:446
  256.0 10.5 %shard_map.100 = f32[2,8,131072]{2,1,0:T(8,128)} custom-call(f32[8,2,4,128,128]{4,3,2,1,0:T(8,128)} %all-to-all-done.2.refs_0_, f32[8,2,4,128,128]{4,3,2,1,0:T(8,128)} %all_to_all.26.refs_1_), custom_call_target="tpu_custom_call" | custom-call | bytes 16777216 | tf_op jit(solution)/shard_map/pallas_call | solution.py:377
  266.5 4.1 slice_bitcast_fusion.7
  270.6 0.6 pad_maximum_fusion
  271.2 188.1 %all_to_all.27 = f32[4,2,8,32768]{3,2,1,0:T(8,128)S(1)} all-to-all(f32[4,2,8,32768]{3,2,1,0:T(8,128)S(1)} %pad_maximum_fusion), channel_id=1, replica_groups=mesh['len'=8,'mem'=4] {'mem'}, dimensions={0} | all-to-all | bytes 16777216 | tf_op jit(solution)/shard_map/all_to_all | solution.py:467
  459.3 3.4 fusion
  462.7 3.5 fusion.2
  466.2 38.0 %psum.7 = f32[32,32]{0,1:T(8,128)S(1)} all-reduce(f32[32,32]{0,1:T(8,128)S(1)} %fusion.2), channel_id=1, replica_groups=mesh['len'=8,'mem'=4] {'len','mem'}, use_global_device_ids=true, to_apply=%region_0.1 | all-reduce | flops 1024 | bytes 8192 | tf_op jit(solution)/shard_map/psum | solution.py:471
  504.3 0.1 copy.12
  504.4 2.9 cholesky.18
  507.3 0.6 compare_reduce_fusion
  508.0 0.6 select_bitcast_fusion
  508.6 0.7 copy.13
  (5 shorter events, 0.1 us)
Async XLA Ops:
  10.9 54.3 %copy-start.2 = (f32[8,2,4,128,128]{4,3,2,1,0:T(8,128)}, f32[8,2,4,128,128]{4,3,2,1,0:T(8,128)S(1)}, u32[]{:S(2)}) copy-start(f32[8,2,4,128,128]{4,3,2,1,0:T(8,128)S(1)} %get-tuple-element.4) | copy-start | bytes 12582916
  65.2 4.7 copy-start.5
  65.2 5.3 %copy-start.3 = (f32[8]{0:T(128)S(1)}, f32[8]{0:T(128)}, u32[]{:S(2)}) copy-start(f32[8]{0:T(128)} %param.11) | copy-start | bytes 100
  65.2 5.3 %copy-start.4 = (f32[8]{0:T(128)S(1)}, f32[8]{0:T(128)}, u32[]{:S(2)}) copy-start(f32[8]{0:T(128)} %param.10) | copy-start | bytes 100
  65.2 53.8 %all-to-all-start = ((f32[8,2,4,128,128]{4,3,2,1,0:T(8,128)}), f32[8,2,4,128,128]{4,3,2,1,0:T(8,128)}, u32[]{:S(2)}, u32[]{:S(2)}) async-start(f32[8,2,4,128,128]{4,3,2,1,0:T(8,128)} %copy-done.2), calls=%async_computation | async-start | bytes 8388608 | tf_op jit(solution)/shard_map/all_to_all | solution.py:446
  73.8 2.2 copy-start
  96.3 43.0 %copy-start.1 = (bf16[2,4,256,512]{3,2,1,0:T(8,128)(2,1)S(1)}, bf16[2,4,256,512]{3,2,1,0:T(8,128)(2,1)}, u32[]{:S(2)}) copy-start(bf16[2,4,256,512]{3,2,1,0:T(8,128)(2,1)} %constant.73.clone.refs_2_) | copy-start | bytes 6291460
  148.7 53.7 %all-to-all-start.2 = ((f32[8,2,4,128,128]{4,3,2,1,0:T(8,128)}), f32[8,2,4,128,128]{4,3,2,1,0:T(8,128)}, u32[]{:S(2)}, u32[]{:S(2)}) async-start(f32[8,2,4,128,128]{4,3,2,1,0:T(8,128)} %shard_map.98), calls=%async_computation.2 | async-start | bytes 8388608 | tf_op jit(solution)/shard_map/all_to_all | solution.py:446

commit v2 on v1

--- a/solution.py
+++ b/solution.py
@@ -19,7 +19,7 @@
 WIDE = 256
 BLOCK_ROWS = 16
 IN_PARTS = 2
-OUT_PARTS = 2
+MIRROR_BLOCK = 2048
 VMEM_LIMIT = 48 * 1024 * 1024
 SIN_HALF = (0.49999999785787, -0.02083332246218, 2.604078316692e-4, -1.547581723527e-6, 5.088214043e-9)
 COS_HALF = (
@@ -287,103 +287,162 @@
 def inner_kernel(*refs):
     mid_refs, (matrix_ref, out_ref, coarse_ref, fine_ref) = refs[:-4], refs[-4:]
     wide, columns = mid_refs[0].shape[2:]
-    shards, _, _, rows, _ = out_ref.shape
+    shards, _, rows, _ = out_ref.shape
 
     def some_rows(step, carry):
         at = pl.multiple_of(step * STEP, STEP)
-        for t in range(2):
-            for half in range(0, QUARTER, 128):
-                parts = [
-                    tuple(
-                        mid_refs[(a * QUARTER + half) // columns][
-                            t, ri, pl.ds(at, STEP), pl.ds((a * QUARTER + half) % columns, 128)
-                        ]
-                        for ri in range(2)
-                    )
-                    for a in range(RADIX)
-                ]
-                mixed = radix_four(parts)
-                for e in range(RADIX):
-                    for ri in range(2):
-                        where = (
-                            e,
-                            pl.ds(pl.multiple_of(t * wide + at, STEP), STEP),
-                            pl.ds(ri * QUARTER + half, 128),
-                        )
-                        store_split(coarse_ref, fine_ref, where, mixed[e][ri])
+        for half in range(0, QUARTER, LANES):
+            parts = [
+                tuple(
+                    mid_refs[(a * QUARTER + half) // columns][
+                        0, ri, pl.ds(at, STEP), pl.ds((a * QUARTER + half) % columns, LANES)
+                    ]
+                    for ri in range(2)
+                )
+                for a in range(RADIX)
+            ]
+            mixed = radix_four(parts)
+            for e in range(RADIX):
+                for ri in range(2):
+                    where = (e, pl.ds(at, STEP), pl.ds(ri * QUARTER + half, LANES))
+                    store_split(coarse_ref, fine_ref, where, mixed[e][ri])
         return carry
 
     lax.fori_loop(0, wide // STEP, some_rows, 0)
     some = rows // RADIX
     for e in range(RADIX):
         value = triple_dot(matrix_ref, e, coarse_ref[e], fine_ref[e], ((1,), (1,)))
-        for t in range(2):
-            for f in range(shards):
-                for tile in range(wide // LANES):
-                    lanes = t * wide + tile * LANES
-                    out_ref[f, t, tile, pl.ds(e, some, stride=RADIX), :] = value[
-                        f * some : (f + 1) * some, lanes : lanes + LANES
-                    ]
-
-
-def part_kernel(left_ref, right_ref, *out_refs):
-    members, _, tiles, rows, _ = out_refs[0].shape
-    flat_refs = [ref.reshape(members * 2 * tiles * rows, LANES) for ref in out_refs]
+        for f in range(shards):
+            for tile in range(wide // LANES):
+                out_ref[f, tile, pl.ds(e, some, stride=RADIX), :] = value[
+                    f * some : (f + 1) * some, tile * LANES : (tile + 1) * LANES
+                ]
+
+
+def part_kernel(part, left_ref, right_ref, out_ref):
+    members, _, tiles, rows, _ = out_ref.shape
+    flat_ref = out_ref.reshape(members * 2 * tiles * rows, LANES)
     for t, ref in enumerate((left_ref, right_ref)):
         for r in range(rows):
-            for part, flat_ref in enumerate(flat_refs):
-                for tile in range(tiles):
-                    at = r * INNER + (part * tiles + tile) * LANES
-                    start = (t * tiles + tile) * rows + r
-                    flat_ref[pl.ds(start, members, stride=2 * tiles * rows), :] = ref[:, at : at + LANES]
+            for tile in range(tiles):
+                at = r * INNER + (part * tiles + tile) * LANES
+                start = (t * tiles + tile) * rows + r
+                flat_ref[pl.ds(start, members, stride=2 * tiles * rows), :] = ref[:, at : at + LANES]
 
 
 def join_kernel(*refs):
-    out_ref = refs[-1]
-    members, _, tiles, rows, _ = refs[0].shape
-    flat_refs = [ref.reshape(members * 2 * tiles * rows, LANES) for ref in refs[:-1]]
-    for t in range(2):
-        for r in range(rows):
-            for part, flat_ref in enumerate(flat_refs):
-                for tile in range(tiles):
-                    at = r * INNER + (part * tiles + tile) * LANES
-                    start = (t * tiles + tile) * rows + r
-                    out_ref[t, :, at : at + LANES] = flat_ref[
-                        pl.ds(start, members, stride=2 * tiles * rows), :
-                    ]
+    in_ref, out_ref = refs[0], refs[-1]
+    members, tiles, rows, _ = in_ref.shape
+    flat_ref = in_ref.reshape(members * tiles * rows, LANES)
+    for r in range(rows):
+        for tile in range(tiles):
+            at = r * INNER + tile * LANES
+            out_ref[0, :, at : at + LANES] = flat_ref[pl.ds(tile * rows + r, members, stride=tiles * rows), :]
+
+
+def mirror_kernel(base_ref, params_ref, *refs):
+    slots = (len(refs) - 2) // 2
+    own_refs, far_refs, (out_ref, last_ref) = refs[:slots], refs[slots : 2 * slots], refs[2 * slots :]
+    _, members, block = own_refs[0].shape
+    tiles = block // LANES
+    first = pl.program_id(0) * block
+    shape = (2 * members, LANES)
+    lane = lax.broadcasted_iota(jnp.int32, shape, 1)
+    mirror = (LANES - lane) % LANES
+
+    @pl.when(pl.program_id(0) == 0)
+    def _():
+        last_ref[...] = jnp.zeros_like(last_ref)
+
+    def one_tile(tile, carry):
+        at = pl.ds(pl.multiple_of(tile * LANES, LANES), LANES)
+        far_at = pl.ds(pl.multiple_of((tiles - 1 - tile) * LANES, LANES), LANES)
+        offset = first + tile * LANES + lane
+        freq = (base_ref[0] + offset).astype(jnp.float32)
+        far_freq = (OUTER * INNER - base_ref[0] - offset).astype(jnp.float32)
+        inner = offset > 0
+        for pair in range(slots // 2):
+            rows = slice(2 * members * pair, 2 * members * (pair + 1))
+            own, far = [], []
+            for t in range(2):
+                own.append(
+                    jnp.concatenate([own_refs[2 * pair][t, :, at], own_refs[2 * pair + 1][t, :, at]], axis=0)
+                )
+                ahead = jnp.concatenate(
+                    [far_refs[2 * pair][t, :, far_at], far_refs[2 * pair + 1][t, :, far_at]], axis=0
+                )
+                turned = jnp.take_along_axis(ahead, mirror, axis=1, mode="promise_in_bounds")
+                far.append(jnp.where(lane == 0, last_ref[pair, t], turned))
+                last_ref[pair, t] = turned
+            scale, exponent, inverse_coherence = (params_ref[n, rows, :] for n in range(3))
+            near_lines = line_spectra(*own, freq, scale, exponent, inverse_coherence)
+            far_lines = line_spectra(*far, far_freq, scale, exponent, inverse_coherence)
+            for t in range(2):
+                real = near_lines[t][0] + far_lines[t][0]
+                imag = near_lines[t][1] - far_lines[t][1]
+                out_ref[t, 0, rows, at] = jnp.where(inner, real, 0.0)
+                out_ref[t, 1, rows, at] = jnp.where(inner, imag, 0.0)
+        return carry
+
+    lax.fori_loop(0, tiles, one_tile, 0)
 
 
 def limits():
     return pltpu.CompilerParams(vmem_limit_bytes=VMEM_LIMIT)
 
 
-def part_call(phase_left, phase_right, parts):
+def part_call(phase_left, phase_right, part, parts):
     members, length = phase_left.shape
     rows = length // INNER
     tiles = INNER // parts // LANES
     return pl.pallas_call(
-        part_kernel,
+        functools.partial(part_kernel, part),
         grid=(rows // BLOCK_ROWS,),
         in_specs=[pl.BlockSpec((members, BLOCK_ROWS * INNER), lambda g: (0, g))] * 2,
-        out_specs=[pl.BlockSpec((members, 2, tiles, BLOCK_ROWS, LANES), lambda g: (0, 0, 0, g, 0))] * parts,
-        out_shape=[jax.ShapeDtypeStruct((members, 2, tiles, rows, LANES), jnp.float32)] * parts,
+        out_specs=pl.BlockSpec((members, 2, tiles, BLOCK_ROWS, LANES), lambda g: (0, 0, 0, g, 0)),
+        out_shape=jax.ShapeDtypeStruct((members, 2, tiles, rows, LANES), jnp.float32),
         compiler_params=limits(),
         cost_estimate=pl.CostEstimate(flops=0, bytes_accessed=16 * members * length, transcendentals=0),
     )(phase_left, phase_right)
 
 
-def join_call(pieces):
-    members, _, tiles, rows, _ = pieces[0].shape
+def join_call(piece, track, so_far):
+    members, tiles, rows, _ = piece.shape
+    operands = (piece,) if so_far is None else (piece, so_far)
     return pl.pallas_call(
         join_kernel,
         grid=(rows // BLOCK_ROWS,),
-        in_specs=[pl.BlockSpec((members, 2, tiles, BLOCK_ROWS, LANES), lambda g: (0, 0, 0, g, 0))]
-        * len(pieces),
-        out_specs=pl.BlockSpec((2, members, BLOCK_ROWS * INNER), lambda g: (0, 0, g)),
+        in_specs=[
+            pl.BlockSpec((members, tiles, BLOCK_ROWS, LANES), lambda g: (0, 0, g, 0)),
+            pl.BlockSpec(memory_space=pl.ANY),
+        ][: len(operands)],
+        out_specs=pl.BlockSpec((1, members, BLOCK_ROWS * INNER), lambda g: (track, 0, g)),
         out_shape=jax.ShapeDtypeStruct((2, members, rows * INNER), jnp.float32),
+        input_output_aliases={} if so_far is None else {1: 0},
         compiler_params=limits(),
-        cost_estimate=pl.CostEstimate(flops=0, bytes_accessed=16 * members * rows * INNER, transcendentals=0),
-    )(*pieces)
+        cost_estimate=pl.CostEstimate(flops=0, bytes_accessed=8 * members * rows * INNER, transcendentals=0),
+    )(*operands)
+
+
+def mirror_call(base, params, own, far):
+    _, members, width = own[0].shape
+    slots = len(own)
+    block = min(width, MIRROR_BLOCK)
+    blocks = width // block
+    return pl.pallas_call(
+        mirror_kernel,
+        grid=(blocks,),
+        in_specs=[pl.BlockSpec(memory_space=pltpu.SMEM), pl.BlockSpec(params.shape, lambda g: (0, 0, 0))]
+        + [pl.BlockSpec((2, members, block), lambda g: (0, 0, g))] * slots
+        + [pl.BlockSpec((2, members, block), lambda g: (0, 0, blocks - 1 - g))] * slots,
+        out_specs=pl.BlockSpec((2, 2, slots * members, block), lambda g: (0, 0, 0, g)),
+        out_shape=jax.ShapeDtypeStruct((2, 2, slots * members, width), jnp.float32),
+        scratch_shapes=[pltpu.VMEM((slots // 2, 2, 2 * members, LANES), jnp.float32)],
+        compiler_params=limits(),
+        cost_estimate=pl.CostEstimate(
+            flops=400 * slots * members * width, bytes_accessed=32 * slots * members * width, transcendentals=0
+        ),
+    )(base, params, *own, *far)
 
 
 def outer_call(params, phases, matrices, twists, part):
@@ -410,70 +469,133 @@
     )(params, phases, matrices, twists)
 
 
-def inner_call(mids, matrices, shards, part, parts):
-    wide = WIDE
+def inner_call(mids, matrices, shards, track):
     rows = INNER // shards
-    columns = OUTER // parts
-    blocks = columns // wide
-
     return pl.pallas_call(
         inner_kernel,
-        grid=(blocks,),
-        in_specs=[
-            pl.BlockSpec((2, 2, wide, mid.shape[-1]), lambda g: (0, 0, part * blocks + g, 0)) for mid in mids
-        ]
+        grid=(OUTER // WIDE,),
+        in_specs=[pl.BlockSpec((1, 2, WIDE, mid.shape[-1]), lambda g: (track, 0, g, 0)) for mid in mids]
         + [pl.BlockSpec(matrices.shape, lambda g: (0, 0, 0, 0))],
-        out_specs=pl.BlockSpec((shards, 2, wide // LANES, rows, LANES), lambda g: (0, 0, g, 0, 0)),
-        out_shape=jax.ShapeDtypeStruct((shards, 2, columns // LANES, rows, LANES), jnp.float32),
-        scratch_shapes=[pltpu.VMEM((RADIX, 2 * wide, 2 * QUARTER), jnp.bfloat16)] * 2,
+        out_specs=pl.BlockSpec((shards, WIDE // LANES, rows, LANES), lambda g: (0, g, 0, 0)),
+        out_shape=jax.ShapeDtypeStruct((shards, OUTER // LANES, rows, LANES), jnp.float32),
+        scratch_shapes=[pltpu.VMEM((RADIX, WIDE, 2 * QUARTER), jnp.bfloat16)] * 2,
         compiler_params=limits(),
         cost_estimate=pl.CostEstimate(
-            flops=24 * OUTER * QUARTER * columns, bytes_accessed=24 * OUTER * columns, transcendentals=0
+            flops=12 * OUTER * QUARTER * INNER, bytes_accessed=12 * OUTER * INNER, transcendentals=0
         ),
     )(*mids, matrices)
 
 
+def line_params(roughness, waviness, coherence):
+    return jnp.stack(
+        [jnp.sqrt(2.0 * roughness * (waviness - 1.0) / ANCHOR), -0.5 * waviness, 1.0 / coherence]
+    )
+
+
+def exchange_lines(phase_left, phase_right):
+    shards, groups = lax.axis_size("len"), lax.axis_size("mem")
+    my_group = lax.axis_index("mem")
+    half = phase_left.shape[1] // 2
+    width = half // groups
+
+    def lines(start):
+        return jnp.stack(
+            [lax.dynamic_slice_in_dim(phase, start, width, 1) for phase in (phase_left, phase_right)]
+        )
+
+    def to_group(piece, slot):
+        return lax.ppermute(piece, "mem", [(z, z ^ slot) for z in range(groups)]) if slot else piece
+
+    far = [
+        to_group(lines(half + (groups - 1 - (my_group ^ slot)) * width), slot) for slot in range(groups)
+    ]
+    own = [to_group(lines((my_group ^ slot) * width), slot) for slot in range(groups)]
+    far = [lax.ppermute(piece, "len", [(d, shards - 1 - d) for d in range(shards)]) for piece in far]
+    return own, far
+
+
+def edge_lines(phase_left, phase_right, params):
+    shards, groups = lax.axis_size("len"), lax.axis_size("mem")
+    members, local_len = phase_left.shape
+    edges = 2 * groups
+    width = local_len // edges
+    columns = [phase[:, n * width : n * width + 1] for phase in (phase_left, phase_right) for n in range(edges)]
+    everything = lax.all_gather(jnp.concatenate(columns + [params.T], axis=1), ("len", "mem"))
+    everything = everything.reshape(shards, groups, members, 2 * edges + 3)
+    all_params = everything[0, :, :, 2 * edges :]
+    phases = [
+        jnp.transpose(everything[..., n * edges : (n + 1) * edges], (1, 2, 0, 3)).reshape(
+            groups * members, shards * edges
+        )
+        for n in range(2)
+    ]
+    return phases, all_params, width
+
+
+def edge_gram(phases, all_params, width):
+    freq = (width * lax.iota(jnp.int32, phases[0].shape[1])).astype(jnp.float32)[None, :]
+    flat = all_params.reshape(-1, 3)
+    lines = line_spectra(*phases, freq, *(flat[:, n : n + 1] for n in range(3)))
+
+    def mirrored(value):
+        return jnp.roll(jnp.flip(value, axis=1), 1, axis=1)
+
+    both = jnp.stack(
+        [line[0] + mirrored(line[0]) for line in lines] + [line[1] - mirrored(line[1]) for line in lines]
+    )
+    return gram_of(both)
+
+
+def gram_by_lines(phase_left, phase_right, roughness, waviness, coherence):
+    shards, groups = lax.axis_size("len"), lax.axis_size("mem")
+    my_index, my_group = lax.axis_index("len"), lax.axis_index("mem")
+    members, local_len = phase_left.shape
+    own, far = exchange_lines(phase_left, phase_right)
+    phases, all_params, width = edge_lines(
+        phase_left, phase_right, line_params(roughness, waviness, coherence)
+    )
+    slot_params = jnp.concatenate(
+        [lax.dynamic_index_in_dim(all_params, my_group ^ slot, 0, keepdims=False) for slot in range(groups)]
+    )
+    slot_params = jnp.broadcast_to(slot_params.T[:, :, None], (3, groups * members, LANES))
+    base = (my_index * local_len + my_group * width).astype(jnp.int32).reshape(1)
+    sums = mirror_call(base, slot_params, own, far)
+    slot_gram = sum(gram_of(sums[t]) for t in range(2))
+    row = lax.broadcasted_iota(jnp.int32, slot_gram.shape, 0)
+    column = lax.broadcasted_iota(jnp.int32, slot_gram.shape, 1)
+    to_slot = (row % members == column % members) & ((row // members) ^ my_group == column // members)
+    to_slot = to_slot.astype(jnp.float32)
+    own_gram = jnp.dot(jnp.dot(to_slot, slot_gram, precision=highest), to_slot.T, precision=highest)
+    inner_gram = jnp.sum(lax.all_gather(own_gram, ("len", "mem")), axis=0)
+    return 0.25 * inner_gram + 0.125 * edge_gram(phases, all_params, width)
+
+
 def per_device_whole(phase_left, phase_right, roughness, waviness, coherence):
-    local_members, local_len = phase_left.shape
     shards = lax.axis_size("len")
     my_index = lax.axis_index("len")
-    points = OUTER * INNER
-
-    def own(values):
-        return lax.dynamic_index_in_dim(values, my_index, 0, keepdims=False)
 
     def swap(piece):
         return lax.all_to_all(piece, "len", split_axis=0, concat_axis=0, tiled=True)
 
-    params = jnp.stack(
-        [
-            own(jnp.sqrt(2.0 * roughness * (waviness - 1.0) / ANCHOR)),
-            own(-0.5 * waviness),
-            own(1.0 / coherence),
-        ]
+    params = lax.dynamic_index_in_dim(
+        line_params(roughness, waviness, coherence), my_index, 1, keepdims=False
     )
     outer_tables = jnp.asarray(outer_matrices())
     inner_tables = jnp.asarray(inner_matrices())
     twists = jnp.asarray(twist_tables())
-    mids = [
-        outer_call(params, swap(piece), outer_tables, twists, part)
-        for part, piece in enumerate(part_call(phase_left, phase_right, IN_PARTS))
-    ]
-    pieces = [swap(inner_call(mids, inner_tables, shards, part, OUT_PARTS)) for part in range(OUT_PARTS)]
-    profile = join_call(pieces)
-    groups = lax.axis_size("mem")
-    stretch = local_len // groups
-    stretches = jnp.stack([profile[:, :, q * stretch : (q + 1) * stretch] for q in range(groups)])
-    together = lax.all_to_all(stretches, "mem", split_axis=0, concat_axis=0, tiled=True)
-    gram_matrix = sum(
-        gram_of(together[:, t].reshape(1, groups * local_members, stretch)) for t in range(2)
-    )
-    gram_matrix = lax.psum(gram_matrix, ("len", "mem")) * (0.5 / points)
+    gram_matrix = gram_by_lines(phase_left, phase_right, roughness, waviness, coherence)
+    mids = []
+    for part in range(IN_PARTS):
+        piece = swap(part_call(phase_left, phase_right, part, IN_PARTS))
+        mids.append(outer_call(params, piece, outer_tables, twists, part))
+    profile = None
+    for track in range(2):
+        profile = join_call(swap(inner_call(mids, inner_tables, shards, track)), track, profile)
     return (profile, upper_of(gram_matrix))
 
 
 def per_device(phase_left, phase_right, roughness, waviness, coherence):
-    whole_members = phase_left.shape[0] == lax.axis_size("len")
+    whole_members = phase_left.shape[0] == lax.axis_size("len") and lax.axis_size("mem") in (2, 4)
     form = per_device_whole if whole_members else per_device_spread
     return form(phase_left, phase_right, roughness, waviness, coherence)
 

time: 510 us -> 570 us (1.12)
  blocking collectives: 334 us -> 245 us
  waiting for transfers between devices: 62.5 us -> 141 us
  Pallas kernels: 80.1 us -> 106 us
  starting transfers between devices: 9.31 us -> 34 us
  other arithmetic: 6.9 us -> 14.7 us
  matrix products: 6.9 us -> 14.6 us
    all_to_all x3 -> x0, blocking collectives: 296 us -> none  [the longest x1 188 us: per_device_whole(): lax.all_to_all(stretches, 'mem', split_axis=0, concat_axis=0, tiled=True)]
    all_gather x0 -> x2, blocking collectives: none -> 245 us  [the longest x1 176 us: edge_lines(): lax.all_gather(jnp.concatenate(columns + [params.T], axis=1), ('len', 'me...]
    ppermute x0 -> x10, waiting for transfers between devices: none -> 83 us  [the longest x4 83 us: exchange_lines(): lax.ppermute(piece, 'len', [(d, shards - 1 - d) for d in range(shards)])]
    psum x1 -> x0, blocking collectives: 38 us -> none  [per_device_whole(): gram_matrix = lax.psum(gram_matrix, ('len', 'mem')) * (0.5 / points)]
    pallas_call x3 -> x5, Pallas kernels: 29.1 us -> 49.8 us  [the longest x2 18.7 us: inner_call(): pl.pallas_call(inner_kernel, grid=(OUTER // WIDE,), in_specs=[pl.BlockSpe...]
    ppermute x0 -> x10, starting transfers between devices: none -> 14.8 us  [the longest x6 9.46 us: to_group(): lax.ppermute(piece, 'mem', [(z, z ^ slot) for z in range(groups)])]
    all_to_all x2 -> x4, starting transfers between devices: 9.31 us -> 19.1 us  [swap(): return lax.all_to_all(piece, 'len', split_axis=0, concat_axis=0, tiled=True)]
    another operation x2 -> x10, other arithmetic: 2.63 us -> 10.1 us  [the longest x8 10 us: lines(): jnp.stack([lax.dynamic_slice_in_dim(phase, start, width, 1) for phase in...]
  transfers between devices with their start and end apart: 2 -> 14, of which waited for: 2 -> 6; matrix products, arithmetic and copies ran while one was open for 1% -> 7% of each run, Pallas kernels for 6% -> 16%
where the time goes in v2:
time: 570 us; the launch traced here: 569 us
  blocking collectives  245 us (43%)
  waiting for transfers between devices  141 us (25%)
  Pallas kernels  106 us (19%)
  starting transfers between devices  34 us (6%)
  other arithmetic  14.7 us (3%)
  matrix products  14.6 us (3%)
  local copies, waits for them, and re-layouts  13.3 us (2%)
    all_gather x1, blocking collectives, edge_lines(): lax.all_gather(jnp.concatenate(columns + [params.T], axis=1), ('len', 'me...  176 us
    ppermute x4, waiting for transfers between devices, exchange_lines(): lax.ppermute(piece, 'len', [(d, shards - 1 - d) for d in range(shards)])  83 us
    all_gather x1, blocking collectives, gram_by_lines(): inner_gram = jnp.sum(lax.all_gather(own_gram, ('len', 'mem')), axis=0)  68.7 us
    all_to_all x4, waiting for transfers between devices, swap(): return lax.all_to_all(piece, 'len', split_axis=0, concat_axis=0, tiled=True)  57.7 us
    pallas_call x2, Pallas kernels, outer_call(): pl.pallas_call(functools.partial(outer_kernel, part * columns), grid=(col...  40.6 us
    all_to_all x4, starting transfers between devices, swap(): return lax.all_to_all(piece, 'len', split_axis=0, concat_axis=0, tiled=True)  19.1 us
    pallas_call x2, Pallas kernels, inner_call(): pl.pallas_call(inner_kernel, grid=(OUTER // WIDE,), in_specs=[pl.BlockSpe...  18.7 us
    pallas_call x1, Pallas kernels, mirror_call(): pl.pallas_call(mirror_kernel, grid=(blocks,), in_specs=[pl.BlockSpec(memo...  17 us
  transfers between devices with their start and end apart: 14, of which 6 were waited for; matrix products, arithmetic and copies ran while one was open for 7% of the time, Pallas kernels for 16%

profile of v2, /device:TPU:0, one launch (start us, length us, event | category | flops | bytes accessed | tf_op | source)
XLA Modules:
  0.0 568.9 jit_solution(10192965240392136319)
XLA Ops:
  0.6 7.1 %shard_map.95 = f32[8,2,4,128,128]{4,3,2,1,0:T(8,128)S(1)} custom-call(f32[8,131072]{1,0:T(8,128)} %left_ref.3, f32[8,131072]{1,0:T(8,128)} %right_ref.3), custom_call_target="tpu_custom_call" | custom-call | bytes 16777216 | tf_op jit(solution)/shard_map/pallas_call | solution.py:398
  7.7 2.0 copy-done
  9.7 5.2 all-to-all-start
  14.9 5.2 dynamic-slice_bitcast_fusion
  20.1 1.1 pad_maximum_fusion.1
  21.2 2.5 collective-permute-start
  23.7 1.1 pad_maximum_fusion.2
  24.7 2.6 collective-permute-start.1
  27.3 1.1 pad_maximum_fusion.5
  28.4 0.4 collective-permute-start.4
  28.8 1.1 pad_maximum_fusion.6
  29.9 1.0 pad_maximum_fusion.7
  31.0 3.9 collective-permute-start.8
  34.9 7.0 %shard_map.97 = f32[8,2,4,128,128]{4,3,2,1,0:T(8,128)S(1)} custom-call(f32[8,131072]{1,0:T(8,128)} %left_ref.3, f32[8,131072]{1,0:T(8,128)} %right_ref.3), custom_call_target="tpu_custom_call" | custom-call | bytes 16777216 | tf_op jit(solution)/shard_map/pallas_call | solution.py:398
  42.0 2.0 copy-done.1
  44.0 0.1 copy.70
  44.1 0.9 fusion.63
  45.0 0.1 concatenate.63
  45.0 176.5 %all-gather = f32[256,19]{1,0:T(8,128)S(1)} all-gather(f32[8,19]{1,0:T(8,128)S(1)} %concatenate.63), channel_id=2, replica_groups=mesh['len'=8,'mem'=4] {'len','mem'}, dimensions={0}, use_global_device_ids=true | all-gather | bytes 20064 | tf_op jit(solution)/shard_map/all_gather | solution.py:523
  221.5 4.6 all-to-all-start.1
  226.2 0.1 slice_bitcast_fusion.11
  226.3 0.1 copy.80
  226.3 0.1 reshape.838
  226.5 0.1 reshape.837
  226.6 0.1 copy.77
  226.6 0.1 reshape.836
  226.7 0.1 reshape.835
  227.3 0.1 fusion.41
  228.0 0.1 copy.74
  228.1 0.1 copy.73
  228.2 0.1 copy.71
  228.3 0.2 fusion.54.params_ref
  228.5 1.2 pad_maximum_fusion.3
  229.7 20.2 %shard_map.96.refs_0_ = f32[2,2,1024,512]{3,2,1,0:T(8,128)} custom-call(f32[3]{0:T(128)S(1)} %fusion.54.params_ref, f32[8,2,4,128,128]{4,3,2,1,0:T(8,128)} %all-to-all-done.phase_ref, bf16[2,4,512,512]{3,2,1,0:T(8,128)(2,1)} %constant.175.clone.matrix_ref, f32[2,4,256,1024]{3,2,1,0:T(8,128)} %constant.177.clone.twist_ref), custom_call_target="tpu_custom_call" | custom-call | flops 6442450944 | bytes 16777216 | tf_op jit(solution)/shard_map/pallas_call | solution.py:451
  249.9 25.4 %all-to-all-done.1.phase_ref = f32[8,2,4,128,128]{4,3,2,1,0:T(8,128)} async-done(((f32[8,2,4,128,128]{4,3,2,1,0:T(8,128)}), f32[8,2,4,128,128]{4,3,2,1,0:T(8,128)}, u32[]{:S(2)}, u32[]{:S(2)}) %all-to-all-start.1) | async-done | bytes 4194336 | tf_op jit(solution)/shard_map/all_to_all | solution.py:578
  275.3 20.4 %shard_map.98.refs_1_ = f32[2,2,1024,512]{3,2,1,0:T(8,128)} custom-call(f32[3]{0:T(128)S(1)} %fusion.54.params_ref, f32[8,2,4,128,128]{4,3,2,1,0:T(8,128)} %all-to-all-done.1.phase_ref, bf16[2,4,512,512]{3,2,1,0:T(8,128)(2,1)} %constant.175.clone.matrix_ref, f32[2,4,256,1024]{3,2,1,0:T(8,128)} %constant.177.clone.twist_ref), custom_call_target="tpu_custom_call" | custom-call | flops 6442450944 | bytes 16777216 | tf_op jit(solution)/shard_map/pallas_call | solution.py:451
  295.7 9.3 %shard_map.100 = f32[8,8,128,128]{3,2,1,0:T(8,128)} custom-call(f32[2,2,1024,512]{3,2,1,0:T(8,128)} %shard_map.96.refs_0_, f32[2,2,1024,512]{3,2,1,0:T(8,128)} %shard_map.98.refs_1_, bf16[2,4,256,512]{3,2,1,0:T(8,128)(2,1)S(1)} %copy-done.2), custom_call_target="tpu_custom_call" | custom-call | flops 3221225472 | bytes 12582912 | tf_op jit(solution)/shard_map/pallas_call | solution.py:474
  305.1 4.6 all-to-all-start.3
  309.8 2.3 pad_maximum_fusion.4
  312.1 0.1 fusion.33
  312.2 9.4 %shard_map.99 = f32[8,8,128,128]{3,2,1,0:T(8,128)} custom-call(f32[2,2,1024,512]{3,2,1,0:T(8,128)} %shard_map.96.refs_0_, f32[2,2,1024,512]{3,2,1,0:T(8,128)} %shard_map.98.refs_1_, bf16[2,4,256,512]{3,2,1,0:T(8,128)(2,1)S(1)} %copy-done.2), custom_call_target="tpu_custom_call" | custom-call | flops 3221225472 | bytes 12582912 | tf_op jit(solution)/shard_map/pallas_call | solution.py:474
  321.6 2.6 collective-permute-start.3
  324.2 0.1 collective-permute-start.5
  324.3 2.6 collective-permute-start.7
  327.0 32.3 %all-to-all-done.3.refs_0_ = f32[8,8,128,128]{3,2,1,0:T(8,128)} async-done(((f32[8,8,128,128]{3,2,1,0:T(8,128)}), f32[8,8,128,128]{3,2,1,0:T(8,128)}, u32[]{:S(2)}, u32[]{:S(2)}) %all-to-all-start.3) | async-done | bytes 4194336 | tf_op jit(solution)/shard_map/all_to_all | solution.py:578
  359.3 4.7 all-to-all-start.2
  364.0 1.3 pad_maximum_fusion.refs_0_
  365.3 15.5 %collective-permute-done.3.refs_4_ = f32[2,8,16384]{2,1,0:T(8,128)S(1)} collective-permute-done((f32[2,8,16384]{2,1,0:T(8,128)}, f32[2,8,16384]{2,1,0:T(8,128)S(1)}, u32[]{:S(2)}, u32[]{:S(2)}) %collective-permute-start.3) | collective-permute-done | bytes 1048608 | tf_op jit(solution)/shard_map/ppermute | solution.py:513
  380.8 22.6 %collective-permute-done.5.refs_5_ = f32[2,8,16384]{2,1,0:T(8,128)} collective-permute-done((f32[2,8,16384]{2,1,0:T(8,128)}, f32[2,8,16384]{2,1,0:T(8,128)}, u32[]{:S(2)}, u32[]{:S(2)}) %collective-permute-start.5) | collective-permute-done | bytes 1048608 | tf_op jit(solution)/shard_map/ppermute | solution.py:513
  403.4 22.5 %collective-permute-done.7.refs_6_ = f32[2,8,16384]{2,1,0:T(8,128)} collective-permute-done((f32[2,8,16384]{2,1,0:T(8,128)}, f32[2,8,16384]{2,1,0:T(8,128)}, u32[]{:S(2)}, u32[]{:S(2)}) %collective-permute-start.7) | collective-permute-done | bytes 1048608 | tf_op jit(solution)/shard_map/ppermute | solution.py:513
  425.8 22.5 %collective-permute-done.9.refs_7_ = f32[2,8,16384]{2,1,0:T(8,128)} collective-permute-done((f32[2,8,16384]{2,1,0:T(8,128)}, f32[2,8,16384]{2,1,0:T(8,128)}, u32[]{:S(2)}, u32[]{:S(2)}) %collective-permute-start.9) | collective-permute-done | bytes 1048608 | tf_op jit(solution)/shard_map/ppermute | solution.py:513
  448.4 17.0 %shard_map.103 = f32[2,2,32,16384]{3,2,1,0:T(8,128)} custom-call(s32[1]{0:T(128)} %bitcast.3.base_ref, f32[3,32,128]{2,1,0:T(8,128)S(1)} %broadcast_in_dim.3.params_ref, f32[2,8,16384]{2,1,0:T(8,128)S(1)} %pad_maximum_fusion.refs_0_, f32[2,8,16384]{2,1,0:T(8,128)S(1)} %collective-permute-done.refs_1_, f32[2,8,16384]{2,1,0:T(8,128)} %collective-permute-done.1.refs_2_, ...), custom_call_target="tpu_custom_call" | custom-call | flops 209715200 | bytes 16777216 | tf_op jit(solution)/shard_map/pallas_call | solution.py:432
  465.4 6.9 %fusion.3 = f32[32,32]{1,0:T(8,128)S(1)} fusion(f32[2,2,32,16384]{3,2,1,0:T(8,128)} %shard_map.103), kind=kOutput, calls=%fused_computation.5 | convolution fusion | flops 402653184 | bytes 4198400 | tf_op jit(solution)/shard_map/tmr,tnr->mn/dot_general | solution.py:87
  472.3 7.1 %fusion.6 = f32[32,32]{1,0:T(8,128)S(1)} fusion(f32[32,32]{1,0:T(8,128)S(1)} %fusion.3, f32[2,2,32,16384]{3,2,1,0:T(8,128)} %shard_map.103), kind=kOutput, calls=%fused_computation.9 | convolution fusion | flops 402654208 | bytes 4202496 | tf_op jit(solution)/shard_map/tmr,tnr->mn/dot_general | solution.py:87
  479.4 0.2 fusion.59
  479.6 0.2 fusion.57
  479.8 68.7 %all-gather.1 = f32[1024,32]{1,0:T(8,128)S(1)} all-gather(f32[32,32]{1,0:T(8,128)S(1)} %fusion.57), channel_id=3, replica_groups=mesh['len'=8,'mem'=4] {'len','mem'}, dimensions={0}, use_global_device_ids=true | all-gather | bytes 135168 | tf_op jit(solution)/shard_map/all_gather | solution.py:569
  548.6 0.2 fusion.5
  548.9 2.9 cholesky.18
  551.9 0.6 compare_reduce_fusion
  552.5 0.6 select_bitcast_fusion
  553.2 0.7 copy.87
  553.8 7.5 %shard_map.101.refs_1_ = f32[2,8,131072]{2,1,0:T(8,128)} custom-call(f32[8,8,128,128]{3,2,1,0:T(8,128)} %all-to-all-done.3.refs_0_), custom_call_target="tpu_custom_call" | custom-call | bytes 8388608 | tf_op jit(solution)/shard_map/pallas_call | solution.py:412
  561.4 7.5 %shard_map.102 = f32[2,8,131072]{2,1,0:T(8,128)} custom-call(f32[8,8,128,128]{3,2,1,0:T(8,128)} %all-to-all-done.2.refs_0_, f32[2,8,131072]{2,1,0:T(8,128)} %shard_map.101.refs_1_), custom_call_target="tpu_custom_call", output_to_operand_aliasing={{}: (1, {})} | custom-call | bytes 8388608 | tf_op jit(solution)/shard_map/pallas_call | solution.py:412
  (54 shorter events, 1.6 us)
Async XLA Ops:
  7.7 2.0 copy-start
  9.7 211.8 %all-to-all-start = ((f32[8,2,4,128,128]{4,3,2,1,0:T(8,128)}), f32[8,2,4,128,128]{4,3,2,1,0:T(8,128)}, u32[]{:S(2)}, u32[]{:S(2)}) async-start(f32[8,2,4,128,128]{4,3,2,1,0:T(8,128)} %copy-done), calls=%async_computation | async-start | bytes 8388608 | tf_op jit(solution)/shard_map/all_to_all | solution.py:578
  21.2 300.4 %collective-permute-start = (f32[2,8,16384]{2,1,0:T(8,128)}, f32[2,8,16384]{2,1,0:T(8,128)S(1)}, u32[]{:S(2)}, u32[]{:S(2)}) collective-permute-start(f32[2,8,16384]{2,1,0:T(8,128)} %pad_maximum_fusion.1), channel_id=1, source_target_pairs={{0,1},{1,0},{2,3},{3,2},{4,5},{5,4},{6,7},{7,6},{8,9},{9,8},{10,11... | collective-permute-start | bytes 3145736 | tf_op jit(solution)/shard_map/ppermute | solution.py:507
  24.7 296.9 %collective-permute-start.1 = (f32[2,8,16384]{2,1,0:T(8,128)}, f32[2,8,16384]{2,1,0:T(8,128)}, u32[]{:S(2)}, u32[]{:S(2)}) collective-permute-start(f32[2,8,16384]{2,1,0:T(8,128)} %pad_maximum_fusion.2), channel_id=1, source_target_pairs={{0,2},{1,3},{2,0},{3,1},{4,6},{5,7},{6,4},{7,5},{8,10},{9,11},{10,... | collective-permute-start | bytes 3145736 | tf_op jit(solution)/shard_map/ppermute | solution.py:507
  28.4 295.8 %collective-permute-start.4 = (f32[2,8,16384]{2,1,0:T(8,128)}, f32[2,8,16384]{2,1,0:T(8,128)}, u32[]{:S(2)}, u32[]{:S(2)}) collective-permute-start(f32[2,8,16384]{2,1,0:T(8,128)} %pad_maximum_fusion.5), channel_id=1, source_target_pairs={{0,1},{1,0},{2,3},{3,2},{4,5},{5,4},{6,7},{7,6},{8,9},{9,8},{10,11... | collective-permute-start | bytes 3145736 | tf_op jit(solution)/shard_map/ppermute | solution.py:507
  29.9 294.4 %collective-permute-start.6 = (f32[2,8,16384]{2,1,0:T(8,128)}, f32[2,8,16384]{2,1,0:T(8,128)}, u32[]{:S(2)}, u32[]{:S(2)}) collective-permute-start(f32[2,8,16384]{2,1,0:T(8,128)} %pad_maximum_fusion.6), channel_id=1, source_target_pairs={{0,2},{1,3},{2,0},{3,1},{4,6},{5,7},{6,4},{7,5},{8,10},{9,11},{10,... | collective-permute-start | bytes 3145736 | tf_op jit(solution)/shard_map/ppermute | solution.py:507
  31.0 13.0 %copy-start.3 = (f32[8]{0:T(128)S(1)}, f32[8]{0:T(128)}, u32[]{:S(2)}) copy-start(f32[8]{0:T(128)} %param.11) | copy-start | bytes 100
  31.0 13.0 %copy-start.4 = (f32[8]{0:T(128)S(1)}, f32[8]{0:T(128)}, u32[]{:S(2)}) copy-start(f32[8]{0:T(128)} %param.10) | copy-start | bytes 100
  31.0 13.0 %copy-start.5 = (f32[8]{0:T(128)S(1)}, f32[8]{0:T(128)}, u32[]{:S(2)}) copy-start(f32[8]{0:T(128)} %param.12) | copy-start | bytes 100
  31.0 295.9 %collective-permute-start.8 = (f32[2,8,16384]{2,1,0:T(8,128)}, f32[2,8,16384]{2,1,0:T(8,128)}, u32[]{:S(2)}, u32[]{:S(2)}) collective-permute-start(f32[2,8,16384]{2,1,0:T(8,128)} %pad_maximum_fusion.7), channel_id=1, source_target_pairs={{0,3},{1,2},{2,1},{3,0},{4,7},{5,6},{6,5},{7,4},{8,11},{9,10},{10,... | collective-permute-start | bytes 3145736 | tf_op jit(solution)/shard_map/ppermute | solution.py:507
  42.0 2.0 copy-start.1
  221.5 53.7 %all-to-all-start.1 = ((f32[8,2,4,128,128]{4,3,2,1,0:T(8,128)}), f32[8,2,4,128,128]{4,3,2,1,0:T(8,128)}, u32[]{:S(2)}, u32[]{:S(2)}) async-start(f32[8,2,4,128,128]{4,3,2,1,0:T(8,128)} %copy-done.1), calls=%async_computation.1 | async-start | bytes 8388608 | tf_op jit(solution)/shard_map/all_to_all | solution.py:578
  249.9 45.8 %copy-start.2 = (bf16[2,4,256,512]{3,2,1,0:T(8,128)(2,1)S(1)}, bf16[2,4,256,512]{3,2,1,0:T(8,128)(2,1)}, u32[]{:S(2)}) copy-start(bf16[2,4,256,512]{3,2,1,0:T(8,128)(2,1)} %constant.176.clone.refs_2_) | copy-start | bytes 6291460
  305.1 54.2 %all-to-all-start.3 = ((f32[8,8,128,128]{3,2,1,0:T(8,128)}), f32[8,8,128,128]{3,2,1,0:T(8,128)}, u32[]{:S(2)}, u32[]{:S(2)}) async-start(f32[8,8,128,128]{3,2,1,0:T(8,128)} %shard_map.100), calls=%async_computation.3 | async-start | bytes 8388608 | tf_op jit(solution)/shard_map/all_to_all | solution.py:578
  321.6 43.7 %collective-permute-start.2 = (f32[2,8,16384]{2,1,0:T(8,128)}, f32[2,8,16384]{2,1,0:T(8,128)S(1)}, u32[]{:S(2)}, u32[]{:S(2)}) collective-permute-start(f32[2,8,16384]{2,1,0:T(8,128)} %pad_maximum_fusion.3), channel_id=1, source_target_pairs={{0,3},{1,2},{2,1},{3,0},{4,7},{5,6},{6,5},{7,4},{8,11},{9,10},{10,... | collective-permute-start | bytes 3145736 | tf_op jit(solution)/shard_map/ppermute | solution.py:507
  321.6 59.2 %collective-permute-start.3 = (f32[2,8,16384]{2,1,0:T(8,128)}, f32[2,8,16384]{2,1,0:T(8,128)S(1)}, u32[]{:S(2)}, u32[]{:S(2)}) collective-permute-start(f32[2,8,16384]{2,1,0:T(8,128)} %pad_maximum_fusion.4), channel_id=1, source_target_pairs={{0,28},{4,24},{8,20},{12,16},{16,12},{20,8},{24,4},{28,0},{1,29},{... | collective-permute-start | bytes 3145736 | tf_op jit(solution)/shard_map/ppermute | solution.py:513
  324.2 79.2 %collective-permute-start.5 = (f32[2,8,16384]{2,1,0:T(8,128)}, f32[2,8,16384]{2,1,0:T(8,128)}, u32[]{:S(2)}, u32[]{:S(2)}) collective-permute-start(f32[2,8,16384]{2,1,0:T(8,128)} %collective-permute-done.4), channel_id=1, source_target_pairs={{0,28},{4,24},{8,20},{12,16},{16,12},{20,8},{24,4},{28,0},{1,29},{... | collective-permute-start | bytes 3145736 | tf_op jit(solution)/shard_map/ppermute | solution.py:513
  324.3 101.5 %collective-permute-start.7 = (f32[2,8,16384]{2,1,0:T(8,128)}, f32[2,8,16384]{2,1,0:T(8,128)}, u32[]{:S(2)}, u32[]{:S(2)}) collective-permute-start(f32[2,8,16384]{2,1,0:T(8,128)} %collective-permute-done.6), channel_id=1, source_target_pairs={{0,28},{4,24},{8,20},{12,16},{16,12},{20,8},{24,4},{28,0},{1,29},{... | collective-permute-start | bytes 3145736 | tf_op jit(solution)/shard_map/ppermute | solution.py:513
  326.9 121.4 %collective-permute-start.9 = (f32[2,8,16384]{2,1,0:T(8,128)}, f32[2,8,16384]{2,1,0:T(8,128)}, u32[]{:S(2)}, u32[]{:S(2)}) collective-permute-start(f32[2,8,16384]{2,1,0:T(8,128)} %collective-permute-done.8), channel_id=1, source_target_pairs={{0,28},{4,24},{8,20},{12,16},{16,12},{20,8},{24,4},{28,0},{1,29},{... | collective-permute-start | bytes 3145736 | tf_op jit(solution)/shard_map/ppermute | solution.py:513
  359.3 202.1 %all-to-all-start.2 = ((f32[8,8,128,128]{3,2,1,0:T(8,128)}), f32[8,8,128,128]{3,2,1,0:T(8,128)}, u32[]{:S(2)}, u32[]{:S(2)}) async-start(f32[8,8,128,128]{3,2,1,0:T(8,128)} %shard_map.99), calls=%async_computation.2 | async-start | bytes 8388608 | tf_op jit(solution)/shard_map/all_to_all | solution.py:578

commit v3 on v1

--- a/solution.py
+++ b/solution.py
@@ -18,7 +18,7 @@
 STEP = 16
 WIDE = 256
 BLOCK_ROWS = 16
-IN_PARTS = 2
+OUTER_TILES = 2
 OUT_PARTS = 2
 VMEM_LIMIT = 48 * 1024 * 1024
 SIN_HALF = (0.49999999785787, -0.02083332246218, 2.604078316692e-4, -1.547581723527e-6, 5.088214043e-9)
@@ -203,6 +203,12 @@
     return twice * half_cos, 1.0 - twice * half_sin
 
 
+def left_lines(left, freq, scale, exponent):
+    amplitude = scale * jnp.exp2(exponent * jnp.log2((freq + ANCHOR) * (1.0 / ANCHOR)))
+    sin_left, cos_left = sin_cos(left)
+    return amplitude * cos_left, amplitude * sin_left
+
+
 def line_spectra(left, right, freq, scale, exponent, inverse_coherence):
     amplitude = scale * jnp.exp2(exponent * jnp.log2((freq + ANCHOR) * (1.0 / ANCHOR)))
     freq_ratio = freq * inverse_coherence
@@ -247,233 +253,250 @@
     )
 
 
-def outer_kernel(base, params_ref, phase_ref, matrix_ref, twist_ref, out_ref, coarse_ref, fine_ref):
+def outer_kernel(track, params_ref, *refs):
+    phase_refs, (matrix_ref, twist_ref, out_ref, coarse_ref, fine_ref) = refs[:-5], refs[-5:]
     scale, exponent, inverse_coherence = params_ref[0], params_ref[1], params_ref[2]
-    rows = phase_ref.shape[3]
-    first_lane = base + pl.program_id(0) * LANES
-    lane = lax.broadcasted_iota(jnp.int32, (STEP, LANES), 1) + first_lane
+    _, tiles, rows, _ = phase_refs[0].shape
+    lane = lax.broadcasted_iota(jnp.int32, (STEP, LANES), 1) + pl.program_id(0) * tiles * LANES
     row = lax.broadcasted_iota(jnp.int32, (STEP, LANES), 0)
     place = row * INNER + lane
 
     def some_rows(step, carry):
         b = step * STEP
-        tracks = []
-        for a in range(RADIX):
-            k1 = a * QUARTER + b
-            source, inside = k1 // rows, pl.multiple_of(k1 % rows, STEP)
-            freq = (place + k1 * INNER).astype(jnp.float32)
-            left = phase_ref[source, 0, 0, pl.ds(inside, STEP), :]
-            right = phase_ref[source, 1, 0, pl.ds(inside, STEP), :]
-            tracks.append(line_spectra(left, right, freq, scale, exponent, inverse_coherence))
-        for t in range(2):
-            mixed = radix_four([track[t] for track in tracks])
+        for tile in range(tiles):
+            lines = []
+            for a in range(RADIX):
+                k1 = a * QUARTER + b
+                source, inside = k1 // rows, pl.multiple_of(k1 % rows, STEP)
+                freq = (place + (k1 * INNER + tile * LANES)).astype(jnp.float32)
+                phases = [ref[source, tile, pl.ds(inside, STEP), :] for ref in phase_refs]
+                if track == 0:
+                    lines.append(left_lines(*phases, freq, scale, exponent))
+                else:
+                    lines.append(line_spectra(*phases, freq, scale, exponent, inverse_coherence)[1])
+            mixed = radix_four(lines)
             for e in range(RADIX):
                 for ri in range(2):
                     at = pl.ds(pl.multiple_of(ri * QUARTER + b, STEP), STEP)
-                    store_split(coarse_ref, fine_ref, (e, at, pl.ds(t * LANES, LANES)), mixed[e][ri])
+                    where = (e, at, pl.ds(tile * LANES, LANES))
+                    store_split(coarse_ref, fine_ref, where, mixed[e][ri])
         return carry
 
     lax.fori_loop(0, QUARTER // STEP, some_rows, 0)
     for e in range(RADIX):
         mid = triple_dot(matrix_ref, e, coarse_ref[e], fine_ref[e], ((1,), (0,)))
-        cos_part, sin_part = twist_ref[0, e], twist_ref[1, e]
-        for t in range(2):
-            real = mid[:QUARTER, t * LANES : (t + 1) * LANES]
-            imag = mid[QUARTER:, t * LANES : (t + 1) * LANES]
-            out_ref[t, 0, pl.ds(e, QUARTER, stride=RADIX), :] = real * cos_part - imag * sin_part
-            out_ref[t, 1, pl.ds(e, QUARTER, stride=RADIX), :] = real * sin_part + imag * cos_part
-
-
-def inner_kernel(*refs):
-    mid_refs, (matrix_ref, out_ref, coarse_ref, fine_ref) = refs[:-4], refs[-4:]
-    wide, columns = mid_refs[0].shape[2:]
-    shards, _, _, rows, _ = out_ref.shape
+        for tile in range(tiles):
+            lanes = slice(tile * LANES, (tile + 1) * LANES)
+            cos_part, sin_part = twist_ref[0, e, :, lanes], twist_ref[1, e, :, lanes]
+            real, imag = mid[:QUARTER, lanes], mid[QUARTER:, lanes]
+            out_ref[tile, 0, pl.ds(e, QUARTER, stride=RADIX), :] = real * cos_part - imag * sin_part
+            out_ref[tile, 1, pl.ds(e, QUARTER, stride=RADIX), :] = real * sin_part + imag * cos_part
+
+
+def inner_kernel(mid_ref, matrix_ref, *refs):
+    out_refs, (coarse_ref, fine_ref) = refs[:-2], refs[-2:]
+    wide = mid_ref.shape[2]
+    shards, _, rows, _ = out_refs[0].shape
 
     def some_rows(step, carry):
         at = pl.multiple_of(step * STEP, STEP)
-        for t in range(2):
-            for half in range(0, QUARTER, 128):
-                parts = [
-                    tuple(
-                        mid_refs[(a * QUARTER + half) // columns][
-                            t, ri, pl.ds(at, STEP), pl.ds((a * QUARTER + half) % columns, 128)
-                        ]
-                        for ri in range(2)
-                    )
-                    for a in range(RADIX)
-                ]
-                mixed = radix_four(parts)
-                for e in range(RADIX):
-                    for ri in range(2):
-                        where = (
-                            e,
-                            pl.ds(pl.multiple_of(t * wide + at, STEP), STEP),
-                            pl.ds(ri * QUARTER + half, 128),
-                        )
-                        store_split(coarse_ref, fine_ref, where, mixed[e][ri])
+        for half in range(0, QUARTER, LANES):
+            parts = [
+                tuple(mid_ref[(a * QUARTER + half) // LANES, ri, pl.ds(at, STEP), :] for ri in range(2))
+                for a in range(RADIX)
+            ]
+            mixed = radix_four(parts)
+            for e in range(RADIX):
+                for ri in range(2):
+                    where = (e, pl.ds(at, STEP), pl.ds(ri * QUARTER + half, LANES))
+                    store_split(coarse_ref, fine_ref, where, mixed[e][ri])
         return carry
 
     lax.fori_loop(0, wide // STEP, some_rows, 0)
     some = rows // RADIX
     for e in range(RADIX):
         value = triple_dot(matrix_ref, e, coarse_ref[e], fine_ref[e], ((1,), (1,)))
-        for t in range(2):
-            for f in range(shards):
+        for f in range(shards):
+            for part, out_ref in enumerate(out_refs):
+                at = (f * len(out_refs) + part) * some
                 for tile in range(wide // LANES):
-                    lanes = t * wide + tile * LANES
-                    out_ref[f, t, tile, pl.ds(e, some, stride=RADIX), :] = value[
-                        f * some : (f + 1) * some, lanes : lanes + LANES
+                    out_ref[f, tile, pl.ds(e, some, stride=RADIX), :] = value[
+                        at : at + some, tile * LANES : (tile + 1) * LANES
                     ]
 
 
-def part_kernel(left_ref, right_ref, *out_refs):
-    members, _, tiles, rows, _ = out_refs[0].shape
-    flat_refs = [ref.reshape(members * 2 * tiles * rows, LANES) for ref in out_refs]
-    for t, ref in enumerate((left_ref, right_ref)):
-        for r in range(rows):
-            for part, flat_ref in enumerate(flat_refs):
-                for tile in range(tiles):
-                    at = r * INNER + (part * tiles + tile) * LANES
-                    start = (t * tiles + tile) * rows + r
-                    flat_ref[pl.ds(start, members, stride=2 * tiles * rows), :] = ref[:, at : at + LANES]
+def part_kernel(in_ref, out_ref):
+    members, tiles, rows, _ = out_ref.shape
+    flat_ref = out_ref.reshape(members * tiles * rows, LANES)
+    for r in range(rows):
+        for tile in range(tiles):
+            at = (r * tiles + tile) * LANES
+            flat_ref[pl.ds(tile * rows + r, members, stride=tiles * rows), :] = in_ref[:, at : at + LANES]
 
 
 def join_kernel(*refs):
-    out_ref = refs[-1]
-    members, _, tiles, rows, _ = refs[0].shape
-    flat_refs = [ref.reshape(members * 2 * tiles * rows, LANES) for ref in refs[:-1]]
-    for t in range(2):
-        for r in range(rows):
-            for part, flat_ref in enumerate(flat_refs):
-                for tile in range(tiles):
-                    at = r * INNER + (part * tiles + tile) * LANES
-                    start = (t * tiles + tile) * rows + r
-                    out_ref[t, :, at : at + LANES] = flat_ref[
-                        pl.ds(start, members, stride=2 * tiles * rows), :
-                    ]
+    in_ref, out_ref, copy_ref = refs[0], refs[-2], refs[-1]
+    members, tiles, rows, _ = in_ref.shape
+    flat_ref = in_ref.reshape(members * tiles * rows, LANES)
+    for r in range(rows):
+        for tile in range(tiles):
+            at = (r * tiles + tile) * LANES
+            value = flat_ref[pl.ds(tile * rows + r, members, stride=tiles * rows), :]
+            out_ref[0, :, at : at + LANES] = value
+            copy_ref[0, :, at : at + LANES] = value
 
 
 def limits():
     return pltpu.CompilerParams(vmem_limit_bytes=VMEM_LIMIT)
 
 
-def part_call(phase_left, phase_right, parts):
-    members, length = phase_left.shape
+def part_call(phase):
+    members, length = phase.shape
     rows = length // INNER
-    tiles = INNER // parts // LANES
+    tiles = INNER // LANES
     return pl.pallas_call(
         part_kernel,
         grid=(rows // BLOCK_ROWS,),
-        in_specs=[pl.BlockSpec((members, BLOCK_ROWS * INNER), lambda g: (0, g))] * 2,
-        out_specs=[pl.BlockSpec((members, 2, tiles, BLOCK_ROWS, LANES), lambda g: (0, 0, 0, g, 0))] * parts,
-        out_shape=[jax.ShapeDtypeStruct((members, 2, tiles, rows, LANES), jnp.float32)] * parts,
+        in_specs=[pl.BlockSpec((members, BLOCK_ROWS * INNER), lambda g: (0, g))],
+        out_specs=pl.BlockSpec((members, tiles, BLOCK_ROWS, LANES), lambda g: (0, 0, g, 0)),
+        out_shape=jax.ShapeDtypeStruct((members, tiles, rows, LANES), jnp.float32),
         compiler_params=limits(),
-        cost_estimate=pl.CostEstimate(flops=0, bytes_accessed=16 * members * length, transcendentals=0),
-    )(phase_left, phase_right)
-
-
-def join_call(pieces):
-    members, _, tiles, rows, _ = pieces[0].shape
+        cost_estimate=pl.CostEstimate(flops=0, bytes_accessed=8 * members * length, transcendentals=0),
+    )(phase)
+
+
+def join_call(piece, place, places, groups, so_far):
+    members, tiles, rows, _ = piece.shape
+    stretch = rows * INNER
+    steps = rows // BLOCK_ROWS
+    track, within = place // (places // 2), place % (places // 2)
+    operands = (piece,) if so_far is None else (piece, so_far)
+    each = steps // groups
     return pl.pallas_call(
         join_kernel,
-        grid=(rows // BLOCK_ROWS,),
-        in_specs=[pl.BlockSpec((members, 2, tiles, BLOCK_ROWS, LANES), lambda g: (0, 0, 0, g, 0))]
-        * len(pieces),
-        out_specs=pl.BlockSpec((2, members, BLOCK_ROWS * INNER), lambda g: (0, 0, g)),
-        out_shape=jax.ShapeDtypeStruct((2, members, rows * INNER), jnp.float32),
+        grid=(steps,),
+        in_specs=[
+            pl.BlockSpec((members, tiles, BLOCK_ROWS, LANES), lambda g: (0, 0, g, 0)),
+            pl.BlockSpec(memory_space=pl.ANY),
+        ][: len(operands)],
+        out_specs=[
+            pl.BlockSpec((1, members, BLOCK_ROWS * INNER), lambda g: (track, 0, within * steps + g)),
+            pl.BlockSpec((1, members, BLOCK_ROWS * INNER), lambda g: (g // each, 0, g % each)),
+        ],
+        out_shape=[
+            jax.ShapeDtypeStruct((2, members, stretch * places // 2), jnp.float32),
+            jax.ShapeDtypeStruct((groups, members, stretch // groups), jnp.float32),
+        ],
+        input_output_aliases={} if so_far is None else {1: 0},
         compiler_params=limits(),
-        cost_estimate=pl.CostEstimate(flops=0, bytes_accessed=16 * members * rows * INNER, transcendentals=0),
-    )(*pieces)
-
-
-def outer_call(params, phases, matrices, twists, part):
-    sources, _, tiles, rows, _ = phases.shape
-    columns = tiles * LANES
+        cost_estimate=pl.CostEstimate(flops=0, bytes_accessed=12 * members * stretch, transcendentals=0),
+    )(*operands)
+
+
+def outer_call(params, phases, matrices, twists, track):
+    sources, tiles, rows, _ = phases[0].shape
+    some = OUTER_TILES
     return pl.pallas_call(
-        functools.partial(outer_kernel, part * columns),
-        grid=(columns // LANES,),
-        in_specs=[
-            pl.BlockSpec(memory_space=pltpu.SMEM),
-            pl.BlockSpec((sources, 2, 1, rows, LANES), lambda g: (0, 0, g, 0, 0)),
+        functools.partial(outer_kernel, track),
+        grid=(tiles // some,),
+        in_specs=[pl.BlockSpec(memory_space=pltpu.SMEM)]
+        + [pl.BlockSpec((sources, some, rows, LANES), lambda g: (0, g, 0, 0))] * len(phases)
+        + [
             pl.BlockSpec(matrices.shape, lambda g: (0, 0, 0, 0)),
-            pl.BlockSpec(
-                (2, RADIX, QUARTER, LANES), lambda g: (0, 0, 0, part * (columns // LANES) + g)
-            ),
+            pl.BlockSpec((2, RADIX, QUARTER, some * LANES), lambda g: (0, 0, 0, g)),
         ],
-        out_specs=pl.BlockSpec((2, 2, OUTER, LANES), lambda g: (0, 0, 0, g)),
-        out_shape=jax.ShapeDtypeStruct((2, 2, OUTER, columns), jnp.float32),
-        scratch_shapes=[pltpu.VMEM((RADIX, 2 * QUARTER, 2 * LANES), jnp.bfloat16)] * 2,
+        out_specs=pl.BlockSpec((some, 2, OUTER, LANES), lambda g: (g, 0, 0, 0)),
+        out_shape=jax.ShapeDtypeStruct((tiles, 2, OUTER, LANES), jnp.float32),
+        scratch_shapes=[pltpu.VMEM((RADIX, 2 * QUARTER, some * LANES), jnp.bfloat16)] * 2,
         compiler_params=limits(),
         cost_estimate=pl.CostEstimate(
-            flops=48 * OUTER * QUARTER * columns, bytes_accessed=32 * OUTER * columns, transcendentals=0
+            flops=24 * OUTER * QUARTER * INNER, bytes_accessed=20 * OUTER * INNER, transcendentals=0
         ),
-    )(params, phases, matrices, twists)
-
-
-def inner_call(mids, matrices, shards, part, parts):
-    wide = WIDE
-    rows = INNER // shards
-    columns = OUTER // parts
-    blocks = columns // wide
-
+    )(params, *phases, matrices, twists)
+
+
+def inner_call(mid, matrices, shards, parts):
+    rows = INNER // shards // parts
+    tiles = OUTER // LANES
     return pl.pallas_call(
         inner_kernel,
-        grid=(blocks,),
+        grid=(OUTER // WIDE,),
         in_specs=[
-            pl.BlockSpec((2, 2, wide, mid.shape[-1]), lambda g: (0, 0, part * blocks + g, 0)) for mid in mids
-        ]
-        + [pl.BlockSpec(matrices.shape, lambda g: (0, 0, 0, 0))],
-        out_specs=pl.BlockSpec((shards, 2, wide // LANES, rows, LANES), lambda g: (0, 0, g, 0, 0)),
-        out_shape=jax.ShapeDtypeStruct((shards, 2, columns // LANES, rows, LANES), jnp.float32),
-        scratch_shapes=[pltpu.VMEM((RADIX, 2 * wide, 2 * QUARTER), jnp.bfloat16)] * 2,
+            pl.BlockSpec((INNER // LANES, 2, WIDE, LANES), lambda g: (0, 0, g, 0)),
+            pl.BlockSpec(matrices.shape, lambda g: (0, 0, 0, 0)),
+        ],
+        out_specs=[pl.BlockSpec((shards, WIDE // LANES, rows, LANES), lambda g: (0, g, 0, 0))] * parts,
+        out_shape=[jax.ShapeDtypeStruct((shards, tiles, rows, LANES), jnp.float32)] * parts,
+        scratch_shapes=[pltpu.VMEM((RADIX, WIDE, 2 * QUARTER), jnp.bfloat16)] * 2,
         compiler_params=limits(),
         cost_estimate=pl.CostEstimate(
-            flops=24 * OUTER * QUARTER * columns, bytes_accessed=24 * OUTER * columns, transcendentals=0
+            flops=12 * OUTER * QUARTER * INNER, bytes_accessed=12 * OUTER * INNER, transcendentals=0
         ),
-    )(*mids, matrices)
+    )(mid, matrices)
+
+
+def line_params(roughness, waviness, coherence):
+    return jnp.stack(
+        [jnp.sqrt(2.0 * roughness * (waviness - 1.0) / ANCHOR), -0.5 * waviness, 1.0 / coherence]
+    )
+
+
+def slot_gram(stretches, groups):
+    my_group = lax.axis_index("mem")
+    received = []
+    for slot in range(groups):
+        piece = lax.dynamic_index_in_dim(stretches, my_group ^ slot, 0, keepdims=False)
+        if slot:
+            piece = lax.ppermute(piece, "mem", [(z, z ^ slot) for z in range(groups)])
+        received.append(piece)
+    together = jnp.concatenate(received, axis=0)
+    return lax.dot_general(together, together, (((1,), (1,)), ((), ())), precision=highest)
+
+
+def in_order(gram_matrix, members):
+    my_group = lax.axis_index("mem")
+    row = lax.broadcasted_iota(jnp.int32, gram_matrix.shape, 0)
+    column = lax.broadcasted_iota(jnp.int32, gram_matrix.shape, 1)
+    to_slot = (row % members == column % members) & ((row // members) ^ my_group == column // members)
+    to_slot = to_slot.astype(jnp.float32)
+    return jnp.dot(jnp.dot(to_slot, gram_matrix, precision=highest), to_slot.T, precision=highest)
+
+
+def summed(value):
+    for axis in ("len", "mem"):
+        value = jnp.sum(lax.all_gather(value, axis), axis=0)
+    return value
 
 
 def per_device_whole(phase_left, phase_right, roughness, waviness, coherence):
-    local_members, local_len = phase_left.shape
-    shards = lax.axis_size("len")
+    shards, groups = lax.axis_size("len"), lax.axis_size("mem")
     my_index = lax.axis_index("len")
-    points = OUTER * INNER
-
-    def own(values):
-        return lax.dynamic_index_in_dim(values, my_index, 0, keepdims=False)
+    members = phase_left.shape[0]
 
     def swap(piece):
         return lax.all_to_all(piece, "len", split_axis=0, concat_axis=0, tiled=True)
 
-    params = jnp.stack(
-        [
-            own(jnp.sqrt(2.0 * roughness * (waviness - 1.0) / ANCHOR)),
-            own(-0.5 * waviness),
-            own(1.0 / coherence),
-        ]
+    params = lax.dynamic_index_in_dim(
+        line_params(roughness, waviness, coherence), my_index, 1, keepdims=False
     )
     outer_tables = jnp.asarray(outer_matrices())
     inner_tables = jnp.asarray(inner_matrices())
     twists = jnp.asarray(twist_tables())
-    mids = [
-        outer_call(params, swap(piece), outer_tables, twists, part)
-        for part, piece in enumerate(part_call(phase_left, phase_right, IN_PARTS))
-    ]
-    pieces = [swap(inner_call(mids, inner_tables, shards, part, OUT_PARTS)) for part in range(OUT_PARTS)]
-    profile = join_call(pieces)
-    groups = lax.axis_size("mem")
-    stretch = local_len // groups
-    stretches = jnp.stack([profile[:, :, q * stretch : (q + 1) * stretch] for q in range(groups)])
-    together = lax.all_to_all(stretches, "mem", split_axis=0, concat_axis=0, tiled=True)
-    gram_matrix = sum(
-        gram_of(together[:, t].reshape(1, groups * local_members, stretch)) for t in range(2)
-    )
-    gram_matrix = lax.psum(gram_matrix, ("len", "mem")) * (0.5 / points)
+    left = swap(part_call(phase_left))
+    right = swap(part_call(phase_right))
+    profile, gram_matrix, place = None, 0.0, 0
+    for track, phases in enumerate(((left,), (left, right))):
+        mid = outer_call(params, phases, outer_tables, twists, track)
+        for piece in inner_call(mid, inner_tables, shards, OUT_PARTS):
+            profile, stretches = join_call(swap(piece), place, 2 * OUT_PARTS, groups, profile)
+            gram_matrix = gram_matrix + slot_gram(stretches, groups)
+            place += 1
+    gram_matrix = summed(in_order(gram_matrix, members)) * (0.5 / (OUTER * INNER))
     return (profile, upper_of(gram_matrix))
 
 
 def per_device(phase_left, phase_right, roughness, waviness, coherence):
-    whole_members = phase_left.shape[0] == lax.axis_size("len")
+    whole_members = phase_left.shape[0] == lax.axis_size("len") and lax.axis_size("mem") in (2, 4)
     form = per_device_whole if whole_members else per_device_spread
     return form(phase_left, phase_right, roughness, waviness, coherence)
 

time: 510 us -> 501 us (0.982)
  blocking collectives: 334 us -> 85.4 us
  starting transfers between devices: 9.31 us -> 133 us
  waiting for transfers between devices: 62.5 us -> 162 us
  Pallas kernels: 80.1 us -> 90.1 us
  local copies, waits for them, and re-layouts: 8.86 us -> 16.8 us
    all_to_all x1 -> x0, blocking collectives: 188 us -> none  [per_device_whole(): lax.all_to_all(stretches, 'mem', split_axis=0, concat_axis=0, tiled=True)]
    ppermute x0 -> x12, starting transfers between devices: none -> 115 us  [slot_gram(): piece = lax.ppermute(piece, 'mem', [(z, z ^ slot) for z in range(groups)])]
    ppermute x0 -> x12, waiting for transfers between devices: none -> 59.8 us  [slot_gram(): piece = lax.ppermute(piece, 'mem', [(z, z ^ slot) for z in range(groups)])]
    all_to_all x2, blocking collectives: 108 us -> 60.8 us  [swap(): return lax.all_to_all(piece, 'len', split_axis=0, concat_axis=0, tiled=True)]
    all_to_all x2 -> x4, waiting for transfers between devices: 62.5 us -> 102 us  [swap(): return lax.all_to_all(piece, 'len', split_axis=0, concat_axis=0, tiled=True)]
    psum x1 -> x0, blocking collectives: 38 us -> none  [per_device_whole(): gram_matrix = lax.psum(gram_matrix, ('len', 'mem')) * (0.5 / points)]
    all_gather x0 -> x2, blocking collectives: none -> 24.6 us  [summed(): value = jnp.sum(lax.all_gather(value, axis), axis=0)]
    unnamed x13 -> x37, local copies, waits for them, and re-layouts: 2.89 us -> 16 us
  transfers between devices with their start and end apart: 2 -> 16, of which waited for: 2 -> 8; matrix products, arithmetic and copies ran while one was open for 1% -> 1% of each run, Pallas kernels for 6% -> 9%
where the time goes in v3:
time: 501 us; the launch traced here: 500 us
  waiting for transfers between devices  162 us (32%)
  starting transfers between devices  133 us (27%)
  Pallas kernels  90.1 us (18%)
  blocking collectives  85.4 us (17%)
  local copies, waits for them, and re-layouts  16.8 us (3%)
  matrix products  7.58 us (2%)
    ppermute x12, starting transfers between devices, slot_gram(): piece = lax.ppermute(piece, 'mem', [(z, z ^ slot) for z in range(groups)])  115 us
    all_to_all x4, waiting for transfers between devices, swap(): return lax.all_to_all(piece, 'len', split_axis=0, concat_axis=0, tiled=True)  102 us
    all_to_all x2, blocking collectives, swap(): return lax.all_to_all(piece, 'len', split_axis=0, concat_axis=0, tiled=True)  60.8 us
    ppermute x12, waiting for transfers between devices, slot_gram(): piece = lax.ppermute(piece, 'mem', [(z, z ^ slot) for z in range(groups)])  59.8 us
    pallas_call x2, Pallas kernels, outer_call(): pl.pallas_call(functools.partial(outer_kernel, track), grid=(tiles // som...  47.2 us
    all_gather x2, blocking collectives, summed(): value = jnp.sum(lax.all_gather(value, axis), axis=0)  24.6 us
    all_to_all x4, starting transfers between devices, swap(): return lax.all_to_all(piece, 'len', split_axis=0, concat_axis=0, tiled=True)  17.9 us
    pallas_call x2, Pallas kernels, inner_call(): pl.pallas_call(inner_kernel, grid=(OUTER // WIDE,), in_specs=[pl.BlockSpe...  17.7 us
  transfers between devices with their start and end apart: 16, of which 8 were waited for; matrix products, arithmetic and copies ran while one was open for 1% of the time, Pallas kernels for 9%

profile of v3, /device:TPU:0, one launch (start us, length us, event | category | flops | bytes accessed | tf_op | source)
XLA Modules:
  0.0 500.4 jit_solution(8179786058050784916)
XLA Ops:
  0.6 6.3 %shard_map.95 = f32[8,8,128,128]{3,2,1,0:T(8,128)S(1)} custom-call(f32[8,131072]{1,0:T(8,128)} %in_ref.2), custom_call_target="tpu_custom_call" | custom-call | bytes 8388608 | tf_op jit(solution)/shard_map/pallas_call | solution.py:357
  7.0 0.0 copy-start.1
  7.0 2.0 copy-done.1
  9.0 5.2 %all-to-all-start = ((f32[8,8,128,128]{3,2,1,0:T(8,128)}), f32[8,8,128,128]{3,2,1,0:T(8,128)}, u32[]{:S(2)}, u32[]{:S(2)}) async-start(f32[8,8,128,128]{3,2,1,0:T(8,128)} %copy-done.1), calls=%async_computation | async-start | bytes 8388608 | tf_op jit(solution)/shard_map/all_to_all | solution.py:477
  14.1 6.3 %shard_map.96 = f32[8,8,128,128]{3,2,1,0:T(8,128)S(1)} custom-call(f32[8,131072]{1,0:T(8,128)} %in_ref.3), custom_call_target="tpu_custom_call" | custom-call | bytes 8388608 | tf_op jit(solution)/shard_map/pallas_call | solution.py:357
  20.5 2.0 copy-done
  22.5 40.9 %all-to-all-done.refs_0_ = f32[8,8,128,128]{3,2,1,0:T(8,128)} async-done(((f32[8,8,128,128]{3,2,1,0:T(8,128)}), f32[8,8,128,128]{3,2,1,0:T(8,128)}, u32[]{:S(2)}, u32[]{:S(2)}) %all-to-all-start) | async-done | bytes 4194336 | tf_op jit(solution)/shard_map/all_to_all | solution.py:477
  63.4 4.6 all-to-all-start.1
  68.0 0.2 fusion.43.params_ref
  68.2 48.9 %all-to-all-done.1.refs_1_ = f32[8,8,128,128]{3,2,1,0:T(8,128)} async-done(((f32[8,8,128,128]{3,2,1,0:T(8,128)}), f32[8,8,128,128]{3,2,1,0:T(8,128)}, u32[]{:S(2)}, u32[]{:S(2)}) %all-to-all-start.1) | async-done | bytes 4194336 | tf_op jit(solution)/shard_map/all_to_all | solution.py:477
  117.1 26.7 %shard_map.97.mid_ref = f32[8,2,1024,128]{3,2,1,0:T(8,128)} custom-call(f32[3]{0:T(128)S(1)} %fusion.43.params_ref, f32[8,8,128,128]{3,2,1,0:T(8,128)} %all-to-all-done.refs_0_, f32[8,8,128,128]{3,2,1,0:T(8,128)} %all-to-all-done.1.refs_1_, bf16[2,4,512,512]{3,2,1,0:T(8,128)(2,1)} %constant.152.clone.refs_2_.refs_1_, ...), custom_call_target="tpu_custom_call" | custom-call | flops 6442450944 | bytes 20971520 | tf_op jit(solution)/shard_map/pallas_call | solution.py:399
  143.7 8.8 %shard_map.98 = (f32[8,8,64,128]{3,2,1,0:T(8,128)S(1)}, f32[8,8,64,128]{3,2,1,0:T(8,128)S(1)}) custom-call(f32[8,2,1024,128]{3,2,1,0:T(8,128)} %shard_map.97.mid_ref, bf16[2,4,256,512]{3,2,1,0:T(8,128)(2,1)} %constant.153.clone.matrix_ref), custom_call_target="tpu_custom_call" | custom-call | flops 3221225472 | bytes 12582912 | tf_op jit(solution)/shard_map/pallas_call | solution.py:421
  152.6 1.4 copy-done.4
  154.0 1.4 copy-done.5
  155.4 3.6 all-to-all-start.3
  159.0 20.6 %shard_map.99.mid_ref = f32[8,2,1024,128]{3,2,1,0:T(8,128)} custom-call(f32[3]{0:T(128)S(1)} %fusion.43.params_ref, f32[8,8,128,128]{3,2,1,0:T(8,128)} %all-to-all-done.refs_0_, bf16[2,4,512,512]{3,2,1,0:T(8,128)(2,1)} %constant.152.clone.refs_2_.refs_1_, f32[2,4,256,1024]{3,2,1,0:T(8,128)} %constant.154.clone.refs_3_.refs_2_), custom_call_target="tpu_custom_call" | custom-call | flops 6442450944 | bytes 20971520 | tf_op jit(solution)/shard_map/pallas_call | solution.py:399
  179.6 8.8 %shard_map.100 = (f32[8,8,64,128]{3,2,1,0:T(8,128)S(1)}, f32[8,8,64,128]{3,2,1,0:T(8,128)S(1)}) custom-call(f32[8,2,1024,128]{3,2,1,0:T(8,128)} %shard_map.99.mid_ref, bf16[2,4,256,512]{3,2,1,0:T(8,128)(2,1)} %constant.153.clone.matrix_ref), custom_call_target="tpu_custom_call" | custom-call | flops 3221225472 | bytes 12582912 | tf_op jit(solution)/shard_map/pallas_call | solution.py:421
  188.4 1.3 copy-done.6
  189.8 1.3 copy-done.8
  191.1 0.0 all-to-all-done.3.refs_0_
  191.1 31.1 %all_to_all.30.refs_0_ = f32[8,8,64,128]{3,2,1,0:T(8,128)} all-to-all(f32[8,8,64,128]{3,2,1,0:T(8,128)} %copy-done.8), channel_id=1, replica_groups=mesh['len'=8,'mem'=4] {'len'}, dimensions={0} | all-to-all | bytes 4194304 | tf_op jit(solution)/shard_map/all_to_all | solution.py:477
  222.1 29.7 %all_to_all.31.refs_0_ = f32[8,8,64,128]{3,2,1,0:T(8,128)} all-to-all(f32[8,8,64,128]{3,2,1,0:T(8,128)S(1)} %copy-done.7), channel_id=1, replica_groups=mesh['len'=8,'mem'=4] {'len'}, dimensions={0} | all-to-all | bytes 4194304 | tf_op jit(solution)/shard_map/all_to_all | solution.py:477
  251.9 4.5 all-to-all-start.2
  256.5 1.7 copy-done.3
  258.2 2.7 shard_map.101
  260.9 1.4 copy-done.9
  262.3 2.7 shard_map.102
  265.0 1.4 copy-done.11
  266.4 2.7 shard_map.103
  269.1 1.4 copy-done.13
  270.5 12.4 %all-to-all-done.2.refs_0_ = f32[8,8,64,128]{3,2,1,0:T(8,128)} async-done(((f32[8,8,64,128]{3,2,1,0:T(8,128)}), f32[8,8,64,128]{3,2,1,0:T(8,128)}, u32[]{:S(2)}, u32[]{:S(2)}) %all-to-all-start.2) | async-done | bytes 2097184 | tf_op jit(solution)/shard_map/all_to_all | solution.py:477
  282.9 4.4 shard_map.104
  287.3 0.1 dynamic-slice_bitcast_fusion.3
  287.4 4.4 collective-permute-start.11
  291.8 0.0 collective-permute-start.10
  291.8 0.6 collective-permute-start.9
  292.5 0.1 dynamic-slice_bitcast_fusion.7
  292.6 3.8 collective-permute-start.8
  296.4 0.0 collective-permute-start.7
  296.4 0.1 dynamic-slice_bitcast_fusion.11
  296.6 8.2 %collective-permute-done.11 = f32[8,16384]{1,0:T(8,128)S(1)} collective-permute-done((f32[8,16384]{1,0:T(8,128)S(1)}, f32[8,16384]{1,0:T(8,128)S(1)}, u32[]{:S(2)}, u32[]{:S(2)}) %collective-permute-start.11) | collective-permute-done | bytes 524320 | tf_op jit(solution)/shard_map/ppermute | solution.py:450
  304.8 37.8 %collective-permute-start.6 = (f32[8,16384]{1,0:T(8,128)S(1)}, f32[8,16384]{1,0:T(8,128)S(1)}, u32[]{:S(2)}, u32[]{:S(2)}) collective-permute-start(f32[8,16384]{1,0:T(8,128)S(1)} %get-tuple-element.43), channel_id=1, source_target_pairs={{0,1},{1,0},{2,3},{3,2},{4,5},{5,4},{6,7},{7,6},{8,9},{9,8},{10,11... | collective-permute-start | bytes 1572872 | tf_op jit(solution)/shard_map/ppermute | solution.py:450
  342.5 14.6 %collective-permute-done.10 = f32[8,16384]{1,0:T(8,128)S(1)} collective-permute-done((f32[8,16384]{1,0:T(8,128)S(1)}, f32[8,16384]{1,0:T(8,128)S(1)}, u32[]{:S(2)}, u32[]{:S(2)}) %collective-permute-start.10) | collective-permute-done | bytes 524320 | tf_op jit(solution)/shard_map/ppermute | solution.py:450
  357.1 3.5 collective-permute-start.5
  360.7 30.9 %collective-permute-start.3 = (f32[8,16384]{1,0:T(8,128)S(1)}, f32[8,16384]{1,0:T(8,128)S(1)}, u32[]{:S(2)}, u32[]{:S(2)}) collective-permute-start(f32[8,16384]{1,0:T(8,128)S(1)} %get-tuple-element.39), channel_id=1, source_target_pairs={{0,1},{1,0},{2,3},{3,2},{4,5},{5,4},{6,7},{7,6},{8,9},{9,8},{10,11... | collective-permute-start | bytes 1572872 | tf_op jit(solution)/shard_map/ppermute | solution.py:450
  391.5 0.1 dynamic-slice_bitcast_fusion.15
  391.7 10.4 %collective-permute-done.7 = f32[8,16384]{1,0:T(8,128)S(1)} collective-permute-done((f32[8,16384]{1,0:T(8,128)S(1)}, f32[8,16384]{1,0:T(8,128)S(1)}, u32[]{:S(2)}, u32[]{:S(2)}) %collective-permute-start.7) | collective-permute-done | bytes 524320 | tf_op jit(solution)/shard_map/ppermute | solution.py:450
  402.1 3.5 collective-permute-start.2
  405.6 30.9 %collective-permute-start = (f32[8,16384]{1,0:T(8,128)S(1)}, f32[8,16384]{1,0:T(8,128)S(1)}, u32[]{:S(2)}, u32[]{:S(2)}) collective-permute-start(f32[8,16384]{1,0:T(8,128)S(1)} %get-tuple-element.35), channel_id=1, source_target_pairs={{0,1},{1,0},{2,3},{3,2},{4,5},{5,4},{6,7},{7,6},{8,9},{9,8},{10,11... | collective-permute-start | bytes 1572872 | tf_op jit(solution)/shard_map/ppermute | solution.py:450
  436.5 1.8 fusion.24
  438.3 1.8 fusion.16
  440.1 7.0 %collective-permute-done.4 = f32[8,16384]{1,0:T(8,128)S(1)} collective-permute-done((f32[8,16384]{1,0:T(8,128)S(1)}, f32[8,16384]{1,0:T(8,128)S(1)}, u32[]{:S(2)}, u32[]{:S(2)}) %collective-permute-start.4) | collective-permute-done | bytes 524320 | tf_op jit(solution)/shard_map/ppermute | solution.py:450
  447.1 1.8 fusion.8
  448.9 19.6 %collective-permute-done.1 = f32[8,16384]{1,0:T(8,128)S(1)} collective-permute-done((f32[8,16384]{1,0:T(8,128)S(1)}, f32[8,16384]{1,0:T(8,128)S(1)}, u32[]{:S(2)}, u32[]{:S(2)}) %collective-permute-start.1) | collective-permute-done | bytes 524320 | tf_op jit(solution)/shard_map/ppermute | solution.py:450
  468.5 1.8 fusion.38
  470.4 0.2 fusion.50
  470.6 0.2 fusion.48
  470.8 11.5 %all-gather = f32[256,32]{1,0:T(8,128)S(1)} all-gather(f32[32,32]{1,0:T(8,128)S(1)} %fusion.48), channel_id=2, replica_groups=mesh['len'=8,'mem'=4] {'len'}, dimensions={0}, use_global_device_ids=true | all-gather | bytes 36864 | tf_op jit(solution)/shard_map/all_gather | solution.py:467
  482.3 13.1 %all-gather.1 = f32[128,32]{1,0:T(8,128)S(1)} all-gather(f32[32,32]{1,0:T(8,128)S(1)} %reduce_sum.20), channel_id=3, replica_groups=mesh['len'=8,'mem'=4] {'mem'}, dimensions={0}, use_global_device_ids=true | all-gather | bytes 20480 | tf_op jit(solution)/shard_map/all_gather | solution.py:467
  495.4 0.1 copy.17
  495.5 2.9 cholesky.18
  498.5 0.6 compare_reduce_fusion
  499.1 0.6 select_bitcast_fusion
  499.8 0.7 copy.18
  (43 shorter events, 0.2 us)
Async XLA Ops:
  7.0 2.0 copy-start.1
  9.0 54.4 %all-to-all-start = ((f32[8,8,128,128]{3,2,1,0:T(8,128)}), f32[8,8,128,128]{3,2,1,0:T(8,128)}, u32[]{:S(2)}, u32[]{:S(2)}) async-start(f32[8,8,128,128]{3,2,1,0:T(8,128)} %copy-done.1), calls=%async_computation | async-start | bytes 8388608 | tf_op jit(solution)/shard_map/all_to_all | solution.py:477
  20.5 2.0 copy-start
  22.5 45.5 %copy-start.15 = (f32[8]{0:T(128)S(1)}, f32[8]{0:T(128)}, u32[]{:S(2)}) copy-start(f32[8]{0:T(128)} %param.11) | copy-start | bytes 100
  22.5 45.5 %copy-start.16 = (f32[8]{0:T(128)S(1)}, f32[8]{0:T(128)}, u32[]{:S(2)}) copy-start(f32[8]{0:T(128)} %param.10) | copy-start | bytes 100
  22.5 45.5 %copy-start.17 = (f32[8]{0:T(128)S(1)}, f32[8]{0:T(128)}, u32[]{:S(2)}) copy-start(f32[8]{0:T(128)} %param.12) | copy-start | bytes 100
  63.4 53.7 %all-to-all-start.1 = ((f32[8,8,128,128]{3,2,1,0:T(8,128)}), f32[8,8,128,128]{3,2,1,0:T(8,128)}, u32[]{:S(2)}, u32[]{:S(2)}) async-start(f32[8,8,128,128]{3,2,1,0:T(8,128)} %copy-done), calls=%async_computation.1 | async-start | bytes 8388608 | tf_op jit(solution)/shard_map/all_to_all | solution.py:477
  152.6 1.4 copy-start.4
  154.0 1.4 copy-start.5
  155.4 35.7 %all-to-all-start.3 = ((f32[8,8,64,128]{3,2,1,0:T(8,128)}), f32[8,8,64,128]{3,2,1,0:T(8,128)S(1)}, u32[]{:S(2)}, u32[]{:S(2)}) async-start(f32[8,8,64,128]{3,2,1,0:T(8,128)} %copy-done.5), calls=%async_computation.3 | async-start | bytes 4194304 | tf_op jit(solution)/shard_map/all_to_all | solution.py:477
  188.4 1.4 copy-start.6
  189.8 1.3 copy-start.8
  191.1 31.1 %copy-start.7 = (f32[8,8,64,128]{3,2,1,0:T(8,128)S(1)}, f32[8,8,64,128]{3,2,1,0:T(8,128)}, u32[]{:S(2)}) copy-start(f32[8,8,64,128]{3,2,1,0:T(8,128)} %copy-done.6) | copy-start | bytes 6291460
  251.9 31.0 %all-to-all-start.2 = ((f32[8,8,64,128]{3,2,1,0:T(8,128)}), f32[8,8,64,128]{3,2,1,0:T(8,128)}, u32[]{:S(2)}, u32[]{:S(2)}) async-start(f32[8,8,64,128]{3,2,1,0:T(8,128)} %copy-done.4), calls=%async_computation.2 | async-start | bytes 4194304 | tf_op jit(solution)/shard_map/all_to_all | solution.py:477
  256.4 5.8 %copy-start.2 = (f32[8,8,64,128]{3,2,1,0:T(8,128)S(1)}, f32[8,8,64,128]{3,2,1,0:T(8,128)}, u32[]{:S(2)}) copy-start(f32[8,8,64,128]{3,2,1,0:T(8,128)} %all_to_all.30.refs_0_) | copy-start | bytes 6291460
  256.5 1.7 copy-start.3
  260.9 1.4 copy-start.9
  265.0 1.4 copy-start.11
  269.1 1.4 copy-start.13
  287.3 5.2 %copy-start.14 = (f32[4,8,16384]{2,1,0:T(8,128)S(1)}, f32[4,8,16384]{2,1,0:T(8,128)}, u32[]{:S(2)}) copy-start(f32[4,8,16384]{2,1,0:T(8,128)} %copy-done.13) | copy-start | bytes 6291460
  287.4 17.3 %collective-permute-start.11 = (f32[8,16384]{1,0:T(8,128)S(1)}, f32[8,16384]{1,0:T(8,128)S(1)}, u32[]{:S(2)}, u32[]{:S(2)}) collective-permute-start(f32[8,16384]{1,0:T(8,128)S(1)} %get-tuple-element.45), channel_id=1, source_target_pairs={{0,3},{1,2},{2,1},{3,0},{4,7},{5,6},{6,5},{7,4},{8,11},{9,10},{10,... | collective-permute-start | bytes 1572872 | tf_op jit(solution)/shard_map/ppermute | solution.py:450
  291.8 65.3 %collective-permute-start.10 = (f32[8,16384]{1,0:T(8,128)S(1)}, f32[8,16384]{1,0:T(8,128)S(1)}, u32[]{:S(2)}, u32[]{:S(2)}) collective-permute-start(f32[8,16384]{1,0:T(8,128)S(1)} %get-tuple-element.46), channel_id=1, source_target_pairs={{0,2},{1,3},{2,0},{3,1},{4,6},{5,7},{6,4},{7,5},{8,10},{9,11},{10,... | collective-permute-start | bytes 1572872 | tf_op jit(solution)/shard_map/ppermute | solution.py:450
  291.8 68.8 %collective-permute-start.9 = (f32[8,16384]{1,0:T(8,128)S(1)}, f32[8,16384]{1,0:T(8,128)S(1)}, u32[]{:S(2)}, u32[]{:S(2)}) collective-permute-start(f32[8,16384]{1,0:T(8,128)S(1)} %get-tuple-element.47), channel_id=1, source_target_pairs={{0,1},{1,0},{2,3},{3,2},{4,5},{5,4},{6,7},{7,6},{8,9},{9,8},{10,11... | collective-permute-start | bytes 1572872 | tf_op jit(solution)/shard_map/ppermute | solution.py:450
  292.5 4.0 copy-start.12
  292.6 68.0 %collective-permute-start.8 = (f32[8,16384]{1,0:T(8,128)S(1)}, f32[8,16384]{1,0:T(8,128)S(1)}, u32[]{:S(2)}, u32[]{:S(2)}) collective-permute-start(f32[8,16384]{1,0:T(8,128)S(1)} %get-tuple-element.41), channel_id=1, source_target_pairs={{0,3},{1,2},{2,1},{3,0},{4,7},{5,6},{6,5},{7,4},{8,11},{9,10},{10,... | collective-permute-start | bytes 1572872 | tf_op jit(solution)/shard_map/ppermute | solution.py:450
  296.4 105.7 %collective-permute-start.7 = (f32[8,16384]{1,0:T(8,128)S(1)}, f32[8,16384]{1,0:T(8,128)S(1)}, u32[]{:S(2)}, u32[]{:S(2)}) collective-permute-start(f32[8,16384]{1,0:T(8,128)S(1)} %get-tuple-element.42), channel_id=1, source_target_pairs={{0,2},{1,3},{2,0},{3,1},{4,6},{5,7},{6,4},{7,5},{8,10},{9,11},{10,... | collective-permute-start | bytes 1572872 | tf_op jit(solution)/shard_map/ppermute | solution.py:450
  296.4 95.1 %copy-start.10 = (f32[4,8,16384]{2,1,0:T(8,128)S(1)}, f32[4,8,16384]{2,1,0:T(8,128)}, u32[]{:S(2)}) copy-start(f32[4,8,16384]{2,1,0:T(8,128)} %copy-done.9) | copy-start | bytes 6291460
  304.8 100.9 %collective-permute-start.6 = (f32[8,16384]{1,0:T(8,128)S(1)}, f32[8,16384]{1,0:T(8,128)S(1)}, u32[]{:S(2)}, u32[]{:S(2)}) collective-permute-start(f32[8,16384]{1,0:T(8,128)S(1)} %get-tuple-element.43), channel_id=1, source_target_pairs={{0,1},{1,0},{2,3},{3,2},{4,5},{5,4},{6,7},{7,6},{8,9},{9,8},{10,11... | collective-permute-start | bytes 1572872 | tf_op jit(solution)/shard_map/ppermute | solution.py:450
  357.1 48.5 %collective-permute-start.5 = (f32[8,16384]{1,0:T(8,128)S(1)}, f32[8,16384]{1,0:T(8,128)S(1)}, u32[]{:S(2)}, u32[]{:S(2)}) collective-permute-start(f32[8,16384]{1,0:T(8,128)S(1)} %get-tuple-element.37), channel_id=1, source_target_pairs={{0,3},{1,2},{2,1},{3,0},{4,7},{5,6},{6,5},{7,4},{8,11},{9,10},{10,... | collective-permute-start | bytes 1572872 | tf_op jit(solution)/shard_map/ppermute | solution.py:450
  360.7 86.4 %collective-permute-start.4 = (f32[8,16384]{1,0:T(8,128)S(1)}, f32[8,16384]{1,0:T(8,128)S(1)}, u32[]{:S(2)}, u32[]{:S(2)}) collective-permute-start(f32[8,16384]{1,0:T(8,128)S(1)} %get-tuple-element.38), channel_id=1, source_target_pairs={{0,2},{1,3},{2,0},{3,1},{4,6},{5,7},{6,4},{7,5},{8,10},{9,11},{10,... | collective-permute-start | bytes 1572872 | tf_op jit(solution)/shard_map/ppermute | solution.py:450
  360.7 86.4 %collective-permute-start.3 = (f32[8,16384]{1,0:T(8,128)S(1)}, f32[8,16384]{1,0:T(8,128)S(1)}, u32[]{:S(2)}, u32[]{:S(2)}) collective-permute-start(f32[8,16384]{1,0:T(8,128)S(1)} %get-tuple-element.39), channel_id=1, source_target_pairs={{0,1},{1,0},{2,3},{3,2},{4,5},{5,4},{6,7},{7,6},{8,9},{9,8},{10,11... | collective-permute-start | bytes 1572872 | tf_op jit(solution)/shard_map/ppermute | solution.py:450
  402.1 46.8 %collective-permute-start.2 = (f32[8,16384]{1,0:T(8,128)S(1)}, f32[8,16384]{1,0:T(8,128)S(1)}, u32[]{:S(2)}, u32[]{:S(2)}) collective-permute-start(f32[8,16384]{1,0:T(8,128)S(1)} %get-tuple-element.33), channel_id=1, source_target_pairs={{0,3},{1,2},{2,1},{3,0},{4,7},{5,6},{6,5},{7,4},{8,11},{9,10},{10,... | collective-permute-start | bytes 1572872 | tf_op jit(solution)/shard_map/ppermute | solution.py:450
  405.6 62.9 %collective-permute-start.1 = (f32[8,16384]{1,0:T(8,128)S(1)}, f32[8,16384]{1,0:T(8,128)S(1)}, u32[]{:S(2)}, u32[]{:S(2)}) collective-permute-start(f32[8,16384]{1,0:T(8,128)S(1)} %get-tuple-element.34), channel_id=1, source_target_pairs={{0,2},{1,3},{2,0},{3,1},{4,6},{5,7},{6,4},{7,5},{8,10},{9,11},{10,... | collective-permute-start | bytes 1572872 | tf_op jit(solution)/shard_map/ppermute | solution.py:450
  405.6 62.9 %collective-permute-start = (f32[8,16384]{1,0:T(8,128)S(1)}, f32[8,16384]{1,0:T(8,128)S(1)}, u32[]{:S(2)}, u32[]{:S(2)}) collective-permute-start(f32[8,16384]{1,0:T(8,128)S(1)} %get-tuple-element.35), channel_id=1, source_target_pairs={{0,1},{1,0},{2,3},{3,2},{4,5},{5,4},{6,7},{7,6},{8,9},{9,8},{10,11... | collective-permute-start | bytes 1572872 | tf_op jit(solution)/shard_map/ppermute | solution.py:450

commit v4 on v3

--- a/solution.py
+++ b/solution.py
@@ -19,7 +19,6 @@
 WIDE = 256
 BLOCK_ROWS = 16
 OUTER_TILES = 2
-OUT_PARTS = 2
 VMEM_LIMIT = 48 * 1024 * 1024
 SIN_HALF = (0.49999999785787, -0.02083332246218, 2.604078316692e-4, -1.547581723527e-6, 5.088214043e-9)
 COS_HALF = (
@@ -344,6 +343,45 @@
             value = flat_ref[pl.ds(tile * rows + r, members, stride=tiles * rows), :]
             out_ref[0, :, at : at + LANES] = value
             copy_ref[0, :, at : at + LANES] = value
+
+
+def mirror_kernel(base_ref, own_ref, far_ref, edge_ref, out_ref):
+    members, length = own_ref.shape
+    tiles = length // LANES - 1
+    shape = (members, LANES)
+    lane = lax.broadcasted_iota(jnp.int32, shape, 1)
+    mirror = (LANES - lane) % LANES
+    first_group, last_group = base_ref[1] == 0, base_ref[1] == base_ref[2] - 1
+    beyond = own_ref[:, tiles * LANES :]
+    scale = jnp.broadcast_to(beyond[:, 1:2], shape)
+    exponent = jnp.broadcast_to(beyond[:, 2:3], shape)
+    half_root = math.sqrt(0.5)
+
+    def tile_of(ref, tile):
+        return ref[:, pl.ds(pl.multiple_of(tile * LANES, LANES), LANES)]
+
+    def turned(value):
+        return jnp.take_along_axis(value, mirror, axis=1, mode="promise_in_bounds")
+
+    def store(tile, own, far, weight):
+        offset = base_ref[0] + tile * LANES + lane
+        near = left_lines(own, offset.astype(jnp.float32), scale, exponent)
+        far_offset = jnp.where(offset == 0, 0, OUTER * INNER - offset)
+        back = left_lines(far, far_offset.astype(jnp.float32), scale, exponent)
+        at = pl.ds(pl.multiple_of(tile * LANES, LANES), LANES)
+        out_ref[0, :, at] = (near[0] + back[0]) * weight
+        out_ref[1, :, at] = (near[1] - back[1]) * weight
+
+    def one_tile(tile, last):
+        ahead = turned(tile_of(far_ref, tiles - 1 - tile))
+        is_edge = (lane == 0) & (tile == 0) & first_group
+        store(tile, tile_of(own_ref, tile), jnp.where(lane == 0, last, ahead), jnp.where(is_edge, half_root, 1.0))
+        return ahead
+
+    start = jnp.where(first_group, turned(edge_ref[...]), turned(tile_of(far_ref, tiles)))
+    last = lax.fori_loop(0, tiles, one_tile, start)
+    lone = (lane == 0) & last_group
+    store(tiles, jnp.where(lone, beyond, 0.0), jnp.where(lone, last, 0.0), jnp.where(lone, half_root, 0.0))
 
 
 def limits():
@@ -435,22 +473,92 @@
     )(mid, matrices)
 
 
+def mirror_call(base, own, far, edge):
+    members, length = own.shape
+    return pl.pallas_call(
+        mirror_kernel,
+        in_specs=[pl.BlockSpec(memory_space=pltpu.SMEM)] + [pl.BlockSpec(memory_space=pltpu.VMEM)] * 3,
+        out_specs=pl.BlockSpec(memory_space=pltpu.VMEM),
+        out_shape=jax.ShapeDtypeStruct((2, members, length), jnp.float32),
+        compiler_params=limits(),
+        cost_estimate=pl.CostEstimate(
+            flops=200 * members * length, bytes_accessed=16 * members * length, transcendentals=0
+        ),
+    )(base, own, far, edge)
+
+
 def line_params(roughness, waviness, coherence):
     return jnp.stack(
         [jnp.sqrt(2.0 * roughness * (waviness - 1.0) / ANCHOR), -0.5 * waviness, 1.0 / coherence]
     )
 
 
-def slot_gram(stretches, groups):
+def to_group(piece, slot):
+    groups = lax.axis_size("mem")
+    return lax.ppermute(piece, "mem", [(z, z ^ slot) for z in range(groups)]) if slot else piece
+
+
+def rows_gram(rows):
+    return lax.dot_general(rows, rows, (((1,), (1,)), ((), ())), precision=highest)
+
+
+def slot_rows(stretches, groups):
     my_group = lax.axis_index("mem")
-    received = []
+    return jnp.concatenate(
+        [
+            to_group(lax.dynamic_index_in_dim(stretches, my_group ^ slot, 0, keepdims=False), slot)
+            for slot in range(groups)
+        ],
+        axis=0,
+    )
+
+
+def own_and_far(phase, params):
+    groups = lax.axis_size("mem")
+    my_group = lax.axis_index("mem")
+    half = phase.shape[1] // 2
+    width = half // groups
+    lane = lax.broadcasted_iota(jnp.int32, (phase.shape[0], LANES), 1)
+
+    def lines(start):
+        return (
+            lax.dynamic_slice_in_dim(phase, start, width, 1),
+            lax.dynamic_slice_in_dim(phase, start + width, LANES, 1),
+        )
+
+    own, far = [], []
     for slot in range(groups):
-        piece = lax.dynamic_index_in_dim(stretches, my_group ^ slot, 0, keepdims=False)
-        if slot:
-            piece = lax.ppermute(piece, "mem", [(z, z ^ slot) for z in range(groups)])
-        received.append(piece)
-    together = jnp.concatenate(received, axis=0)
-    return lax.dot_general(together, together, (((1,), (1,)), ((), ())), precision=highest)
+        group = my_group ^ slot
+        inner, beyond = lines(group * width)
+        for n in range(2):
+            beyond = jnp.where(lane == n + 1, params[n][:, None], beyond)
+        far_inner, far_beyond = lines(half + (groups - 1 - group) * width)
+        message = jnp.concatenate(
+            [
+                jnp.concatenate([inner, beyond], axis=1)[None],
+                jnp.concatenate([far_inner, far_beyond], axis=1)[None],
+            ]
+        )
+        message = to_group(message, slot)
+        own.append(message[0])
+        far.append(message[1])
+    return jnp.concatenate(own, axis=0), jnp.concatenate(far, axis=0)
+
+
+def edge_of(own):
+    shards = lax.axis_size("len")
+    return lax.ppermute(own[:, :LANES], "len", [(d, (shards - d) % shards) for d in range(shards)])
+
+
+def lines_gram(own, far, edge):
+    shards, groups = lax.axis_size("len"), lax.axis_size("mem")
+    my_index, my_group = lax.axis_index("len"), lax.axis_index("mem")
+    width = own.shape[1] - LANES
+    far = lax.ppermute(far, "len", [(d, shards - 1 - d) for d in range(shards)])
+    base = (my_index * (2 * groups) + my_group) * width
+    base = jnp.stack([base, my_group, jnp.full_like(my_group, groups)]).astype(jnp.int32)
+    sums = mirror_call(base, own, far, edge)
+    return rows_gram(sums[0]) + rows_gram(sums[1])
 
 
 def in_order(gram_matrix, members):
@@ -476,23 +584,40 @@
     def swap(piece):
         return lax.all_to_all(piece, "len", split_axis=0, concat_axis=0, tiled=True)
 
-    params = lax.dynamic_index_in_dim(
-        line_params(roughness, waviness, coherence), my_index, 1, keepdims=False
-    )
+    all_params = line_params(roughness, waviness, coherence)
+    params = lax.dynamic_index_in_dim(all_params, my_index, 1, keepdims=False)
     outer_tables = jnp.asarray(outer_matrices())
     inner_tables = jnp.asarray(inner_matrices())
     twists = jnp.asarray(twist_tables())
+    places = 4
+
+    def transform(phases, track):
+        mid = outer_call(params, phases, outer_tables, twists, track)
+        return list(inner_call(mid, inner_tables, shards, 2))
+
     left = swap(part_call(phase_left))
+    own, far = own_and_far(phase_left, all_params)
     right = swap(part_call(phase_right))
-    profile, gram_matrix, place = None, 0.0, 0
-    for track, phases in enumerate(((left,), (left, right))):
-        mid = outer_call(params, phases, outer_tables, twists, track)
-        for piece in inner_call(mid, inner_tables, shards, OUT_PARTS):
-            profile, stretches = join_call(swap(piece), place, 2 * OUT_PARTS, groups, profile)
-            gram_matrix = gram_matrix + slot_gram(stretches, groups)
-            place += 1
-    gram_matrix = summed(in_order(gram_matrix, members)) * (0.5 / (OUTER * INNER))
-    return (profile, upper_of(gram_matrix))
+    first = transform((left,), 0)
+    left, right, *first = lax.optimization_barrier((left, right, *first))
+    early = swap(first[0])
+    second = transform((left, right), 1)
+    early, second[0] = lax.optimization_barrier((early, second[0]))
+    ahead = swap(second[0])
+    edge = edge_of(own)
+    ahead, edge, second[1] = lax.optimization_barrier((ahead, edge, second[1]))
+    profile, ahead = join_call(ahead, 2, places, groups, None)
+    behind = swap(second[1])
+    behind, first[1], far = lax.optimization_barrier((behind, first[1], far))
+    line_gram = lines_gram(own, far, edge)
+    profile, behind = join_call(behind, 3, places, groups, profile)
+    late = swap(first[1])
+    point_gram = rows_gram(slot_rows(ahead, groups)) + rows_gram(slot_rows(behind, groups))
+    late, point_gram = lax.optimization_barrier((late, point_gram))
+    profile, _ = join_call(early, 0, places, groups, profile)
+    profile, _ = join_call(late, 1, places, groups, profile)
+    gram_matrix = 0.25 * line_gram + (0.5 / (OUTER * INNER)) * point_gram
+    return (profile, upper_of(summed(in_order(gram_matrix, members))))
 
 
 def per_device(phase_left, phase_right, roughness, waviness, coherence):

time: 501 us -> 397 us (0.79)
  starting transfers between devices: 133 us -> 39.9 us
  blocking collectives: 85.4 us -> 32.3 us
  Pallas kernels: 90.1 us -> 109 us
  other arithmetic: 4.32 us -> 12.9 us
  local copies, waits for them, and re-layouts: 16.8 us -> 24.5 us
  matrix products: 7.58 us -> 14.5 us
    ppermute x12 -> x11, starting transfers between devices: 115 us -> 13.9 us  [the longest x9 13.2 us: to_group(): lax.ppermute(piece, 'mem', [(z, z ^ slot) for z in range(groups)])]
    all_to_all x2 -> x0, blocking collectives: 60.8 us -> none  [swap(): return lax.all_to_all(piece, 'len', split_axis=0, concat_axis=0, tiled=True)]
    all_to_all x4 -> x6, waiting for transfers between devices: 102 us -> 76.9 us  [swap(): return lax.all_to_all(piece, 'len', split_axis=0, concat_axis=0, tiled=True)]
    ppermute x12 -> x11, waiting for transfers between devices: 59.8 us -> 84.5 us  [the longest x9 84.5 us: to_group(): lax.ppermute(piece, 'mem', [(z, z ^ slot) for z in range(groups)])]
    pallas_call x0 -> x1, Pallas kernels: none -> 15.4 us  [mirror_call(): pl.pallas_call(mirror_kernel, in_specs=[pl.BlockSpec(memory_space=pltpu.S...]
    all_to_all x4 -> x6, starting transfers between devices: 17.9 us -> 26 us  [swap(): return lax.all_to_all(piece, 'len', split_axis=0, concat_axis=0, tiled=True)]
    all_gather x2, blocking collectives: 24.6 us -> 32.3 us  [summed(): value = jnp.sum(lax.all_gather(value, axis), axis=0)]
    squeeze x4 -> x5, local copies, waits for them, and re-layouts: 0.55 us -> 8.16 us  [the longest x3 5.24 us: own_and_far(): far.append(message[1])]
  transfers between devices with their start and end apart: 16 -> 17, of which waited for: 8 -> 9; matrix products, arithmetic and copies ran while one was open for 1% -> 5% of each run, Pallas kernels for 9% -> 24%
where the time goes in v4:
time: 397 us; the launch traced here: 396 us
  waiting for transfers between devices  161 us (41%)
  Pallas kernels  109 us (27%)
  starting transfers between devices  39.9 us (10%)
  blocking collectives  32.3 us (8%)
  local copies, waits for them, and re-layouts  24.5 us (6%)
  matrix products  14.5 us (4%)
  other arithmetic  12.9 us (3%)
    ppermute x9, waiting for transfers between devices, to_group(): lax.ppermute(piece, 'mem', [(z, z ^ slot) for z in range(groups)])  84.5 us
    all_to_all x6, waiting for transfers between devices, swap(): return lax.all_to_all(piece, 'len', split_axis=0, concat_axis=0, tiled=True)  76.9 us
    pallas_call x2, Pallas kernels, outer_call(): pl.pallas_call(functools.partial(outer_kernel, track), grid=(tiles // som...  47.2 us
    all_gather x2, blocking collectives, summed(): value = jnp.sum(lax.all_gather(value, axis), axis=0)  32.3 us
    all_to_all x6, starting transfers between devices, swap(): return lax.all_to_all(piece, 'len', split_axis=0, concat_axis=0, tiled=True)  26 us
    pallas_call x2, Pallas kernels, inner_call(): pl.pallas_call(inner_kernel, grid=(OUTER // WIDE,), in_specs=[pl.BlockSpe...  17.7 us
    pallas_call x4, Pallas kernels, join_call(): pl.pallas_call(join_kernel, grid=(steps,), in_specs=[pl.BlockSpec((member...  16.6 us
    pallas_call x1, Pallas kernels, mirror_call(): pl.pallas_call(mirror_kernel, in_specs=[pl.BlockSpec(memory_space=pltpu.S...  15.4 us
  transfers between devices with their start and end apart: 17, of which 9 were waited for; matrix products, arithmetic and copies ran while one was open for 5% of the time, Pallas kernels for 24%

profile of v4, /device:TPU:0, one launch (start us, length us, event | category | flops | bytes accessed | tf_op | source)
XLA Modules:
  0.0 396.0 jit_solution(9330701381084300067)
XLA Ops:
  0.8 0.7 broadcast_multiply_fusion
  1.4 3.4 constant_dynamic-slice_fusion.1
  4.9 0.9 constant_dynamic-slice_fusion
  6.0 3.1 collective-permute-start
  9.1 1.1 pad_maximum_fusion.3
  10.2 2.6 collective-permute-start.1
  12.9 1.1 pad_maximum_fusion.4
  14.0 6.3 %shard_map.95 = f32[8,8,128,128]{3,2,1,0:T(8,128)S(1)} custom-call(f32[8,131072]{1,0:T(8,128)} %in_ref.2), custom_call_target="tpu_custom_call" | custom-call | bytes 8388608 | tf_op jit(solution)/shard_map/pallas_call | solution.py:395
  20.4 2.0 copy-done.1
  22.4 4.6 %all-to-all-start = ((f32[8,8,128,128]{3,2,1,0:T(8,128)}), f32[8,8,128,128]{3,2,1,0:T(8,128)}, u32[]{:S(2)}, u32[]{:S(2)}) async-start(f32[8,8,128,128]{3,2,1,0:T(8,128)} %copy-done.1), calls=%async_computation | async-start | bytes 8388608 | tf_op jit(solution)/shard_map/all_to_all | solution.py:585
  26.9 6.3 %shard_map.96 = f32[8,8,128,128]{3,2,1,0:T(8,128)S(1)} custom-call(f32[8,131072]{1,0:T(8,128)} %in_ref.3), custom_call_target="tpu_custom_call" | custom-call | bytes 8388608 | tf_op jit(solution)/shard_map/pallas_call | solution.py:395
  33.3 2.0 copy-done
  35.5 18.2 %collective-permute-done = f32[2,8,16512]{2,1,0:T(8,128)} collective-permute-done((f32[2,8,16512]{2,1,0:T(8,128)S(1)}, f32[2,8,16512]{2,1,0:T(8,128)}, u32[]{:S(2)}, u32[]{:S(2)}) %collective-permute-start) | collective-permute-done | bytes 1056800 | tf_op jit(solution)/shard_map/ppermute | solution.py:498
  53.6 2.1 slice_bitcast_fusion.12
  55.7 20.3 %all-to-all-done.refs_0_ = f32[8,8,128,128]{3,2,1,0:T(8,128)} async-done(((f32[8,8,128,128]{3,2,1,0:T(8,128)}), f32[8,8,128,128]{3,2,1,0:T(8,128)}, u32[]{:S(2)}, u32[]{:S(2)}) %all-to-all-start) | async-done | bytes 4194336 | tf_op jit(solution)/shard_map/all_to_all | solution.py:585
  76.0 4.6 %all-to-all-start.1 = ((f32[8,8,128,128]{3,2,1,0:T(8,128)}), f32[8,8,128,128]{3,2,1,0:T(8,128)}, u32[]{:S(2)}, u32[]{:S(2)}) async-start(f32[8,8,128,128]{3,2,1,0:T(8,128)} %copy-done), calls=%async_computation.1 | async-start | bytes 8388608 | tf_op jit(solution)/shard_map/all_to_all | solution.py:585
  80.6 2.3 collective-permute-done.1
  82.9 0.9 slice_bitcast_fusion.11
  83.8 20.5 %shard_map.97.mid_ref = f32[8,2,1024,128]{3,2,1,0:T(8,128)} custom-call(f32[3]{0:T(128)S(1)} %fusion.34.params_ref, f32[8,8,128,128]{3,2,1,0:T(8,128)} %all-to-all-done.refs_0_, bf16[2,4,512,512]{3,2,1,0:T(8,128)(2,1)} %constant.169.clone.refs_1_.refs_2_, f32[2,4,256,1024]{3,2,1,0:T(8,128)} %constant.171.clone.refs_2_.refs_3_), custom_call_target="tpu_custom_call" | custom-call | flops 6442450944 | bytes 20971520 | tf_op jit(solution)/shard_map/pallas_call | solution.py:437
  104.3 8.8 %shard_map.98 = (f32[8,8,64,128]{3,2,1,0:T(8,128)S(1)}, f32[8,8,64,128]{3,2,1,0:T(8,128)S(1)}) custom-call(f32[8,2,1024,128]{3,2,1,0:T(8,128)} %shard_map.97.mid_ref, bf16[2,4,256,512]{3,2,1,0:T(8,128)(2,1)} %constant.170.clone.matrix_ref), custom_call_target="tpu_custom_call" | custom-call | flops 3221225472 | bytes 12582912 | tf_op jit(solution)/shard_map/pallas_call | solution.py:459
  113.2 1.3 copy-done.4
  114.5 1.3 copy-done.7
  115.8 14.0 %all-to-all-done.1.refs_1_ = f32[8,8,128,128]{3,2,1,0:T(8,128)} async-done(((f32[8,8,128,128]{3,2,1,0:T(8,128)}), f32[8,8,128,128]{3,2,1,0:T(8,128)}, u32[]{:S(2)}, u32[]{:S(2)}) %all-to-all-start.1) | async-done | bytes 4194336 | tf_op jit(solution)/shard_map/all_to_all | solution.py:585
  129.7 3.6 all-to-all-start.2
  133.4 2.3 slice_bitcast_fusion.10
  135.6 26.7 %shard_map.99.mid_ref = f32[8,2,1024,128]{3,2,1,0:T(8,128)} custom-call(f32[3]{0:T(128)S(1)} %fusion.34.params_ref, f32[8,8,128,128]{3,2,1,0:T(8,128)} %all-to-all-done.refs_0_, f32[8,8,128,128]{3,2,1,0:T(8,128)} %all-to-all-done.1.refs_1_, bf16[2,4,512,512]{3,2,1,0:T(8,128)(2,1)} %constant.169.clone.refs_1_.refs_2_, ...), custom_call_target="tpu_custom_call" | custom-call | flops 6442450944 | bytes 20971520 | tf_op jit(solution)/shard_map/pallas_call | solution.py:437
  162.3 8.8 %shard_map.100 = (f32[8,8,64,128]{3,2,1,0:T(8,128)S(1)}, f32[8,8,64,128]{3,2,1,0:T(8,128)S(1)}) custom-call(f32[8,2,1024,128]{3,2,1,0:T(8,128)} %shard_map.99.mid_ref, bf16[2,4,256,512]{3,2,1,0:T(8,128)(2,1)} %constant.170.clone.matrix_ref), custom_call_target="tpu_custom_call" | custom-call | flops 3221225472 | bytes 12582912 | tf_op jit(solution)/shard_map/pallas_call | solution.py:459
  171.2 1.4 copy-done.5
  172.6 1.3 copy-done.6
  173.9 1.3 copy-done.2
  175.2 4.4 %all-to-all-start.3 = ((f32[8,8,64,128]{3,2,1,0:T(8,128)}), f32[8,8,64,128]{3,2,1,0:T(8,128)}, u32[]{:S(2)}, u32[]{:S(2)}) async-start(f32[8,8,64,128]{3,2,1,0:T(8,128)} %copy-done.6), calls=%async_computation.3 | async-start | bytes 4194304 | tf_op jit(solution)/shard_map/all_to_all | solution.py:585
  179.6 1.7 pad_maximum_fusion.own_ref
  181.2 0.7 collective-permute-start.3
  182.0 24.4 %all-to-all-done.3.refs_0_ = f32[8,8,64,128]{3,2,1,0:T(8,128)} async-done(((f32[8,8,64,128]{3,2,1,0:T(8,128)}), f32[8,8,64,128]{3,2,1,0:T(8,128)}, u32[]{:S(2)}, u32[]{:S(2)}) %all-to-all-start.3) | async-done | bytes 2097184 | tf_op jit(solution)/shard_map/all_to_all | solution.py:585
  206.4 4.4 %all-to-all-start.4 = ((f32[8,8,64,128]{3,2,1,0:T(8,128)}), f32[8,8,64,128]{3,2,1,0:T(8,128)}, u32[]{:S(2)}, u32[]{:S(2)}) async-start(f32[8,8,64,128]{3,2,1,0:T(8,128)} %copy-done.5), calls=%async_computation.4 | async-start | bytes 4194304 | tf_op jit(solution)/shard_map/all_to_all | solution.py:585
  210.8 2.7 pad_maximum_fusion.1
  213.5 4.4 %shard_map.101 = (f32[2,8,131072]{2,1,0:T(8,128)}, f32[4,8,16384]{2,1,0:T(8,128)S(1)}) custom-call(f32[8,8,64,128]{3,2,1,0:T(8,128)} %all-to-all-done.3.refs_0_), custom_call_target="tpu_custom_call" | custom-call | bytes 6291456 | tf_op jit(solution)/shard_map/pallas_call | solution.py:413
  217.9 1.4 copy-done.8
  219.3 18.2 %all-to-all-done.4.refs_0_ = f32[8,8,64,128]{3,2,1,0:T(8,128)} async-done(((f32[8,8,64,128]{3,2,1,0:T(8,128)}), f32[8,8,64,128]{3,2,1,0:T(8,128)}, u32[]{:S(2)}, u32[]{:S(2)}) %all-to-all-start.4) | async-done | bytes 2097184 | tf_op jit(solution)/shard_map/all_to_all | solution.py:585
  237.4 4.4 %shard_map.102 = (f32[2,8,131072]{2,1,0:T(8,128)}, f32[4,8,16384]{2,1,0:T(8,128)S(1)}) custom-call(f32[8,8,64,128]{3,2,1,0:T(8,128)} %all-to-all-done.4.refs_0_, f32[2,8,131072]{2,1,0:T(8,128)} %get-tuple-element.40.refs_1_), custom_call_target="tpu_custom_call", output_to_operand_aliasing={{0}: (1, {})} | custom-call | bytes 6291456 | tf_op jit(solution)/shard_map/pallas_call | solution.py:413
  241.8 1.1 dynamic-slice_bitcast_fusion.3
  242.9 0.9 collective-permute-start.7
  243.8 3.5 collective-permute-start.8
  247.3 4.5 %all-to-all-start.5 = ((f32[8,8,64,128]{3,2,1,0:T(8,128)}), f32[8,8,64,128]{3,2,1,0:T(8,128)}, u32[]{:S(2)}, u32[]{:S(2)}) async-start(f32[8,8,64,128]{3,2,1,0:T(8,128)} %copy-done.4), calls=%async_computation.5 | async-start | bytes 4194304 | tf_op jit(solution)/shard_map/all_to_all | solution.py:585
  251.9 1.8 dynamic-slice_bitcast_fusion.7
  253.7 0.6 collective-permute-start.4
  254.3 14.7 %collective-permute-done.7 = f32[8,16384]{1,0:T(8,128)} collective-permute-done((f32[8,16384]{1,0:T(8,128)}, f32[8,16384]{1,0:T(8,128)}, u32[]{:S(2)}, u32[]{:S(2)}) %collective-permute-start.7) | collective-permute-done | bytes 524320 | tf_op jit(solution)/shard_map/ppermute | solution.py:498
  269.2 13.8 %collective-permute-done.8 = f32[8,16384]{1,0:T(8,128)} collective-permute-done((f32[8,16384]{1,0:T(8,128)}, f32[8,16384]{1,0:T(8,128)}, u32[]{:S(2)}, u32[]{:S(2)}) %collective-permute-start.8) | collective-permute-done | bytes 524320 | tf_op jit(solution)/shard_map/ppermute | solution.py:498
  282.9 2.4 collective-permute-start.6
  285.4 3.1 shard_map.103
  288.5 3.7 fusion.10
  292.2 35.5 %collective-permute-done.5 = f32[8,16384]{1,0:T(8,128)S(1)} collective-permute-done((f32[8,16384]{1,0:T(8,128)S(1)}, f32[8,16384]{1,0:T(8,128)S(1)}, u32[]{:S(2)}, u32[]{:S(2)}) %collective-permute-start.5) | collective-permute-done | bytes 524320 | tf_op jit(solution)/shard_map/ppermute | solution.py:498
  327.8 1.8 fusion.21
  329.6 4.7 %shard_map.104 = (f32[2,8,131072]{2,1,0:T(8,128)}, f32[4,8,16384]{2,1,0:T(8,128)}) custom-call(f32[8,8,64,128]{3,2,1,0:T(8,128)} %all-to-all-done.5.refs_0_, f32[2,8,131072]{2,1,0:T(8,128)} %get-tuple-element.45.refs_1_), custom_call_target="tpu_custom_call", output_to_operand_aliasing={{0}: (1, {})} | custom-call | bytes 6291456 | tf_op jit(solution)/shard_map/pallas_call | solution.py:413
  334.4 15.4 %shard_map.105 = f32[2,32,16512]{2,1,0:T(8,128)} custom-call(s32[3]{0:T(128)S(1)} %pad_add_fusion.base_ref, f32[32,16512]{1,0:T(8,128)S(1)} %pad_maximum_fusion.own_ref, f32[32,16512]{1,0:T(8,128)} %collective-permute-done.10.far_ref, f32[32,128]{1,0:T(8,128)S(1)} %collective-permute-done.3.edge_ref), custom_call_target="tpu_custom_call" | custom-call | flops 105676800 | bytes 8454144 | tf_op jit(solution)/shard_map/pallas_call | solution.py:478
  349.7 4.2 %fusion = f32[32,32]{1,0:T(8,128)S(1)} fusion(f32[2,32,16512]{2,1,0:T(8,128)} %shard_map.105), kind=kOutput, calls=%fused_computation.1 | convolution fusion | flops 202899456 | bytes 2117632 | tf_op jit(solution)/shard_map/dot_general | solution.py:502
  354.0 4.2 %fusion.20 = f32[32,32]{1,0:T(8,128)S(1)} fusion(f32[32,32]{1,0:T(8,128)S(1)} %fusion, f32[2,32,16512]{2,1,0:T(8,128)} %shard_map.105, f32[32,32]{1,0:T(8,128)S(1)} %fusion.21), kind=kOutput, calls=%fused_computation.24 | convolution fusion | flops 202903552 | bytes 2125824 | tf_op jit(solution)/shard_map/dot_general | solution.py:502
  358.4 0.2 fusion.38
  358.7 9.3 %all-gather = f32[256,32]{1,0:T(8,128)S(1)} all-gather(f32[32,32]{1,0:T(8,128)S(1)} %fusion.38), channel_id=2, replica_groups=mesh['len'=8,'mem'=4] {'len'}, dimensions={0}, use_global_device_ids=true | all-gather | bytes 36864 | tf_op jit(solution)/shard_map/all_gather | solution.py:575
  368.0 23.0 %all-gather.1 = f32[128,32]{1,0:T(8,128)S(1)} all-gather(f32[32,32]{1,0:T(8,128)S(1)} %reduce_sum.18), channel_id=3, replica_groups=mesh['len'=8,'mem'=4] {'mem'}, dimensions={0}, use_global_device_ids=true | all-gather | bytes 20480 | tf_op jit(solution)/shard_map/all_gather | solution.py:575
  391.1 2.9 cholesky.18
  394.0 0.6 compare_reduce_fusion
  394.7 0.6 select_bitcast_fusion
  395.3 0.7 copy.18
  (44 shorter events, 1.2 us)
Async XLA Ops:
  6.0 47.7 %collective-permute-start = (f32[2,8,16512]{2,1,0:T(8,128)S(1)}, f32[2,8,16512]{2,1,0:T(8,128)}, u32[]{:S(2)}, u32[]{:S(2)}) collective-permute-start(f32[2,8,16512]{2,1,0:T(8,128)S(1)} %pad_maximum_fusion.2), channel_id=1, source_target_pairs={{0,1},{1,0},{2,3},{3,2},{4,5},{5,4},{6,7},{7,6},{8,9},{9,8},{10,11... | collective-permute-start | bytes 3170312 | tf_op jit(solution)/shard_map/ppermute | solution.py:498
  10.2 72.7 %collective-permute-start.1 = (f32[2,8,16512]{2,1,0:T(8,128)}, f32[2,8,16512]{2,1,0:T(8,128)S(1)}, u32[]{:S(2)}, u32[]{:S(2)}) collective-permute-start(f32[2,8,16512]{2,1,0:T(8,128)} %pad_maximum_fusion.3), channel_id=1, source_target_pairs={{0,2},{1,3},{2,0},{3,1},{4,6},{5,7},{6,4},{7,5},{8,10},{9,11},{10,... | collective-permute-start | bytes 3170312 | tf_op jit(solution)/shard_map/ppermute | solution.py:498
  14.0 119.3 %collective-permute-start.2 = (f32[2,8,16512]{2,1,0:T(8,128)}, f32[2,8,16512]{2,1,0:T(8,128)}, u32[]{:S(2)}, u32[]{:S(2)}) collective-permute-start(f32[2,8,16512]{2,1,0:T(8,128)} %pad_maximum_fusion.4), channel_id=1, source_target_pairs={{0,3},{1,2},{2,1},{3,0},{4,7},{5,6},{6,5},{7,4},{8,11},{9,10},{10,... | collective-permute-start | bytes 3170312 | tf_op jit(solution)/shard_map/ppermute | solution.py:498
  20.3 2.0 copy-start.1
  22.4 53.7 %all-to-all-start = ((f32[8,8,128,128]{3,2,1,0:T(8,128)}), f32[8,8,128,128]{3,2,1,0:T(8,128)}, u32[]{:S(2)}, u32[]{:S(2)}) async-start(f32[8,8,128,128]{3,2,1,0:T(8,128)} %copy-done.1), calls=%async_computation | async-start | bytes 8388608 | tf_op jit(solution)/shard_map/all_to_all | solution.py:585
  26.9 8.3 %copy-start.9 = (f32[8]{0:T(128)S(1)}, f32[8]{0:T(128)}, u32[]{:S(2)}) copy-start(f32[8]{0:T(128)} %param.12) | copy-start | bytes 100
  33.3 2.0 copy-start
  76.0 53.7 %all-to-all-start.1 = ((f32[8,8,128,128]{3,2,1,0:T(8,128)}), f32[8,8,128,128]{3,2,1,0:T(8,128)}, u32[]{:S(2)}, u32[]{:S(2)}) async-start(f32[8,8,128,128]{3,2,1,0:T(8,128)} %copy-done), calls=%async_computation.1 | async-start | bytes 8388608 | tf_op jit(solution)/shard_map/all_to_all | solution.py:585
  113.2 1.3 copy-start.4
  114.5 1.3 copy-start.7
  129.7 44.1 %all-to-all-start.2 = ((f32[8,8,64,128]{3,2,1,0:T(8,128)}), f32[8,8,64,128]{3,2,1,0:T(8,128)S(1)}, u32[]{:S(2)}, u32[]{:S(2)}) async-start(f32[8,8,64,128]{3,2,1,0:T(8,128)} %copy-done.7), calls=%async_computation.2 | async-start | bytes 4194304 | tf_op jit(solution)/shard_map/all_to_all | solution.py:585
  171.2 1.4 copy-start.5
  172.6 1.3 copy-start.6
  173.9 1.3 copy-start.2
  175.2 31.2 %all-to-all-start.3 = ((f32[8,8,64,128]{3,2,1,0:T(8,128)}), f32[8,8,64,128]{3,2,1,0:T(8,128)}, u32[]{:S(2)}, u32[]{:S(2)}) async-start(f32[8,8,64,128]{3,2,1,0:T(8,128)} %copy-done.6), calls=%async_computation.3 | async-start | bytes 4194304 | tf_op jit(solution)/shard_map/all_to_all | solution.py:585
  181.2 0.7 collective-permute-start.3
  206.4 31.0 %all-to-all-start.4 = ((f32[8,8,64,128]{3,2,1,0:T(8,128)}), f32[8,8,64,128]{3,2,1,0:T(8,128)}, u32[]{:S(2)}, u32[]{:S(2)}) async-start(f32[8,8,64,128]{3,2,1,0:T(8,128)} %copy-done.5), calls=%async_computation.4 | async-start | bytes 4194304 | tf_op jit(solution)/shard_map/all_to_all | solution.py:585
  217.9 1.4 copy-start.8
  237.4 96.9 %collective-permute-start.10 = (f32[32,16512]{1,0:T(8,128)}, f32[32,16512]{1,0:T(8,128)}, u32[]{:S(2)}, u32[]{:S(2)}) collective-permute-start(f32[32,16512]{1,0:T(8,128)} %pad_maximum_fusion.1), channel_id=1, source_target_pairs={{0,28},{4,24},{8,20},{12,16},{16,12},{20,8},{24,4},{28,0},{1,29},{... | collective-permute-start | bytes 6340616 | tf_op jit(solution)/shard_map/ppermute | solution.py:557
  242.9 26.1 %collective-permute-start.7 = (f32[8,16384]{1,0:T(8,128)}, f32[8,16384]{1,0:T(8,128)}, u32[]{:S(2)}, u32[]{:S(2)}) collective-permute-start(f32[8,16384]{1,0:T(8,128)} %get-tuple-element.83), channel_id=1, source_target_pairs={{0,1},{1,0},{2,3},{3,2},{4,5},{5,4},{6,7},{7,6},{8,9},{9,8},{10,11... | collective-permute-start | bytes 1572872 | tf_op jit(solution)/shard_map/ppermute | solution.py:498
  243.8 39.1 %collective-permute-start.8 = (f32[8,16384]{1,0:T(8,128)}, f32[8,16384]{1,0:T(8,128)}, u32[]{:S(2)}, u32[]{:S(2)}) collective-permute-start(f32[8,16384]{1,0:T(8,128)} %get-tuple-element.82), channel_id=1, source_target_pairs={{0,2},{1,3},{2,0},{3,1},{4,6},{5,7},{6,4},{7,5},{8,10},{9,11},{10,... | collective-permute-start | bytes 1572872 | tf_op jit(solution)/shard_map/ppermute | solution.py:498
  247.3 41.2 %collective-permute-start.9 = (f32[8,16384]{1,0:T(8,128)S(1)}, f32[8,16384]{1,0:T(8,128)}, u32[]{:S(2)}, u32[]{:S(2)}) collective-permute-start(f32[8,16384]{1,0:T(8,128)S(1)} %get-tuple-element.81), channel_id=1, source_target_pairs={{0,3},{1,2},{2,1},{3,0},{4,7},{5,6},{6,5},{7,4},{8,11},{9,10},{10,... | collective-permute-start | bytes 1572872 | tf_op jit(solution)/shard_map/ppermute | solution.py:498
  247.3 82.3 %all-to-all-start.5 = ((f32[8,8,64,128]{3,2,1,0:T(8,128)}), f32[8,8,64,128]{3,2,1,0:T(8,128)}, u32[]{:S(2)}, u32[]{:S(2)}) async-start(f32[8,8,64,128]{3,2,1,0:T(8,128)} %copy-done.4), calls=%async_computation.5 | async-start | bytes 4194304 | tf_op jit(solution)/shard_map/all_to_all | solution.py:585
  251.8 33.6 %copy-start.3 = (f32[8,8,64,128]{3,2,1,0:T(8,128)S(1)}, f32[8,8,64,128]{3,2,1,0:T(8,128)}, u32[]{:S(2)}) copy-start(f32[8,8,64,128]{3,2,1,0:T(8,128)} %copy-done.2) | copy-start | bytes 6291460
  253.7 38.6 %collective-permute-start.4 = (f32[8,16384]{1,0:T(8,128)S(1)}, f32[8,16384]{1,0:T(8,128)S(1)}, u32[]{:S(2)}, u32[]{:S(2)}) collective-permute-start(f32[8,16384]{1,0:T(8,128)S(1)} %get-tuple-element.79), channel_id=1, source_target_pairs={{0,1},{1,0},{2,3},{3,2},{4,5},{5,4},{6,7},{7,6},{8,9},{9,8},{10,11... | collective-permute-start | bytes 1572872 | tf_op jit(solution)/shard_map/ppermute | solution.py:498
  269.0 58.8 %collective-permute-start.5 = (f32[8,16384]{1,0:T(8,128)S(1)}, f32[8,16384]{1,0:T(8,128)S(1)}, u32[]{:S(2)}, u32[]{:S(2)}) collective-permute-start(f32[8,16384]{1,0:T(8,128)S(1)} %get-tuple-element.78), channel_id=1, source_target_pairs={{0,2},{1,3},{2,0},{3,1},{4,6},{5,7},{6,4},{7,5},{8,10},{9,11},{10,... | collective-permute-start | bytes 1572872 | tf_op jit(solution)/shard_map/ppermute | solution.py:498
  282.9 44.8 %collective-permute-start.6 = (f32[8,16384]{1,0:T(8,128)S(1)}, f32[8,16384]{1,0:T(8,128)S(1)}, u32[]{:S(2)}, u32[]{:S(2)}) collective-permute-start(f32[8,16384]{1,0:T(8,128)S(1)} %get-tuple-element.77), channel_id=1, source_target_pairs={{0,3},{1,2},{2,1},{3,0},{4,7},{5,6},{6,5},{7,4},{8,11},{9,10},{10,... | collective-permute-start | bytes 1572872 | tf_op jit(solution)/shard_map/ppermute | solution.py:498

commit v5 on v4

--- a/solution.py
+++ b/solution.py
@@ -333,16 +333,16 @@
             flat_ref[pl.ds(tile * rows + r, members, stride=tiles * rows), :] = in_ref[:, at : at + LANES]
 
 
-def join_kernel(*refs):
-    in_ref, out_ref, copy_ref = refs[0], refs[-2], refs[-1]
+def join_kernel(extra, in_ref, *refs):
+    out_refs = refs[-2:] if extra else refs[-1:]
     members, tiles, rows, _ = in_ref.shape
     flat_ref = in_ref.reshape(members * tiles * rows, LANES)
     for r in range(rows):
         for tile in range(tiles):
             at = (r * tiles + tile) * LANES
             value = flat_ref[pl.ds(tile * rows + r, members, stride=tiles * rows), :]
-            out_ref[0, :, at : at + LANES] = value
-            copy_ref[0, :, at : at + LANES] = value
+            for out_ref in out_refs:
+                out_ref[0, :, at : at + LANES] = value
 
 
 def mirror_kernel(base_ref, own_ref, far_ref, edge_ref, out_ref):
@@ -397,21 +397,20 @@
         grid=(rows // BLOCK_ROWS,),
         in_specs=[pl.BlockSpec((members, BLOCK_ROWS * INNER), lambda g: (0, g))],
         out_specs=pl.BlockSpec((members, tiles, BLOCK_ROWS, LANES), lambda g: (0, 0, g, 0)),
-        out_shape=jax.ShapeDtypeStruct((members, tiles, rows, LANES), jnp.float32),
+        out_shape=pltpu.HBM((members, tiles, rows, LANES), jnp.float32),
         compiler_params=limits(),
         cost_estimate=pl.CostEstimate(flops=0, bytes_accessed=8 * members * length, transcendentals=0),
     )(phase)
 
 
-def join_call(piece, place, places, groups, so_far):
+def join_call(piece, track, within, length, groups, so_far):
     members, tiles, rows, _ = piece.shape
     stretch = rows * INNER
     steps = rows // BLOCK_ROWS
-    track, within = place // (places // 2), place % (places // 2)
     operands = (piece,) if so_far is None else (piece, so_far)
-    each = steps // groups
+    each = max(steps // max(groups, 1), 1)
     return pl.pallas_call(
-        join_kernel,
+        functools.partial(join_kernel, groups > 0),
         grid=(steps,),
         in_specs=[
             pl.BlockSpec((members, tiles, BLOCK_ROWS, LANES), lambda g: (0, 0, g, 0)),
@@ -420,11 +419,11 @@
         out_specs=[
             pl.BlockSpec((1, members, BLOCK_ROWS * INNER), lambda g: (track, 0, within * steps + g)),
             pl.BlockSpec((1, members, BLOCK_ROWS * INNER), lambda g: (g // each, 0, g % each)),
-        ],
+        ][: 2 if groups else 1],
         out_shape=[
-            jax.ShapeDtypeStruct((2, members, stretch * places // 2), jnp.float32),
-            jax.ShapeDtypeStruct((groups, members, stretch // groups), jnp.float32),
-        ],
+            jax.ShapeDtypeStruct((2, members, length), jnp.float32),
+            jax.ShapeDtypeStruct((max(groups, 1), members, stretch // max(groups, 1)), jnp.float32),
+        ][: 2 if groups else 1],
         input_output_aliases={} if so_far is None else {1: 0},
         compiler_params=limits(),
         cost_estimate=pl.CostEstimate(flops=0, bytes_accessed=12 * members * stretch, transcendentals=0),
@@ -464,7 +463,7 @@
             pl.BlockSpec(matrices.shape, lambda g: (0, 0, 0, 0)),
         ],
         out_specs=[pl.BlockSpec((shards, WIDE // LANES, rows, LANES), lambda g: (0, g, 0, 0))] * parts,
-        out_shape=[jax.ShapeDtypeStruct((shards, tiles, rows, LANES), jnp.float32)] * parts,
+        out_shape=[pltpu.HBM((shards, tiles, rows, LANES), jnp.float32)] * parts,
         scratch_shapes=[pltpu.VMEM((RADIX, WIDE, 2 * QUARTER), jnp.bfloat16)] * 2,
         compiler_params=limits(),
         cost_estimate=pl.CostEstimate(
@@ -513,9 +512,8 @@
     )
 
 
-def own_and_far(phase, params):
+def own_and_far(phase, params, my_group):
     groups = lax.axis_size("mem")
-    my_group = lax.axis_index("mem")
     half = phase.shape[1] // 2
     width = half // groups
     lane = lax.broadcasted_iota(jnp.int32, (phase.shape[0], LANES), 1)
@@ -550,11 +548,15 @@
     return lax.ppermute(own[:, :LANES], "len", [(d, (shards - d) % shards) for d in range(shards)])
 
 
+def across(far):
+    shards = lax.axis_size("len")
+    return lax.ppermute(far, "len", [(d, shards - 1 - d) for d in range(shards)])
+
+
 def lines_gram(own, far, edge):
-    shards, groups = lax.axis_size("len"), lax.axis_size("mem")
+    groups = lax.axis_size("mem")
     my_index, my_group = lax.axis_index("len"), lax.axis_index("mem")
     width = own.shape[1] - LANES
-    far = lax.ppermute(far, "len", [(d, shards - 1 - d) for d in range(shards)])
     base = (my_index * (2 * groups) + my_group) * width
     base = jnp.stack([base, my_group, jnp.full_like(my_group, groups)]).astype(jnp.int32)
     sums = mirror_call(base, own, far, edge)
@@ -589,33 +591,34 @@
     outer_tables = jnp.asarray(outer_matrices())
     inner_tables = jnp.asarray(inner_matrices())
     twists = jnp.asarray(twist_tables())
-    places = 4
-
-    def transform(phases, track):
+    local_len = phase_left.shape[1]
+
+    def transform(phases, track, parts):
         mid = outer_call(params, phases, outer_tables, twists, track)
-        return list(inner_call(mid, inner_tables, shards, 2))
-
-    left = swap(part_call(phase_left))
-    own, far = own_and_far(phase_left, all_params)
+        return list(inner_call(mid, inner_tables, shards, parts))
+
+    left = part_call(phase_left)
+    left, my_group = lax.optimization_barrier((left, lax.axis_index("mem")))
+    left = swap(left)
+    own, far = own_and_far(phase_left, all_params, my_group)
     right = swap(part_call(phase_right))
-    first = transform((left,), 0)
-    left, right, *first = lax.optimization_barrier((left, right, *first))
-    early = swap(first[0])
-    second = transform((left, right), 1)
-    early, second[0] = lax.optimization_barrier((early, second[0]))
+    first = transform((left,), 0, 1)[0]
+    edge = edge_of(own)
+    left, right, first, far, edge = lax.optimization_barrier((left, right, first, far, edge))
+    far = across(far)
+    second = transform((left, right), 1, 2)
     ahead = swap(second[0])
-    edge = edge_of(own)
-    ahead, edge, second[1] = lax.optimization_barrier((ahead, edge, second[1]))
-    profile, ahead = join_call(ahead, 2, places, groups, None)
+    line_gram = lines_gram(own, far, edge)
+    ahead, line_gram, second[1] = lax.optimization_barrier((ahead, line_gram, second[1]))
     behind = swap(second[1])
-    behind, first[1], far = lax.optimization_barrier((behind, first[1], far))
-    line_gram = lines_gram(own, far, edge)
-    profile, behind = join_call(behind, 3, places, groups, profile)
-    late = swap(first[1])
-    point_gram = rows_gram(slot_rows(ahead, groups)) + rows_gram(slot_rows(behind, groups))
-    late, point_gram = lax.optimization_barrier((late, point_gram))
-    profile, _ = join_call(early, 0, places, groups, profile)
-    profile, _ = join_call(late, 1, places, groups, profile)
+    profile, ahead = join_call(ahead, 1, 0, local_len, groups, None)
+    point_gram = rows_gram(slot_rows(ahead, groups))
+    behind, point_gram, first = lax.optimization_barrier((behind, point_gram, first))
+    first = swap(first)
+    profile, behind = join_call(behind, 1, 1, local_len, groups, profile)
+    point_gram = point_gram + rows_gram(slot_rows(behind, groups))
+    first, point_gram = lax.optimization_barrier((first, point_gram))
+    (profile,) = join_call(first, 0, 0, local_len, 0, profile)
     gram_matrix = 0.25 * line_gram + (0.5 / (OUTER * INNER)) * point_gram
     return (profile, upper_of(summed(in_order(gram_matrix, members))))
 

time: 397 us -> 391 us (0.985)
  starting transfers between devices: 39.9 us -> 63.1 us
  waiting for transfers between devices: 161 us -> 153 us
  local copies, waits for them, and re-layouts: 24.5 us -> 17.1 us
  blocking collectives: 32.3 us -> 25.6 us
    all_to_all x6 -> x5, waiting for transfers between devices: 76.9 us -> 15.2 us  [swap(): return lax.all_to_all(piece, 'len', split_axis=0, concat_axis=0, tiled=True)]
    ppermute x9, waiting for transfers between devices: 84.5 us -> 129 us  [to_group(): lax.ppermute(piece, 'mem', [(z, z ^ slot) for z in range(groups)])]
    ppermute x9, starting transfers between devices: 13.2 us -> 40.6 us  [to_group(): lax.ppermute(piece, 'mem', [(z, z ^ slot) for z in range(groups)])]
    ppermute x1, waiting for transfers between devices: 0.01 us -> 8.71 us  [across(): lax.ppermute(far, 'len', [(d, shards - 1 - d) for d in range(shards)])]
    all_gather x2, blocking collectives: 32.3 us -> 25.6 us  [summed(): value = jnp.sum(lax.all_gather(value, axis), axis=0)]
    unnamed x21, local copies, waits for them, and re-layouts: 12.7 us -> 6.39 us
    all_to_all x6 -> x5, starting transfers between devices: 26 us -> 21.8 us  [swap(): return lax.all_to_all(piece, 'len', split_axis=0, concat_axis=0, tiled=True)]
    pallas_call x4 -> x3, Pallas kernels: 16.6 us -> 14.7 us  [join_call(): pl.pallas_call(functools.partial(join_kernel, groups > 0), grid=(steps,),...]
  transfers between devices with their start and end apart: 17 -> 16, of which waited for: 9 -> 9; matrix products, arithmetic and copies ran while one was open for 5% -> 6% of each run, Pallas kernels for 24% -> 23%
where the time goes in v5:
time: 391 us; the launch traced here: 390 us
  waiting for transfers between devices  153 us (39%)
  Pallas kernels  107 us (27%)
  starting transfers between devices  63.1 us (16%)
  blocking collectives  25.6 us (7%)
  local copies, waits for them, and re-layouts  17.1 us (4%)
  matrix products  12.4 us (3%)
  other arithmetic  11.2 us (3%)
    ppermute x9, waiting for transfers between devices, to_group(): lax.ppermute(piece, 'mem', [(z, z ^ slot) for z in range(groups)])  129 us
    pallas_call x2, Pallas kernels, outer_call(): pl.pallas_call(functools.partial(outer_kernel, track), grid=(tiles // som...  47.5 us
    ppermute x9, starting transfers between devices, to_group(): lax.ppermute(piece, 'mem', [(z, z ^ slot) for z in range(groups)])  40.6 us
    all_gather x2, blocking collectives, summed(): value = jnp.sum(lax.all_gather(value, axis), axis=0)  25.6 us
    all_to_all x5, starting transfers between devices, swap(): return lax.all_to_all(piece, 'len', split_axis=0, concat_axis=0, tiled=True)  21.8 us
    pallas_call x2, Pallas kernels, inner_call(): pl.pallas_call(inner_kernel, grid=(OUTER // WIDE,), in_specs=[pl.BlockSpe...  18.8 us
    pallas_call x1, Pallas kernels, mirror_call(): pl.pallas_call(mirror_kernel, in_specs=[pl.BlockSpec(memory_space=pltpu.S...  15.4 us
    all_to_all x5, waiting for transfers between devices, swap(): return lax.all_to_all(piece, 'len', split_axis=0, concat_axis=0, tiled=True)  15.2 us
  transfers between devices with their start and end apart: 16, of which 9 were waited for; matrix products, arithmetic and copies ran while one was open for 6% of the time, Pallas kernels for 23%

profile of v5, /device:TPU:0, one launch (start us, length us, event | category | flops | bytes accessed | tf_op | source)
XLA Modules:
  0.0 389.8 jit_solution(16356756502019199298)
XLA Ops:
  0.6 2.2 copy-done
  2.8 5.0 %shard_map.95 = f32[8,8,128,128]{3,2,1,0:T(8,128)} custom-call(f32[8,131072]{1,0:T(8,128)S(1)} %copy-done), custom_call_target="tpu_custom_call" | custom-call | bytes 8388608 | tf_op jit(solution)/shard_map/pallas_call | solution.py:395
  7.9 3.5 constant_dynamic-slice_fusion.1
  11.4 0.9 fusion.34
  12.3 0.1 maximum_bitcast_fusion
  12.4 0.1 pad_maximum_fusion.2
  12.5 3.1 collective-permute-start
  15.6 1.2 pad_maximum_fusion.3
  16.8 2.6 collective-permute-start.1
  19.4 0.1 maximum_bitcast_fusion.4
  19.5 1.1 pad_maximum_fusion.4
  20.6 4.5 %all-to-all-start = ((f32[8,8,128,128]{3,2,1,0:T(8,128)}), f32[8,8,128,128]{3,2,1,0:T(8,128)}, u32[]{:S(2)}, u32[]{:S(2)}) async-start(f32[8,8,128,128]{3,2,1,0:T(8,128)} %shard_map.95), calls=%async_computation | async-start | bytes 8388608 | tf_op jit(solution)/shard_map/all_to_all | solution.py:587
  25.2 2.2 copy-done.1
  27.4 5.3 %shard_map.96 = f32[8,8,128,128]{3,2,1,0:T(8,128)} custom-call(f32[8,131072]{1,0:T(8,128)S(1)} %copy-done.1), custom_call_target="tpu_custom_call" | custom-call | bytes 8388608 | tf_op jit(solution)/shard_map/pallas_call | solution.py:395
  32.6 0.2 fusion.35.params_ref
  32.8 27.2 %collective-permute-done = f32[2,8,16512]{2,1,0:T(8,128)S(1)} collective-permute-done((f32[2,8,16512]{2,1,0:T(8,128)S(1)}, f32[2,8,16512]{2,1,0:T(8,128)S(1)}, u32[]{:S(2)}, u32[]{:S(2)}) %collective-permute-start) | collective-permute-done | bytes 1056800 | tf_op jit(solution)/shard_map/ppermute | solution.py:497
  60.0 0.9 slice_bitcast_fusion.8
  60.9 28.7 %collective-permute-done.1 = f32[2,8,16512]{2,1,0:T(8,128)} collective-permute-done((f32[2,8,16512]{2,1,0:T(8,128)}, f32[2,8,16512]{2,1,0:T(8,128)}, u32[]{:S(2)}, u32[]{:S(2)}) %collective-permute-start.1) | collective-permute-done | bytes 1056800 | tf_op jit(solution)/shard_map/ppermute | solution.py:497
  89.6 2.1 slice_bitcast_fusion.7
  91.6 2.3 slice_bitcast_fusion.6
  93.9 4.6 %all-to-all-start.1 = ((f32[8,8,128,128]{3,2,1,0:T(8,128)}), f32[8,8,128,128]{3,2,1,0:T(8,128)}, u32[]{:S(2)}, u32[]{:S(2)}) async-start(f32[8,8,128,128]{3,2,1,0:T(8,128)} %shard_map.96), calls=%async_computation.1 | async-start | bytes 8388608 | tf_op jit(solution)/shard_map/all_to_all | solution.py:587
  98.5 1.7 pad_maximum_fusion.1.own_ref
  100.3 0.7 collective-permute-start.3
  101.0 1.5 pad_maximum_fusion
  102.5 20.7 %shard_map.97.mid_ref = f32[8,2,1024,128]{3,2,1,0:T(8,128)} custom-call(f32[3]{0:T(128)S(1)} %fusion.35.params_ref, f32[8,8,128,128]{3,2,1,0:T(8,128)} %all-to-all-done.refs_0_, bf16[2,4,512,512]{3,2,1,0:T(8,128)(2,1)} %constant.169.clone.refs_1_.refs_2_, f32[2,4,256,1024]{3,2,1,0:T(8,128)} %constant.171.clone.refs_2_.refs_3_), custom_call_target="tpu_custom_call" | custom-call | flops 6442450944 | bytes 20971520 | tf_op jit(solution)/shard_map/pallas_call | solution.py:436
  123.1 9.4 %shard_map.98 = f32[8,8,128,128]{3,2,1,0:T(8,128)} custom-call(f32[8,2,1024,128]{3,2,1,0:T(8,128)} %shard_map.97.mid_ref, bf16[2,4,256,512]{3,2,1,0:T(8,128)(2,1)S(1)} %copy-done.2), custom_call_target="tpu_custom_call" | custom-call | flops 3221225472 | bytes 12582912 | tf_op jit(solution)/shard_map/pallas_call | solution.py:458
  132.6 15.2 %all-to-all-done.1.refs_1_ = f32[8,8,128,128]{3,2,1,0:T(8,128)} async-done(((f32[8,8,128,128]{3,2,1,0:T(8,128)}), f32[8,8,128,128]{3,2,1,0:T(8,128)}, u32[]{:S(2)}, u32[]{:S(2)}) %all-to-all-start.1) | async-done | bytes 4194336 | tf_op jit(solution)/shard_map/all_to_all | solution.py:587
  147.8 26.8 %shard_map.99.mid_ref = f32[8,2,1024,128]{3,2,1,0:T(8,128)} custom-call(f32[3]{0:T(128)S(1)} %fusion.35.params_ref, f32[8,8,128,128]{3,2,1,0:T(8,128)} %all-to-all-done.refs_0_, f32[8,8,128,128]{3,2,1,0:T(8,128)} %all-to-all-done.1.refs_1_, bf16[2,4,512,512]{3,2,1,0:T(8,128)(2,1)} %constant.169.clone.refs_1_.refs_2_, ...), custom_call_target="tpu_custom_call" | custom-call | flops 6442450944 | bytes 20971520 | tf_op jit(solution)/shard_map/pallas_call | solution.py:436
  174.6 9.4 %shard_map.100 = (f32[8,8,64,128]{3,2,1,0:T(8,128)}, f32[8,8,64,128]{3,2,1,0:T(8,128)}) custom-call(f32[8,2,1024,128]{3,2,1,0:T(8,128)} %shard_map.99.mid_ref, bf16[2,4,256,512]{3,2,1,0:T(8,128)(2,1)S(1)} %copy-done.3), custom_call_target="tpu_custom_call" | custom-call | flops 3221225472 | bytes 12582912 | tf_op jit(solution)/shard_map/pallas_call | solution.py:458
  184.0 4.5 %all-to-all-start.2 = ((f32[8,8,64,128]{3,2,1,0:T(8,128)}), f32[8,8,64,128]{3,2,1,0:T(8,128)}, u32[]{:S(2)}, u32[]{:S(2)}) async-start(f32[8,8,64,128]{3,2,1,0:T(8,128)} %get-tuple-element.27), calls=%async_computation.2 | async-start | bytes 4194304 | tf_op jit(solution)/shard_map/all_to_all | solution.py:587
  188.6 0.1 pad_add_fusion.base_ref
  188.7 8.7 %collective-permute-done.4.far_ref = f32[32,16512]{1,0:T(8,128)} collective-permute-done((f32[32,16512]{1,0:T(8,128)}, f32[32,16512]{1,0:T(8,128)}, u32[]{:S(2)}, u32[]{:S(2)}) %collective-permute-start.4) | collective-permute-done | bytes 2113568 | tf_op jit(solution)/shard_map/ppermute | solution.py:553
  197.4 15.4 %shard_map.101 = f32[2,32,16512]{2,1,0:T(8,128)} custom-call(s32[3]{0:T(128)S(1)} %pad_add_fusion.base_ref, f32[32,16512]{1,0:T(8,128)S(1)} %pad_maximum_fusion.1.own_ref, f32[32,16512]{1,0:T(8,128)} %collective-permute-done.4.far_ref, f32[32,128]{1,0:T(8,128)S(1)} %collective-permute-done.3.edge_ref), custom_call_target="tpu_custom_call" | custom-call | flops 105676800 | bytes 8454144 | tf_op jit(solution)/shard_map/pallas_call | solution.py:477
  212.8 4.3 %fusion = f32[32,32]{1,0:T(8,128)S(1)} fusion(f32[2,32,16512]{2,1,0:T(8,128)} %shard_map.101), kind=kOutput, calls=%fused_computation.1 | convolution fusion | flops 202899456 | bytes 2117632 | tf_op jit(solution)/shard_map/dot_general | solution.py:501
  217.1 4.2 %fusion.18 = f32[32,32]{1,0:T(8,128)S(1)} fusion(f32[32,32]{1,0:T(8,128)S(1)} %fusion, f32[2,32,16512]{2,1,0:T(8,128)} %shard_map.101), kind=kOutput, calls=%fused_computation.22 | convolution fusion | flops 202900480 | bytes 2121728 | tf_op jit(solution)/shard_map/dot_general | solution.py:501
  221.3 4.4 %shard_map.102 = (f32[2,8,131072]{2,1,0:T(8,128)}, f32[4,8,16384]{2,1,0:T(8,128)S(1)}) custom-call(f32[8,8,64,128]{3,2,1,0:T(8,128)} %all-to-all-done.2.in_ref), custom_call_target="tpu_custom_call" | custom-call | bytes 6291456 | tf_op jit(solution)/shard_map/pallas_call | solution.py:412
  225.7 1.3 copy-done.4
  227.1 3.6 all-to-all-start.3
  230.7 1.7 dynamic-slice_bitcast_fusion.7
  232.3 19.8 %collective-permute-start.5 = (f32[8,16384]{1,0:T(8,128)S(1)}, f32[8,16384]{1,0:T(8,128)S(1)}, u32[]{:S(2)}, u32[]{:S(2)}) collective-permute-start(f32[8,16384]{1,0:T(8,128)S(1)} %get-tuple-element.73), channel_id=1, source_target_pairs={{0,1},{1,0},{2,3},{3,2},{4,5},{5,4},{6,7},{7,6},{8,9},{9,8},{10,11... | collective-permute-start | bytes 1572872 | tf_op jit(solution)/shard_map/ppermute | solution.py:497
  252.1 1.1 collective-permute-start.6
  253.2 1.4 collective-permute-start.7
  254.6 20.7 %collective-permute-done.5 = f32[8,16384]{1,0:T(8,128)S(1)} collective-permute-done((f32[8,16384]{1,0:T(8,128)S(1)}, f32[8,16384]{1,0:T(8,128)S(1)}, u32[]{:S(2)}, u32[]{:S(2)}) %collective-permute-start.5) | collective-permute-done | bytes 524320 | tf_op jit(solution)/shard_map/ppermute | solution.py:497
  275.3 15.0 %collective-permute-done.6 = f32[8,16384]{1,0:T(8,128)S(1)} collective-permute-done((f32[8,16384]{1,0:T(8,128)S(1)}, f32[8,16384]{1,0:T(8,128)S(1)}, u32[]{:S(2)}, u32[]{:S(2)}) %collective-permute-start.6) | collective-permute-done | bytes 524320 | tf_op jit(solution)/shard_map/ppermute | solution.py:497
  290.3 1.8 fusion.2
  292.1 4.6 %all-to-all-start.4 = ((f32[8,8,128,128]{3,2,1,0:T(8,128)}), f32[8,8,128,128]{3,2,1,0:T(8,128)}, u32[]{:S(2)}, u32[]{:S(2)}) async-start(f32[8,8,128,128]{3,2,1,0:T(8,128)} %shard_map.98), calls=%async_computation.4 | async-start | bytes 8388608 | tf_op jit(solution)/shard_map/all_to_all | solution.py:587
  296.7 2.7 shard_map.103
  299.4 0.1 dynamic-slice_bitcast_fusion.3
  299.6 2.6 collective-permute-start.10
  302.1 10.0 %collective-permute-start.8 = (f32[8,16384]{1,0:T(8,128)S(1)}, f32[8,16384]{1,0:T(8,128)S(1)}, u32[]{:S(2)}, u32[]{:S(2)}) collective-permute-start(f32[8,16384]{1,0:T(8,128)S(1)} %get-tuple-element.69), channel_id=1, source_target_pairs={{0,1},{1,0},{2,3},{3,2},{4,5},{5,4},{6,7},{7,6},{8,9},{9,8},{10,11... | collective-permute-start | bytes 1572872 | tf_op jit(solution)/shard_map/ppermute | solution.py:497
  312.2 4.0 %collective-permute-done.10 = f32[8,16384]{1,0:T(8,128)S(1)} collective-permute-done((f32[8,16384]{1,0:T(8,128)S(1)}, f32[8,16384]{1,0:T(8,128)S(1)}, u32[]{:S(2)}, u32[]{:S(2)}) %collective-permute-start.10) | collective-permute-done | bytes 524320 | tf_op jit(solution)/shard_map/ppermute | solution.py:497
  316.2 10.6 %collective-permute-done.8 = f32[8,16384]{1,0:T(8,128)S(1)} collective-permute-done((f32[8,16384]{1,0:T(8,128)S(1)}, f32[8,16384]{1,0:T(8,128)S(1)}, u32[]{:S(2)}, u32[]{:S(2)}) %collective-permute-start.8) | collective-permute-done | bytes 524320 | tf_op jit(solution)/shard_map/ppermute | solution.py:497
  326.9 22.5 %collective-permute-done.9 = f32[8,16384]{1,0:T(8,128)S(1)} collective-permute-done((f32[8,16384]{1,0:T(8,128)S(1)}, f32[8,16384]{1,0:T(8,128)S(1)}, u32[]{:S(2)}, u32[]{:S(2)}) %collective-permute-start.9) | collective-permute-done | bytes 524320 | tf_op jit(solution)/shard_map/ppermute | solution.py:497
  349.3 1.8 fusion.10
  351.1 0.2 fusion.20
  351.3 0.2 fusion.41
  351.6 9.4 %all-gather = f32[256,32]{1,0:T(8,128)S(1)} all-gather(f32[32,32]{1,0:T(8,128)S(1)} %fusion.41), channel_id=2, replica_groups=mesh['len'=8,'mem'=4] {'len'}, dimensions={0}, use_global_device_ids=true | all-gather | bytes 36864 | tf_op jit(solution)/shard_map/all_gather | solution.py:577
  361.0 16.2 %all-gather.1 = f32[128,32]{1,0:T(8,128)S(1)} all-gather(f32[32,32]{1,0:T(8,128)S(1)} %reduce_sum.18), channel_id=3, replica_groups=mesh['len'=8,'mem'=4] {'mem'}, dimensions={0}, use_global_device_ids=true | all-gather | bytes 20480 | tf_op jit(solution)/shard_map/all_gather | solution.py:577
  377.2 0.1 copy.16
  377.3 2.9 cholesky.18
  380.3 0.6 compare_reduce_fusion
  380.9 0.6 select_bitcast_fusion
  381.6 0.7 copy.17
  382.3 7.5 %shard_map.104 = f32[2,8,131072]{2,1,0:T(8,128)} custom-call(f32[8,8,128,128]{3,2,1,0:T(8,128)} %all-to-all-done.4.in_ref, f32[2,8,131072]{2,1,0:T(8,128)} %get-tuple-element.41.refs_0_), custom_call_target="tpu_custom_call", output_to_operand_aliasing={{}: (1, {})} | custom-call | bytes 12582912 | tf_op jit(solution)/shard_map/pallas_call | solution.py:412
  (42 shorter events, 0.3 us)
Async XLA Ops:
  0.6 2.2 copy-start
  2.8 5.1 %copy-start.7 = (f32[8]{0:T(128)S(1)}, f32[8]{0:T(128)}, u32[]{:S(2)}) copy-start(f32[8]{0:T(128)} %param.11) | copy-start | bytes 100
  2.8 5.1 %copy-start.8 = (f32[8]{0:T(128)S(1)}, f32[8]{0:T(128)}, u32[]{:S(2)}) copy-start(f32[8]{0:T(128)} %param.10) | copy-start | bytes 100
  12.5 47.5 %collective-permute-start = (f32[2,8,16512]{2,1,0:T(8,128)S(1)}, f32[2,8,16512]{2,1,0:T(8,128)S(1)}, u32[]{:S(2)}, u32[]{:S(2)}) collective-permute-start(f32[2,8,16512]{2,1,0:T(8,128)S(1)} %pad_maximum_fusion.2), channel_id=1, source_target_pairs={{0,1},{1,0},{2,3},{3,2},{4,5},{5,4},{6,7},{7,6},{8,9},{9,8},{10,11... | collective-permute-start | bytes 3170312 | tf_op jit(solution)/shard_map/ppermute | solution.py:497
  16.8 72.8 %collective-permute-start.1 = (f32[2,8,16512]{2,1,0:T(8,128)}, f32[2,8,16512]{2,1,0:T(8,128)}, u32[]{:S(2)}, u32[]{:S(2)}) collective-permute-start(f32[2,8,16512]{2,1,0:T(8,128)} %pad_maximum_fusion.3), channel_id=1, source_target_pairs={{0,2},{1,3},{2,0},{3,1},{4,6},{5,7},{6,4},{7,5},{8,10},{9,11},{10,... | collective-permute-start | bytes 3170312 | tf_op jit(solution)/shard_map/ppermute | solution.py:497
  20.6 71.0 %collective-permute-start.2 = (f32[2,8,16512]{2,1,0:T(8,128)}, f32[2,8,16512]{2,1,0:T(8,128)}, u32[]{:S(2)}, u32[]{:S(2)}) collective-permute-start(f32[2,8,16512]{2,1,0:T(8,128)} %pad_maximum_fusion.4), channel_id=1, source_target_pairs={{0,3},{1,2},{2,1},{3,0},{4,7},{5,6},{6,5},{7,4},{8,11},{9,10},{10,... | collective-permute-start | bytes 3170312 | tf_op jit(solution)/shard_map/ppermute | solution.py:497
  20.6 73.3 %all-to-all-start = ((f32[8,8,128,128]{3,2,1,0:T(8,128)}), f32[8,8,128,128]{3,2,1,0:T(8,128)}, u32[]{:S(2)}, u32[]{:S(2)}) async-start(f32[8,8,128,128]{3,2,1,0:T(8,128)} %shard_map.95), calls=%async_computation | async-start | bytes 8388608 | tf_op jit(solution)/shard_map/all_to_all | solution.py:587
  25.2 2.2 copy-start.1
  27.4 5.3 %copy-start.9 = (f32[8]{0:T(128)S(1)}, f32[8]{0:T(128)}, u32[]{:S(2)}) copy-start(f32[8]{0:T(128)} %param.12) | copy-start | bytes 100
  93.9 53.9 %all-to-all-start.1 = ((f32[8,8,128,128]{3,2,1,0:T(8,128)}), f32[8,8,128,128]{3,2,1,0:T(8,128)}, u32[]{:S(2)}, u32[]{:S(2)}) async-start(f32[8,8,128,128]{3,2,1,0:T(8,128)} %shard_map.96), calls=%async_computation.1 | async-start | bytes 8388608 | tf_op jit(solution)/shard_map/all_to_all | solution.py:587
  98.5 2.4 copy-start.5
  98.5 2.4 copy-start.6
  100.3 32.3 %collective-permute-start.3 = (f32[32,128]{1,0:T(8,128)S(1)}, f32[32,128]{1,0:T(8,128)S(1)}, u32[]{:S(2)}, u32[]{:S(2)}) collective-permute-start(f32[32,128]{1,0:T(8,128)S(1)} %slice.48), channel_id=1, source_target_pairs={{0,0},{4,28},{8,24},{12,20},{16,16},{20,12},{24,8},{28,4},{1,1},{5... | collective-permute-start | bytes 49160 | tf_op jit(solution)/shard_map/ppermute | solution.py:548
  102.5 20.7 %copy-start.2 = (bf16[2,4,256,512]{3,2,1,0:T(8,128)(2,1)S(1)}, bf16[2,4,256,512]{3,2,1,0:T(8,128)(2,1)}, u32[]{:S(2)}) copy-start(bf16[2,4,256,512]{3,2,1,0:T(8,128)(2,1)} %constant.170.clone.matrix_ref) | copy-start | bytes 6291460
  147.8 26.8 %copy-start.3 = (bf16[2,4,256,512]{3,2,1,0:T(8,128)(2,1)S(1)}, bf16[2,4,256,512]{3,2,1,0:T(8,128)(2,1)}, u32[]{:S(2)}) copy-start(bf16[2,4,256,512]{3,2,1,0:T(8,128)(2,1)} %constant.170.clone.matrix_ref) | copy-start | bytes 6291460
  147.8 49.6 %collective-permute-start.4 = (f32[32,16512]{1,0:T(8,128)}, f32[32,16512]{1,0:T(8,128)}, u32[]{:S(2)}, u32[]{:S(2)}) collective-permute-start(f32[32,16512]{1,0:T(8,128)} %pad_maximum_fusion), channel_id=1, source_target_pairs={{0,28},{4,24},{8,20},{12,16},{16,12},{20,8},{24,4},{28,0},{1,29},{... | collective-permute-start | bytes 6340616 | tf_op jit(solution)/shard_map/ppermute | solution.py:553
  184.0 37.3 %all-to-all-start.2 = ((f32[8,8,64,128]{3,2,1,0:T(8,128)}), f32[8,8,64,128]{3,2,1,0:T(8,128)}, u32[]{:S(2)}, u32[]{:S(2)}) async-start(f32[8,8,64,128]{3,2,1,0:T(8,128)} %get-tuple-element.27), calls=%async_computation.2 | async-start | bytes 4194304 | tf_op jit(solution)/shard_map/all_to_all | solution.py:587
  225.7 1.3 copy-start.4
  227.1 65.1 %all-to-all-start.3 = ((f32[8,8,64,128]{3,2,1,0:T(8,128)}), f32[8,8,64,128]{3,2,1,0:T(8,128)S(1)}, u32[]{:S(2)}, u32[]{:S(2)}) async-start(f32[8,8,64,128]{3,2,1,0:T(8,128)} %get-tuple-element.31), calls=%async_computation.3 | async-start | bytes 4194304 | tf_op jit(solution)/shard_map/all_to_all | solution.py:587
  232.3 43.0 %collective-permute-start.5 = (f32[8,16384]{1,0:T(8,128)S(1)}, f32[8,16384]{1,0:T(8,128)S(1)}, u32[]{:S(2)}, u32[]{:S(2)}) collective-permute-start(f32[8,16384]{1,0:T(8,128)S(1)} %get-tuple-element.73), channel_id=1, source_target_pairs={{0,1},{1,0},{2,3},{3,2},{4,5},{5,4},{6,7},{7,6},{8,9},{9,8},{10,11... | collective-permute-start | bytes 1572872 | tf_op jit(solution)/shard_map/ppermute | solution.py:497
  252.1 38.2 %collective-permute-start.6 = (f32[8,16384]{1,0:T(8,128)S(1)}, f32[8,16384]{1,0:T(8,128)S(1)}, u32[]{:S(2)}, u32[]{:S(2)}) collective-permute-start(f32[8,16384]{1,0:T(8,128)S(1)} %get-tuple-element.72), channel_id=1, source_target_pairs={{0,2},{1,3},{2,0},{3,1},{4,6},{5,7},{6,4},{7,5},{8,10},{9,11},{10,... | collective-permute-start | bytes 1572872 | tf_op jit(solution)/shard_map/ppermute | solution.py:497
  253.2 37.1 %collective-permute-start.7 = (f32[8,16384]{1,0:T(8,128)S(1)}, f32[8,16384]{1,0:T(8,128)S(1)}, u32[]{:S(2)}, u32[]{:S(2)}) collective-permute-start(f32[8,16384]{1,0:T(8,128)S(1)} %get-tuple-element.71), channel_id=1, source_target_pairs={{0,3},{1,2},{2,1},{3,0},{4,7},{5,6},{6,5},{7,4},{8,11},{9,10},{10,... | collective-permute-start | bytes 1572872 | tf_op jit(solution)/shard_map/ppermute | solution.py:497
  292.1 59.0 %all-to-all-start.4 = ((f32[8,8,128,128]{3,2,1,0:T(8,128)}), f32[8,8,128,128]{3,2,1,0:T(8,128)}, u32[]{:S(2)}, u32[]{:S(2)}) async-start(f32[8,8,128,128]{3,2,1,0:T(8,128)} %shard_map.98), calls=%async_computation.4 | async-start | bytes 8388608 | tf_op jit(solution)/shard_map/all_to_all | solution.py:587
  299.6 16.7 %collective-permute-start.10 = (f32[8,16384]{1,0:T(8,128)S(1)}, f32[8,16384]{1,0:T(8,128)S(1)}, u32[]{:S(2)}, u32[]{:S(2)}) collective-permute-start(f32[8,16384]{1,0:T(8,128)S(1)} %get-tuple-element.67), channel_id=1, source_target_pairs={{0,3},{1,2},{2,1},{3,0},{4,7},{5,6},{6,5},{7,4},{8,11},{9,10},{10,... | collective-permute-start | bytes 1572872 | tf_op jit(solution)/shard_map/ppermute | solution.py:497
  302.1 24.7 %collective-permute-start.8 = (f32[8,16384]{1,0:T(8,128)S(1)}, f32[8,16384]{1,0:T(8,128)S(1)}, u32[]{:S(2)}, u32[]{:S(2)}) collective-permute-start(f32[8,16384]{1,0:T(8,128)S(1)} %get-tuple-element.69), channel_id=1, source_target_pairs={{0,1},{1,0},{2,3},{3,2},{4,5},{5,4},{6,7},{7,6},{8,9},{9,8},{10,11... | collective-permute-start | bytes 1572872 | tf_op jit(solution)/shard_map/ppermute | solution.py:497
  312.2 37.2 %collective-permute-start.9 = (f32[8,16384]{1,0:T(8,128)S(1)}, f32[8,16384]{1,0:T(8,128)S(1)}, u32[]{:S(2)}, u32[]{:S(2)}) collective-permute-start(f32[8,16384]{1,0:T(8,128)S(1)} %get-tuple-element.68), channel_id=1, source_target_pairs={{0,2},{1,3},{2,0},{3,1},{4,6},{5,7},{6,4},{7,5},{8,10},{9,11},{10,... | collective-permute-start | bytes 1572872 | tf_op jit(solution)/shard_map/ppermute | solution.py:497

commit v6 on v5

--- a/solution.py
+++ b/solution.py
@@ -202,27 +202,14 @@
     return twice * half_cos, 1.0 - twice * half_sin
 
 
+def amplitude_of(freq, scale, exponent):
+    return scale * jnp.exp2(exponent * jnp.log2((freq + ANCHOR) * (1.0 / ANCHOR)))
+
+
 def left_lines(left, freq, scale, exponent):
-    amplitude = scale * jnp.exp2(exponent * jnp.log2((freq + ANCHOR) * (1.0 / ANCHOR)))
+    amplitude = amplitude_of(freq, scale, exponent)
     sin_left, cos_left = sin_cos(left)
     return amplitude * cos_left, amplitude * sin_left
-
-
-def line_spectra(left, right, freq, scale, exponent, inverse_coherence):
-    amplitude = scale * jnp.exp2(exponent * jnp.log2((freq + ANCHOR) * (1.0 / ANCHOR)))
-    freq_ratio = freq * inverse_coherence
-    ratio_square = freq_ratio * freq_ratio
-    coherent = 1.0 / (1.0 + ratio_square)
-    incoherent = freq_ratio * jnp.sqrt(2.0 + ratio_square) * coherent
-    sin_left, cos_left = sin_cos(left)
-    sin_right, cos_right = sin_cos(right)
-    independent = amplitude * incoherent
-    first = (amplitude * cos_left, amplitude * sin_left)
-    second = (
-        coherent * first[0] + independent * cos_right,
-        coherent * first[1] + independent * sin_right,
-    )
-    return first, second
 
 
 def radix_four(parts):
@@ -252,10 +239,36 @@
     )
 
 
-def outer_kernel(track, params_ref, *refs):
-    phase_refs, (matrix_ref, twist_ref, out_ref, coarse_ref, fine_ref) = refs[:-5], refs[-5:]
+def first_lines(params_ref, left_ref, kept_refs, where, freq):
     scale, exponent, inverse_coherence = params_ref[0], params_ref[1], params_ref[2]
-    _, tiles, rows, _ = phase_refs[0].shape
+    amplitude = amplitude_of(freq, scale, exponent)
+    freq_ratio = freq * inverse_coherence
+    ratio_square = freq_ratio * freq_ratio
+    coherent = 1.0 / (1.0 + ratio_square)
+    incoherent = freq_ratio * jnp.sqrt(2.0 + ratio_square) * coherent
+    sin_left, cos_left = sin_cos(left_ref[where])
+    real, imag = amplitude * cos_left, amplitude * sin_left
+    kept_refs[0][where] = coherent * real
+    kept_refs[1][where] = coherent * imag
+    kept_refs[2][where] = amplitude * incoherent
+    return real, imag
+
+
+def second_lines(right_ref, kept_refs, where):
+    sin_right, cos_right = sin_cos(right_ref[where])
+    independent = kept_refs[2][where]
+    return (
+        kept_refs[0][where] + independent * cos_right,
+        kept_refs[1][where] + independent * sin_right,
+    )
+
+
+def outer_kernel(track, params_ref, phase_ref, *refs):
+    if track == 0:
+        matrix_ref, twist_ref, out_ref, *kept_refs, coarse_ref, fine_ref = refs
+    else:
+        *kept_refs, matrix_ref, twist_ref, out_ref, coarse_ref, fine_ref = refs
+    _, tiles, rows, _ = phase_ref.shape
     lane = lax.broadcasted_iota(jnp.int32, (STEP, LANES), 1) + pl.program_id(0) * tiles * LANES
     row = lax.broadcasted_iota(jnp.int32, (STEP, LANES), 0)
     place = row * INNER + lane
@@ -266,13 +279,12 @@
             lines = []
             for a in range(RADIX):
                 k1 = a * QUARTER + b
-                source, inside = k1 // rows, pl.multiple_of(k1 % rows, STEP)
-                freq = (place + (k1 * INNER + tile * LANES)).astype(jnp.float32)
-                phases = [ref[source, tile, pl.ds(inside, STEP), :] for ref in phase_refs]
+                where = (k1 // rows, tile, pl.ds(pl.multiple_of(k1 % rows, STEP), STEP))
                 if track == 0:
-                    lines.append(left_lines(*phases, freq, scale, exponent))
+                    freq = (place + (k1 * INNER + tile * LANES)).astype(jnp.float32)
+                    lines.append(first_lines(params_ref, phase_ref, kept_refs, where, freq))
                 else:
-                    lines.append(line_spectra(*phases, freq, scale, exponent, inverse_coherence)[1])
+                    lines.append(second_lines(phase_ref, kept_refs, where))
             mixed = radix_four(lines)
             for e in range(RADIX):
                 for ri in range(2):
@@ -400,7 +412,7 @@
         out_shape=pltpu.HBM((members, tiles, rows, LANES), jnp.float32),
         compiler_params=limits(),
         cost_estimate=pl.CostEstimate(flops=0, bytes_accessed=8 * members * length, transcendentals=0),
-    )(phase)
+    )(pltpu.with_memory_space_constraint(phase, pltpu.HBM))
 
 
 def join_call(piece, track, within, length, groups, so_far):
@@ -430,26 +442,30 @@
     )(*operands)
 
 
-def outer_call(params, phases, matrices, twists, track):
-    sources, tiles, rows, _ = phases[0].shape
+def outer_call(params, phase, kept, matrices, twists):
+    track = 1 if kept else 0
+    sources, tiles, rows, _ = phase.shape
     some = OUTER_TILES
+    lines = pl.BlockSpec((sources, some, rows, LANES), lambda g: (0, g, 0, 0))
+    more = 0 if kept else 3
     return pl.pallas_call(
         functools.partial(outer_kernel, track),
         grid=(tiles // some,),
         in_specs=[pl.BlockSpec(memory_space=pltpu.SMEM)]
-        + [pl.BlockSpec((sources, some, rows, LANES), lambda g: (0, g, 0, 0))] * len(phases)
+        + [lines] * (1 + len(kept))
         + [
             pl.BlockSpec(matrices.shape, lambda g: (0, 0, 0, 0)),
             pl.BlockSpec((2, RADIX, QUARTER, some * LANES), lambda g: (0, 0, 0, g)),
         ],
-        out_specs=pl.BlockSpec((some, 2, OUTER, LANES), lambda g: (g, 0, 0, 0)),
-        out_shape=jax.ShapeDtypeStruct((tiles, 2, OUTER, LANES), jnp.float32),
+        out_specs=[pl.BlockSpec((some, 2, OUTER, LANES), lambda g: (g, 0, 0, 0))] + [lines] * more,
+        out_shape=[jax.ShapeDtypeStruct((tiles, 2, OUTER, LANES), jnp.float32)]
+        + [jax.ShapeDtypeStruct(phase.shape, jnp.float32)] * more,
         scratch_shapes=[pltpu.VMEM((RADIX, 2 * QUARTER, some * LANES), jnp.bfloat16)] * 2,
         compiler_params=limits(),
         cost_estimate=pl.CostEstimate(
-            flops=24 * OUTER * QUARTER * INNER, bytes_accessed=20 * OUTER * INNER, transcendentals=0
+            flops=24 * OUTER * QUARTER * INNER, bytes_accessed=32 * OUTER * INNER, transcendentals=0
         ),
-    )(params, *phases, matrices, twists)
+    )(params, phase, *kept, matrices, twists)
 
 
 def inner_call(mid, matrices, shards, parts):
@@ -503,13 +519,10 @@
 
 def slot_rows(stretches, groups):
     my_group = lax.axis_index("mem")
-    return jnp.concatenate(
-        [
-            to_group(lax.dynamic_index_in_dim(stretches, my_group ^ slot, 0, keepdims=False), slot)
-            for slot in range(groups)
-        ],
-        axis=0,
-    )
+    return [
+        to_group(lax.dynamic_index_in_dim(stretches, my_group ^ slot, 0, keepdims=False), slot)
+        for slot in range(groups)
+    ]
 
 
 def own_and_far(phase, params, my_group):
@@ -593,33 +606,28 @@
     twists = jnp.asarray(twist_tables())
     local_len = phase_left.shape[1]
 
-    def transform(phases, track, parts):
-        mid = outer_call(params, phases, outer_tables, twists, track)
-        return list(inner_call(mid, inner_tables, shards, parts))
-
-    left = part_call(phase_left)
-    left, my_group = lax.optimization_barrier((left, lax.axis_index("mem")))
-    left = swap(left)
+    left, right = part_call(phase_left), part_call(phase_right)
+    right, my_group = lax.optimization_barrier((right, lax.axis_index("mem")))
+    left, right = swap(left), swap(right)
     own, far = own_and_far(phase_left, all_params, my_group)
-    right = swap(part_call(phase_right))
-    first = transform((left,), 0, 1)[0]
-    edge = edge_of(own)
-    left, right, first, far, edge = lax.optimization_barrier((left, right, first, far, edge))
-    far = across(far)
-    second = transform((left, right), 1, 2)
-    ahead = swap(second[0])
-    line_gram = lines_gram(own, far, edge)
-    ahead, line_gram, second[1] = lax.optimization_barrier((ahead, line_gram, second[1]))
-    behind = swap(second[1])
-    profile, ahead = join_call(ahead, 1, 0, local_len, groups, None)
-    point_gram = rows_gram(slot_rows(ahead, groups))
-    behind, point_gram, first = lax.optimization_barrier((behind, point_gram, first))
-    first = swap(first)
-    profile, behind = join_call(behind, 1, 1, local_len, groups, profile)
-    point_gram = point_gram + rows_gram(slot_rows(behind, groups))
-    first, point_gram = lax.optimization_barrier((first, point_gram))
-    (profile,) = join_call(first, 0, 0, local_len, 0, profile)
-    gram_matrix = 0.25 * line_gram + (0.5 / (OUTER * INNER)) * point_gram
+    mid, *kept = outer_call(params, left, (), outer_tables, twists)
+    first = list(inner_call(mid, inner_tables, shards, 2))
+    right, *first = lax.optimization_barrier((right, *first))
+    early = swap(first[0])
+    (mid,) = outer_call(params, right, kept, outer_tables, twists)
+    (second,) = inner_call(mid, inner_tables, shards, 1)
+    early, second = lax.optimization_barrier((early, second))
+    second = swap(second)
+    second, first[1], own, far = lax.optimization_barrier((second, first[1], own, far))
+    profile, points = join_call(second, 1, 0, local_len, groups, None)
+    late = swap(first[1])
+    line_gram = lines_gram(own, across(far), edge_of(own))
+    (profile,) = join_call(early, 0, 0, local_len, 0, profile)
+    late, line_gram = lax.optimization_barrier((late, line_gram))
+    (profile,) = join_call(late, 0, 1, local_len, 0, profile)
+    rows = slot_rows(points, groups)
+    profile, line_gram, rows = lax.optimization_barrier((profile, line_gram, rows))
+    gram_matrix = 0.25 * line_gram + (0.5 / (OUTER * INNER)) * rows_gram(jnp.concatenate(rows, axis=0))
     return (profile, upper_of(summed(in_order(gram_matrix, members))))
 
 

time: 391 us -> 371 us (0.949)
  waiting for transfers between devices: 153 us -> 126 us
  blocking collectives: 25.6 us -> 42.2 us
  starting transfers between devices: 63.1 us -> 51.3 us
    ppermute x9 -> x6, waiting for transfers between devices: 129 us -> 4.27 us  [to_group(): lax.ppermute(piece, 'mem', [(z, z ^ slot) for z in range(groups)])]
    all_to_all x5, waiting for transfers between devices: 15.2 us -> 88.1 us  [swap(): return lax.all_to_all(piece, 'len', split_axis=0, concat_axis=0, tiled=True)]
    ppermute x1, waiting for transfers between devices: 8.71 us -> 33.7 us  [across(): lax.ppermute(far, 'len', [(d, shards - 1 - d) for d in range(shards)])]
    all_gather x2, blocking collectives: 25.6 us -> 42.2 us  [summed(): value = jnp.sum(lax.all_gather(value, axis), axis=0)]
    ppermute x9 -> x6, starting transfers between devices: 40.6 us -> 25.6 us  [to_group(): lax.ppermute(piece, 'mem', [(z, z ^ slot) for z in range(groups)])]
    pallas_call x2, Pallas kernels: 10.2 us -> 15.6 us  [part_call(): pl.pallas_call(part_kernel, grid=(rows // BLOCK_ROWS,), in_specs=[pl.Bloc...]
    dot_general x4 -> x3, matrix products: 12 us -> 14.7 us  [rows_gram(): lax.dot_general(rows, rows, (((1,), (1,)), ((), ())), precision=highest)]
  transfers between devices with their start and end apart: 16 -> 13, of which waited for: 9 -> 6; matrix products, arithmetic and copies ran while one was open for 6% -> 6% of each run, Pallas kernels for 23% -> 27%
where the time goes in v6:
time: 371 us; the launch traced here: 370 us
  waiting for transfers between devices  126 us (34%)
  Pallas kernels  109 us (29%)
  starting transfers between devices  51.3 us (14%)
  blocking collectives  42.2 us (11%)
  local copies, waits for them, and re-layouts  15.5 us (4%)
  matrix products  15.1 us (4%)
  other arithmetic  9.42 us (3%)
    all_to_all x5, waiting for transfers between devices, swap(): return lax.all_to_all(piece, 'len', split_axis=0, concat_axis=0, tiled=True)  88.1 us
    pallas_call x2, Pallas kernels, outer_call(): pl.pallas_call(functools.partial(outer_kernel, track), grid=(tiles // som...  44.6 us
    all_gather x2, blocking collectives, summed(): value = jnp.sum(lax.all_gather(value, axis), axis=0)  42.2 us
    ppermute x1, waiting for transfers between devices, across(): lax.ppermute(far, 'len', [(d, shards - 1 - d) for d in range(shards)])  33.7 us
    ppermute x6, starting transfers between devices, to_group(): lax.ppermute(piece, 'mem', [(z, z ^ slot) for z in range(groups)])  25.6 us
    all_to_all x5, starting transfers between devices, swap(): return lax.all_to_all(piece, 'len', split_axis=0, concat_axis=0, tiled=True)  22.2 us
    pallas_call x2, Pallas kernels, inner_call(): pl.pallas_call(inner_kernel, grid=(OUTER // WIDE,), in_specs=[pl.BlockSpe...  18.9 us
    pallas_call x2, Pallas kernels, part_call(): pl.pallas_call(part_kernel, grid=(rows // BLOCK_ROWS,), in_specs=[pl.Bloc...  15.6 us
  transfers between devices with their start and end apart: 13, of which 6 were waited for; matrix products, arithmetic and copies ran while one was open for 6% of the time, Pallas kernels for 27%

profile of v6, /device:TPU:0, one launch (start us, length us, event | category | flops | bytes accessed | tf_op | source)
XLA Modules:
  0.0 369.7 jit_solution(18199630036026746495)
XLA Ops:
  0.6 7.7 %shard_map.96 = f32[8,8,128,128]{3,2,1,0:T(8,128)} custom-call(f32[8,131072]{1,0:T(8,128)} %in_ref.3), custom_call_target="tpu_custom_call" | custom-call | bytes 8388608 | tf_op jit(solution)/shard_map/pallas_call | solution.py:407
  8.3 5.2 %all-to-all-start.1 = ((f32[8,8,128,128]{3,2,1,0:T(8,128)}), f32[8,8,128,128]{3,2,1,0:T(8,128)}, u32[]{:S(2)}, u32[]{:S(2)}) async-start(f32[8,8,128,128]{3,2,1,0:T(8,128)} %shard_map.96), calls=%async_computation.1 | async-start | bytes 8388608 | tf_op jit(solution)/shard_map/all_to_all | solution.py:600
  13.5 0.0 copy-start.10
  13.5 7.9 %shard_map.95 = f32[8,8,128,128]{3,2,1,0:T(8,128)} custom-call(f32[8,131072]{1,0:T(8,128)} %in_ref.2), custom_call_target="tpu_custom_call" | custom-call | bytes 8388608 | tf_op jit(solution)/shard_map/pallas_call | solution.py:407
  21.6 3.5 constant_dynamic-slice_fusion.1
  25.1 0.9 constant_dynamic-slice_fusion
  26.0 0.1 pad_maximum_fusion.4
  26.1 4.5 %collective-permute-start.2 = (f32[2,8,16512]{2,1,0:T(8,128)S(1)}, f32[2,8,16512]{2,1,0:T(8,128)S(1)}, u32[]{:S(2)}, u32[]{:S(2)}) collective-permute-start(f32[2,8,16512]{2,1,0:T(8,128)S(1)} %pad_maximum_fusion.4), channel_id=1, source_target_pairs={{0,3},{1,2},{2,1},{3,0},{4,7},{5,6},{6,5},{7,4},{8,11},{9,10},{10,... | collective-permute-start | bytes 3170312 | tf_op jit(solution)/shard_map/ppermute | solution.py:513
  30.7 1.1 pad_maximum_fusion.3
  31.8 0.0 collective-permute-start.1
  31.9 1.0 pad_maximum_fusion.2
  32.9 0.6 collective-permute-start
  33.5 0.2 fusion.28.params_ref
  33.7 29.0 %all-to-all-done.1.phase_ref = f32[8,8,128,128]{3,2,1,0:T(8,128)} async-done(((f32[8,8,128,128]{3,2,1,0:T(8,128)}), f32[8,8,128,128]{3,2,1,0:T(8,128)}, u32[]{:S(2)}, u32[]{:S(2)}) %all-to-all-start.1) | async-done | bytes 4194336 | tf_op jit(solution)/shard_map/all_to_all | solution.py:600
  62.7 4.6 %all-to-all-start = ((f32[8,8,128,128]{3,2,1,0:T(8,128)}), f32[8,8,128,128]{3,2,1,0:T(8,128)}, u32[]{:S(2)}, u32[]{:S(2)}) async-start(f32[8,8,128,128]{3,2,1,0:T(8,128)} %shard_map.95), calls=%async_computation | async-start | bytes 8388608 | tf_op jit(solution)/shard_map/all_to_all | solution.py:600
  67.3 0.0 collective-permute-done.2
  67.3 0.1 slice_bitcast_fusion.6
  67.4 0.0 copy-start.3
  67.4 23.9 %shard_map.97 = (f32[8,2,1024,128]{3,2,1,0:T(8,128)}, f32[8,8,128,128]{3,2,1,0:T(8,128)S(1)}, f32[8,8,128,128]{3,2,1,0:T(8,128)}, f32[8,8,128,128]{3,2,1,0:T(8,128)}) custom-call(f32[3]{0:T(128)S(1)} %fusion.28.params_ref, f32[8,8,128,128]{3,2,1,0:T(8,128)} %all-to-all-done.1.phase_ref, bf16[2,4,512,512]{3,2,1,0:T(8,128)(2,1)} %constant.161.clone.refs_0_.refs_3_, ...), custom_call_target="tpu_custom_call" | custom-call | flops 6442450944 | bytes 33554432 | tf_op jit(solution)/shard_map/pallas_call | solution.py:451
  91.3 2.1 copy-done.2
  93.4 9.4 %shard_map.98 = (f32[8,8,64,128]{3,2,1,0:T(8,128)}, f32[8,8,64,128]{3,2,1,0:T(8,128)}) custom-call(f32[8,2,1024,128]{3,2,1,0:T(8,128)} %get-tuple-element.30.mid_ref, bf16[2,4,256,512]{3,2,1,0:T(8,128)(2,1)S(1)} %copy-done.3), custom_call_target="tpu_custom_call" | custom-call | flops 3221225472 | bytes 12582912 | tf_op jit(solution)/shard_map/pallas_call | solution.py:474
  102.8 13.6 %all-to-all-done.phase_ref = f32[8,8,128,128]{3,2,1,0:T(8,128)} async-done(((f32[8,8,128,128]{3,2,1,0:T(8,128)}), f32[8,8,128,128]{3,2,1,0:T(8,128)}, u32[]{:S(2)}, u32[]{:S(2)}) %all-to-all-start) | async-done | bytes 4194336 | tf_op jit(solution)/shard_map/all_to_all | solution.py:600
  116.4 3.6 all-to-all-start.2
  120.0 1.6 collective-permute-done.1
  121.7 2.3 slice_bitcast_fusion.7
  124.0 20.7 %shard_map.99.mid_ref = f32[8,2,1024,128]{3,2,1,0:T(8,128)} custom-call(f32[3]{0:T(128)S(1)} %fusion.28.params_ref, f32[8,8,128,128]{3,2,1,0:T(8,128)} %all-to-all-done.phase_ref, f32[8,8,128,128]{3,2,1,0:T(8,128)} %copy-done.2, f32[8,8,128,128]{3,2,1,0:T(8,128)} %get-tuple-element.36.refs_1_, f32[8,8,128,128]{3,2,1,0:T(8,128)} %get-tuple-element.37.refs_2_, ...), custom_call_target="tpu_custom_call" | custom-call | flops 6442450944 | bytes 33554432 | tf_op jit(solution)/shard_map/pallas_call | solution.py:451
  144.7 9.4 %shard_map.100 = f32[8,8,128,128]{3,2,1,0:T(8,128)} custom-call(f32[8,2,1024,128]{3,2,1,0:T(8,128)} %shard_map.99.mid_ref, bf16[2,4,256,512]{3,2,1,0:T(8,128)(2,1)S(1)} %copy-done.4), custom_call_target="tpu_custom_call" | custom-call | flops 3221225472 | bytes 12582912 | tf_op jit(solution)/shard_map/pallas_call | solution.py:474
  154.2 0.0 all-to-all-done.2.in_ref
  154.2 1.3 copy-done
  155.5 4.5 %all-to-all-start.3 = ((f32[8,8,128,128]{3,2,1,0:T(8,128)}), f32[8,8,128,128]{3,2,1,0:T(8,128)}, u32[]{:S(2)}, u32[]{:S(2)}) async-start(f32[8,8,128,128]{3,2,1,0:T(8,128)} %shard_map.100), calls=%async_computation.3 | async-start | bytes 8388608 | tf_op jit(solution)/shard_map/all_to_all | solution.py:600
  160.1 1.4 slice_bitcast_fusion.8
  161.5 0.0 copy-done.6
  161.6 0.2 copy-done.7
  161.7 0.2 copy-done.8
  161.9 1.7 pad_maximum_fusion
  163.6 45.6 %all-to-all-done.3.in_ref = f32[8,8,128,128]{3,2,1,0:T(8,128)} async-done(((f32[8,8,128,128]{3,2,1,0:T(8,128)}), f32[8,8,128,128]{3,2,1,0:T(8,128)}, u32[]{:S(2)}, u32[]{:S(2)}) %all-to-all-start.3) | async-done | bytes 4194336 | tf_op jit(solution)/shard_map/all_to_all | solution.py:600
  209.2 4.3 %all-to-all-start.4 = ((f32[8,8,64,128]{3,2,1,0:T(8,128)}), f32[8,8,64,128]{3,2,1,0:T(8,128)}, u32[]{:S(2)}, u32[]{:S(2)}) async-start(f32[8,8,64,128]{3,2,1,0:T(8,128)} %get-tuple-element.41), calls=%async_computation.4 | async-start | bytes 4194304 | tf_op jit(solution)/shard_map/all_to_all | solution.py:600
  213.5 2.6 collective-permute-start.3
  216.1 7.6 %shard_map.102 = (f32[2,8,131072]{2,1,0:T(8,128)}, f32[4,8,32768]{2,1,0:T(8,128)S(1)}) custom-call(f32[8,8,128,128]{3,2,1,0:T(8,128)} %all-to-all-done.3.in_ref), custom_call_target="tpu_custom_call" | custom-call | bytes 12582912 | tf_op jit(solution)/shard_map/pallas_call | solution.py:424
  223.7 1.9 dynamic-slice_bitcast_fusion
  225.6 18.0 %collective-permute-start.5 = (f32[8,32768]{1,0:T(8,128)}, f32[8,32768]{1,0:T(8,128)}, u32[]{:S(2)}, u32[]{:S(2)}) collective-permute-start(f32[8,32768]{1,0:T(8,128)} %get-tuple-element.68), channel_id=1, source_target_pairs={{0,1},{1,0},{2,3},{3,2},{4,5},{5,4},{6,7},{7,6},{8,9},{9,8},{10,11... | collective-permute-start | bytes 3145736 | tf_op jit(solution)/shard_map/ppermute | solution.py:513
  243.6 1.0 collective-permute-start.6
  244.6 1.5 collective-permute-start.7
  246.1 0.8 collective-permute-start.4
  246.9 0.1 pad_add_fusion.base_ref
  247.0 1.6 copy-done.1
  248.6 2.7 shard_map.103.refs_0_
  251.3 0.0 collective-permute-done.4.edge_ref
  251.3 33.7 %collective-permute-done.3.far_ref = f32[32,16512]{1,0:T(8,128)} collective-permute-done((f32[32,16512]{1,0:T(8,128)}, f32[32,16512]{1,0:T(8,128)}, u32[]{:S(2)}, u32[]{:S(2)}) %collective-permute-start.3) | collective-permute-done | bytes 2113568 | tf_op jit(solution)/shard_map/ppermute | solution.py:566
  285.0 15.4 %shard_map.101 = f32[2,32,16512]{2,1,0:T(8,128)} custom-call(s32[3]{0:T(128)S(1)} %pad_add_fusion.base_ref, f32[32,16512]{1,0:T(8,128)S(1)} %get-tuple-element.42.own_ref, f32[32,16512]{1,0:T(8,128)} %collective-permute-done.3.far_ref, f32[32,128]{1,0:T(8,128)S(1)} %collective-permute-done.4.edge_ref), custom_call_target="tpu_custom_call" | custom-call | flops 105676800 | bytes 8454144 | tf_op jit(solution)/shard_map/pallas_call | solution.py:493
  300.4 4.2 %fusion.8 = f32[32,32]{1,0:T(8,128)S(1)} fusion(f32[2,32,16512]{2,1,0:T(8,128)} %shard_map.101), kind=kOutput, calls=%fused_computation.9 | convolution fusion | flops 202899456 | bytes 2117632 | tf_op jit(solution)/shard_map/dot_general | solution.py:517
  304.6 4.2 %fusion.10 = f32[32,32]{1,0:T(8,128)S(1)} fusion(f32[32,32]{1,0:T(8,128)S(1)} %fusion.8, f32[2,32,16512]{2,1,0:T(8,128)} %shard_map.101), kind=kOutput, calls=%fused_computation.14 | convolution fusion | flops 202900480 | bytes 2121728 | tf_op jit(solution)/shard_map/dot_general | solution.py:517
  308.8 4.4 %shard_map.104 = f32[2,8,131072]{2,1,0:T(8,128)} custom-call(f32[8,8,64,128]{3,2,1,0:T(8,128)} %all-to-all-done.4.in_ref, f32[2,8,131072]{2,1,0:T(8,128)} %shard_map.103.refs_0_), custom_call_target="tpu_custom_call", output_to_operand_aliasing={{}: (1, {})} | custom-call | bytes 6291456 | tf_op jit(solution)/shard_map/pallas_call | solution.py:424
  313.2 2.6 collective-permute-done.6
  315.8 6.2 %fusion.11 = f32[32,32]{1,0:T(8,128)S(1)} fusion(f32[8,32768]{1,0:T(8,128)} %collective-permute-done.7, f32[8,32768]{1,0:T(8,128)} %collective-permute-done.6, f32[8,32768]{1,0:T(8,128)} %collective-permute-done.5, f32[8,32768]{1,0:T(8,128)S(1)} %get-tuple-element.52), kind=kOutput, calls=%fused_computation.22 | convolution fusion | flops 405799936 | bytes 4198400 | tf_op jit(solution)/shard_map/dot_general | solution.py:517
  322.1 0.2 fusion.15
  322.3 0.2 fusion.32
  322.5 8.3 %all-gather = f32[256,32]{1,0:T(8,128)S(1)} all-gather(f32[32,32]{1,0:T(8,128)S(1)} %fusion.32), channel_id=2, replica_groups=mesh['len'=8,'mem'=4] {'len'}, dimensions={0}, use_global_device_ids=true | all-gather | bytes 36864 | tf_op jit(solution)/shard_map/all_gather | solution.py:590
  330.8 33.9 %all-gather.1 = f32[128,32]{1,0:T(8,128)S(1)} all-gather(f32[32,32]{1,0:T(8,128)S(1)} %reduce_sum.18), channel_id=3, replica_groups=mesh['len'=8,'mem'=4] {'mem'}, dimensions={0}, use_global_device_ids=true | all-gather | bytes 20480 | tf_op jit(solution)/shard_map/all_gather | solution.py:590
  364.7 0.1 copy.16
  364.8 2.9 cholesky.18
  367.7 0.6 compare_reduce_fusion
  368.4 0.6 select_bitcast_fusion
  369.0 0.7 copy.17
  (39 shorter events, 0.4 us)
Async XLA Ops:
  8.3 54.4 %all-to-all-start.1 = ((f32[8,8,128,128]{3,2,1,0:T(8,128)}), f32[8,8,128,128]{3,2,1,0:T(8,128)}, u32[]{:S(2)}, u32[]{:S(2)}) async-start(f32[8,8,128,128]{3,2,1,0:T(8,128)} %shard_map.96), calls=%async_computation.1 | async-start | bytes 8388608 | tf_op jit(solution)/shard_map/all_to_all | solution.py:600
  13.5 8.0 %copy-start.9 = (f32[8]{0:T(128)S(1)}, f32[8]{0:T(128)}, u32[]{:S(2)}) copy-start(f32[8]{0:T(128)} %param.11) | copy-start | bytes 100
  13.5 8.0 %copy-start.10 = (f32[8]{0:T(128)S(1)}, f32[8]{0:T(128)}, u32[]{:S(2)}) copy-start(f32[8]{0:T(128)} %param.10) | copy-start | bytes 100
  26.1 41.2 %collective-permute-start.2 = (f32[2,8,16512]{2,1,0:T(8,128)S(1)}, f32[2,8,16512]{2,1,0:T(8,128)S(1)}, u32[]{:S(2)}, u32[]{:S(2)}) collective-permute-start(f32[2,8,16512]{2,1,0:T(8,128)S(1)} %pad_maximum_fusion.4), channel_id=1, source_target_pairs={{0,3},{1,2},{2,1},{3,0},{4,7},{5,6},{6,5},{7,4},{8,11},{9,10},{10,... | collective-permute-start | bytes 3170312 | tf_op jit(solution)/shard_map/ppermute | solution.py:513
  31.8 89.9 %collective-permute-start.1 = (f32[2,8,16512]{2,1,0:T(8,128)}, f32[2,8,16512]{2,1,0:T(8,128)}, u32[]{:S(2)}, u32[]{:S(2)}) collective-permute-start(f32[2,8,16512]{2,1,0:T(8,128)} %pad_maximum_fusion.3), channel_id=1, source_target_pairs={{0,2},{1,3},{2,0},{3,1},{4,6},{5,7},{6,4},{7,5},{8,10},{9,11},{10,... | collective-permute-start | bytes 3170312 | tf_op jit(solution)/shard_map/ppermute | solution.py:513
  31.8 1.7 copy-start.11
  32.9 127.1 %collective-permute-start = (f32[2,8,16512]{2,1,0:T(8,128)}, f32[2,8,16512]{2,1,0:T(8,128)}, u32[]{:S(2)}, u32[]{:S(2)}) collective-permute-start(f32[2,8,16512]{2,1,0:T(8,128)} %pad_maximum_fusion.2), channel_id=1, source_target_pairs={{0,1},{1,0},{2,3},{3,2},{4,5},{5,4},{6,7},{7,6},{8,9},{9,8},{10,11... | collective-permute-start | bytes 3170312 | tf_op jit(solution)/shard_map/ppermute | solution.py:513
  62.7 53.7 %all-to-all-start = ((f32[8,8,128,128]{3,2,1,0:T(8,128)}), f32[8,8,128,128]{3,2,1,0:T(8,128)}, u32[]{:S(2)}, u32[]{:S(2)}) async-start(f32[8,8,128,128]{3,2,1,0:T(8,128)} %shard_map.95), calls=%async_computation | async-start | bytes 8388608 | tf_op jit(solution)/shard_map/all_to_all | solution.py:600
  67.4 26.0 %copy-start.3 = (bf16[2,4,256,512]{3,2,1,0:T(8,128)(2,1)S(1)}, bf16[2,4,256,512]{3,2,1,0:T(8,128)(2,1)}, u32[]{:S(2)}) copy-start(bf16[2,4,256,512]{3,2,1,0:T(8,128)(2,1)} %constant.162.clone.matrix_ref) | copy-start | bytes 6291460
  91.3 2.1 copy-start.2
  116.4 37.8 %all-to-all-start.2 = ((f32[8,8,64,128]{3,2,1,0:T(8,128)}), f32[8,8,64,128]{3,2,1,0:T(8,128)S(1)}, u32[]{:S(2)}, u32[]{:S(2)}) async-start(f32[8,8,64,128]{3,2,1,0:T(8,128)} %get-tuple-element.33), calls=%async_computation.2 | async-start | bytes 4194304 | tf_op jit(solution)/shard_map/all_to_all | solution.py:600
  124.0 20.7 %copy-start.4 = (bf16[2,4,256,512]{3,2,1,0:T(8,128)(2,1)S(1)}, bf16[2,4,256,512]{3,2,1,0:T(8,128)(2,1)}, u32[]{:S(2)}) copy-start(bf16[2,4,256,512]{3,2,1,0:T(8,128)(2,1)} %constant.162.clone.matrix_ref) | copy-start | bytes 6291460
  154.2 1.3 copy-start
  155.5 53.7 %all-to-all-start.3 = ((f32[8,8,128,128]{3,2,1,0:T(8,128)}), f32[8,8,128,128]{3,2,1,0:T(8,128)}, u32[]{:S(2)}, u32[]{:S(2)}) async-start(f32[8,8,128,128]{3,2,1,0:T(8,128)} %shard_map.100), calls=%async_computation.3 | async-start | bytes 8388608 | tf_op jit(solution)/shard_map/all_to_all | solution.py:600
  160.0 1.5 copy-start.5
  160.1 1.5 copy-start.6
  160.1 1.7 copy-start.7
  160.1 1.8 copy-start.8
  209.2 99.7 %all-to-all-start.4 = ((f32[8,8,64,128]{3,2,1,0:T(8,128)}), f32[8,8,64,128]{3,2,1,0:T(8,128)}, u32[]{:S(2)}, u32[]{:S(2)}) async-start(f32[8,8,64,128]{3,2,1,0:T(8,128)} %get-tuple-element.41), calls=%async_computation.4 | async-start | bytes 4194304 | tf_op jit(solution)/shard_map/all_to_all | solution.py:600
  213.5 71.5 %collective-permute-start.3 = (f32[32,16512]{1,0:T(8,128)}, f32[32,16512]{1,0:T(8,128)}, u32[]{:S(2)}, u32[]{:S(2)}) collective-permute-start(f32[32,16512]{1,0:T(8,128)} %get-tuple-element.43), channel_id=1, source_target_pairs={{0,28},{4,24},{8,20},{12,16},{16,12},{20,8},{24,4},{28,0},{1,29},{... | collective-permute-start | bytes 6340616 | tf_op jit(solution)/shard_map/ppermute | solution.py:566
  225.6 87.6 %collective-permute-start.5 = (f32[8,32768]{1,0:T(8,128)}, f32[8,32768]{1,0:T(8,128)}, u32[]{:S(2)}, u32[]{:S(2)}) collective-permute-start(f32[8,32768]{1,0:T(8,128)} %get-tuple-element.68), channel_id=1, source_target_pairs={{0,1},{1,0},{2,3},{3,2},{4,5},{5,4},{6,7},{7,6},{8,9},{9,8},{10,11... | collective-permute-start | bytes 3145736 | tf_op jit(solution)/shard_map/ppermute | solution.py:513
  243.6 72.2 %collective-permute-start.6 = (f32[8,32768]{1,0:T(8,128)}, f32[8,32768]{1,0:T(8,128)}, u32[]{:S(2)}, u32[]{:S(2)}) collective-permute-start(f32[8,32768]{1,0:T(8,128)} %get-tuple-element.67), channel_id=1, source_target_pairs={{0,2},{1,3},{2,0},{3,1},{4,6},{5,7},{6,4},{7,5},{8,10},{9,11},{10,... | collective-permute-start | bytes 3145736 | tf_op jit(solution)/shard_map/ppermute | solution.py:513
  244.6 71.2 %collective-permute-start.7 = (f32[8,32768]{1,0:T(8,128)}, f32[8,32768]{1,0:T(8,128)}, u32[]{:S(2)}, u32[]{:S(2)}) collective-permute-start(f32[8,32768]{1,0:T(8,128)} %get-tuple-element.66), channel_id=1, source_target_pairs={{0,3},{1,2},{2,1},{3,0},{4,7},{5,6},{6,5},{7,4},{8,11},{9,10},{10,... | collective-permute-start | bytes 3145736 | tf_op jit(solution)/shard_map/ppermute | solution.py:513
  246.1 5.2 %collective-permute-start.4 = (f32[32,128]{1,0:T(8,128)S(1)}, f32[32,128]{1,0:T(8,128)S(1)}, u32[]{:S(2)}, u32[]{:S(2)}) collective-permute-start(f32[32,128]{1,0:T(8,128)S(1)} %slice.39), channel_id=1, source_target_pairs={{0,0},{4,28},{8,24},{12,20},{16,16},{20,12},{24,8},{28,4},{1,1},{5... | collective-permute-start | bytes 49160 | tf_op jit(solution)/shard_map/ppermute | solution.py:561
  247.0 1.6 copy-start.1

commit v7 on v6

--- a/solution.py
+++ b/solution.py
@@ -16,6 +16,8 @@
 QUARTER = 256
 LANES = 128
 STEP = 16
+IN_PARTS = 2
+SUBLANES = 8
 WIDE = 256
 BLOCK_ROWS = 16
 OUTER_TILES = 2
@@ -304,17 +306,18 @@
             out_ref[tile, 1, pl.ds(e, QUARTER, stride=RADIX), :] = real * sin_part + imag * cos_part
 
 
-def inner_kernel(mid_ref, matrix_ref, *refs):
-    out_refs, (coarse_ref, fine_ref) = refs[:-2], refs[-2:]
-    wide = mid_ref.shape[2]
-    shards, _, rows, _ = out_refs[0].shape
+def inner_kernel(*refs):
+    mid_refs, (matrix_ref, out_ref, coarse_ref, fine_ref) = refs[:-4], refs[-4:]
+    some, _, wide, _ = mid_refs[0].shape
+    shards, _, rows, _ = out_ref.shape
 
     def some_rows(step, carry):
         at = pl.multiple_of(step * STEP, STEP)
         for half in range(0, QUARTER, LANES):
+            tiles = [(a * QUARTER + half) // LANES for a in range(RADIX)]
             parts = [
-                tuple(mid_ref[(a * QUARTER + half) // LANES, ri, pl.ds(at, STEP), :] for ri in range(2))
-                for a in range(RADIX)
+                tuple(mid_refs[tile // some][tile % some, ri, pl.ds(at, STEP), :] for ri in range(2))
+                for tile in tiles
             ]
             mixed = radix_four(parts)
             for e in range(RADIX):
@@ -324,37 +327,38 @@
         return carry
 
     lax.fori_loop(0, wide // STEP, some_rows, 0)
-    some = rows // RADIX
+    each = rows // RADIX
     for e in range(RADIX):
         value = triple_dot(matrix_ref, e, coarse_ref[e], fine_ref[e], ((1,), (1,)))
         for f in range(shards):
-            for part, out_ref in enumerate(out_refs):
-                at = (f * len(out_refs) + part) * some
-                for tile in range(wide // LANES):
-                    out_ref[f, tile, pl.ds(e, some, stride=RADIX), :] = value[
-                        at : at + some, tile * LANES : (tile + 1) * LANES
-                    ]
-
-
-def part_kernel(in_ref, out_ref):
-    members, tiles, rows, _ = out_ref.shape
-    flat_ref = out_ref.reshape(members * tiles * rows, LANES)
-    for r in range(rows):
-        for tile in range(tiles):
-            at = (r * tiles + tile) * LANES
-            flat_ref[pl.ds(tile * rows + r, members, stride=tiles * rows), :] = in_ref[:, at : at + LANES]
+            for tile in range(wide // LANES):
+                out_ref[f, tile, pl.ds(e, each, stride=RADIX), :] = value[
+                    f * each : (f + 1) * each, tile * LANES : (tile + 1) * LANES
+                ]
+
+
+def part_kernel(in_ref, *out_refs):
+    members, some, rows, _ = out_refs[0].shape
+    tiles = some * len(out_refs)
+    for tile in range(tiles):
+        out_ref = out_refs[tile // some]
+        for start in range(0, rows, SUBLANES):
+            columns = [((start + r) * tiles + tile) * LANES for r in range(SUBLANES)]
+            turned = jnp.transpose(jnp.stack([in_ref[:, at : at + LANES] for at in columns]), (1, 0, 2))
+            for m in range(members):
+                out_ref[m, tile % some, start : start + SUBLANES, :] = turned[m]
 
 
 def join_kernel(extra, in_ref, *refs):
     out_refs = refs[-2:] if extra else refs[-1:]
     members, tiles, rows, _ = in_ref.shape
-    flat_ref = in_ref.reshape(members * tiles * rows, LANES)
-    for r in range(rows):
-        for tile in range(tiles):
-            at = (r * tiles + tile) * LANES
-            value = flat_ref[pl.ds(tile * rows + r, members, stride=tiles * rows), :]
-            for out_ref in out_refs:
-                out_ref[0, :, at : at + LANES] = value
+    for tile in range(tiles):
+        for start in range(0, rows, SUBLANES):
+            turned = jnp.transpose(in_ref[:, tile, start : start + SUBLANES, :], (1, 0, 2))
+            for r in range(SUBLANES):
+                at = ((start + r) * tiles + tile) * LANES
+                for out_ref in out_refs:
+                    out_ref[0, :, at : at + LANES] = turned[r]
 
 
 def mirror_kernel(base_ref, own_ref, far_ref, edge_ref, out_ref):
@@ -400,16 +404,16 @@
     return pltpu.CompilerParams(vmem_limit_bytes=VMEM_LIMIT)
 
 
-def part_call(phase):
+def part_call(phase, parts):
     members, length = phase.shape
     rows = length // INNER
-    tiles = INNER // LANES
+    tiles = INNER // LANES // parts
     return pl.pallas_call(
         part_kernel,
         grid=(rows // BLOCK_ROWS,),
         in_specs=[pl.BlockSpec((members, BLOCK_ROWS * INNER), lambda g: (0, g))],
-        out_specs=pl.BlockSpec((members, tiles, BLOCK_ROWS, LANES), lambda g: (0, 0, g, 0)),
-        out_shape=pltpu.HBM((members, tiles, rows, LANES), jnp.float32),
+        out_specs=[pl.BlockSpec((members, tiles, BLOCK_ROWS, LANES), lambda g: (0, 0, g, 0))] * parts,
+        out_shape=[pltpu.HBM((members, tiles, rows, LANES), jnp.float32)] * parts,
         compiler_params=limits(),
         cost_estimate=pl.CostEstimate(flops=0, bytes_accessed=8 * members * length, transcendentals=0),
     )(pltpu.with_memory_space_constraint(phase, pltpu.HBM))
@@ -442,50 +446,54 @@
     )(*operands)
 
 
-def outer_call(params, phase, kept, matrices, twists):
+def outer_call(params, phase, kept, matrices, twists, part):
     track = 1 if kept else 0
     sources, tiles, rows, _ = phase.shape
     some = OUTER_TILES
-    lines = pl.BlockSpec((sources, some, rows, LANES), lambda g: (0, g, 0, 0))
+    first = part * (tiles // some)
+
+    def lines(first):
+        return pl.BlockSpec((sources, some, rows, LANES), lambda g: (0, first + g, 0, 0))
+
     more = 0 if kept else 3
     return pl.pallas_call(
         functools.partial(outer_kernel, track),
         grid=(tiles // some,),
-        in_specs=[pl.BlockSpec(memory_space=pltpu.SMEM)]
-        + [lines] * (1 + len(kept))
+        in_specs=[pl.BlockSpec(memory_space=pltpu.SMEM), lines(0)]
+        + [lines(first)] * len(kept)
         + [
             pl.BlockSpec(matrices.shape, lambda g: (0, 0, 0, 0)),
-            pl.BlockSpec((2, RADIX, QUARTER, some * LANES), lambda g: (0, 0, 0, g)),
+            pl.BlockSpec((2, RADIX, QUARTER, some * LANES), lambda g: (0, 0, 0, first + g)),
         ],
-        out_specs=[pl.BlockSpec((some, 2, OUTER, LANES), lambda g: (g, 0, 0, 0))] + [lines] * more,
+        out_specs=[pl.BlockSpec((some, 2, OUTER, LANES), lambda g: (g, 0, 0, 0))] + [lines(0)] * more,
         out_shape=[jax.ShapeDtypeStruct((tiles, 2, OUTER, LANES), jnp.float32)]
-        + [jax.ShapeDtypeStruct(phase.shape, jnp.float32)] * more,
+        + [pltpu.HBM(phase.shape, jnp.float32)] * more,
         scratch_shapes=[pltpu.VMEM((RADIX, 2 * QUARTER, some * LANES), jnp.bfloat16)] * 2,
         compiler_params=limits(),
         cost_estimate=pl.CostEstimate(
-            flops=24 * OUTER * QUARTER * INNER, bytes_accessed=32 * OUTER * INNER, transcendentals=0
+            flops=24 * OUTER * QUARTER * tiles * LANES,
+            bytes_accessed=32 * OUTER * tiles * LANES,
+            transcendentals=0,
         ),
     )(params, phase, *kept, matrices, twists)
 
 
-def inner_call(mid, matrices, shards, parts):
-    rows = INNER // shards // parts
+def inner_call(mids, matrices, shards):
+    rows = INNER // shards
     tiles = OUTER // LANES
     return pl.pallas_call(
         inner_kernel,
         grid=(OUTER // WIDE,),
-        in_specs=[
-            pl.BlockSpec((INNER // LANES, 2, WIDE, LANES), lambda g: (0, 0, g, 0)),
-            pl.BlockSpec(matrices.shape, lambda g: (0, 0, 0, 0)),
-        ],
-        out_specs=[pl.BlockSpec((shards, WIDE // LANES, rows, LANES), lambda g: (0, g, 0, 0))] * parts,
-        out_shape=[pltpu.HBM((shards, tiles, rows, LANES), jnp.float32)] * parts,
+        in_specs=[pl.BlockSpec((mid.shape[0], 2, WIDE, LANES), lambda g: (0, 0, g, 0)) for mid in mids]
+        + [pl.BlockSpec(matrices.shape, lambda g: (0, 0, 0, 0))],
+        out_specs=pl.BlockSpec((shards, WIDE // LANES, rows, LANES), lambda g: (0, g, 0, 0)),
+        out_shape=pltpu.HBM((shards, tiles, rows, LANES), jnp.float32),
         scratch_shapes=[pltpu.VMEM((RADIX, WIDE, 2 * QUARTER), jnp.bfloat16)] * 2,
         compiler_params=limits(),
         cost_estimate=pl.CostEstimate(
             flops=12 * OUTER * QUARTER * INNER, bytes_accessed=12 * OUTER * INNER, transcendentals=0
         ),
-    )(mid, matrices)
+    )(*mids, matrices)
 
 
 def mirror_call(base, own, far, edge):
@@ -513,8 +521,8 @@
     return lax.ppermute(piece, "mem", [(z, z ^ slot) for z in range(groups)]) if slot else piece
 
 
-def rows_gram(rows):
-    return lax.dot_general(rows, rows, (((1,), (1,)), ((), ())), precision=highest)
+def rows_gram(rows, precision=highest):
+    return lax.dot_general(rows, rows, (((1,), (1,)), ((), ())), precision=precision)
 
 
 def slot_rows(stretches, groups):
@@ -606,28 +614,26 @@
     twists = jnp.asarray(twist_tables())
     local_len = phase_left.shape[1]
 
-    left, right = part_call(phase_left), part_call(phase_right)
+    (left,), right = part_call(phase_left, 1), part_call(phase_right, IN_PARTS)
     right, my_group = lax.optimization_barrier((right, lax.axis_index("mem")))
-    left, right = swap(left), swap(right)
+    left, right = swap(left), [swap(piece) for piece in right]
     own, far = own_and_far(phase_left, all_params, my_group)
-    mid, *kept = outer_call(params, left, (), outer_tables, twists)
-    first = list(inner_call(mid, inner_tables, shards, 2))
-    right, *first = lax.optimization_barrier((right, *first))
-    early = swap(first[0])
-    (mid,) = outer_call(params, right, kept, outer_tables, twists)
-    (second,) = inner_call(mid, inner_tables, shards, 1)
-    early, second = lax.optimization_barrier((early, second))
-    second = swap(second)
-    second, first[1], own, far = lax.optimization_barrier((second, first[1], own, far))
+    mid, *kept = outer_call(params, left, (), outer_tables, twists, 0)
+    first = inner_call([mid], inner_tables, shards)
+    first, kept, right[0] = lax.optimization_barrier((first, kept, right[0]))
+    mids = [outer_call(params, piece, kept, outer_tables, twists, n)[0] for n, piece in enumerate(right)]
+    second = swap(inner_call(mids, inner_tables, shards))
     profile, points = join_call(second, 1, 0, local_len, groups, None)
-    late = swap(first[1])
-    line_gram = lines_gram(own, across(far), edge_of(own))
-    (profile,) = join_call(early, 0, 0, local_len, 0, profile)
-    late, line_gram = lax.optimization_barrier((late, line_gram))
-    (profile,) = join_call(late, 0, 1, local_len, 0, profile)
+    _, own, far = lax.optimization_barrier((points, own, far))
     rows = slot_rows(points, groups)
-    profile, line_gram, rows = lax.optimization_barrier((profile, line_gram, rows))
-    gram_matrix = 0.25 * line_gram + (0.5 / (OUTER * INNER)) * rows_gram(jnp.concatenate(rows, axis=0))
+    far = across(far)
+    edge = edge_of(own)
+    far, first = lax.optimization_barrier((far, first))
+    line_gram = lines_gram(own, far, edge)
+    (profile,) = join_call(swap(first), 0, 0, local_len, 0, profile)
+    profile, rows, line_gram = lax.optimization_barrier((profile, rows, line_gram))
+    point_gram = rows_gram(jnp.concatenate(rows, axis=0), lax.Precision.HIGH)
+    gram_matrix = 0.25 * line_gram + (0.5 / (OUTER * INNER)) * point_gram
     return (profile, upper_of(summed(in_order(gram_matrix, members))))
 
 

time: 371 us -> 430 us (1.16)
  waiting for transfers between devices: 126 us -> 199 us
  starting transfers between devices: 51.3 us -> 33.1 us
    ppermute x6, waiting for transfers between devices: 4.27 us -> 34 us  [to_group(): lax.ppermute(piece, 'mem', [(z, z ^ slot) for z in range(groups)])]
    all_to_all x5, waiting for transfers between devices: 88.1 us -> 117 us  [swap(): return lax.all_to_all(piece, 'len', split_axis=0, concat_axis=0, tiled=True)]
    ppermute x6, starting transfers between devices: 25.6 us -> 8.85 us  [to_group(): lax.ppermute(piece, 'mem', [(z, z ^ slot) for z in range(groups)])]
    ppermute x1, waiting for transfers between devices: 33.7 us -> 47.7 us  [across(): lax.ppermute(far, 'len', [(d, shards - 1 - d) for d in range(shards)])]
    pallas_call x2 -> x3, Pallas kernels: 44.6 us -> 49.8 us  [outer_call(): pl.pallas_call(functools.partial(outer_kernel, track), grid=(tiles // som...]
    pallas_call x3 -> x2, Pallas kernels: 14.6 us -> 13.9 us  [join_call(): pl.pallas_call(functools.partial(join_kernel, groups > 0), grid=(steps,),...]
  transfers between devices with their start and end apart: 13 -> 13, of which waited for: 6 -> 8; matrix products, arithmetic and copies ran while one was open for 6% -> 6% of each run, Pallas kernels for 27% -> 23%
where the time goes in v7:
time: 430 us; the launch traced here: 429 us
  waiting for transfers between devices  199 us (46%)
  Pallas kernels  112 us (26%)
  blocking collectives  43.6 us (10%)
  starting transfers between devices  33.1 us (8%)
  local copies, waits for them, and re-layouts  17 us (4%)
  matrix products  13.5 us (3%)
  other arithmetic  9.46 us (2%)
    all_to_all x5, waiting for transfers between devices, swap(): return lax.all_to_all(piece, 'len', split_axis=0, concat_axis=0, tiled=True)  117 us
    pallas_call x3, Pallas kernels, outer_call(): pl.pallas_call(functools.partial(outer_kernel, track), grid=(tiles // som...  49.8 us
    ppermute x1, waiting for transfers between devices, across(): lax.ppermute(far, 'len', [(d, shards - 1 - d) for d in range(shards)])  47.7 us
    all_gather x2, blocking collectives, summed(): value = jnp.sum(lax.all_gather(value, axis), axis=0)  43.6 us
    ppermute x6, waiting for transfers between devices, to_group(): lax.ppermute(piece, 'mem', [(z, z ^ slot) for z in range(groups)])  34 us
    all_to_all x5, starting transfers between devices, swap(): return lax.all_to_all(piece, 'len', split_axis=0, concat_axis=0, tiled=True)  23.4 us
    pallas_call x2, Pallas kernels, inner_call(): pl.pallas_call(inner_kernel, grid=(OUTER // WIDE,), in_specs=[pl.BlockSpe...  18.9 us
    pallas_call x1, Pallas kernels, mirror_call(): pl.pallas_call(mirror_kernel, in_specs=[pl.BlockSpec(memory_space=pltpu.S...  15.4 us
  transfers between devices with their start and end apart: 13, of which 8 were waited for; matrix products, arithmetic and copies ran while one was open for 6% of the time, Pallas kernels for 23%

profile of v7, /device:TPU:0, one launch (start us, length us, event | category | flops | bytes accessed | tf_op | source)
XLA Modules:
  0.0 428.6 jit_solution(13547689174194002325)
XLA Ops:
  0.6 7.0 %shard_map.98 = (f32[8,4,128,128]{3,2,1,0:T(8,128)}, f32[8,4,128,128]{3,2,1,0:T(8,128)}) custom-call(f32[8,131072]{1,0:T(8,128)} %in_ref.3), custom_call_target="tpu_custom_call" | custom-call | bytes 8388608 | tf_op jit(solution)/shard_map/pallas_call | solution.py:411
  7.6 5.3 %all-to-all-start.1 = ((f32[8,4,128,128]{3,2,1,0:T(8,128)}), f32[8,4,128,128]{3,2,1,0:T(8,128)S(1)}, u32[]{:S(2)}, u32[]{:S(2)}) async-start(f32[8,4,128,128]{3,2,1,0:T(8,128)} %get-tuple-element.34), calls=%async_computation.1 | async-start | bytes 4194304 | tf_op jit(solution)/shard_map/all_to_all | solution.py:608
  13.1 3.5 constant_dynamic-slice_fusion.1
  16.6 0.9 constant_dynamic-slice_fusion
  17.6 0.1 pad_maximum_fusion.4
  17.6 3.7 collective-permute-start.2
  21.4 1.1 pad_maximum_fusion.3
  22.5 0.0 collective-permute-start.1
  22.6 1.0 pad_maximum_fusion.2
  23.6 0.8 collective-permute-start
  24.4 6.8 %shard_map.95 = f32[8,8,128,128]{3,2,1,0:T(8,128)} custom-call(f32[8,131072]{1,0:T(8,128)} %in_ref.2), custom_call_target="tpu_custom_call" | custom-call | bytes 8388608 | tf_op jit(solution)/shard_map/pallas_call | solution.py:411
  31.2 0.2 fusion.28.params_ref
  31.4 8.2 %all-to-all-done.1.phase_ref = f32[8,4,128,128]{3,2,1,0:T(8,128)S(1)} async-done(((f32[8,4,128,128]{3,2,1,0:T(8,128)}), f32[8,4,128,128]{3,2,1,0:T(8,128)S(1)}, u32[]{:S(2)}, u32[]{:S(2)}) %all-to-all-start.1) | async-done | bytes 2097184 | tf_op jit(solution)/shard_map/all_to_all | solution.py:608
  39.6 1.3 copy-done.1
  40.9 4.6 %all-to-all-start = ((f32[8,8,128,128]{3,2,1,0:T(8,128)}), f32[8,8,128,128]{3,2,1,0:T(8,128)}, u32[]{:S(2)}, u32[]{:S(2)}) async-start(f32[8,8,128,128]{3,2,1,0:T(8,128)} %shard_map.95), calls=%async_computation | async-start | bytes 8388608 | tf_op jit(solution)/shard_map/all_to_all | solution.py:608
  45.5 0.4 collective-permute-done.2
  45.9 1.3 slice_bitcast_fusion.6
  47.2 47.4 %all-to-all-done.phase_ref = f32[8,8,128,128]{3,2,1,0:T(8,128)} async-done(((f32[8,8,128,128]{3,2,1,0:T(8,128)}), f32[8,8,128,128]{3,2,1,0:T(8,128)}, u32[]{:S(2)}, u32[]{:S(2)}) %all-to-all-start) | async-done | bytes 4194336 | tf_op jit(solution)/shard_map/all_to_all | solution.py:608
  94.6 4.4 %all-to-all-start.2 = ((f32[8,4,128,128]{3,2,1,0:T(8,128)}), f32[8,4,128,128]{3,2,1,0:T(8,128)}, u32[]{:S(2)}, u32[]{:S(2)}) async-start(f32[8,4,128,128]{3,2,1,0:T(8,128)} %get-tuple-element.39), calls=%async_computation.2 | async-start | bytes 4194304 | tf_op jit(solution)/shard_map/all_to_all | solution.py:608
  99.0 13.5 %collective-permute-done.1 = f32[2,8,16512]{2,1,0:T(8,128)} collective-permute-done((f32[2,8,16512]{2,1,0:T(8,128)}, f32[2,8,16512]{2,1,0:T(8,128)}, u32[]{:S(2)}, u32[]{:S(2)}) %collective-permute-start.1) | collective-permute-done | bytes 1056800 | tf_op jit(solution)/shard_map/ppermute | solution.py:521
  112.5 2.3 slice_bitcast_fusion.7
  114.8 24.1 %shard_map.96 = (f32[8,2,1024,128]{3,2,1,0:T(8,128)}, f32[8,8,128,128]{3,2,1,0:T(8,128)}, f32[8,8,128,128]{3,2,1,0:T(8,128)}, f32[8,8,128,128]{3,2,1,0:T(8,128)}) custom-call(f32[3]{0:T(128)S(1)} %fusion.28.params_ref, f32[8,8,128,128]{3,2,1,0:T(8,128)} %all-to-all-done.phase_ref, bf16[2,4,512,512]{3,2,1,0:T(8,128)(2,1)} %constant.161.clone.refs_0_.refs_3_, ...), custom_call_target="tpu_custom_call" | custom-call | flops 6442450944 | bytes 33554432 | tf_op jit(solution)/shard_map/pallas_call | solution.py:459
  138.9 9.6 %shard_map.97 = f32[8,8,128,128]{3,2,1,0:T(8,128)} custom-call(f32[8,2,1024,128]{3,2,1,0:T(8,128)} %get-tuple-element.28.refs_0_, bf16[2,4,256,512]{3,2,1,0:T(8,128)(2,1)S(1)} %copy-done), custom_call_target="tpu_custom_call" | custom-call | flops 3221225472 | bytes 12582912 | tf_op jit(solution)/shard_map/pallas_call | solution.py:484
  148.5 12.7 %shard_map.99.refs_0_ = f32[4,2,1024,128]{3,2,1,0:T(8,128)} custom-call(f32[3]{0:T(128)S(1)} %fusion.28.params_ref, f32[8,4,128,128]{3,2,1,0:T(8,128)S(1)} %copy-done.2, f32[8,8,128,128]{3,2,1,0:T(8,128)} %get-tuple-element.36.refs_0_, f32[8,8,128,128]{3,2,1,0:T(8,128)} %get-tuple-element.37.refs_1_, f32[8,8,128,128]{3,2,1,0:T(8,128)} %get-tuple-element.38.refs_2_, ...), custom_call_target="tpu_custom_call" | custom-call | flops 3221225472 | bytes 16777216 | tf_op jit(solution)/shard_map/pallas_call | solution.py:459
  161.2 0.0 all-to-all-done.2.phase_ref
  161.2 13.0 %shard_map.100.refs_1_ = f32[4,2,1024,128]{3,2,1,0:T(8,128)} custom-call(f32[3]{0:T(128)S(1)} %fusion.28.params_ref, f32[8,4,128,128]{3,2,1,0:T(8,128)} %all-to-all-done.2.phase_ref, f32[8,8,128,128]{3,2,1,0:T(8,128)} %get-tuple-element.36.refs_0_, f32[8,8,128,128]{3,2,1,0:T(8,128)} %get-tuple-element.37.refs_1_, ...), custom_call_target="tpu_custom_call" | custom-call | flops 3221225472 | bytes 16777216 | tf_op jit(solution)/shard_map/pallas_call | solution.py:459
  174.3 9.3 %shard_map.101 = f32[8,8,128,128]{3,2,1,0:T(8,128)} custom-call(f32[4,2,1024,128]{3,2,1,0:T(8,128)} %shard_map.99.refs_0_, f32[4,2,1024,128]{3,2,1,0:T(8,128)} %shard_map.100.refs_1_, bf16[2,4,256,512]{3,2,1,0:T(8,128)(2,1)S(1)} %copy-done), custom_call_target="tpu_custom_call" | custom-call | flops 3221225472 | bytes 12582912 | tf_op jit(solution)/shard_map/pallas_call | solution.py:484
  183.6 4.6 %all-to-all-start.3 = ((f32[8,8,128,128]{3,2,1,0:T(8,128)}), f32[8,8,128,128]{3,2,1,0:T(8,128)}, u32[]{:S(2)}, u32[]{:S(2)}) async-start(f32[8,8,128,128]{3,2,1,0:T(8,128)} %shard_map.101), calls=%async_computation.3 | async-start | bytes 8388608 | tf_op jit(solution)/shard_map/all_to_all | solution.py:608
  188.2 0.0 collective-permute-done
  188.3 1.4 slice_bitcast_fusion.8
  189.7 0.0 copy-done.5
  189.7 0.2 copy-done.6
  189.9 0.2 copy-done.7
  190.0 1.8 pad_maximum_fusion
  191.8 45.5 %all-to-all-done.3.in_ref = f32[8,8,128,128]{3,2,1,0:T(8,128)} async-done(((f32[8,8,128,128]{3,2,1,0:T(8,128)}), f32[8,8,128,128]{3,2,1,0:T(8,128)}, u32[]{:S(2)}, u32[]{:S(2)}) %all-to-all-start.3) | async-done | bytes 4194336 | tf_op jit(solution)/shard_map/all_to_all | solution.py:608
  237.3 7.1 %shard_map.102 = (f32[2,8,131072]{2,1,0:T(8,128)}, f32[4,8,32768]{2,1,0:T(8,128)S(1)}) custom-call(f32[8,8,128,128]{3,2,1,0:T(8,128)} %all-to-all-done.3.in_ref), custom_call_target="tpu_custom_call" | custom-call | bytes 12582912 | tf_op jit(solution)/shard_map/pallas_call | solution.py:428
  244.4 1.9 copy-done.3
  246.3 47.7 %collective-permute-done.3.far_ref = f32[32,16512]{1,0:T(8,128)} collective-permute-done((f32[32,16512]{1,0:T(8,128)}, f32[32,16512]{1,0:T(8,128)}, u32[]{:S(2)}, u32[]{:S(2)}) %collective-permute-start.3) | collective-permute-done | bytes 2113568 | tf_op jit(solution)/shard_map/ppermute | solution.py:574
  294.1 4.6 %all-to-all-start.4 = ((f32[8,8,128,128]{3,2,1,0:T(8,128)}), f32[8,8,128,128]{3,2,1,0:T(8,128)}, u32[]{:S(2)}, u32[]{:S(2)}) async-start(f32[8,8,128,128]{3,2,1,0:T(8,128)} %shard_map.97), calls=%async_computation.4 | async-start | bytes 8388608 | tf_op jit(solution)/shard_map/all_to_all | solution.py:608
  298.7 4.0 dynamic-slice_bitcast_fusion
  302.6 0.0 collective-permute-start.4
  302.6 3.1 collective-permute-start.5
  305.7 1.3 collective-permute-start.6
  307.1 0.8 collective-permute-start.7
  307.9 0.1 pad_add_fusion.base_ref
  308.0 0.0 collective-permute-done.7.edge_ref
  308.0 15.4 %shard_map.104 = f32[2,32,16512]{2,1,0:T(8,128)} custom-call(s32[3]{0:T(128)S(1)} %pad_add_fusion.base_ref, f32[32,16512]{1,0:T(8,128)S(1)} %get-tuple-element.46.own_ref, f32[32,16512]{1,0:T(8,128)} %collective-permute-done.3.far_ref, f32[32,128]{1,0:T(8,128)S(1)} %collective-permute-done.7.edge_ref), custom_call_target="tpu_custom_call" | custom-call | flops 105676800 | bytes 8454144 | tf_op jit(solution)/shard_map/pallas_call | solution.py:501
  323.4 4.2 fusion.8
  327.6 4.2 fusion.10
  331.8 16.1 %all-to-all-done.4.in_ref = f32[8,8,128,128]{3,2,1,0:T(8,128)} async-done(((f32[8,8,128,128]{3,2,1,0:T(8,128)}), f32[8,8,128,128]{3,2,1,0:T(8,128)}, u32[]{:S(2)}, u32[]{:S(2)}) %all-to-all-start.4) | async-done | bytes 4194336 | tf_op jit(solution)/shard_map/all_to_all | solution.py:608
  348.0 6.9 %shard_map.103 = f32[2,8,131072]{2,1,0:T(8,128)} custom-call(f32[8,8,128,128]{3,2,1,0:T(8,128)} %all-to-all-done.4.in_ref, f32[2,8,131072]{2,1,0:T(8,128)} %get-tuple-element.45.refs_0_), custom_call_target="tpu_custom_call", output_to_operand_aliasing={{}: (1, {})} | custom-call | bytes 12582912 | tf_op jit(solution)/shard_map/pallas_call | solution.py:428
  354.8 0.0 collective-permute-done.4
  354.8 20.1 %collective-permute-done.5 = f32[8,32768]{1,0:T(8,128)} collective-permute-done((f32[8,32768]{1,0:T(8,128)}, f32[8,32768]{1,0:T(8,128)}, u32[]{:S(2)}, u32[]{:S(2)}) %collective-permute-start.5) | collective-permute-done | bytes 1048608 | tf_op jit(solution)/shard_map/ppermute | solution.py:521
  374.9 0.0 collective-permute-done.6
  374.9 4.6 %fusion.11 = f32[32,32]{1,0:T(8,128)S(1)} fusion(f32[8,32768]{1,0:T(8,128)} %collective-permute-done.6, f32[8,32768]{1,0:T(8,128)} %collective-permute-done.5, f32[8,32768]{1,0:T(8,128)} %collective-permute-done.4, f32[8,32768]{1,0:T(8,128)S(1)} %get-tuple-element.50), kind=kOutput, calls=%fused_computation.22 | convolution fusion | flops 204473344 | bytes 4198400 | tf_op jit(solution)/shard_map/dot_general | solution.py:525
  379.6 0.2 fusion.15
  379.8 0.2 fusion.32
  380.0 12.1 %all-gather = f32[256,32]{1,0:T(8,128)S(1)} all-gather(f32[32,32]{1,0:T(8,128)S(1)} %fusion.32), channel_id=2, replica_groups=mesh['len'=8,'mem'=4] {'len'}, dimensions={0}, use_global_device_ids=true | all-gather | bytes 36864 | tf_op jit(solution)/shard_map/all_gather | solution.py:598
  392.1 31.5 %all-gather.1 = f32[128,32]{1,0:T(8,128)S(1)} all-gather(f32[32,32]{1,0:T(8,128)S(1)} %reduce_sum.18), channel_id=3, replica_groups=mesh['len'=8,'mem'=4] {'mem'}, dimensions={0}, use_global_device_ids=true | all-gather | bytes 20480 | tf_op jit(solution)/shard_map/all_gather | solution.py:598
  423.6 0.1 copy.15
  423.7 2.9 cholesky.18
  426.6 0.6 compare_reduce_fusion
  427.3 0.6 select_bitcast_fusion
  427.9 0.7 copy.16
  (37 shorter events, 0.4 us)
Async XLA Ops:
  7.6 5.4 %copy-start.8 = (f32[8]{0:T(128)S(1)}, f32[8]{0:T(128)}, u32[]{:S(2)}) copy-start(f32[8]{0:T(128)} %param.11) | copy-start | bytes 100
  7.6 5.4 %copy-start.9 = (f32[8]{0:T(128)S(1)}, f32[8]{0:T(128)}, u32[]{:S(2)}) copy-start(f32[8]{0:T(128)} %param.10) | copy-start | bytes 100
  7.6 31.9 %all-to-all-start.1 = ((f32[8,4,128,128]{3,2,1,0:T(8,128)}), f32[8,4,128,128]{3,2,1,0:T(8,128)S(1)}, u32[]{:S(2)}, u32[]{:S(2)}) async-start(f32[8,4,128,128]{3,2,1,0:T(8,128)} %get-tuple-element.34), calls=%async_computation.1 | async-start | bytes 4194304 | tf_op jit(solution)/shard_map/all_to_all | solution.py:608
  17.6 28.2 %collective-permute-start.2 = (f32[2,8,16512]{2,1,0:T(8,128)S(1)}, f32[2,8,16512]{2,1,0:T(8,128)}, u32[]{:S(2)}, u32[]{:S(2)}) collective-permute-start(f32[2,8,16512]{2,1,0:T(8,128)S(1)} %pad_maximum_fusion.4), channel_id=1, source_target_pairs={{0,3},{1,2},{2,1},{3,0},{4,7},{5,6},{6,5},{7,4},{8,11},{9,10},{10,... | collective-permute-start | bytes 3170312 | tf_op jit(solution)/shard_map/ppermute | solution.py:521
  22.5 90.0 %collective-permute-start.1 = (f32[2,8,16512]{2,1,0:T(8,128)}, f32[2,8,16512]{2,1,0:T(8,128)}, u32[]{:S(2)}, u32[]{:S(2)}) collective-permute-start(f32[2,8,16512]{2,1,0:T(8,128)} %pad_maximum_fusion.3), channel_id=1, source_target_pairs={{0,2},{1,3},{2,0},{3,1},{4,6},{5,7},{6,4},{7,5},{8,10},{9,11},{10,... | collective-permute-start | bytes 3170312 | tf_op jit(solution)/shard_map/ppermute | solution.py:521
  23.6 7.6 %copy-start.10 = (f32[8]{0:T(128)S(1)}, f32[8]{0:T(128)}, u32[]{:S(2)}) copy-start(f32[8]{0:T(128)} %param.12) | copy-start | bytes 100
  23.6 164.6 %collective-permute-start = (f32[2,8,16512]{2,1,0:T(8,128)}, f32[2,8,16512]{2,1,0:T(8,128)}, u32[]{:S(2)}, u32[]{:S(2)}) collective-permute-start(f32[2,8,16512]{2,1,0:T(8,128)} %pad_maximum_fusion.2), channel_id=1, source_target_pairs={{0,1},{1,0},{2,3},{3,2},{4,5},{5,4},{6,7},{7,6},{8,9},{9,8},{10,11... | collective-permute-start | bytes 3170312 | tf_op jit(solution)/shard_map/ppermute | solution.py:521
  39.6 1.3 copy-start.1
  40.9 53.7 %all-to-all-start = ((f32[8,8,128,128]{3,2,1,0:T(8,128)}), f32[8,8,128,128]{3,2,1,0:T(8,128)}, u32[]{:S(2)}, u32[]{:S(2)}) async-start(f32[8,8,128,128]{3,2,1,0:T(8,128)} %shard_map.95), calls=%async_computation | async-start | bytes 8388608 | tf_op jit(solution)/shard_map/all_to_all | solution.py:608
  94.6 66.6 %all-to-all-start.2 = ((f32[8,4,128,128]{3,2,1,0:T(8,128)}), f32[8,4,128,128]{3,2,1,0:T(8,128)}, u32[]{:S(2)}, u32[]{:S(2)}) async-start(f32[8,4,128,128]{3,2,1,0:T(8,128)} %get-tuple-element.39), calls=%async_computation.2 | async-start | bytes 4194304 | tf_op jit(solution)/shard_map/all_to_all | solution.py:608
  114.8 24.1 %copy-start = (bf16[2,4,256,512]{3,2,1,0:T(8,128)(2,1)S(1)}, bf16[2,4,256,512]{3,2,1,0:T(8,128)(2,1)}, u32[]{:S(2)}) copy-start(bf16[2,4,256,512]{3,2,1,0:T(8,128)(2,1)} %constant.162.clone.refs_1_.refs_2_) | copy-start | bytes 6291460
  138.9 9.6 %copy-start.2 = (f32[8,4,128,128]{3,2,1,0:T(8,128)S(1)}, f32[8,4,128,128]{3,2,1,0:T(8,128)}, u32[]{:S(2)}) copy-start(f32[8,4,128,128]{3,2,1,0:T(8,128)} %copy-done.1) | copy-start | bytes 6291460
  183.6 53.7 %all-to-all-start.3 = ((f32[8,8,128,128]{3,2,1,0:T(8,128)}), f32[8,8,128,128]{3,2,1,0:T(8,128)}, u32[]{:S(2)}, u32[]{:S(2)}) async-start(f32[8,8,128,128]{3,2,1,0:T(8,128)} %shard_map.101), calls=%async_computation.3 | async-start | bytes 8388608 | tf_op jit(solution)/shard_map/all_to_all | solution.py:608
  188.2 1.5 copy-start.4
  188.2 1.5 copy-start.5
  188.2 1.7 copy-start.6
  188.2 1.8 copy-start.7
  244.4 2.0 copy-start.3
  246.3 47.7 %collective-permute-start.3 = (f32[32,16512]{1,0:T(8,128)}, f32[32,16512]{1,0:T(8,128)}, u32[]{:S(2)}, u32[]{:S(2)}) collective-permute-start(f32[32,16512]{1,0:T(8,128)} %get-tuple-element.42), channel_id=1, source_target_pairs={{0,28},{4,24},{8,20},{12,16},{16,12},{20,8},{24,4},{28,0},{1,29},{... | collective-permute-start | bytes 6340616 | tf_op jit(solution)/shard_map/ppermute | solution.py:574
  294.1 53.9 %all-to-all-start.4 = ((f32[8,8,128,128]{3,2,1,0:T(8,128)}), f32[8,8,128,128]{3,2,1,0:T(8,128)}, u32[]{:S(2)}, u32[]{:S(2)}) async-start(f32[8,8,128,128]{3,2,1,0:T(8,128)} %shard_map.97), calls=%async_computation.4 | async-start | bytes 8388608 | tf_op jit(solution)/shard_map/all_to_all | solution.py:608
  302.6 52.2 %collective-permute-start.4 = (f32[8,32768]{1,0:T(8,128)}, f32[8,32768]{1,0:T(8,128)}, u32[]{:S(2)}, u32[]{:S(2)}) collective-permute-start(f32[8,32768]{1,0:T(8,128)} %get-tuple-element.66), channel_id=1, source_target_pairs={{0,1},{1,0},{2,3},{3,2},{4,5},{5,4},{6,7},{7,6},{8,9},{9,8},{10,11... | collective-permute-start | bytes 3145736 | tf_op jit(solution)/shard_map/ppermute | solution.py:521
  302.6 72.3 %collective-permute-start.5 = (f32[8,32768]{1,0:T(8,128)}, f32[8,32768]{1,0:T(8,128)}, u32[]{:S(2)}, u32[]{:S(2)}) collective-permute-start(f32[8,32768]{1,0:T(8,128)} %get-tuple-element.65), channel_id=1, source_target_pairs={{0,2},{1,3},{2,0},{3,1},{4,6},{5,7},{6,4},{7,5},{8,10},{9,11},{10,... | collective-permute-start | bytes 3145736 | tf_op jit(solution)/shard_map/ppermute | solution.py:521
  305.7 69.3 %collective-permute-start.6 = (f32[8,32768]{1,0:T(8,128)}, f32[8,32768]{1,0:T(8,128)}, u32[]{:S(2)}, u32[]{:S(2)}) collective-permute-start(f32[8,32768]{1,0:T(8,128)} %get-tuple-element.64), channel_id=1, source_target_pairs={{0,3},{1,2},{2,1},{3,0},{4,7},{5,6},{6,5},{7,4},{8,11},{9,10},{10,... | collective-permute-start | bytes 3145736 | tf_op jit(solution)/shard_map/ppermute | solution.py:521
  307.1 0.9 collective-permute-start.7

commit v8 on v6

--- a/solution.py
+++ b/solution.py
@@ -16,6 +16,7 @@
 QUARTER = 256
 LANES = 128
 STEP = 16
+SUBLANES = 8
 WIDE = 256
 BLOCK_ROWS = 16
 OUTER_TILES = 2
@@ -338,23 +339,24 @@
 
 def part_kernel(in_ref, out_ref):
     members, tiles, rows, _ = out_ref.shape
-    flat_ref = out_ref.reshape(members * tiles * rows, LANES)
-    for r in range(rows):
-        for tile in range(tiles):
-            at = (r * tiles + tile) * LANES
-            flat_ref[pl.ds(tile * rows + r, members, stride=tiles * rows), :] = in_ref[:, at : at + LANES]
+    for tile in range(tiles):
+        for start in range(0, rows, SUBLANES):
+            columns = [((start + r) * tiles + tile) * LANES for r in range(SUBLANES)]
+            turned = jnp.transpose(jnp.stack([in_ref[:, at : at + LANES] for at in columns]), (1, 0, 2))
+            for m in range(members):
+                out_ref[m, tile, start : start + SUBLANES, :] = turned[m]
 
 
 def join_kernel(extra, in_ref, *refs):
     out_refs = refs[-2:] if extra else refs[-1:]
     members, tiles, rows, _ = in_ref.shape
-    flat_ref = in_ref.reshape(members * tiles * rows, LANES)
-    for r in range(rows):
-        for tile in range(tiles):
-            at = (r * tiles + tile) * LANES
-            value = flat_ref[pl.ds(tile * rows + r, members, stride=tiles * rows), :]
-            for out_ref in out_refs:
-                out_ref[0, :, at : at + LANES] = value
+    for tile in range(tiles):
+        for start in range(0, rows, SUBLANES):
+            turned = jnp.transpose(in_ref[:, tile, start : start + SUBLANES, :], (1, 0, 2))
+            for r in range(SUBLANES):
+                at = ((start + r) * tiles + tile) * LANES
+                for out_ref in out_refs:
+                    out_ref[0, :, at : at + LANES] = turned[r]
 
 
 def mirror_kernel(base_ref, own_ref, far_ref, edge_ref, out_ref):
@@ -459,7 +461,7 @@
         ],
         out_specs=[pl.BlockSpec((some, 2, OUTER, LANES), lambda g: (g, 0, 0, 0))] + [lines] * more,
         out_shape=[jax.ShapeDtypeStruct((tiles, 2, OUTER, LANES), jnp.float32)]
-        + [jax.ShapeDtypeStruct(phase.shape, jnp.float32)] * more,
+        + [pltpu.HBM(phase.shape, jnp.float32)] * more,
         scratch_shapes=[pltpu.VMEM((RADIX, 2 * QUARTER, some * LANES), jnp.bfloat16)] * 2,
         compiler_params=limits(),
         cost_estimate=pl.CostEstimate(
@@ -513,16 +515,17 @@
     return lax.ppermute(piece, "mem", [(z, z ^ slot) for z in range(groups)]) if slot else piece
 
 
-def rows_gram(rows):
-    return lax.dot_general(rows, rows, (((1,), (1,)), ((), ())), precision=highest)
+def rows_gram(rows, precision=highest):
+    return lax.dot_general(rows, rows, (((1,), (1,)), ((), ())), precision=precision)
 
 
 def slot_rows(stretches, groups):
     my_group = lax.axis_index("mem")
-    return [
+    rows = [
         to_group(lax.dynamic_index_in_dim(stretches, my_group ^ slot, 0, keepdims=False), slot)
-        for slot in range(groups)
+        for slot in reversed(range(groups))
     ]
+    return rows[::-1]
 
 
 def own_and_far(phase, params, my_group):
@@ -608,7 +611,8 @@
 
     left, right = part_call(phase_left), part_call(phase_right)
     right, my_group = lax.optimization_barrier((right, lax.axis_index("mem")))
-    left, right = swap(left), swap(right)
+    left, right = lax.optimization_barrier((swap(left), right))
+    right = swap(right)
     own, far = own_and_far(phase_left, all_params, my_group)
     mid, *kept = outer_call(params, left, (), outer_tables, twists)
     first = list(inner_call(mid, inner_tables, shards, 2))
@@ -617,17 +621,17 @@
     (mid,) = outer_call(params, right, kept, outer_tables, twists)
     (second,) = inner_call(mid, inner_tables, shards, 1)
     early, second = lax.optimization_barrier((early, second))
-    second = swap(second)
-    second, first[1], own, far = lax.optimization_barrier((second, first[1], own, far))
+    second, own, far = lax.optimization_barrier((swap(second), own, far))
     profile, points = join_call(second, 1, 0, local_len, groups, None)
+    rows = slot_rows(points, groups)
+    _, first[1], own, far = lax.optimization_barrier((points, first[1], own, far))
     late = swap(first[1])
     line_gram = lines_gram(own, across(far), edge_of(own))
     (profile,) = join_call(early, 0, 0, local_len, 0, profile)
     late, line_gram = lax.optimization_barrier((late, line_gram))
     (profile,) = join_call(late, 0, 1, local_len, 0, profile)
-    rows = slot_rows(points, groups)
     profile, line_gram, rows = lax.optimization_barrier((profile, line_gram, rows))
-    gram_matrix = 0.25 * line_gram + (0.5 / (OUTER * INNER)) * rows_gram(jnp.concatenate(rows, axis=0))
+    gram_matrix = 0.25 * line_gram + (0.5 / (OUTER * INNER)) * rows_gram(jnp.concatenate(rows, axis=0), lax.Precision.HIGH)
     return (profile, upper_of(summed(in_order(gram_matrix, members))))
 
 

time: 371 us -> 369 us (level)
  waiting for transfers between devices: 126 us -> 133 us
  blocking collectives: 42.2 us -> 37.8 us
    ppermute x1, waiting for transfers between devices: 33.7 us -> 41.7 us  [across(): lax.ppermute(far, 'len', [(d, shards - 1 - d) for d in range(shards)])]
    all_gather x2, blocking collectives: 42.2 us -> 37.8 us  [summed(): value = jnp.sum(lax.all_gather(value, axis), axis=0)]
  transfers between devices with their start and end apart: 13 -> 13, of which waited for: 6 -> 5; matrix products, arithmetic and copies ran while one was open for 6% -> 7% of each run, Pallas kernels for 27% -> 25%
where the time goes in v8:
time: 369 us; the launch traced here: 368 us
  waiting for transfers between devices  133 us (36%)
  Pallas kernels  106 us (29%)
  starting transfers between devices  49.6 us (13%)
  blocking collectives  37.8 us (10%)
  local copies, waits for them, and re-layouts  17.3 us (5%)
  matrix products  13.5 us (4%)
  other arithmetic  9.47 us (3%)
    all_to_all x5, waiting for transfers between devices, swap(): return lax.all_to_all(piece, 'len', split_axis=0, concat_axis=0, tiled=True)  90.8 us
    pallas_call x2, Pallas kernels, outer_call(): pl.pallas_call(functools.partial(outer_kernel, track), grid=(tiles // som...  44.8 us
    ppermute x1, waiting for transfers between devices, across(): lax.ppermute(far, 'len', [(d, shards - 1 - d) for d in range(shards)])  41.7 us
    all_gather x2, blocking collectives, summed(): value = jnp.sum(lax.all_gather(value, axis), axis=0)  37.8 us
    ppermute x6, starting transfers between devices, to_group(): lax.ppermute(piece, 'mem', [(z, z ^ slot) for z in range(groups)])  23.8 us
    all_to_all x5, starting transfers between devices, swap(): return lax.all_to_all(piece, 'len', split_axis=0, concat_axis=0, tiled=True)  22.3 us
    pallas_call x2, Pallas kernels, inner_call(): pl.pallas_call(inner_kernel, grid=(OUTER // WIDE,), in_specs=[pl.BlockSpe...  18.9 us
    pallas_call x1, Pallas kernels, mirror_call(): pl.pallas_call(mirror_kernel, in_specs=[pl.BlockSpec(memory_space=pltpu.S...  15.4 us
  transfers between devices with their start and end apart: 13, of which 5 were waited for; matrix products, arithmetic and copies ran while one was open for 7% of the time, Pallas kernels for 25%

profile of v8, /device:TPU:0, one launch (start us, length us, event | category | flops | bytes accessed | tf_op | source)
XLA Modules:
  0.0 368.0 jit_solution(13131864720872491225)
XLA Ops:
  0.6 6.8 %shard_map.95 = f32[8,8,128,128]{3,2,1,0:T(8,128)} custom-call(f32[8,131072]{1,0:T(8,128)} %in_ref.2), custom_call_target="tpu_custom_call" | custom-call | bytes 8388608 | tf_op jit(solution)/shard_map/pallas_call | solution.py:409
  7.5 5.2 %all-to-all-start = ((f32[8,8,128,128]{3,2,1,0:T(8,128)}), f32[8,8,128,128]{3,2,1,0:T(8,128)}, u32[]{:S(2)}, u32[]{:S(2)}) async-start(f32[8,8,128,128]{3,2,1,0:T(8,128)} %shard_map.95), calls=%async_computation | async-start | bytes 8388608 | tf_op jit(solution)/shard_map/all_to_all | solution.py:603
  12.6 0.0 copy-start.10
  12.7 7.0 %shard_map.96 = f32[8,8,128,128]{3,2,1,0:T(8,128)} custom-call(f32[8,131072]{1,0:T(8,128)} %in_ref.3), custom_call_target="tpu_custom_call" | custom-call | bytes 8388608 | tf_op jit(solution)/shard_map/pallas_call | solution.py:409
  19.9 3.5 constant_dynamic-slice_fusion.1
  23.3 0.9 constant_dynamic-slice_fusion
  24.3 0.1 pad_maximum_fusion.4
  24.3 4.5 %collective-permute-start.2 = (f32[2,8,16512]{2,1,0:T(8,128)S(1)}, f32[2,8,16512]{2,1,0:T(8,128)S(1)}, u32[]{:S(2)}, u32[]{:S(2)}) collective-permute-start(f32[2,8,16512]{2,1,0:T(8,128)S(1)} %pad_maximum_fusion.4), channel_id=1, source_target_pairs={{0,3},{1,2},{2,1},{3,0},{4,7},{5,6},{6,5},{7,4},{8,11},{9,10},{10,... | collective-permute-start | bytes 3170312 | tf_op jit(solution)/shard_map/ppermute | solution.py:515
  29.0 1.1 pad_maximum_fusion.3
  30.0 0.0 collective-permute-start.1
  30.1 1.0 pad_maximum_fusion.2
  31.2 0.6 collective-permute-start
  31.8 0.2 fusion.28.params_ref
  32.0 29.9 %all-to-all-done.phase_ref = f32[8,8,128,128]{3,2,1,0:T(8,128)} async-done(((f32[8,8,128,128]{3,2,1,0:T(8,128)}), f32[8,8,128,128]{3,2,1,0:T(8,128)}, u32[]{:S(2)}, u32[]{:S(2)}) %all-to-all-start) | async-done | bytes 4194336 | tf_op jit(solution)/shard_map/all_to_all | solution.py:603
  61.9 4.6 %all-to-all-start.1 = ((f32[8,8,128,128]{3,2,1,0:T(8,128)}), f32[8,8,128,128]{3,2,1,0:T(8,128)}, u32[]{:S(2)}, u32[]{:S(2)}) async-start(f32[8,8,128,128]{3,2,1,0:T(8,128)} %shard_map.96), calls=%async_computation.1 | async-start | bytes 8388608 | tf_op jit(solution)/shard_map/all_to_all | solution.py:603
  66.5 0.1 slice_bitcast_fusion.6
  66.6 0.0 copy-start.3
  66.6 24.1 %shard_map.97 = (f32[8,2,1024,128]{3,2,1,0:T(8,128)}, f32[8,8,128,128]{3,2,1,0:T(8,128)}, f32[8,8,128,128]{3,2,1,0:T(8,128)}, f32[8,8,128,128]{3,2,1,0:T(8,128)}) custom-call(f32[3]{0:T(128)S(1)} %fusion.28.params_ref, f32[8,8,128,128]{3,2,1,0:T(8,128)} %all-to-all-done.phase_ref, bf16[2,4,512,512]{3,2,1,0:T(8,128)(2,1)} %constant.161.clone.refs_0_.refs_3_, ...), custom_call_target="tpu_custom_call" | custom-call | flops 6442450944 | bytes 33554432 | tf_op jit(solution)/shard_map/pallas_call | solution.py:453
  90.7 9.5 %shard_map.98 = (f32[8,8,64,128]{3,2,1,0:T(8,128)}, f32[8,8,64,128]{3,2,1,0:T(8,128)}) custom-call(f32[8,2,1024,128]{3,2,1,0:T(8,128)} %get-tuple-element.36.mid_ref, bf16[2,4,256,512]{3,2,1,0:T(8,128)(2,1)S(1)} %copy-done.3), custom_call_target="tpu_custom_call" | custom-call | flops 3221225472 | bytes 12582912 | tf_op jit(solution)/shard_map/pallas_call | solution.py:476
  100.2 15.4 %all-to-all-done.1.phase_ref = f32[8,8,128,128]{3,2,1,0:T(8,128)} async-done(((f32[8,8,128,128]{3,2,1,0:T(8,128)}), f32[8,8,128,128]{3,2,1,0:T(8,128)}, u32[]{:S(2)}, u32[]{:S(2)}) %all-to-all-start.1) | async-done | bytes 4194336 | tf_op jit(solution)/shard_map/all_to_all | solution.py:603
  115.6 3.6 all-to-all-start.2
  119.2 0.7 collective-permute-done.1
  119.9 2.3 slice_bitcast_fusion.7
  122.2 20.7 %shard_map.99.mid_ref = f32[8,2,1024,128]{3,2,1,0:T(8,128)} custom-call(f32[3]{0:T(128)S(1)} %fusion.28.params_ref, f32[8,8,128,128]{3,2,1,0:T(8,128)} %all-to-all-done.1.phase_ref, f32[8,8,128,128]{3,2,1,0:T(8,128)} %get-tuple-element.41.refs_0_, f32[8,8,128,128]{3,2,1,0:T(8,128)} %get-tuple-element.42.refs_1_, ...), custom_call_target="tpu_custom_call" | custom-call | flops 6442450944 | bytes 33554432 | tf_op jit(solution)/shard_map/pallas_call | solution.py:453
  142.9 9.4 %shard_map.100 = f32[8,8,128,128]{3,2,1,0:T(8,128)} custom-call(f32[8,2,1024,128]{3,2,1,0:T(8,128)} %shard_map.99.mid_ref, bf16[2,4,256,512]{3,2,1,0:T(8,128)(2,1)S(1)} %copy-done.4), custom_call_target="tpu_custom_call" | custom-call | flops 3221225472 | bytes 12582912 | tf_op jit(solution)/shard_map/pallas_call | solution.py:476
  152.3 0.0 all-to-all-done.2.in_ref
  152.3 1.4 copy-done
  153.7 4.6 %all-to-all-start.3 = ((f32[8,8,128,128]{3,2,1,0:T(8,128)}), f32[8,8,128,128]{3,2,1,0:T(8,128)}, u32[]{:S(2)}, u32[]{:S(2)}) async-start(f32[8,8,128,128]{3,2,1,0:T(8,128)} %shard_map.100), calls=%async_computation.3 | async-start | bytes 8388608 | tf_op jit(solution)/shard_map/all_to_all | solution.py:603
  158.3 1.4 slice_bitcast_fusion.8
  159.7 0.0 copy-done.6
  159.8 0.2 copy-done.7
  159.9 0.2 copy-done.8
  160.1 1.8 pad_maximum_fusion
  161.9 45.5 %all-to-all-done.3.in_ref = f32[8,8,128,128]{3,2,1,0:T(8,128)} async-done(((f32[8,8,128,128]{3,2,1,0:T(8,128)}), f32[8,8,128,128]{3,2,1,0:T(8,128)}, u32[]{:S(2)}, u32[]{:S(2)}) %all-to-all-start.3) | async-done | bytes 4194336 | tf_op jit(solution)/shard_map/all_to_all | solution.py:603
  207.4 7.1 %shard_map.101 = (f32[2,8,131072]{2,1,0:T(8,128)}, f32[4,8,32768]{2,1,0:T(8,128)S(1)}) custom-call(f32[8,8,128,128]{3,2,1,0:T(8,128)} %all-to-all-done.3.in_ref), custom_call_target="tpu_custom_call" | custom-call | bytes 12582912 | tf_op jit(solution)/shard_map/pallas_call | solution.py:426
  214.4 2.0 copy-done.2
  216.4 4.4 %all-to-all-start.4 = ((f32[8,8,64,128]{3,2,1,0:T(8,128)}), f32[8,8,64,128]{3,2,1,0:T(8,128)}, u32[]{:S(2)}, u32[]{:S(2)}) async-start(f32[8,8,64,128]{3,2,1,0:T(8,128)} %get-tuple-element.51), calls=%async_computation.4 | async-start | bytes 4194304 | tf_op jit(solution)/shard_map/all_to_all | solution.py:603
  220.8 2.6 collective-permute-start.3
  223.3 3.9 %dynamic-slice_bitcast_fusion = (f32[8,32768]{1,0:T(8,128)}, f32[8,32768]{1,0:T(8,128)}, f32[8,32768]{1,0:T(8,128)}, f32[8,32768]{1,0:T(8,128)S(1)}) fusion(f32[4,8,32768]{2,1,0:T(8,128)} %copy-done.2, s32[]{:T(128)S(6)} %select_n.141, s32[]{:T(128)S(6)} %select_n.140, s32[]{:T(128)S(6)} %select_n.139, s32[]{:T(128)S(6)} %select_n.138), kind=kLoop, calls=%fused_computation.18 | loop fusion | bytes 8388624 | tf_op jit(solution)/shard_map/jit(dynamic_index_in_dim)/squeeze | solution.py:525
  227.2 16.2 %collective-permute-start.5 = (f32[8,32768]{1,0:T(8,128)}, f32[8,32768]{1,0:T(8,128)}, u32[]{:S(2)}, u32[]{:S(2)}) collective-permute-start(f32[8,32768]{1,0:T(8,128)} %get-tuple-element.76), channel_id=1, source_target_pairs={{0,1},{1,0},{2,3},{3,2},{4,5},{5,4},{6,7},{7,6},{8,9},{9,8},{10,11... | collective-permute-start | bytes 3145736 | tf_op jit(solution)/shard_map/ppermute | solution.py:515
  243.4 1.0 collective-permute-start.6
  244.5 1.5 collective-permute-start.7
  246.0 0.8 collective-permute-start.4
  246.8 0.1 pad_add_fusion.base_ref
  246.9 1.6 copy-done.1
  248.5 2.1 shard_map.103.refs_0_
  250.6 0.0 collective-permute-done.4.edge_ref
  250.6 41.7 %collective-permute-done.3.far_ref = f32[32,16512]{1,0:T(8,128)} collective-permute-done((f32[32,16512]{1,0:T(8,128)}, f32[32,16512]{1,0:T(8,128)}, u32[]{:S(2)}, u32[]{:S(2)}) %collective-permute-start.3) | collective-permute-done | bytes 2113568 | tf_op jit(solution)/shard_map/ppermute | solution.py:569
  292.2 15.4 %shard_map.102 = f32[2,32,16512]{2,1,0:T(8,128)} custom-call(s32[3]{0:T(128)S(1)} %pad_add_fusion.base_ref, f32[32,16512]{1,0:T(8,128)S(1)} %get-tuple-element.52.own_ref, f32[32,16512]{1,0:T(8,128)} %collective-permute-done.3.far_ref, f32[32,128]{1,0:T(8,128)S(1)} %collective-permute-done.4.edge_ref), custom_call_target="tpu_custom_call" | custom-call | flops 105676800 | bytes 8454144 | tf_op jit(solution)/shard_map/pallas_call | solution.py:495
  307.6 4.2 %fusion.8 = f32[32,32]{1,0:T(8,128)S(1)} fusion(f32[2,32,16512]{2,1,0:T(8,128)} %shard_map.102), kind=kOutput, calls=%fused_computation.9 | convolution fusion | flops 202899456 | bytes 2117632 | tf_op jit(solution)/shard_map/dot_general | solution.py:519
  311.8 4.2 %fusion.10 = f32[32,32]{1,0:T(8,128)S(1)} fusion(f32[32,32]{1,0:T(8,128)S(1)} %fusion.8, f32[2,32,16512]{2,1,0:T(8,128)} %shard_map.102), kind=kOutput, calls=%fused_computation.14 | convolution fusion | flops 202900480 | bytes 2121728 | tf_op jit(solution)/shard_map/dot_general | solution.py:519
  316.1 4.0 %shard_map.104 = f32[2,8,131072]{2,1,0:T(8,128)} custom-call(f32[8,8,64,128]{3,2,1,0:T(8,128)} %all-to-all-done.4.in_ref, f32[2,8,131072]{2,1,0:T(8,128)} %shard_map.103.refs_0_), custom_call_target="tpu_custom_call", output_to_operand_aliasing={{}: (1, {})} | custom-call | bytes 6291456 | tf_op jit(solution)/shard_map/pallas_call | solution.py:426
  320.0 0.0 collective-permute-done.5
  320.0 0.0 collective-permute-done.6
  320.1 4.6 %fusion.11 = f32[32,32]{1,0:T(8,128)S(1)} fusion(f32[8,32768]{1,0:T(8,128)} %collective-permute-done.7, f32[8,32768]{1,0:T(8,128)} %collective-permute-done.6, f32[8,32768]{1,0:T(8,128)} %collective-permute-done.5, f32[8,32768]{1,0:T(8,128)S(1)} %get-tuple-element.60), kind=kOutput, calls=%fused_computation.22 | convolution fusion | flops 204473344 | bytes 4198400 | tf_op jit(solution)/shard_map/dot_general | solution.py:519
  324.7 0.2 fusion.15
  324.9 0.2 fusion.32
  325.1 9.0 %all-gather = f32[256,32]{1,0:T(8,128)S(1)} all-gather(f32[32,32]{1,0:T(8,128)S(1)} %fusion.32), channel_id=2, replica_groups=mesh['len'=8,'mem'=4] {'len'}, dimensions={0}, use_global_device_ids=true | all-gather | bytes 36864 | tf_op jit(solution)/shard_map/all_gather | solution.py:593
  334.2 28.8 %all-gather.1 = f32[128,32]{1,0:T(8,128)S(1)} all-gather(f32[32,32]{1,0:T(8,128)S(1)} %reduce_sum.18), channel_id=3, replica_groups=mesh['len'=8,'mem'=4] {'mem'}, dimensions={0}, use_global_device_ids=true | all-gather | bytes 20480 | tf_op jit(solution)/shard_map/all_gather | solution.py:593
  362.9 0.1 copy.16
  363.0 2.9 cholesky.18
  366.0 0.6 compare_reduce_fusion
  366.6 0.6 select_bitcast_fusion
  367.3 0.7 copy.17
  (39 shorter events, 0.4 us)
Async XLA Ops:
  7.5 54.4 %all-to-all-start = ((f32[8,8,128,128]{3,2,1,0:T(8,128)}), f32[8,8,128,128]{3,2,1,0:T(8,128)}, u32[]{:S(2)}, u32[]{:S(2)}) async-start(f32[8,8,128,128]{3,2,1,0:T(8,128)} %shard_map.95), calls=%async_computation | async-start | bytes 8388608 | tf_op jit(solution)/shard_map/all_to_all | solution.py:603
  12.6 7.1 %copy-start.9 = (f32[8]{0:T(128)S(1)}, f32[8]{0:T(128)}, u32[]{:S(2)}) copy-start(f32[8]{0:T(128)} %param.11) | copy-start | bytes 100
  12.6 7.1 %copy-start.10 = (f32[8]{0:T(128)S(1)}, f32[8]{0:T(128)}, u32[]{:S(2)}) copy-start(f32[8]{0:T(128)} %param.10) | copy-start | bytes 100
  24.3 42.1 %collective-permute-start.2 = (f32[2,8,16512]{2,1,0:T(8,128)S(1)}, f32[2,8,16512]{2,1,0:T(8,128)S(1)}, u32[]{:S(2)}, u32[]{:S(2)}) collective-permute-start(f32[2,8,16512]{2,1,0:T(8,128)S(1)} %pad_maximum_fusion.4), channel_id=1, source_target_pairs={{0,3},{1,2},{2,1},{3,0},{4,7},{5,6},{6,5},{7,4},{8,11},{9,10},{10,... | collective-permute-start | bytes 3170312 | tf_op jit(solution)/shard_map/ppermute | solution.py:515
  30.0 89.9 %collective-permute-start.1 = (f32[2,8,16512]{2,1,0:T(8,128)}, f32[2,8,16512]{2,1,0:T(8,128)}, u32[]{:S(2)}, u32[]{:S(2)}) collective-permute-start(f32[2,8,16512]{2,1,0:T(8,128)} %pad_maximum_fusion.3), channel_id=1, source_target_pairs={{0,2},{1,3},{2,0},{3,1},{4,6},{5,7},{6,4},{7,5},{8,10},{9,11},{10,... | collective-permute-start | bytes 3170312 | tf_op jit(solution)/shard_map/ppermute | solution.py:515
  30.0 1.7 copy-start.11
  31.2 127.1 %collective-permute-start = (f32[2,8,16512]{2,1,0:T(8,128)}, f32[2,8,16512]{2,1,0:T(8,128)}, u32[]{:S(2)}, u32[]{:S(2)}) collective-permute-start(f32[2,8,16512]{2,1,0:T(8,128)} %pad_maximum_fusion.2), channel_id=1, source_target_pairs={{0,1},{1,0},{2,3},{3,2},{4,5},{5,4},{6,7},{7,6},{8,9},{9,8},{10,11... | collective-permute-start | bytes 3170312 | tf_op jit(solution)/shard_map/ppermute | solution.py:515
  61.9 53.8 %all-to-all-start.1 = ((f32[8,8,128,128]{3,2,1,0:T(8,128)}), f32[8,8,128,128]{3,2,1,0:T(8,128)}, u32[]{:S(2)}, u32[]{:S(2)}) async-start(f32[8,8,128,128]{3,2,1,0:T(8,128)} %shard_map.96), calls=%async_computation.1 | async-start | bytes 8388608 | tf_op jit(solution)/shard_map/all_to_all | solution.py:603
  66.6 24.1 %copy-start.3 = (bf16[2,4,256,512]{3,2,1,0:T(8,128)(2,1)S(1)}, bf16[2,4,256,512]{3,2,1,0:T(8,128)(2,1)}, u32[]{:S(2)}) copy-start(bf16[2,4,256,512]{3,2,1,0:T(8,128)(2,1)} %constant.162.clone.matrix_ref) | copy-start | bytes 6291460
  115.6 36.7 %all-to-all-start.2 = ((f32[8,8,64,128]{3,2,1,0:T(8,128)}), f32[8,8,64,128]{3,2,1,0:T(8,128)S(1)}, u32[]{:S(2)}, u32[]{:S(2)}) async-start(f32[8,8,64,128]{3,2,1,0:T(8,128)} %get-tuple-element.39), calls=%async_computation.2 | async-start | bytes 4194304 | tf_op jit(solution)/shard_map/all_to_all | solution.py:603
  122.2 20.7 %copy-start.4 = (bf16[2,4,256,512]{3,2,1,0:T(8,128)(2,1)S(1)}, bf16[2,4,256,512]{3,2,1,0:T(8,128)(2,1)}, u32[]{:S(2)}) copy-start(bf16[2,4,256,512]{3,2,1,0:T(8,128)(2,1)} %constant.162.clone.matrix_ref) | copy-start | bytes 6291460
  152.3 1.4 copy-start
  153.7 53.7 %all-to-all-start.3 = ((f32[8,8,128,128]{3,2,1,0:T(8,128)}), f32[8,8,128,128]{3,2,1,0:T(8,128)}, u32[]{:S(2)}, u32[]{:S(2)}) async-start(f32[8,8,128,128]{3,2,1,0:T(8,128)} %shard_map.100), calls=%async_computation.3 | async-start | bytes 8388608 | tf_op jit(solution)/shard_map/all_to_all | solution.py:603
  158.2 1.5 copy-start.5
  158.3 1.5 copy-start.6
  158.3 1.7 copy-start.7
  158.3 1.8 copy-start.8
  214.4 2.0 copy-start.2
  216.4 99.7 %all-to-all-start.4 = ((f32[8,8,64,128]{3,2,1,0:T(8,128)}), f32[8,8,64,128]{3,2,1,0:T(8,128)}, u32[]{:S(2)}, u32[]{:S(2)}) async-start(f32[8,8,64,128]{3,2,1,0:T(8,128)} %get-tuple-element.51), calls=%async_computation.4 | async-start | bytes 4194304 | tf_op jit(solution)/shard_map/all_to_all | solution.py:603
  220.8 71.5 %collective-permute-start.3 = (f32[32,16512]{1,0:T(8,128)}, f32[32,16512]{1,0:T(8,128)}, u32[]{:S(2)}, u32[]{:S(2)}) collective-permute-start(f32[32,16512]{1,0:T(8,128)} %get-tuple-element.53), channel_id=1, source_target_pairs={{0,28},{4,24},{8,20},{12,16},{16,12},{20,8},{24,4},{28,0},{1,29},{... | collective-permute-start | bytes 6340616 | tf_op jit(solution)/shard_map/ppermute | solution.py:569
  227.2 92.8 %collective-permute-start.5 = (f32[8,32768]{1,0:T(8,128)}, f32[8,32768]{1,0:T(8,128)}, u32[]{:S(2)}, u32[]{:S(2)}) collective-permute-start(f32[8,32768]{1,0:T(8,128)} %get-tuple-element.76), channel_id=1, source_target_pairs={{0,1},{1,0},{2,3},{3,2},{4,5},{5,4},{6,7},{7,6},{8,9},{9,8},{10,11... | collective-permute-start | bytes 3145736 | tf_op jit(solution)/shard_map/ppermute | solution.py:515
  243.4 76.6 %collective-permute-start.6 = (f32[8,32768]{1,0:T(8,128)}, f32[8,32768]{1,0:T(8,128)}, u32[]{:S(2)}, u32[]{:S(2)}) collective-permute-start(f32[8,32768]{1,0:T(8,128)} %get-tuple-element.75), channel_id=1, source_target_pairs={{0,2},{1,3},{2,0},{3,1},{4,6},{5,7},{6,4},{7,5},{8,10},{9,11},{10,... | collective-permute-start | bytes 3145736 | tf_op jit(solution)/shard_map/ppermute | solution.py:515
  244.5 75.6 %collective-permute-start.7 = (f32[8,32768]{1,0:T(8,128)}, f32[8,32768]{1,0:T(8,128)}, u32[]{:S(2)}, u32[]{:S(2)}) collective-permute-start(f32[8,32768]{1,0:T(8,128)} %get-tuple-element.74), channel_id=1, source_target_pairs={{0,3},{1,2},{2,1},{3,0},{4,7},{5,6},{6,5},{7,4},{8,11},{9,10},{10,... | collective-permute-start | bytes 3145736 | tf_op jit(solution)/shard_map/ppermute | solution.py:515
  246.0 4.6 %collective-permute-start.4 = (f32[32,128]{1,0:T(8,128)S(1)}, f32[32,128]{1,0:T(8,128)S(1)}, u32[]{:S(2)}, u32[]{:S(2)}) collective-permute-start(f32[32,128]{1,0:T(8,128)S(1)} %slice.39), channel_id=1, source_target_pairs={{0,0},{4,28},{8,24},{12,20},{16,16},{20,12},{24,8},{28,4},{1,1},{5... | collective-permute-start | bytes 49160 | tf_op jit(solution)/shard_map/ppermute | solution.py:564
  246.9 1.6 copy-start.1

commit v9 on v8

--- a/solution.py
+++ b/solution.py
@@ -359,16 +359,33 @@
                     out_ref[0, :, at : at + LANES] = turned[r]
 
 
-def mirror_kernel(base_ref, own_ref, far_ref, edge_ref, out_ref):
+def near_kernel(base_ref, own_ref, out_ref):
     members, length = own_ref.shape
+    tiles = length // LANES - 1
+    scale, exponent = tile_params(own_ref[:, tiles * LANES :])
+    lane = lax.broadcasted_iota(jnp.int32, (members, LANES), 1)
+
+    def one_tile(tile, carry):
+        at = pl.ds(pl.multiple_of(tile * LANES, LANES), LANES)
+        freq = (base_ref[0] + tile * LANES + lane).astype(jnp.float32)
+        out_ref[0, :, at], out_ref[1, :, at] = left_lines(own_ref[:, at], freq, scale, exponent)
+        return carry
+
+    lax.fori_loop(0, tiles + 1, one_tile, 0)
+
+
+def tile_params(beyond):
+    return (jnp.broadcast_to(beyond[:, n : n + 1], beyond.shape) for n in (1, 2))
+
+
+def mirror_kernel(base_ref, near_ref, far_ref, edge_ref, beyond_ref, out_ref):
+    members, length = far_ref.shape
     tiles = length // LANES - 1
     shape = (members, LANES)
     lane = lax.broadcasted_iota(jnp.int32, shape, 1)
     mirror = (LANES - lane) % LANES
     first_group, last_group = base_ref[1] == 0, base_ref[1] == base_ref[2] - 1
-    beyond = own_ref[:, tiles * LANES :]
-    scale = jnp.broadcast_to(beyond[:, 1:2], shape)
-    exponent = jnp.broadcast_to(beyond[:, 2:3], shape)
+    scale, exponent = tile_params(beyond_ref[...])
     half_root = math.sqrt(0.5)
 
     def tile_of(ref, tile):
@@ -377,25 +394,24 @@
     def turned(value):
         return jnp.take_along_axis(value, mirror, axis=1, mode="promise_in_bounds")
 
-    def store(tile, own, far, weight):
+    def store(tile, far, keep, weight):
         offset = base_ref[0] + tile * LANES + lane
-        near = left_lines(own, offset.astype(jnp.float32), scale, exponent)
         far_offset = jnp.where(offset == 0, 0, OUTER * INNER - offset)
         back = left_lines(far, far_offset.astype(jnp.float32), scale, exponent)
         at = pl.ds(pl.multiple_of(tile * LANES, LANES), LANES)
-        out_ref[0, :, at] = (near[0] + back[0]) * weight
-        out_ref[1, :, at] = (near[1] - back[1]) * weight
+        real, imag = near_ref[0, :, at] + back[0], near_ref[1, :, at] - back[1]
+        out_ref[0, :, at] = jnp.where(keep, real * weight, 0.0)
+        out_ref[1, :, at] = jnp.where(keep, imag * weight, 0.0)
 
     def one_tile(tile, last):
         ahead = turned(tile_of(far_ref, tiles - 1 - tile))
         is_edge = (lane == 0) & (tile == 0) & first_group
-        store(tile, tile_of(own_ref, tile), jnp.where(lane == 0, last, ahead), jnp.where(is_edge, half_root, 1.0))
+        store(tile, jnp.where(lane == 0, last, ahead), lane >= 0, jnp.where(is_edge, half_root, 1.0))
         return ahead
 
     start = jnp.where(first_group, turned(edge_ref[...]), turned(tile_of(far_ref, tiles)))
     last = lax.fori_loop(0, tiles, one_tile, start)
-    lone = (lane == 0) & last_group
-    store(tiles, jnp.where(lone, beyond, 0.0), jnp.where(lone, last, 0.0), jnp.where(lone, half_root, 0.0))
+    store(tiles, jnp.where(lane == 0, last, 0.0), (lane == 0) & last_group, half_root)
 
 
 def limits():
@@ -436,7 +452,7 @@
         ][: 2 if groups else 1],
         out_shape=[
             jax.ShapeDtypeStruct((2, members, length), jnp.float32),
-            jax.ShapeDtypeStruct((max(groups, 1), members, stretch // max(groups, 1)), jnp.float32),
+            pltpu.HBM((max(groups, 1), members, stretch // max(groups, 1)), jnp.float32),
         ][: 2 if groups else 1],
         input_output_aliases={} if so_far is None else {1: 0},
         compiler_params=limits(),
@@ -490,18 +506,32 @@
     )(mid, matrices)
 
 
-def mirror_call(base, own, far, edge):
+def near_call(base, own):
     members, length = own.shape
     return pl.pallas_call(
-        mirror_kernel,
-        in_specs=[pl.BlockSpec(memory_space=pltpu.SMEM)] + [pl.BlockSpec(memory_space=pltpu.VMEM)] * 3,
+        near_kernel,
+        in_specs=[pl.BlockSpec(memory_space=pltpu.SMEM), pl.BlockSpec(memory_space=pltpu.VMEM)],
         out_specs=pl.BlockSpec(memory_space=pltpu.VMEM),
         out_shape=jax.ShapeDtypeStruct((2, members, length), jnp.float32),
         compiler_params=limits(),
         cost_estimate=pl.CostEstimate(
-            flops=200 * members * length, bytes_accessed=16 * members * length, transcendentals=0
+            flops=100 * members * length, bytes_accessed=12 * members * length, transcendentals=0
         ),
-    )(base, own, far, edge)
+    )(base, own)
+
+
+def mirror_call(base, near, far, edge, beyond):
+    members, length = far.shape
+    return pl.pallas_call(
+        mirror_kernel,
+        in_specs=[pl.BlockSpec(memory_space=pltpu.SMEM)] + [pl.BlockSpec(memory_space=pltpu.VMEM)] * 4,
+        out_specs=pl.BlockSpec(memory_space=pltpu.VMEM),
+        out_shape=jax.ShapeDtypeStruct((2, members, length), jnp.float32),
+        compiler_params=limits(),
+        cost_estimate=pl.CostEstimate(
+            flops=100 * members * length, bytes_accessed=20 * members * length, transcendentals=0
+        ),
+    )(base, near, far, edge, beyond)
 
 
 def line_params(roughness, waviness, coherence):
@@ -515,17 +545,13 @@
     return lax.ppermute(piece, "mem", [(z, z ^ slot) for z in range(groups)]) if slot else piece
 
 
-def rows_gram(rows, precision=highest):
-    return lax.dot_general(rows, rows, (((1,), (1,)), ((), ())), precision=precision)
-
-
-def slot_rows(stretches, groups):
+def rows_gram(rows):
+    return lax.dot_general(rows, rows, (((1,), (1,)), ((), ())), precision=lax.Precision.HIGH)
+
+
+def by_slot(stretches, groups):
     my_group = lax.axis_index("mem")
-    rows = [
-        to_group(lax.dynamic_index_in_dim(stretches, my_group ^ slot, 0, keepdims=False), slot)
-        for slot in reversed(range(groups))
-    ]
-    return rows[::-1]
+    return [lax.dynamic_index_in_dim(stretches, my_group ^ slot, 0, keepdims=False) for slot in range(groups)]
 
 
 def own_and_far(phase, params, my_group):
@@ -569,13 +595,15 @@
     return lax.ppermute(far, "len", [(d, shards - 1 - d) for d in range(shards)])
 
 
-def lines_gram(own, far, edge):
+def line_base(width):
     groups = lax.axis_size("mem")
     my_index, my_group = lax.axis_index("len"), lax.axis_index("mem")
-    width = own.shape[1] - LANES
     base = (my_index * (2 * groups) + my_group) * width
-    base = jnp.stack([base, my_group, jnp.full_like(my_group, groups)]).astype(jnp.int32)
-    sums = mirror_call(base, own, far, edge)
+    return jnp.stack([base, my_group, jnp.full_like(my_group, groups)]).astype(jnp.int32)
+
+
+def lines_gram(base, near, far, edge, beyond):
+    sums = mirror_call(base, near, far, edge, beyond)
     return rows_gram(sums[0]) + rows_gram(sums[1])
 
 
@@ -621,17 +649,20 @@
     (mid,) = outer_call(params, right, kept, outer_tables, twists)
     (second,) = inner_call(mid, inner_tables, shards, 1)
     early, second = lax.optimization_barrier((early, second))
-    second, own, far = lax.optimization_barrier((swap(second), own, far))
+    base = line_base(own.shape[1] - LANES)
+    near = near_call(base, own)
+    second, near, far = lax.optimization_barrier((swap(second), near, far))
     profile, points = join_call(second, 1, 0, local_len, groups, None)
-    rows = slot_rows(points, groups)
-    _, first[1], own, far = lax.optimization_barrier((points, first[1], own, far))
+    pieces = by_slot(points, groups)
+    rows = [to_group(piece, slot) for slot, piece in enumerate(pieces)]
+    _, first[1], edge, far = lax.optimization_barrier((pieces, first[1], own, far))
     late = swap(first[1])
-    line_gram = lines_gram(own, across(far), edge_of(own))
+    line_gram = lines_gram(base, near, across(far), edge_of(edge), own[:, -LANES:])
     (profile,) = join_call(early, 0, 0, local_len, 0, profile)
     late, line_gram = lax.optimization_barrier((late, line_gram))
     (profile,) = join_call(late, 0, 1, local_len, 0, profile)
     profile, line_gram, rows = lax.optimization_barrier((profile, line_gram, rows))
-    gram_matrix = 0.25 * line_gram + (0.5 / (OUTER * INNER)) * rows_gram(jnp.concatenate(rows, axis=0), lax.Precision.HIGH)
+    gram_matrix = 0.25 * line_gram + (0.5 / (OUTER * INNER)) * rows_gram(jnp.concatenate(rows, axis=0))
     return (profile, upper_of(summed(in_order(gram_matrix, members))))
 
 

time: 369 us -> 367 us (level)
  waiting for transfers between devices: 133 us -> 124 us
  Pallas kernels: 106 us -> 114 us
  blocking collectives: 37.8 us -> 43.4 us
    ppermute x1, waiting for transfers between devices: 41.7 us -> 22 us  [across(): lax.ppermute(far, 'len', [(d, shards - 1 - d) for d in range(shards)])]
    ppermute x6, waiting for transfers between devices: 0.72 us -> 16.8 us  [to_group(): lax.ppermute(piece, 'mem', [(z, z ^ slot) for z in range(groups)])]
    all_to_all x5, waiting for transfers between devices: 90.8 us -> 85 us  [swap(): return lax.all_to_all(piece, 'len', split_axis=0, concat_axis=0, tiled=True)]
    pallas_call x0 -> x1, Pallas kernels: none -> 5.78 us  [near_call(): pl.pallas_call(near_kernel, in_specs=[pl.BlockSpec(memory_space=pltpu.SME...]
    all_gather x2, blocking collectives: 37.8 us -> 43.4 us  [summed(): value = jnp.sum(lax.all_gather(value, axis), axis=0)]
  transfers between devices with their start and end apart: 13 -> 13, of which waited for: 5 -> 6; matrix products, arithmetic and copies ran while one was open for 7% -> 5% of each run, Pallas kernels for 25% -> 27%
where the time goes in v9:
time: 367 us; the launch traced here: 365 us
  waiting for transfers between devices  124 us (34%)
  Pallas kernels  114 us (31%)
  starting transfers between devices  46.9 us (13%)
  blocking collectives  43.4 us (12%)
  local copies, waits for them, and re-layouts  15.5 us (4%)
  matrix products  11.6 us (3%)
  other arithmetic  9.49 us (3%)
    all_to_all x5, waiting for transfers between devices, swap(): return lax.all_to_all(piece, 'len', split_axis=0, concat_axis=0, tiled=True)  85 us
    pallas_call x2, Pallas kernels, outer_call(): pl.pallas_call(functools.partial(outer_kernel, track), grid=(tiles // som...  44.8 us
    all_gather x2, blocking collectives, summed(): value = jnp.sum(lax.all_gather(value, axis), axis=0)  43.4 us
    ppermute x6, starting transfers between devices, to_group(): lax.ppermute(piece, 'mem', [(z, z ^ slot) for z in range(groups)])  23.8 us
    all_to_all x5, starting transfers between devices, swap(): return lax.all_to_all(piece, 'len', split_axis=0, concat_axis=0, tiled=True)  22.2 us
    ppermute x1, waiting for transfers between devices, across(): lax.ppermute(far, 'len', [(d, shards - 1 - d) for d in range(shards)])  22 us
    pallas_call x2, Pallas kernels, inner_call(): pl.pallas_call(inner_kernel, grid=(OUTER // WIDE,), in_specs=[pl.BlockSpe...  18.9 us
    ppermute x6, waiting for transfers between devices, to_group(): lax.ppermute(piece, 'mem', [(z, z ^ slot) for z in range(groups)])  16.8 us
  transfers between devices with their start and end apart: 13, of which 6 were waited for; matrix products, arithmetic and copies ran while one was open for 5% of the time, Pallas kernels for 27%

profile of v9, /device:TPU:0, one launch (start us, length us, event | category | flops | bytes accessed | tf_op | source)
XLA Modules:
  0.0 365.4 jit_solution(2049897138640106653)
XLA Ops:
  0.6 6.8 %shard_map.95 = f32[8,8,128,128]{3,2,1,0:T(8,128)} custom-call(f32[8,131072]{1,0:T(8,128)} %in_ref.2), custom_call_target="tpu_custom_call" | custom-call | bytes 8388608 | tf_op jit(solution)/shard_map/pallas_call | solution.py:425
  7.5 5.2 %all-to-all-start = ((f32[8,8,128,128]{3,2,1,0:T(8,128)}), f32[8,8,128,128]{3,2,1,0:T(8,128)}, u32[]{:S(2)}, u32[]{:S(2)}) async-start(f32[8,8,128,128]{3,2,1,0:T(8,128)} %shard_map.95), calls=%async_computation | async-start | bytes 8388608 | tf_op jit(solution)/shard_map/all_to_all | solution.py:631
  12.6 0.0 copy-start.9
  12.7 6.9 %shard_map.96 = f32[8,8,128,128]{3,2,1,0:T(8,128)} custom-call(f32[8,131072]{1,0:T(8,128)} %in_ref.3), custom_call_target="tpu_custom_call" | custom-call | bytes 8388608 | tf_op jit(solution)/shard_map/pallas_call | solution.py:425
  19.8 3.5 constant_dynamic-slice_fusion.1
  23.2 0.9 constant_dynamic-slice_fusion
  24.2 0.1 pad_maximum_fusion.4
  24.3 4.5 %collective-permute-start.2 = (f32[2,8,16512]{2,1,0:T(8,128)S(1)}, f32[2,8,16512]{2,1,0:T(8,128)S(1)}, u32[]{:S(2)}, u32[]{:S(2)}) collective-permute-start(f32[2,8,16512]{2,1,0:T(8,128)S(1)} %pad_maximum_fusion.4), channel_id=1, source_target_pairs={{0,3},{1,2},{2,1},{3,0},{4,7},{5,6},{6,5},{7,4},{8,11},{9,10},{10,... | collective-permute-start | bytes 3170312 | tf_op jit(solution)/shard_map/ppermute | solution.py:545
  28.9 1.1 pad_maximum_fusion.3
  30.0 0.0 collective-permute-start.1
  30.1 1.0 pad_maximum_fusion.2
  31.1 0.6 collective-permute-start
  31.7 0.2 fusion.28.params_ref
  31.9 0.1 pad_add_fusion.base_ref
  32.0 29.9 %all-to-all-done.phase_ref = f32[8,8,128,128]{3,2,1,0:T(8,128)} async-done(((f32[8,8,128,128]{3,2,1,0:T(8,128)}), f32[8,8,128,128]{3,2,1,0:T(8,128)}, u32[]{:S(2)}, u32[]{:S(2)}) %all-to-all-start) | async-done | bytes 4194336 | tf_op jit(solution)/shard_map/all_to_all | solution.py:631
  61.9 4.6 %all-to-all-start.1 = ((f32[8,8,128,128]{3,2,1,0:T(8,128)}), f32[8,8,128,128]{3,2,1,0:T(8,128)}, u32[]{:S(2)}, u32[]{:S(2)}) async-start(f32[8,8,128,128]{3,2,1,0:T(8,128)} %shard_map.96), calls=%async_computation.1 | async-start | bytes 8388608 | tf_op jit(solution)/shard_map/all_to_all | solution.py:631
  66.4 0.0 collective-permute-done.2
  66.4 0.1 slice_bitcast_fusion.6
  66.5 0.0 copy-start.2
  66.5 24.1 %shard_map.97 = (f32[8,2,1024,128]{3,2,1,0:T(8,128)}, f32[8,8,128,128]{3,2,1,0:T(8,128)}, f32[8,8,128,128]{3,2,1,0:T(8,128)}, f32[8,8,128,128]{3,2,1,0:T(8,128)}) custom-call(f32[3]{0:T(128)S(1)} %fusion.28.params_ref, f32[8,8,128,128]{3,2,1,0:T(8,128)} %all-to-all-done.phase_ref, bf16[2,4,512,512]{3,2,1,0:T(8,128)(2,1)} %constant.161.clone.refs_0_.refs_3_, ...), custom_call_target="tpu_custom_call" | custom-call | flops 6442450944 | bytes 33554432 | tf_op jit(solution)/shard_map/pallas_call | solution.py:469
  90.7 9.5 %shard_map.98 = (f32[8,8,64,128]{3,2,1,0:T(8,128)}, f32[8,8,64,128]{3,2,1,0:T(8,128)}) custom-call(f32[8,2,1024,128]{3,2,1,0:T(8,128)} %get-tuple-element.36.mid_ref, bf16[2,4,256,512]{3,2,1,0:T(8,128)(2,1)S(1)} %copy-done.2), custom_call_target="tpu_custom_call" | custom-call | flops 3221225472 | bytes 12582912 | tf_op jit(solution)/shard_map/pallas_call | solution.py:492
  100.1 15.4 %all-to-all-done.1.phase_ref = f32[8,8,128,128]{3,2,1,0:T(8,128)} async-done(((f32[8,8,128,128]{3,2,1,0:T(8,128)}), f32[8,8,128,128]{3,2,1,0:T(8,128)}, u32[]{:S(2)}, u32[]{:S(2)}) %all-to-all-start.1) | async-done | bytes 4194336 | tf_op jit(solution)/shard_map/all_to_all | solution.py:631
  115.5 3.6 all-to-all-start.2
  119.2 0.7 collective-permute-done.1
  119.9 2.3 slice_bitcast_fusion.7
  122.2 20.7 %shard_map.99.mid_ref = f32[8,2,1024,128]{3,2,1,0:T(8,128)} custom-call(f32[3]{0:T(128)S(1)} %fusion.28.params_ref, f32[8,8,128,128]{3,2,1,0:T(8,128)} %all-to-all-done.1.phase_ref, f32[8,8,128,128]{3,2,1,0:T(8,128)} %get-tuple-element.41.refs_0_, f32[8,8,128,128]{3,2,1,0:T(8,128)} %get-tuple-element.42.refs_1_, ...), custom_call_target="tpu_custom_call" | custom-call | flops 6442450944 | bytes 33554432 | tf_op jit(solution)/shard_map/pallas_call | solution.py:469
  142.9 9.5 %shard_map.100 = f32[8,8,128,128]{3,2,1,0:T(8,128)} custom-call(f32[8,2,1024,128]{3,2,1,0:T(8,128)} %shard_map.99.mid_ref, bf16[2,4,256,512]{3,2,1,0:T(8,128)(2,1)S(1)} %copy-done.3), custom_call_target="tpu_custom_call" | custom-call | flops 3221225472 | bytes 12582912 | tf_op jit(solution)/shard_map/pallas_call | solution.py:492
  152.3 0.0 all-to-all-done.2.in_ref
  152.3 1.3 copy-done
  153.7 4.6 %all-to-all-start.3 = ((f32[8,8,128,128]{3,2,1,0:T(8,128)}), f32[8,8,128,128]{3,2,1,0:T(8,128)}, u32[]{:S(2)}, u32[]{:S(2)}) async-start(f32[8,8,128,128]{3,2,1,0:T(8,128)} %shard_map.100), calls=%async_computation.3 | async-start | bytes 8388608 | tf_op jit(solution)/shard_map/all_to_all | solution.py:631
  158.3 0.0 collective-permute-done
  158.3 1.4 slice_bitcast_fusion.8
  159.7 0.0 copy-done.5
  159.8 0.2 copy-done.6
  159.9 0.2 copy-done.7
  160.1 1.8 pad_maximum_fusion
  161.9 5.8 %shard_map.101.near_ref = f32[2,32,16512]{2,1,0:T(8,128)} custom-call(s32[3]{0:T(128)S(1)} %pad_add_fusion.base_ref, f32[32,16512]{1,0:T(8,128)S(1)} %get-tuple-element.53.own_ref), custom_call_target="tpu_custom_call" | custom-call | flops 52838400 | bytes 6340608 | tf_op jit(solution)/shard_map/pallas_call | solution.py:511
  167.7 39.7 %all-to-all-done.3.in_ref = f32[8,8,128,128]{3,2,1,0:T(8,128)} async-done(((f32[8,8,128,128]{3,2,1,0:T(8,128)}), f32[8,8,128,128]{3,2,1,0:T(8,128)}, u32[]{:S(2)}, u32[]{:S(2)}) %all-to-all-start.3) | async-done | bytes 4194336 | tf_op jit(solution)/shard_map/all_to_all | solution.py:631
  207.4 7.7 %shard_map.102 = (f32[2,8,131072]{2,1,0:T(8,128)}, f32[4,8,32768]{2,1,0:T(8,128)}) custom-call(f32[8,8,128,128]{3,2,1,0:T(8,128)} %all-to-all-done.3.in_ref), custom_call_target="tpu_custom_call" | custom-call | bytes 12582912 | tf_op jit(solution)/shard_map/pallas_call | solution.py:442
  215.1 3.9 %dynamic-slice_bitcast_fusion = (f32[8,32768]{1,0:T(8,128)}, f32[8,32768]{1,0:T(8,128)}, f32[8,32768]{1,0:T(8,128)}, f32[8,32768]{1,0:T(8,128)S(1)}) fusion(f32[4,8,32768]{2,1,0:T(8,128)} %get-tuple-element.47, s32[]{:T(128)S(6)} %select_n.141, s32[]{:T(128)S(6)} %select_n.140, s32[]{:T(128)S(6)} %select_n.139, s32[]{:T(128)S(6)} %select_n.138), kind=kLoop, calls=%fused_computation.18 | loop fusion | bytes 8388624 | tf_op jit(solution)/shard_map/jit(dynamic_index_in_dim)/squeeze | solution.py:554
  219.0 0.0 collective-permute-start.3
  219.0 4.3 %all-to-all-start.4 = ((f32[8,8,64,128]{3,2,1,0:T(8,128)}), f32[8,8,64,128]{3,2,1,0:T(8,128)}, u32[]{:S(2)}, u32[]{:S(2)}) async-start(f32[8,8,64,128]{3,2,1,0:T(8,128)} %get-tuple-element.50), calls=%async_computation.4 | async-start | bytes 4194304 | tf_op jit(solution)/shard_map/all_to_all | solution.py:631
  223.4 16.2 %collective-permute-start.5 = (f32[8,32768]{1,0:T(8,128)}, f32[8,32768]{1,0:T(8,128)}, u32[]{:S(2)}, u32[]{:S(2)}) collective-permute-start(f32[8,32768]{1,0:T(8,128)} %get-tuple-element.76), channel_id=1, source_target_pairs={{0,1},{1,0},{2,3},{3,2},{4,5},{5,4},{6,7},{7,6},{8,9},{9,8},{10,11... | collective-permute-start | bytes 3145736 | tf_op jit(solution)/shard_map/ppermute | solution.py:545
  239.6 1.1 collective-permute-start.6
  240.7 1.4 collective-permute-start.7
  242.1 0.8 collective-permute-start.4
  243.0 1.6 copy-done.1
  244.6 2.1 shard_map.104.refs_0_
  246.7 22.0 %collective-permute-done.3.far_ref = f32[32,16512]{1,0:T(8,128)} collective-permute-done((f32[32,16512]{1,0:T(8,128)}, f32[32,16512]{1,0:T(8,128)}, u32[]{:S(2)}, u32[]{:S(2)}) %collective-permute-start.3) | collective-permute-done | bytes 2113568 | tf_op jit(solution)/shard_map/ppermute | solution.py:595
  268.6 16.6 %shard_map.103 = f32[2,32,16512]{2,1,0:T(8,128)} custom-call(s32[3]{0:T(128)S(1)} %pad_add_fusion.base_ref, f32[2,32,16512]{2,1,0:T(8,128)} %shard_map.101.near_ref, f32[32,16512]{1,0:T(8,128)} %collective-permute-done.3.far_ref, f32[32,128]{1,0:T(8,128)S(1)} %collective-permute-done.4.edge_ref, f32[32,128]{1,0:T(8,128)S(1)} %slice.52.beyond_ref), custom_call_target="tpu_custom_call" | custom-call | flops 52838400 | bytes 10567680 | tf_op jit(solution)/shard_map/pallas_call | solution.py:525
  285.2 3.2 fusion.8
  288.5 3.3 fusion.10
  291.8 4.0 %shard_map.105 = f32[2,8,131072]{2,1,0:T(8,128)} custom-call(f32[8,8,64,128]{3,2,1,0:T(8,128)} %all-to-all-done.4.in_ref, f32[2,8,131072]{2,1,0:T(8,128)} %shard_map.104.refs_0_), custom_call_target="tpu_custom_call", output_to_operand_aliasing={{}: (1, {})} | custom-call | bytes 6291456 | tf_op jit(solution)/shard_map/pallas_call | solution.py:442
  295.7 16.0 %collective-permute-done.6 = f32[8,32768]{1,0:T(8,128)} collective-permute-done((f32[8,32768]{1,0:T(8,128)}, f32[8,32768]{1,0:T(8,128)}, u32[]{:S(2)}, u32[]{:S(2)}) %collective-permute-start.6) | collective-permute-done | bytes 1048608 | tf_op jit(solution)/shard_map/ppermute | solution.py:545
  311.8 4.7 %fusion.11 = f32[32,32]{1,0:T(8,128)S(1)} fusion(f32[8,32768]{1,0:T(8,128)} %collective-permute-done.7, f32[8,32768]{1,0:T(8,128)} %collective-permute-done.6, f32[8,32768]{1,0:T(8,128)} %collective-permute-done.5, f32[8,32768]{1,0:T(8,128)S(1)} %get-tuple-element.60), kind=kOutput, calls=%fused_computation.22 | convolution fusion | flops 204473344 | bytes 4198400 | tf_op jit(solution)/shard_map/dot_general | solution.py:549
  316.5 0.2 fusion.15
  316.7 0.2 fusion.32
  316.9 14.8 %all-gather = f32[256,32]{1,0:T(8,128)S(1)} all-gather(f32[32,32]{1,0:T(8,128)S(1)} %fusion.32), channel_id=2, replica_groups=mesh['len'=8,'mem'=4] {'len'}, dimensions={0}, use_global_device_ids=true | all-gather | bytes 36864 | tf_op jit(solution)/shard_map/all_gather | solution.py:621
  331.7 28.6 %all-gather.1 = f32[128,32]{1,0:T(8,128)S(1)} all-gather(f32[32,32]{1,0:T(8,128)S(1)} %reduce_sum.18), channel_id=3, replica_groups=mesh['len'=8,'mem'=4] {'mem'}, dimensions={0}, use_global_device_ids=true | all-gather | bytes 20480 | tf_op jit(solution)/shard_map/all_gather | solution.py:621
  360.3 0.1 copy.16
  360.4 2.9 cholesky.18
  363.4 0.6 compare_reduce_fusion
  364.0 0.6 select_bitcast_fusion
  364.7 0.7 copy.17
  (39 shorter events, 0.4 us)
Async XLA Ops:
  7.5 54.4 %all-to-all-start = ((f32[8,8,128,128]{3,2,1,0:T(8,128)}), f32[8,8,128,128]{3,2,1,0:T(8,128)}, u32[]{:S(2)}, u32[]{:S(2)}) async-start(f32[8,8,128,128]{3,2,1,0:T(8,128)} %shard_map.95), calls=%async_computation | async-start | bytes 8388608 | tf_op jit(solution)/shard_map/all_to_all | solution.py:631
  12.6 7.0 %copy-start.8 = (f32[8]{0:T(128)S(1)}, f32[8]{0:T(128)}, u32[]{:S(2)}) copy-start(f32[8]{0:T(128)} %param.11) | copy-start | bytes 100
  12.6 7.0 %copy-start.9 = (f32[8]{0:T(128)S(1)}, f32[8]{0:T(128)}, u32[]{:S(2)}) copy-start(f32[8]{0:T(128)} %param.10) | copy-start | bytes 100
  24.3 42.2 %collective-permute-start.2 = (f32[2,8,16512]{2,1,0:T(8,128)S(1)}, f32[2,8,16512]{2,1,0:T(8,128)S(1)}, u32[]{:S(2)}, u32[]{:S(2)}) collective-permute-start(f32[2,8,16512]{2,1,0:T(8,128)S(1)} %pad_maximum_fusion.4), channel_id=1, source_target_pairs={{0,3},{1,2},{2,1},{3,0},{4,7},{5,6},{6,5},{7,4},{8,11},{9,10},{10,... | collective-permute-start | bytes 3170312 | tf_op jit(solution)/shard_map/ppermute | solution.py:545
  30.0 89.9 %collective-permute-start.1 = (f32[2,8,16512]{2,1,0:T(8,128)}, f32[2,8,16512]{2,1,0:T(8,128)}, u32[]{:S(2)}, u32[]{:S(2)}) collective-permute-start(f32[2,8,16512]{2,1,0:T(8,128)} %pad_maximum_fusion.3), channel_id=1, source_target_pairs={{0,2},{1,3},{2,0},{3,1},{4,6},{5,7},{6,4},{7,5},{8,10},{9,11},{10,... | collective-permute-start | bytes 3170312 | tf_op jit(solution)/shard_map/ppermute | solution.py:545
  30.0 1.7 copy-start.10
  31.1 127.2 %collective-permute-start = (f32[2,8,16512]{2,1,0:T(8,128)}, f32[2,8,16512]{2,1,0:T(8,128)}, u32[]{:S(2)}, u32[]{:S(2)}) collective-permute-start(f32[2,8,16512]{2,1,0:T(8,128)} %pad_maximum_fusion.2), channel_id=1, source_target_pairs={{0,1},{1,0},{2,3},{3,2},{4,5},{5,4},{6,7},{7,6},{8,9},{9,8},{10,11... | collective-permute-start | bytes 3170312 | tf_op jit(solution)/shard_map/ppermute | solution.py:545
  61.9 53.7 %all-to-all-start.1 = ((f32[8,8,128,128]{3,2,1,0:T(8,128)}), f32[8,8,128,128]{3,2,1,0:T(8,128)}, u32[]{:S(2)}, u32[]{:S(2)}) async-start(f32[8,8,128,128]{3,2,1,0:T(8,128)} %shard_map.96), calls=%async_computation.1 | async-start | bytes 8388608 | tf_op jit(solution)/shard_map/all_to_all | solution.py:631
  66.5 24.1 %copy-start.2 = (bf16[2,4,256,512]{3,2,1,0:T(8,128)(2,1)S(1)}, bf16[2,4,256,512]{3,2,1,0:T(8,128)(2,1)}, u32[]{:S(2)}) copy-start(bf16[2,4,256,512]{3,2,1,0:T(8,128)(2,1)} %constant.162.clone.matrix_ref) | copy-start | bytes 6291460
  115.5 36.8 %all-to-all-start.2 = ((f32[8,8,64,128]{3,2,1,0:T(8,128)}), f32[8,8,64,128]{3,2,1,0:T(8,128)S(1)}, u32[]{:S(2)}, u32[]{:S(2)}) async-start(f32[8,8,64,128]{3,2,1,0:T(8,128)} %get-tuple-element.39), calls=%async_computation.2 | async-start | bytes 4194304 | tf_op jit(solution)/shard_map/all_to_all | solution.py:631
  122.2 20.7 %copy-start.3 = (bf16[2,4,256,512]{3,2,1,0:T(8,128)(2,1)S(1)}, bf16[2,4,256,512]{3,2,1,0:T(8,128)(2,1)}, u32[]{:S(2)}) copy-start(bf16[2,4,256,512]{3,2,1,0:T(8,128)(2,1)} %constant.162.clone.matrix_ref) | copy-start | bytes 6291460
  152.3 1.3 copy-start
  153.7 53.7 %all-to-all-start.3 = ((f32[8,8,128,128]{3,2,1,0:T(8,128)}), f32[8,8,128,128]{3,2,1,0:T(8,128)}, u32[]{:S(2)}, u32[]{:S(2)}) async-start(f32[8,8,128,128]{3,2,1,0:T(8,128)} %shard_map.100), calls=%async_computation.3 | async-start | bytes 8388608 | tf_op jit(solution)/shard_map/all_to_all | solution.py:631
  158.2 1.5 copy-start.4
  158.3 1.5 copy-start.5
  158.3 1.7 copy-start.6
  158.3 1.8 copy-start.7
  219.0 49.6 %collective-permute-start.3 = (f32[32,16512]{1,0:T(8,128)}, f32[32,16512]{1,0:T(8,128)}, u32[]{:S(2)}, u32[]{:S(2)}) collective-permute-start(f32[32,16512]{1,0:T(8,128)} %get-tuple-element.52), channel_id=1, source_target_pairs={{0,28},{4,24},{8,20},{12,16},{16,12},{20,8},{24,4},{28,0},{1,29},{... | collective-permute-start | bytes 6340616 | tf_op jit(solution)/shard_map/ppermute | solution.py:595
  219.0 72.8 %all-to-all-start.4 = ((f32[8,8,64,128]{3,2,1,0:T(8,128)}), f32[8,8,64,128]{3,2,1,0:T(8,128)}, u32[]{:S(2)}, u32[]{:S(2)}) async-start(f32[8,8,64,128]{3,2,1,0:T(8,128)} %get-tuple-element.50), calls=%async_computation.4 | async-start | bytes 4194304 | tf_op jit(solution)/shard_map/all_to_all | solution.py:631
  223.4 72.4 %collective-permute-start.5 = (f32[8,32768]{1,0:T(8,128)}, f32[8,32768]{1,0:T(8,128)}, u32[]{:S(2)}, u32[]{:S(2)}) collective-permute-start(f32[8,32768]{1,0:T(8,128)} %get-tuple-element.76), channel_id=1, source_target_pairs={{0,1},{1,0},{2,3},{3,2},{4,5},{5,4},{6,7},{7,6},{8,9},{9,8},{10,11... | collective-permute-start | bytes 3145736 | tf_op jit(solution)/shard_map/ppermute | solution.py:545
  239.6 72.2 %collective-permute-start.6 = (f32[8,32768]{1,0:T(8,128)}, f32[8,32768]{1,0:T(8,128)}, u32[]{:S(2)}, u32[]{:S(2)}) collective-permute-start(f32[8,32768]{1,0:T(8,128)} %get-tuple-element.75), channel_id=1, source_target_pairs={{0,2},{1,3},{2,0},{3,1},{4,6},{5,7},{6,4},{7,5},{8,10},{9,11},{10,... | collective-permute-start | bytes 3145736 | tf_op jit(solution)/shard_map/ppermute | solution.py:545
  240.7 71.1 %collective-permute-start.7 = (f32[8,32768]{1,0:T(8,128)}, f32[8,32768]{1,0:T(8,128)}, u32[]{:S(2)}, u32[]{:S(2)}) collective-permute-start(f32[8,32768]{1,0:T(8,128)} %get-tuple-element.74), channel_id=1, source_target_pairs={{0,3},{1,2},{2,1},{3,0},{4,7},{5,6},{6,5},{7,4},{8,11},{9,10},{10,... | collective-permute-start | bytes 3145736 | tf_op jit(solution)/shard_map/ppermute | solution.py:545
  242.1 4.6 %collective-permute-start.4 = (f32[32,128]{1,0:T(8,128)S(1)}, f32[32,128]{1,0:T(8,128)S(1)}, u32[]{:S(2)}, u32[]{:S(2)}) collective-permute-start(f32[32,128]{1,0:T(8,128)S(1)} %slice.42), channel_id=1, source_target_pairs={{0,0},{4,28},{8,24},{12,20},{16,16},{20,12},{24,8},{28,4},{1,1},{5... | collective-permute-start | bytes 49160 | tf_op jit(solution)/shard_map/ppermute | solution.py:590
  243.0 1.6 copy-start.1

commit v10 on v9

--- a/solution.py
+++ b/solution.py
@@ -437,6 +437,7 @@
     members, tiles, rows, _ = piece.shape
     stretch = rows * INNER
     steps = rows // BLOCK_ROWS
+    piece = pltpu.with_memory_space_constraint(piece, pltpu.HBM)
     operands = (piece,) if so_far is None else (piece, so_far)
     each = max(steps // max(groups, 1), 1)
     return pl.pallas_call(
@@ -551,7 +552,14 @@
 
 def by_slot(stretches, groups):
     my_group = lax.axis_index("mem")
-    return [lax.dynamic_index_in_dim(stretches, my_group ^ slot, 0, keepdims=False) for slot in range(groups)]
+    return [
+        lax.dynamic_index_in_dim(stretches, my_group ^ slot, 0, keepdims=False)
+        for slot in nearest_last(groups)
+    ]
+
+
+def nearest_last(groups):
+    return [(groups - n) % groups for n in range(groups)]
 
 
 def own_and_far(phase, params, my_group):
@@ -567,7 +575,7 @@
         )
 
     own, far = [], []
-    for slot in range(groups):
+    for slot in nearest_last(groups):
         group = my_group ^ slot
         inner, beyond = lines(group * width)
         for n in range(2):
@@ -607,12 +615,14 @@
     return rows_gram(sums[0]) + rows_gram(sums[1])
 
 
-def in_order(gram_matrix, members):
+def in_order(gram_matrix, members, slots):
     my_group = lax.axis_index("mem")
     row = lax.broadcasted_iota(jnp.int32, gram_matrix.shape, 0)
     column = lax.broadcasted_iota(jnp.int32, gram_matrix.shape, 1)
-    to_slot = (row % members == column % members) & ((row // members) ^ my_group == column // members)
-    to_slot = to_slot.astype(jnp.float32)
+    to_slot = False
+    for n, slot in enumerate(slots):
+        to_slot = to_slot | (((row // members) ^ slot == my_group) & (column // members == n))
+    to_slot = (to_slot & (row % members == column % members)).astype(jnp.float32)
     return jnp.dot(jnp.dot(to_slot, gram_matrix, precision=highest), to_slot.T, precision=highest)
 
 
@@ -654,7 +664,7 @@
     second, near, far = lax.optimization_barrier((swap(second), near, far))
     profile, points = join_call(second, 1, 0, local_len, groups, None)
     pieces = by_slot(points, groups)
-    rows = [to_group(piece, slot) for slot, piece in enumerate(pieces)]
+    rows = [to_group(piece, slot) for slot, piece in zip(nearest_last(groups), pieces)]
     _, first[1], edge, far = lax.optimization_barrier((pieces, first[1], own, far))
     late = swap(first[1])
     line_gram = lines_gram(base, near, across(far), edge_of(edge), own[:, -LANES:])
@@ -663,7 +673,7 @@
     (profile,) = join_call(late, 0, 1, local_len, 0, profile)
     profile, line_gram, rows = lax.optimization_barrier((profile, line_gram, rows))
     gram_matrix = 0.25 * line_gram + (0.5 / (OUTER * INNER)) * rows_gram(jnp.concatenate(rows, axis=0))
-    return (profile, upper_of(summed(in_order(gram_matrix, members))))
+    return (profile, upper_of(summed(in_order(gram_matrix, members, nearest_last(groups)))))
 
 
 def per_device(phase_left, phase_right, roughness, waviness, coherence):

time: 367 us -> 351 us (0.956)
  blocking collectives: 43.4 us -> 22.3 us
  waiting for transfers between devices: 124 us -> 143 us
  starting transfers between devices: 46.9 us -> 34 us
    all_gather x2, blocking collectives: 43.4 us -> 22.3 us  [summed(): value = jnp.sum(lax.all_gather(value, axis), axis=0)]
    ppermute x6, starting transfers between devices: 23.8 us -> 10.2 us  [to_group(): lax.ppermute(piece, 'mem', [(z, z ^ slot) for z in range(groups)])]
    ppermute x1, waiting for transfers between devices: 22 us -> 35.3 us  [across(): lax.ppermute(far, 'len', [(d, shards - 1 - d) for d in range(shards)])]
    ppermute x6, waiting for transfers between devices: 16.8 us -> 28.3 us  [to_group(): lax.ppermute(piece, 'mem', [(z, z ^ slot) for z in range(groups)])]
    all_to_all x5, waiting for transfers between devices: 85 us -> 79.7 us  [swap(): return lax.all_to_all(piece, 'len', split_axis=0, concat_axis=0, tiled=True)]
  transfers between devices with their start and end apart: 13 -> 13, of which waited for: 6 -> 6; matrix products, arithmetic and copies ran while one was open for 5% -> 6% of each run, Pallas kernels for 27% -> 29%
where the time goes in v10:
time: 351 us; the launch traced here: 350 us
  waiting for transfers between devices  143 us (41%)
  Pallas kernels  115 us (33%)
  starting transfers between devices  34 us (10%)
  blocking collectives  22.3 us (6%)
  local copies, waits for them, and re-layouts  12.5 us (4%)
  matrix products  11.6 us (3%)
  other arithmetic  9.56 us (3%)
    all_to_all x5, waiting for transfers between devices, swap(): return lax.all_to_all(piece, 'len', split_axis=0, concat_axis=0, tiled=True)  79.7 us
    pallas_call x2, Pallas kernels, outer_call(): pl.pallas_call(functools.partial(outer_kernel, track), grid=(tiles // som...  44.6 us
    ppermute x1, waiting for transfers between devices, across(): lax.ppermute(far, 'len', [(d, shards - 1 - d) for d in range(shards)])  35.3 us
    ppermute x6, waiting for transfers between devices, to_group(): lax.ppermute(piece, 'mem', [(z, z ^ slot) for z in range(groups)])  28.3 us
    all_to_all x5, starting transfers between devices, swap(): return lax.all_to_all(piece, 'len', split_axis=0, concat_axis=0, tiled=True)  23 us
    all_gather x2, blocking collectives, summed(): value = jnp.sum(lax.all_gather(value, axis), axis=0)  22.3 us
    pallas_call x2, Pallas kernels, inner_call(): pl.pallas_call(inner_kernel, grid=(OUTER // WIDE,), in_specs=[pl.BlockSpe...  18.9 us
    pallas_call x1, Pallas kernels, mirror_call(): pl.pallas_call(mirror_kernel, in_specs=[pl.BlockSpec(memory_space=pltpu.S...  16.6 us
  transfers between devices with their start and end apart: 13, of which 6 were waited for; matrix products, arithmetic and copies ran while one was open for 6% of the time, Pallas kernels for 29%

profile of v10, /device:TPU:0, one launch (start us, length us, event | category | flops | bytes accessed | tf_op | source)
XLA Modules:
  0.0 349.6 jit_solution(5297169822235097194)
XLA Ops:
  0.6 6.8 %shard_map.95 = f32[8,8,128,128]{3,2,1,0:T(8,128)} custom-call(f32[8,131072]{1,0:T(8,128)} %in_ref.2), custom_call_target="tpu_custom_call" | custom-call | bytes 8388608 | tf_op jit(solution)/shard_map/pallas_call | solution.py:425
  7.5 5.2 %all-to-all-start = ((f32[8,8,128,128]{3,2,1,0:T(8,128)}), f32[8,8,128,128]{3,2,1,0:T(8,128)}, u32[]{:S(2)}, u32[]{:S(2)}) async-start(f32[8,8,128,128]{3,2,1,0:T(8,128)} %shard_map.95), calls=%async_computation | async-start | bytes 8388608 | tf_op jit(solution)/shard_map/all_to_all | solution.py:641
  12.6 0.0 copy-start.6
  12.7 6.9 %shard_map.96 = f32[8,8,128,128]{3,2,1,0:T(8,128)} custom-call(f32[8,131072]{1,0:T(8,128)} %in_ref.3), custom_call_target="tpu_custom_call" | custom-call | bytes 8388608 | tf_op jit(solution)/shard_map/pallas_call | solution.py:425
  19.8 3.5 constant_dynamic-slice_fusion.1
  23.2 0.9 constant_dynamic-slice_fusion
  24.2 0.1 pad_maximum_fusion.4
  24.3 2.5 collective-permute-start.2
  26.9 1.1 pad_maximum_fusion.3
  28.0 2.6 collective-permute-start.1
  30.6 1.1 pad_maximum_fusion.2
  31.7 0.0 collective-permute-start
  31.7 0.2 fusion.38.params_ref
  31.9 0.1 pad_add_fusion.base_ref
  32.0 29.8 %all-to-all-done.phase_ref = f32[8,8,128,128]{3,2,1,0:T(8,128)} async-done(((f32[8,8,128,128]{3,2,1,0:T(8,128)}), f32[8,8,128,128]{3,2,1,0:T(8,128)}, u32[]{:S(2)}, u32[]{:S(2)}) %all-to-all-start) | async-done | bytes 4194336 | tf_op jit(solution)/shard_map/all_to_all | solution.py:641
  61.9 4.5 %all-to-all-start.1 = ((f32[8,8,128,128]{3,2,1,0:T(8,128)}), f32[8,8,128,128]{3,2,1,0:T(8,128)}, u32[]{:S(2)}, u32[]{:S(2)}) async-start(f32[8,8,128,128]{3,2,1,0:T(8,128)} %shard_map.96), calls=%async_computation.1 | async-start | bytes 8388608 | tf_op jit(solution)/shard_map/all_to_all | solution.py:641
  66.4 5.4 %collective-permute-done.2 = f32[2,8,16512]{2,1,0:T(8,128)S(1)} collective-permute-done((f32[2,8,16512]{2,1,0:T(8,128)S(1)}, f32[2,8,16512]{2,1,0:T(8,128)S(1)}, u32[]{:S(2)}, u32[]{:S(2)}) %collective-permute-start.2) | collective-permute-done | bytes 1056800 | tf_op jit(solution)/shard_map/ppermute | solution.py:546
  71.8 0.1 slice_bitcast_fusion.6
  71.9 0.0 copy-start
  71.9 24.1 %shard_map.97 = (f32[8,2,1024,128]{3,2,1,0:T(8,128)}, f32[8,8,128,128]{3,2,1,0:T(8,128)}, f32[8,8,128,128]{3,2,1,0:T(8,128)}, f32[8,8,128,128]{3,2,1,0:T(8,128)}) custom-call(f32[3]{0:T(128)S(1)} %fusion.38.params_ref, f32[8,8,128,128]{3,2,1,0:T(8,128)} %all-to-all-done.phase_ref, bf16[2,4,512,512]{3,2,1,0:T(8,128)(2,1)} %constant.177.clone.refs_0_.refs_3_, ...), custom_call_target="tpu_custom_call" | custom-call | flops 6442450944 | bytes 33554432 | tf_op jit(solution)/shard_map/pallas_call | solution.py:470
  96.0 9.4 %shard_map.98 = (f32[8,8,64,128]{3,2,1,0:T(8,128)}, f32[8,8,64,128]{3,2,1,0:T(8,128)}) custom-call(f32[8,2,1024,128]{3,2,1,0:T(8,128)} %get-tuple-element.36.mid_ref, bf16[2,4,256,512]{3,2,1,0:T(8,128)(2,1)S(1)} %copy-done), custom_call_target="tpu_custom_call" | custom-call | flops 3221225472 | bytes 12582912 | tf_op jit(solution)/shard_map/pallas_call | solution.py:493
  105.4 10.1 %all-to-all-done.1.phase_ref = f32[8,8,128,128]{3,2,1,0:T(8,128)} async-done(((f32[8,8,128,128]{3,2,1,0:T(8,128)}), f32[8,8,128,128]{3,2,1,0:T(8,128)}, u32[]{:S(2)}, u32[]{:S(2)}) %all-to-all-start.1) | async-done | bytes 4194336 | tf_op jit(solution)/shard_map/all_to_all | solution.py:641
  115.5 4.3 %all-to-all-start.2 = ((f32[8,8,64,128]{3,2,1,0:T(8,128)}), f32[8,8,64,128]{3,2,1,0:T(8,128)}, u32[]{:S(2)}, u32[]{:S(2)}) async-start(f32[8,8,64,128]{3,2,1,0:T(8,128)} %get-tuple-element.39), calls=%async_computation.2 | async-start | bytes 4194304 | tf_op jit(solution)/shard_map/all_to_all | solution.py:641
  119.9 0.0 collective-permute-done.1
  119.9 2.3 slice_bitcast_fusion.7
  122.2 20.6 %shard_map.99.mid_ref = f32[8,2,1024,128]{3,2,1,0:T(8,128)} custom-call(f32[3]{0:T(128)S(1)} %fusion.38.params_ref, f32[8,8,128,128]{3,2,1,0:T(8,128)} %all-to-all-done.1.phase_ref, f32[8,8,128,128]{3,2,1,0:T(8,128)} %get-tuple-element.41.refs_0_, f32[8,8,128,128]{3,2,1,0:T(8,128)} %get-tuple-element.42.refs_1_, ...), custom_call_target="tpu_custom_call" | custom-call | flops 6442450944 | bytes 33554432 | tf_op jit(solution)/shard_map/pallas_call | solution.py:470
  142.8 9.5 %shard_map.100 = f32[8,8,128,128]{3,2,1,0:T(8,128)} custom-call(f32[8,2,1024,128]{3,2,1,0:T(8,128)} %shard_map.99.mid_ref, bf16[2,4,256,512]{3,2,1,0:T(8,128)(2,1)S(1)} %copy-done), custom_call_target="tpu_custom_call" | custom-call | flops 3221225472 | bytes 12582912 | tf_op jit(solution)/shard_map/pallas_call | solution.py:493
  152.2 0.0 all-to-all-done.2.in_ref
  152.3 4.6 %all-to-all-start.3 = ((f32[8,8,128,128]{3,2,1,0:T(8,128)}), f32[8,8,128,128]{3,2,1,0:T(8,128)}, u32[]{:S(2)}, u32[]{:S(2)}) async-start(f32[8,8,128,128]{3,2,1,0:T(8,128)} %shard_map.100), calls=%async_computation.3 | async-start | bytes 8388608 | tf_op jit(solution)/shard_map/all_to_all | solution.py:641
  156.9 0.0 collective-permute-done
  156.9 1.4 slice_bitcast_fusion.8
  158.3 0.0 copy-done.2
  158.3 0.2 copy-done.3
  158.5 0.2 copy-done.4
  158.7 1.8 pad_maximum_fusion
  160.5 5.8 %shard_map.101.near_ref = f32[2,32,16512]{2,1,0:T(8,128)} custom-call(s32[3]{0:T(128)S(1)} %pad_add_fusion.base_ref, f32[32,16512]{1,0:T(8,128)S(1)} %get-tuple-element.53.own_ref), custom_call_target="tpu_custom_call" | custom-call | flops 52838400 | bytes 6340608 | tf_op jit(solution)/shard_map/pallas_call | solution.py:512
  166.3 39.7 %all-to-all-done.3.in_ref = f32[8,8,128,128]{3,2,1,0:T(8,128)} async-done(((f32[8,8,128,128]{3,2,1,0:T(8,128)}), f32[8,8,128,128]{3,2,1,0:T(8,128)}, u32[]{:S(2)}, u32[]{:S(2)}) %all-to-all-start.3) | async-done | bytes 4194336 | tf_op jit(solution)/shard_map/all_to_all | solution.py:641
  205.9 7.7 %shard_map.102 = (f32[2,8,131072]{2,1,0:T(8,128)}, f32[4,8,32768]{2,1,0:T(8,128)}) custom-call(f32[8,8,128,128]{3,2,1,0:T(8,128)} %all-to-all-done.3.in_ref), custom_call_target="tpu_custom_call" | custom-call | bytes 12582912 | tf_op jit(solution)/shard_map/pallas_call | solution.py:443
  213.6 3.9 %dynamic-slice_bitcast_fusion = (f32[8,32768]{1,0:T(8,128)}, f32[8,32768]{1,0:T(8,128)}, f32[8,32768]{1,0:T(8,128)}, f32[8,32768]{1,0:T(8,128)S(1)}) fusion(f32[4,8,32768]{2,1,0:T(8,128)} %get-tuple-element.47, s32[]{:T(128)S(6)} %select_n.159, s32[]{:T(128)S(6)} %select_n.158, s32[]{:T(128)S(6)} %select_n.157, s32[]{:T(128)S(6)} %select_n.156), kind=kLoop, calls=%fused_computation.18 | loop fusion | bytes 8388624 | tf_op jit(solution)/shard_map/jit(dynamic_index_in_dim)/squeeze | solution.py:556
  217.5 4.4 %all-to-all-start.4 = ((f32[8,8,64,128]{3,2,1,0:T(8,128)}), f32[8,8,64,128]{3,2,1,0:T(8,128)}, u32[]{:S(2)}, u32[]{:S(2)}) async-start(f32[8,8,64,128]{3,2,1,0:T(8,128)} %get-tuple-element.50), calls=%async_computation.4 | async-start | bytes 4194304 | tf_op jit(solution)/shard_map/all_to_all | solution.py:641
  221.9 4.4 %collective-permute-start.5 = (f32[8,32768]{1,0:T(8,128)}, f32[8,32768]{1,0:T(8,128)}, u32[]{:S(2)}, u32[]{:S(2)}) collective-permute-start(f32[8,32768]{1,0:T(8,128)} %get-tuple-element.76), channel_id=1, source_target_pairs={{0,3},{1,2},{2,1},{3,0},{4,7},{5,6},{6,5},{7,4},{8,11},{9,10},{10,... | collective-permute-start | bytes 3145736 | tf_op jit(solution)/shard_map/ppermute | solution.py:546
  226.3 0.0 collective-permute-start.6
  226.3 0.7 collective-permute-start.7
  227.0 0.8 collective-permute-start.4
  227.8 3.9 %shard_map.104.refs_0_ = f32[2,8,131072]{2,1,0:T(8,128)} custom-call(f32[8,8,64,128]{3,2,1,0:T(8,128)} %all-to-all-done.2.in_ref, f32[2,8,131072]{2,1,0:T(8,128)} %get-tuple-element.56.refs_0_), custom_call_target="tpu_custom_call", output_to_operand_aliasing={{}: (1, {})} | custom-call | bytes 6291456 | tf_op jit(solution)/shard_map/pallas_call | solution.py:443
  231.8 0.0 collective-permute-done.4.edge_ref
  231.8 35.3 %collective-permute-done.3.far_ref = f32[32,16512]{1,0:T(8,128)} collective-permute-done((f32[32,16512]{1,0:T(8,128)}, f32[32,16512]{1,0:T(8,128)}, u32[]{:S(2)}, u32[]{:S(2)}) %collective-permute-start.3) | collective-permute-done | bytes 2113568 | tf_op jit(solution)/shard_map/ppermute | solution.py:603
  267.1 16.6 %shard_map.103 = f32[2,32,16512]{2,1,0:T(8,128)} custom-call(s32[3]{0:T(128)S(1)} %pad_add_fusion.base_ref, f32[2,32,16512]{2,1,0:T(8,128)} %shard_map.101.near_ref, f32[32,16512]{1,0:T(8,128)} %collective-permute-done.3.far_ref, f32[32,128]{1,0:T(8,128)S(1)} %collective-permute-done.4.edge_ref, f32[32,128]{1,0:T(8,128)S(1)} %slice.52.beyond_ref), custom_call_target="tpu_custom_call" | custom-call | flops 52838400 | bytes 10567680 | tf_op jit(solution)/shard_map/pallas_call | solution.py:526
  283.7 3.2 fusion.8
  287.0 3.3 fusion.10
  290.3 0.0 all-to-all-done.4.in_ref
  290.3 4.0 %shard_map.105 = f32[2,8,131072]{2,1,0:T(8,128)} custom-call(f32[8,8,64,128]{3,2,1,0:T(8,128)} %all-to-all-done.4.in_ref, f32[2,8,131072]{2,1,0:T(8,128)} %shard_map.104.refs_0_), custom_call_target="tpu_custom_call", output_to_operand_aliasing={{}: (1, {})} | custom-call | bytes 6291456 | tf_op jit(solution)/shard_map/pallas_call | solution.py:443
  294.2 22.9 %collective-permute-done.6 = f32[8,32768]{1,0:T(8,128)} collective-permute-done((f32[8,32768]{1,0:T(8,128)}, f32[8,32768]{1,0:T(8,128)}, u32[]{:S(2)}, u32[]{:S(2)}) %collective-permute-start.6) | collective-permute-done | bytes 1048608 | tf_op jit(solution)/shard_map/ppermute | solution.py:546
  317.1 0.0 collective-permute-done.7
  317.1 4.7 %fusion.11 = f32[32,32]{1,0:T(8,128)S(1)} fusion(f32[8,32768]{1,0:T(8,128)} %collective-permute-done.7, f32[8,32768]{1,0:T(8,128)} %collective-permute-done.6, f32[8,32768]{1,0:T(8,128)} %collective-permute-done.5, f32[8,32768]{1,0:T(8,128)S(1)} %get-tuple-element.60), kind=kOutput, calls=%fused_computation.22 | convolution fusion | flops 204473344 | bytes 4198400 | tf_op jit(solution)/shard_map/dot_general | solution.py:550
  321.8 0.2 fusion.18
  322.0 0.2 fusion.42
  322.3 9.1 %all-gather = f32[256,32]{1,0:T(8,128)S(1)} all-gather(f32[32,32]{1,0:T(8,128)S(1)} %fusion.42), channel_id=2, replica_groups=mesh['len'=8,'mem'=4] {'len'}, dimensions={0}, use_global_device_ids=true | all-gather | bytes 36864 | tf_op jit(solution)/shard_map/all_gather | solution.py:631
  331.4 13.1 %all-gather.1 = f32[128,32]{1,0:T(8,128)S(1)} all-gather(f32[32,32]{1,0:T(8,128)S(1)} %reduce_sum.18), channel_id=3, replica_groups=mesh['len'=8,'mem'=4] {'mem'}, dimensions={0}, use_global_device_ids=true | all-gather | bytes 20480 | tf_op jit(solution)/shard_map/all_gather | solution.py:631
  344.6 0.1 copy.16
  344.7 2.9 cholesky.18
  347.6 0.6 compare_reduce_fusion
  348.3 0.6 select_bitcast_fusion
  348.9 0.7 copy.17
  (33 shorter events, 0.4 us)
Async XLA Ops:
  7.5 54.4 %all-to-all-start = ((f32[8,8,128,128]{3,2,1,0:T(8,128)}), f32[8,8,128,128]{3,2,1,0:T(8,128)}, u32[]{:S(2)}, u32[]{:S(2)}) async-start(f32[8,8,128,128]{3,2,1,0:T(8,128)} %shard_map.95), calls=%async_computation | async-start | bytes 8388608 | tf_op jit(solution)/shard_map/all_to_all | solution.py:641
  12.6 7.0 %copy-start.5 = (f32[8]{0:T(128)S(1)}, f32[8]{0:T(128)}, u32[]{:S(2)}) copy-start(f32[8]{0:T(128)} %param.11) | copy-start | bytes 100
  12.6 7.0 %copy-start.6 = (f32[8]{0:T(128)S(1)}, f32[8]{0:T(128)}, u32[]{:S(2)}) copy-start(f32[8]{0:T(128)} %param.10) | copy-start | bytes 100
  24.3 47.5 %collective-permute-start.2 = (f32[2,8,16512]{2,1,0:T(8,128)S(1)}, f32[2,8,16512]{2,1,0:T(8,128)S(1)}, u32[]{:S(2)}, u32[]{:S(2)}) collective-permute-start(f32[2,8,16512]{2,1,0:T(8,128)S(1)} %pad_maximum_fusion.4), channel_id=1, source_target_pairs={{0,1},{1,0},{2,3},{3,2},{4,5},{5,4},{6,7},{7,6},{8,9},{9,8},{10,11... | collective-permute-start | bytes 3170312 | tf_op jit(solution)/shard_map/ppermute | solution.py:546
  28.0 91.9 %collective-permute-start.1 = (f32[2,8,16512]{2,1,0:T(8,128)}, f32[2,8,16512]{2,1,0:T(8,128)}, u32[]{:S(2)}, u32[]{:S(2)}) collective-permute-start(f32[2,8,16512]{2,1,0:T(8,128)} %pad_maximum_fusion.3), channel_id=1, source_target_pairs={{0,2},{1,3},{2,0},{3,1},{4,6},{5,7},{6,4},{7,5},{8,10},{9,11},{10,... | collective-permute-start | bytes 3170312 | tf_op jit(solution)/shard_map/ppermute | solution.py:546
  30.6 1.2 copy-start.7
  31.7 125.1 %collective-permute-start = (f32[2,8,16512]{2,1,0:T(8,128)}, f32[2,8,16512]{2,1,0:T(8,128)}, u32[]{:S(2)}, u32[]{:S(2)}) collective-permute-start(f32[2,8,16512]{2,1,0:T(8,128)} %pad_maximum_fusion.2), channel_id=1, source_target_pairs={{0,3},{1,2},{2,1},{3,0},{4,7},{5,6},{6,5},{7,4},{8,11},{9,10},{10,... | collective-permute-start | bytes 3170312 | tf_op jit(solution)/shard_map/ppermute | solution.py:546
  61.9 53.7 %all-to-all-start.1 = ((f32[8,8,128,128]{3,2,1,0:T(8,128)}), f32[8,8,128,128]{3,2,1,0:T(8,128)}, u32[]{:S(2)}, u32[]{:S(2)}) async-start(f32[8,8,128,128]{3,2,1,0:T(8,128)} %shard_map.96), calls=%async_computation.1 | async-start | bytes 8388608 | tf_op jit(solution)/shard_map/all_to_all | solution.py:641
  71.9 24.1 %copy-start = (bf16[2,4,256,512]{3,2,1,0:T(8,128)(2,1)S(1)}, bf16[2,4,256,512]{3,2,1,0:T(8,128)(2,1)}, u32[]{:S(2)}) copy-start(bf16[2,4,256,512]{3,2,1,0:T(8,128)(2,1)} %constant.178.clone.matrix_ref) | copy-start | bytes 6291460
  115.5 36.7 %all-to-all-start.2 = ((f32[8,8,64,128]{3,2,1,0:T(8,128)}), f32[8,8,64,128]{3,2,1,0:T(8,128)}, u32[]{:S(2)}, u32[]{:S(2)}) async-start(f32[8,8,64,128]{3,2,1,0:T(8,128)} %get-tuple-element.39), calls=%async_computation.2 | async-start | bytes 4194304 | tf_op jit(solution)/shard_map/all_to_all | solution.py:641
  152.3 53.7 %all-to-all-start.3 = ((f32[8,8,128,128]{3,2,1,0:T(8,128)}), f32[8,8,128,128]{3,2,1,0:T(8,128)}, u32[]{:S(2)}, u32[]{:S(2)}) async-start(f32[8,8,128,128]{3,2,1,0:T(8,128)} %shard_map.100), calls=%async_computation.3 | async-start | bytes 8388608 | tf_op jit(solution)/shard_map/all_to_all | solution.py:641
  156.8 1.5 copy-start.1
  156.8 1.5 copy-start.2
  156.8 1.7 copy-start.3
  156.8 1.8 copy-start.4
  217.5 49.6 %collective-permute-start.3 = (f32[32,16512]{1,0:T(8,128)}, f32[32,16512]{1,0:T(8,128)}, u32[]{:S(2)}, u32[]{:S(2)}) collective-permute-start(f32[32,16512]{1,0:T(8,128)} %get-tuple-element.52), channel_id=1, source_target_pairs={{0,28},{4,24},{8,20},{12,16},{16,12},{20,8},{24,4},{28,0},{1,29},{... | collective-permute-start | bytes 6340616 | tf_op jit(solution)/shard_map/ppermute | solution.py:603
  217.5 72.7 %all-to-all-start.4 = ((f32[8,8,64,128]{3,2,1,0:T(8,128)}), f32[8,8,64,128]{3,2,1,0:T(8,128)}, u32[]{:S(2)}, u32[]{:S(2)}) async-start(f32[8,8,64,128]{3,2,1,0:T(8,128)} %get-tuple-element.50), calls=%async_computation.4 | async-start | bytes 4194304 | tf_op jit(solution)/shard_map/all_to_all | solution.py:641
  221.9 72.3 %collective-permute-start.5 = (f32[8,32768]{1,0:T(8,128)}, f32[8,32768]{1,0:T(8,128)}, u32[]{:S(2)}, u32[]{:S(2)}) collective-permute-start(f32[8,32768]{1,0:T(8,128)} %get-tuple-element.76), channel_id=1, source_target_pairs={{0,3},{1,2},{2,1},{3,0},{4,7},{5,6},{6,5},{7,4},{8,11},{9,10},{10,... | collective-permute-start | bytes 3145736 | tf_op jit(solution)/shard_map/ppermute | solution.py:546
  226.3 90.8 %collective-permute-start.6 = (f32[8,32768]{1,0:T(8,128)}, f32[8,32768]{1,0:T(8,128)}, u32[]{:S(2)}, u32[]{:S(2)}) collective-permute-start(f32[8,32768]{1,0:T(8,128)} %get-tuple-element.75), channel_id=1, source_target_pairs={{0,2},{1,3},{2,0},{3,1},{4,6},{5,7},{6,4},{7,5},{8,10},{9,11},{10,... | collective-permute-start | bytes 3145736 | tf_op jit(solution)/shard_map/ppermute | solution.py:546
  226.3 90.8 %collective-permute-start.7 = (f32[8,32768]{1,0:T(8,128)}, f32[8,32768]{1,0:T(8,128)}, u32[]{:S(2)}, u32[]{:S(2)}) collective-permute-start(f32[8,32768]{1,0:T(8,128)} %get-tuple-element.74), channel_id=1, source_target_pairs={{0,1},{1,0},{2,3},{3,2},{4,5},{5,4},{6,7},{7,6},{8,9},{9,8},{10,11... | collective-permute-start | bytes 3145736 | tf_op jit(solution)/shard_map/ppermute | solution.py:546
  227.0 4.8 %collective-permute-start.4 = (f32[32,128]{1,0:T(8,128)S(1)}, f32[32,128]{1,0:T(8,128)S(1)}, u32[]{:S(2)}, u32[]{:S(2)}) collective-permute-start(f32[32,128]{1,0:T(8,128)S(1)} %slice.42), channel_id=1, source_target_pairs={{0,0},{4,28},{8,24},{12,20},{16,16},{20,12},{24,8},{28,4},{1,1},{5... | collective-permute-start | bytes 49160 | tf_op jit(solution)/shard_map/ppermute | solution.py:598

commit v11 on v10

--- a/solution.py
+++ b/solution.py
@@ -347,16 +347,26 @@
                 out_ref[m, tile, start : start + SUBLANES, :] = turned[m]
 
 
-def join_kernel(extra, in_ref, *refs):
-    out_refs = refs[-2:] if extra else refs[-1:]
-    members, tiles, rows, _ = in_ref.shape
+def join_kernel(in_ref, *refs):
+    join_rows(in_ref, refs[-1].at[0])
+
+
+def join_rows(in_ref, out_ref):
+    _, tiles, rows, _ = in_ref.shape
     for tile in range(tiles):
         for start in range(0, rows, SUBLANES):
             turned = jnp.transpose(in_ref[:, tile, start : start + SUBLANES, :], (1, 0, 2))
             for r in range(SUBLANES):
                 at = ((start + r) * tiles + tile) * LANES
-                for out_ref in out_refs:
-                    out_ref[0, :, at : at + LANES] = turned[r]
+                out_ref[:, at : at + LANES] = turned[r]
+
+
+def pieces_kernel(each, group_ref, in_ref, *out_refs):
+    for n, out_ref in enumerate(out_refs):
+
+        @pl.when(pl.program_id(0) // each == n)
+        def _(out_ref=out_ref):
+            join_rows(in_ref, out_ref)
 
 
 def near_kernel(base_ref, own_ref, out_ref):
@@ -433,32 +443,49 @@
     )(pltpu.with_memory_space_constraint(phase, pltpu.HBM))
 
 
-def join_call(piece, track, within, length, groups, so_far):
+def join_call(piece, track, within, length, so_far):
     members, tiles, rows, _ = piece.shape
-    stretch = rows * INNER
     steps = rows // BLOCK_ROWS
     piece = pltpu.with_memory_space_constraint(piece, pltpu.HBM)
     operands = (piece,) if so_far is None else (piece, so_far)
-    each = max(steps // max(groups, 1), 1)
     return pl.pallas_call(
-        functools.partial(join_kernel, groups > 0),
+        join_kernel,
         grid=(steps,),
         in_specs=[
             pl.BlockSpec((members, tiles, BLOCK_ROWS, LANES), lambda g: (0, 0, g, 0)),
             pl.BlockSpec(memory_space=pl.ANY),
         ][: len(operands)],
-        out_specs=[
-            pl.BlockSpec((1, members, BLOCK_ROWS * INNER), lambda g: (track, 0, within * steps + g)),
-            pl.BlockSpec((1, members, BLOCK_ROWS * INNER), lambda g: (g // each, 0, g % each)),
-        ][: 2 if groups else 1],
-        out_shape=[
-            jax.ShapeDtypeStruct((2, members, length), jnp.float32),
-            pltpu.HBM((max(groups, 1), members, stretch // max(groups, 1)), jnp.float32),
-        ][: 2 if groups else 1],
+        out_specs=pl.BlockSpec((1, members, BLOCK_ROWS * INNER), lambda g: (track, 0, within * steps + g)),
+        out_shape=jax.ShapeDtypeStruct((2, members, length), jnp.float32),
         input_output_aliases={} if so_far is None else {1: 0},
         compiler_params=limits(),
-        cost_estimate=pl.CostEstimate(flops=0, bytes_accessed=12 * members * stretch, transcendentals=0),
+        cost_estimate=pl.CostEstimate(flops=0, bytes_accessed=8 * members * rows * INNER, transcendentals=0),
     )(*operands)
+
+
+def pieces_call(my_group, piece, groups):
+    members, tiles, rows, _ = piece.shape
+    each = rows // BLOCK_ROWS // groups
+
+    def source(g, group_ref):
+        slot = (groups - g // each) % groups
+        return (0, 0, (slot ^ group_ref[0]) * each + g % each, 0)
+
+    def place(n):
+        return lambda g, group_ref: (0, jnp.clip(g - n * each, 0, each - 1))
+
+    return pl.pallas_call(
+        functools.partial(pieces_kernel, each),
+        grid_spec=pltpu.PrefetchScalarGridSpec(
+            num_scalar_prefetch=1,
+            grid=(groups * each,),
+            in_specs=[pl.BlockSpec((members, tiles, BLOCK_ROWS, LANES), source)],
+            out_specs=[pl.BlockSpec((members, BLOCK_ROWS * INNER), place(n)) for n in range(groups)],
+        ),
+        out_shape=[pltpu.HBM((members, rows // groups * INNER), jnp.float32)] * groups,
+        compiler_params=limits(),
+        cost_estimate=pl.CostEstimate(flops=0, bytes_accessed=8 * members * rows * INNER, transcendentals=0),
+    )(my_group.astype(jnp.int32).reshape(1), pltpu.with_memory_space_constraint(piece, pltpu.HBM))
 
 
 def outer_call(params, phase, kept, matrices, twists):
@@ -550,14 +577,6 @@
     return lax.dot_general(rows, rows, (((1,), (1,)), ((), ())), precision=lax.Precision.HIGH)
 
 
-def by_slot(stretches, groups):
-    my_group = lax.axis_index("mem")
-    return [
-        lax.dynamic_index_in_dim(stretches, my_group ^ slot, 0, keepdims=False)
-        for slot in nearest_last(groups)
-    ]
-
-
 def nearest_last(groups):
     return [(groups - n) % groups for n in range(groups)]
 
@@ -662,15 +681,15 @@
     base = line_base(own.shape[1] - LANES)
     near = near_call(base, own)
     second, near, far = lax.optimization_barrier((swap(second), near, far))
-    profile, points = join_call(second, 1, 0, local_len, groups, None)
-    pieces = by_slot(points, groups)
+    pieces = pieces_call(lax.axis_index("mem"), second, groups)
     rows = [to_group(piece, slot) for slot, piece in zip(nearest_last(groups), pieces)]
-    _, first[1], edge, far = lax.optimization_barrier((pieces, first[1], own, far))
+    _, first[1], edge, far, second = lax.optimization_barrier((pieces, first[1], own, far, second))
+    profile = join_call(second, 1, 0, local_len, None)
     late = swap(first[1])
     line_gram = lines_gram(base, near, across(far), edge_of(edge), own[:, -LANES:])
-    (profile,) = join_call(early, 0, 0, local_len, 0, profile)
+    profile = join_call(early, 0, 0, local_len, profile)
     late, line_gram = lax.optimization_barrier((late, line_gram))
-    (profile,) = join_call(late, 0, 1, local_len, 0, profile)
+    profile = join_call(late, 0, 1, local_len, profile)
     profile, line_gram, rows = lax.optimization_barrier((profile, line_gram, rows))
     gram_matrix = 0.25 * line_gram + (0.5 / (OUTER * INNER)) * rows_gram(jnp.concatenate(rows, axis=0))
     return (profile, upper_of(summed(in_order(gram_matrix, members, nearest_last(groups)))))

time: 351 us -> 347 us (0.989)
  Pallas kernels: 115 us -> 122 us
  waiting for transfers between devices: 143 us -> 136 us
  local copies, waits for them, and re-layouts: 12.5 us -> 8.57 us
    ppermute x1, waiting for transfers between devices: 35.3 us -> 28.3 us  [across(): lax.ppermute(far, 'len', [(d, shards - 1 - d) for d in range(shards)])]
    pallas_call x3 -> x4, Pallas kernels: 15.6 us -> 22.1 us  [the longest x3 14.9 us: join_call(): pl.pallas_call(join_kernel, grid=(steps,), in_specs=[pl.BlockSpec((member...]
    squeeze x1 -> x0, local copies, waits for them, and re-layouts: 3.87 us -> none  [by_slot(): lax.dynamic_index_in_dim(stretches, my_group ^ slot, 0, keepdims=False)]
  transfers between devices with their start and end apart: 13 -> 13, of which waited for: 6 -> 6; matrix products, arithmetic and copies ran while one was open for 6% -> 6% of each run, Pallas kernels for 29% -> 31%
where the time goes in v11:
time: 347 us; the launch traced here: 345 us
  waiting for transfers between devices  136 us (39%)
  Pallas kernels  122 us (35%)
  starting transfers between devices  34.2 us (10%)
  blocking collectives  22.3 us (6%)
  matrix products  11.6 us (3%)
  other arithmetic  9.46 us (3%)
  local copies, waits for them, and re-layouts  8.57 us (2%)
    all_to_all x5, waiting for transfers between devices, swap(): return lax.all_to_all(piece, 'len', split_axis=0, concat_axis=0, tiled=True)  79.8 us
    pallas_call x2, Pallas kernels, outer_call(): pl.pallas_call(functools.partial(outer_kernel, track), grid=(tiles // som...  44.7 us
    ppermute x1, waiting for transfers between devices, across(): lax.ppermute(far, 'len', [(d, shards - 1 - d) for d in range(shards)])  28.3 us
    ppermute x6, waiting for transfers between devices, to_group(): lax.ppermute(piece, 'mem', [(z, z ^ slot) for z in range(groups)])  28.1 us
    all_to_all x5, starting transfers between devices, swap(): return lax.all_to_all(piece, 'len', split_axis=0, concat_axis=0, tiled=True)  23.2 us
    all_gather x2, blocking collectives, summed(): value = jnp.sum(lax.all_gather(value, axis), axis=0)  22.3 us
    pallas_call x2, Pallas kernels, inner_call(): pl.pallas_call(inner_kernel, grid=(OUTER // WIDE,), in_specs=[pl.BlockSpe...  18.9 us
    pallas_call x1, Pallas kernels, mirror_call(): pl.pallas_call(mirror_kernel, in_specs=[pl.BlockSpec(memory_space=pltpu.S...  16.6 us
  transfers between devices with their start and end apart: 13, of which 6 were waited for; matrix products, arithmetic and copies ran while one was open for 6% of the time, Pallas kernels for 31%

profile of v11, /device:TPU:0, one launch (start us, length us, event | category | flops | bytes accessed | tf_op | source)
XLA Modules:
  0.0 345.4 jit_solution(14038882036074945337)
XLA Ops:
  0.6 6.8 %shard_map.95 = f32[8,8,128,128]{3,2,1,0:T(8,128)} custom-call(f32[8,131072]{1,0:T(8,128)} %in_ref.2), custom_call_target="tpu_custom_call" | custom-call | bytes 8388608 | tf_op jit(solution)/shard_map/pallas_call | solution.py:435
  7.5 5.2 %all-to-all-start = ((f32[8,8,128,128]{3,2,1,0:T(8,128)}), f32[8,8,128,128]{3,2,1,0:T(8,128)}, u32[]{:S(2)}, u32[]{:S(2)}) async-start(f32[8,8,128,128]{3,2,1,0:T(8,128)} %shard_map.95), calls=%async_computation | async-start | bytes 8388608 | tf_op jit(solution)/shard_map/all_to_all | solution.py:660
  12.6 0.0 copy-start.6
  12.7 6.9 %shard_map.96 = f32[8,8,128,128]{3,2,1,0:T(8,128)} custom-call(f32[8,131072]{1,0:T(8,128)} %in_ref.3), custom_call_target="tpu_custom_call" | custom-call | bytes 8388608 | tf_op jit(solution)/shard_map/pallas_call | solution.py:435
  19.8 3.4 constant_dynamic-slice_fusion.1
  23.2 0.9 constant_dynamic-slice_fusion
  24.2 0.1 pad_maximum_fusion.4
  24.3 2.5 collective-permute-start.2
  26.9 1.1 pad_maximum_fusion.3
  27.9 2.6 collective-permute-start.1
  30.6 1.1 pad_maximum_fusion.2
  31.7 0.0 collective-permute-start
  31.7 0.2 fusion.38.params_ref
  31.9 0.1 pad_add_fusion.base_ref
  32.0 29.9 %all-to-all-done.phase_ref = f32[8,8,128,128]{3,2,1,0:T(8,128)} async-done(((f32[8,8,128,128]{3,2,1,0:T(8,128)}), f32[8,8,128,128]{3,2,1,0:T(8,128)}, u32[]{:S(2)}, u32[]{:S(2)}) %all-to-all-start) | async-done | bytes 4194336 | tf_op jit(solution)/shard_map/all_to_all | solution.py:660
  61.9 4.6 %all-to-all-start.1 = ((f32[8,8,128,128]{3,2,1,0:T(8,128)}), f32[8,8,128,128]{3,2,1,0:T(8,128)}, u32[]{:S(2)}, u32[]{:S(2)}) async-start(f32[8,8,128,128]{3,2,1,0:T(8,128)} %shard_map.96), calls=%async_computation.1 | async-start | bytes 8388608 | tf_op jit(solution)/shard_map/all_to_all | solution.py:660
  66.5 5.3 %collective-permute-done.2 = f32[2,8,16512]{2,1,0:T(8,128)S(1)} collective-permute-done((f32[2,8,16512]{2,1,0:T(8,128)S(1)}, f32[2,8,16512]{2,1,0:T(8,128)S(1)}, u32[]{:S(2)}, u32[]{:S(2)}) %collective-permute-start.2) | collective-permute-done | bytes 1056800 | tf_op jit(solution)/shard_map/ppermute | solution.py:573
  71.8 0.1 slice_bitcast_fusion.6
  71.9 0.0 copy-start
  71.9 24.2 %shard_map.97 = (f32[8,2,1024,128]{3,2,1,0:T(8,128)}, f32[8,8,128,128]{3,2,1,0:T(8,128)}, f32[8,8,128,128]{3,2,1,0:T(8,128)}, f32[8,8,128,128]{3,2,1,0:T(8,128)}) custom-call(f32[3]{0:T(128)S(1)} %fusion.38.params_ref, f32[8,8,128,128]{3,2,1,0:T(8,128)} %all-to-all-done.phase_ref, bf16[2,4,512,512]{3,2,1,0:T(8,128)(2,1)} %constant.166.clone.refs_0_.refs_3_, ...), custom_call_target="tpu_custom_call" | custom-call | flops 6442450944 | bytes 33554432 | tf_op jit(solution)/shard_map/pallas_call | solution.py:497
  96.0 9.5 %shard_map.98 = (f32[8,8,64,128]{3,2,1,0:T(8,128)}, f32[8,8,64,128]{3,2,1,0:T(8,128)}) custom-call(f32[8,2,1024,128]{3,2,1,0:T(8,128)} %get-tuple-element.39.mid_ref, bf16[2,4,256,512]{3,2,1,0:T(8,128)(2,1)S(1)} %copy-done), custom_call_target="tpu_custom_call" | custom-call | flops 3221225472 | bytes 12582912 | tf_op jit(solution)/shard_map/pallas_call | solution.py:520
  105.5 10.1 %all-to-all-done.1.phase_ref = f32[8,8,128,128]{3,2,1,0:T(8,128)} async-done(((f32[8,8,128,128]{3,2,1,0:T(8,128)}), f32[8,8,128,128]{3,2,1,0:T(8,128)}, u32[]{:S(2)}, u32[]{:S(2)}) %all-to-all-start.1) | async-done | bytes 4194336 | tf_op jit(solution)/shard_map/all_to_all | solution.py:660
  115.6 4.4 %all-to-all-start.2 = ((f32[8,8,64,128]{3,2,1,0:T(8,128)}), f32[8,8,64,128]{3,2,1,0:T(8,128)}, u32[]{:S(2)}, u32[]{:S(2)}) async-start(f32[8,8,64,128]{3,2,1,0:T(8,128)} %get-tuple-element.42), calls=%async_computation.2 | async-start | bytes 4194304 | tf_op jit(solution)/shard_map/all_to_all | solution.py:660
  120.0 0.0 collective-permute-done.1
  120.0 2.3 slice_bitcast_fusion.7
  122.3 20.6 %shard_map.99.mid_ref = f32[8,2,1024,128]{3,2,1,0:T(8,128)} custom-call(f32[3]{0:T(128)S(1)} %fusion.38.params_ref, f32[8,8,128,128]{3,2,1,0:T(8,128)} %all-to-all-done.1.phase_ref, f32[8,8,128,128]{3,2,1,0:T(8,128)} %get-tuple-element.44.refs_0_, f32[8,8,128,128]{3,2,1,0:T(8,128)} %get-tuple-element.45.refs_1_, ...), custom_call_target="tpu_custom_call" | custom-call | flops 6442450944 | bytes 33554432 | tf_op jit(solution)/shard_map/pallas_call | solution.py:497
  142.8 9.4 %shard_map.100 = f32[8,8,128,128]{3,2,1,0:T(8,128)} custom-call(f32[8,2,1024,128]{3,2,1,0:T(8,128)} %shard_map.99.mid_ref, bf16[2,4,256,512]{3,2,1,0:T(8,128)(2,1)S(1)} %copy-done), custom_call_target="tpu_custom_call" | custom-call | flops 3221225472 | bytes 12582912 | tf_op jit(solution)/shard_map/pallas_call | solution.py:520
  152.3 0.0 all-to-all-done.2.in_ref
  152.3 4.6 %all-to-all-start.3 = ((f32[8,8,128,128]{3,2,1,0:T(8,128)}), f32[8,8,128,128]{3,2,1,0:T(8,128)}, u32[]{:S(2)}, u32[]{:S(2)}) async-start(f32[8,8,128,128]{3,2,1,0:T(8,128)} %shard_map.100), calls=%async_computation.3 | async-start | bytes 8388608 | tf_op jit(solution)/shard_map/all_to_all | solution.py:660
  156.9 0.0 collective-permute-done
  156.9 1.4 slice_bitcast_fusion.8
  158.3 0.0 copy-done.2
  158.4 0.2 copy-done.3
  158.5 0.2 copy-done.4
  158.7 1.7 pad_maximum_fusion
  160.4 5.7 %shard_map.101.near_ref = f32[2,32,16512]{2,1,0:T(8,128)} custom-call(s32[3]{0:T(128)S(1)} %pad_add_fusion.base_ref, f32[32,16512]{1,0:T(8,128)S(1)} %get-tuple-element.59.own_ref), custom_call_target="tpu_custom_call" | custom-call | flops 52838400 | bytes 6340608 | tf_op jit(solution)/shard_map/pallas_call | solution.py:539
  166.1 39.9 %all-to-all-done.3.in_ref = f32[8,8,128,128]{3,2,1,0:T(8,128)} async-done(((f32[8,8,128,128]{3,2,1,0:T(8,128)}), f32[8,8,128,128]{3,2,1,0:T(8,128)}, u32[]{:S(2)}, u32[]{:S(2)}) %all-to-all-start.3) | async-done | bytes 4194336 | tf_op jit(solution)/shard_map/all_to_all | solution.py:660
  206.0 7.3 %shard_map.102 = (f32[8,32768]{1,0:T(8,128)}, f32[8,32768]{1,0:T(8,128)}, f32[8,32768]{1,0:T(8,128)}, f32[8,32768]{1,0:T(8,128)}) custom-call(s32[1]{0:T(128)} %bitcast.group_ref, f32[8,8,128,128]{3,2,1,0:T(8,128)} %all-to-all-done.3.in_ref), custom_call_target="tpu_custom_call" | custom-call | bytes 8388608 | tf_op jit(solution)/shard_map/pallas_call | solution.py:477
  213.2 0.0 collective-permute-start.3
  213.2 4.5 %all-to-all-start.4 = ((f32[8,8,64,128]{3,2,1,0:T(8,128)}), f32[8,8,64,128]{3,2,1,0:T(8,128)}, u32[]{:S(2)}, u32[]{:S(2)}) async-start(f32[8,8,64,128]{3,2,1,0:T(8,128)} %get-tuple-element.56), calls=%async_computation.4 | async-start | bytes 4194304 | tf_op jit(solution)/shard_map/all_to_all | solution.py:660
  217.7 4.4 %collective-permute-start.5 = (f32[8,32768]{1,0:T(8,128)}, f32[8,32768]{1,0:T(8,128)}, u32[]{:S(2)}, u32[]{:S(2)}) collective-permute-start(f32[8,32768]{1,0:T(8,128)} %get-tuple-element.51), channel_id=1, source_target_pairs={{0,3},{1,2},{2,1},{3,0},{4,7},{5,6},{6,5},{7,4},{8,11},{9,10},{10,... | collective-permute-start | bytes 3145736 | tf_op jit(solution)/shard_map/ppermute | solution.py:573
  222.2 0.6 collective-permute-start.7
  222.8 0.8 collective-permute-start.4
  223.7 6.9 %shard_map.104.refs_0_ = f32[2,8,131072]{2,1,0:T(8,128)} custom-call(f32[8,8,128,128]{3,2,1,0:T(8,128)} %all-to-all-done.3.in_ref), custom_call_target="tpu_custom_call" | custom-call | bytes 8388608 | tf_op jit(solution)/shard_map/pallas_call | solution.py:451
  230.6 3.9 %shard_map.105.refs_0_ = f32[2,8,131072]{2,1,0:T(8,128)} custom-call(f32[8,8,64,128]{3,2,1,0:T(8,128)} %all-to-all-done.2.in_ref, f32[2,8,131072]{2,1,0:T(8,128)} %shard_map.104.refs_0_), custom_call_target="tpu_custom_call", output_to_operand_aliasing={{}: (1, {})} | custom-call | bytes 4194304 | tf_op jit(solution)/shard_map/pallas_call | solution.py:451
  234.5 28.3 %collective-permute-done.3.far_ref = f32[32,16512]{1,0:T(8,128)} collective-permute-done((f32[32,16512]{1,0:T(8,128)}, f32[32,16512]{1,0:T(8,128)}, u32[]{:S(2)}, u32[]{:S(2)}) %collective-permute-start.3) | collective-permute-done | bytes 2113568 | tf_op jit(solution)/shard_map/ppermute | solution.py:622
  262.8 16.6 %shard_map.103 = f32[2,32,16512]{2,1,0:T(8,128)} custom-call(s32[3]{0:T(128)S(1)} %pad_add_fusion.base_ref, f32[2,32,16512]{2,1,0:T(8,128)} %shard_map.101.near_ref, f32[32,16512]{1,0:T(8,128)} %collective-permute-done.3.far_ref, f32[32,128]{1,0:T(8,128)S(1)} %collective-permute-done.4.edge_ref, f32[32,128]{1,0:T(8,128)S(1)} %slice.52.beyond_ref), custom_call_target="tpu_custom_call" | custom-call | flops 52838400 | bytes 10567680 | tf_op jit(solution)/shard_map/pallas_call | solution.py:553
  279.5 3.2 fusion.8
  282.7 3.3 fusion.10
  286.0 0.0 all-to-all-done.4.in_ref
  286.0 4.0 %shard_map.106 = f32[2,8,131072]{2,1,0:T(8,128)} custom-call(f32[8,8,64,128]{3,2,1,0:T(8,128)} %all-to-all-done.4.in_ref, f32[2,8,131072]{2,1,0:T(8,128)} %shard_map.105.refs_0_), custom_call_target="tpu_custom_call", output_to_operand_aliasing={{}: (1, {})} | custom-call | bytes 4194304 | tf_op jit(solution)/shard_map/pallas_call | solution.py:451
  290.0 0.0 collective-permute-done.5
  290.0 22.8 %collective-permute-done.6 = f32[8,32768]{1,0:T(8,128)} collective-permute-done((f32[8,32768]{1,0:T(8,128)}, f32[8,32768]{1,0:T(8,128)}, u32[]{:S(2)}, u32[]{:S(2)}) %collective-permute-start.6) | collective-permute-done | bytes 1048608 | tf_op jit(solution)/shard_map/ppermute | solution.py:573
  312.9 0.0 collective-permute-done.7
  312.9 4.7 %fusion.11 = f32[32,32]{1,0:T(8,128)S(1)} fusion(f32[8,32768]{1,0:T(8,128)} %collective-permute-done.7, f32[8,32768]{1,0:T(8,128)} %collective-permute-done.6, f32[8,32768]{1,0:T(8,128)} %collective-permute-done.5, f32[8,32768]{1,0:T(8,128)S(1)} %copy-done.7), kind=kOutput, calls=%fused_computation.18 | convolution fusion | flops 204473344 | bytes 4198400 | tf_op jit(solution)/shard_map/dot_general | solution.py:577
  317.5 0.2 fusion.18
  317.7 0.2 fusion.42
  318.0 9.2 %all-gather = f32[256,32]{1,0:T(8,128)S(1)} all-gather(f32[32,32]{1,0:T(8,128)S(1)} %fusion.42), channel_id=2, replica_groups=mesh['len'=8,'mem'=4] {'len'}, dimensions={0}, use_global_device_ids=true | all-gather | bytes 36864 | tf_op jit(solution)/shard_map/all_gather | solution.py:650
  327.2 13.1 %all-gather.1 = f32[128,32]{1,0:T(8,128)S(1)} all-gather(f32[32,32]{1,0:T(8,128)S(1)} %reduce_sum.18), channel_id=3, replica_groups=mesh['len'=8,'mem'=4] {'mem'}, dimensions={0}, use_global_device_ids=true | all-gather | bytes 20480 | tf_op jit(solution)/shard_map/all_gather | solution.py:650
  340.3 0.1 copy.16
  340.4 2.9 cholesky.18
  343.4 0.6 compare_reduce_fusion
  344.0 0.6 select_bitcast_fusion
  344.7 0.7 copy.17
  (37 shorter events, 0.4 us)
Async XLA Ops:
  7.5 54.4 %all-to-all-start = ((f32[8,8,128,128]{3,2,1,0:T(8,128)}), f32[8,8,128,128]{3,2,1,0:T(8,128)}, u32[]{:S(2)}, u32[]{:S(2)}) async-start(f32[8,8,128,128]{3,2,1,0:T(8,128)} %shard_map.95), calls=%async_computation | async-start | bytes 8388608 | tf_op jit(solution)/shard_map/all_to_all | solution.py:660
  12.6 7.0 %copy-start.5 = (f32[8]{0:T(128)S(1)}, f32[8]{0:T(128)}, u32[]{:S(2)}) copy-start(f32[8]{0:T(128)} %param.11) | copy-start | bytes 100
  12.6 7.0 %copy-start.6 = (f32[8]{0:T(128)S(1)}, f32[8]{0:T(128)}, u32[]{:S(2)}) copy-start(f32[8]{0:T(128)} %param.10) | copy-start | bytes 100
  24.3 47.5 %collective-permute-start.2 = (f32[2,8,16512]{2,1,0:T(8,128)S(1)}, f32[2,8,16512]{2,1,0:T(8,128)S(1)}, u32[]{:S(2)}, u32[]{:S(2)}) collective-permute-start(f32[2,8,16512]{2,1,0:T(8,128)S(1)} %pad_maximum_fusion.4), channel_id=1, source_target_pairs={{0,1},{1,0},{2,3},{3,2},{4,5},{5,4},{6,7},{7,6},{8,9},{9,8},{10,11... | collective-permute-start | bytes 3170312 | tf_op jit(solution)/shard_map/ppermute | solution.py:573
  27.9 92.0 %collective-permute-start.1 = (f32[2,8,16512]{2,1,0:T(8,128)}, f32[2,8,16512]{2,1,0:T(8,128)}, u32[]{:S(2)}, u32[]{:S(2)}) collective-permute-start(f32[2,8,16512]{2,1,0:T(8,128)} %pad_maximum_fusion.3), channel_id=1, source_target_pairs={{0,2},{1,3},{2,0},{3,1},{4,6},{5,7},{6,4},{7,5},{8,10},{9,11},{10,... | collective-permute-start | bytes 3170312 | tf_op jit(solution)/shard_map/ppermute | solution.py:573
  30.5 1.2 copy-start.9
  31.7 125.2 %collective-permute-start = (f32[2,8,16512]{2,1,0:T(8,128)}, f32[2,8,16512]{2,1,0:T(8,128)}, u32[]{:S(2)}, u32[]{:S(2)}) collective-permute-start(f32[2,8,16512]{2,1,0:T(8,128)} %pad_maximum_fusion.2), channel_id=1, source_target_pairs={{0,3},{1,2},{2,1},{3,0},{4,7},{5,6},{6,5},{7,4},{8,11},{9,10},{10,... | collective-permute-start | bytes 3170312 | tf_op jit(solution)/shard_map/ppermute | solution.py:573
  61.9 53.7 %all-to-all-start.1 = ((f32[8,8,128,128]{3,2,1,0:T(8,128)}), f32[8,8,128,128]{3,2,1,0:T(8,128)}, u32[]{:S(2)}, u32[]{:S(2)}) async-start(f32[8,8,128,128]{3,2,1,0:T(8,128)} %shard_map.96), calls=%async_computation.1 | async-start | bytes 8388608 | tf_op jit(solution)/shard_map/all_to_all | solution.py:660
  71.9 24.2 %copy-start = (bf16[2,4,256,512]{3,2,1,0:T(8,128)(2,1)S(1)}, bf16[2,4,256,512]{3,2,1,0:T(8,128)(2,1)}, u32[]{:S(2)}) copy-start(bf16[2,4,256,512]{3,2,1,0:T(8,128)(2,1)} %constant.167.clone.matrix_ref) | copy-start | bytes 6291460
  115.6 36.6 %all-to-all-start.2 = ((f32[8,8,64,128]{3,2,1,0:T(8,128)}), f32[8,8,64,128]{3,2,1,0:T(8,128)}, u32[]{:S(2)}, u32[]{:S(2)}) async-start(f32[8,8,64,128]{3,2,1,0:T(8,128)} %get-tuple-element.42), calls=%async_computation.2 | async-start | bytes 4194304 | tf_op jit(solution)/shard_map/all_to_all | solution.py:660
  152.3 53.7 %all-to-all-start.3 = ((f32[8,8,128,128]{3,2,1,0:T(8,128)}), f32[8,8,128,128]{3,2,1,0:T(8,128)}, u32[]{:S(2)}, u32[]{:S(2)}) async-start(f32[8,8,128,128]{3,2,1,0:T(8,128)} %shard_map.100), calls=%async_computation.3 | async-start | bytes 8388608 | tf_op jit(solution)/shard_map/all_to_all | solution.py:660
  156.8 1.5 copy-start.1
  156.9 1.5 copy-start.2
  156.9 1.7 copy-start.3
  156.9 1.8 copy-start.4
  213.2 8.9 %copy-start.8 = (f32[8,32768]{1,0:T(8,128)S(1)}, f32[8,32768]{1,0:T(8,128)}, u32[]{:S(2)}) copy-start(f32[8,32768]{1,0:T(8,128)} %get-tuple-element.53) | copy-start | bytes 3145732
  213.2 49.6 %collective-permute-start.3 = (f32[32,16512]{1,0:T(8,128)}, f32[32,16512]{1,0:T(8,128)}, u32[]{:S(2)}, u32[]{:S(2)}) collective-permute-start(f32[32,16512]{1,0:T(8,128)} %get-tuple-element.58), channel_id=1, source_target_pairs={{0,28},{4,24},{8,20},{12,16},{16,12},{20,8},{24,4},{28,0},{1,29},{... | collective-permute-start | bytes 6340616 | tf_op jit(solution)/shard_map/ppermute | solution.py:622
  213.2 72.8 %all-to-all-start.4 = ((f32[8,8,64,128]{3,2,1,0:T(8,128)}), f32[8,8,64,128]{3,2,1,0:T(8,128)}, u32[]{:S(2)}, u32[]{:S(2)}) async-start(f32[8,8,64,128]{3,2,1,0:T(8,128)} %get-tuple-element.56), calls=%async_computation.4 | async-start | bytes 4194304 | tf_op jit(solution)/shard_map/all_to_all | solution.py:660
  217.7 72.3 %collective-permute-start.5 = (f32[8,32768]{1,0:T(8,128)}, f32[8,32768]{1,0:T(8,128)}, u32[]{:S(2)}, u32[]{:S(2)}) collective-permute-start(f32[8,32768]{1,0:T(8,128)} %get-tuple-element.51), channel_id=1, source_target_pairs={{0,3},{1,2},{2,1},{3,0},{4,7},{5,6},{6,5},{7,4},{8,11},{9,10},{10,... | collective-permute-start | bytes 3145736 | tf_op jit(solution)/shard_map/ppermute | solution.py:573
  222.1 90.7 %collective-permute-start.6 = (f32[8,32768]{1,0:T(8,128)}, f32[8,32768]{1,0:T(8,128)}, u32[]{:S(2)}, u32[]{:S(2)}) collective-permute-start(f32[8,32768]{1,0:T(8,128)} %get-tuple-element.52), channel_id=1, source_target_pairs={{0,2},{1,3},{2,0},{3,1},{4,6},{5,7},{6,4},{7,5},{8,10},{9,11},{10,... | collective-permute-start | bytes 3145736 | tf_op jit(solution)/shard_map/ppermute | solution.py:573
  222.2 90.7 %collective-permute-start.7 = (f32[8,32768]{1,0:T(8,128)S(1)}, f32[8,32768]{1,0:T(8,128)}, u32[]{:S(2)}, u32[]{:S(2)}) collective-permute-start(f32[8,32768]{1,0:T(8,128)S(1)} %copy-done.8), channel_id=1, source_target_pairs={{0,1},{1,0},{2,3},{3,2},{4,5},{5,4},{6,7},{7,6},{8,9},{9,8},{10,11... | collective-permute-start | bytes 3145736 | tf_op jit(solution)/shard_map/ppermute | solution.py:573
  222.8 11.7 %collective-permute-start.4 = (f32[32,128]{1,0:T(8,128)S(1)}, f32[32,128]{1,0:T(8,128)S(1)}, u32[]{:S(2)}, u32[]{:S(2)}) collective-permute-start(f32[32,128]{1,0:T(8,128)S(1)} %slice.42), channel_id=1, source_target_pairs={{0,0},{4,28},{8,24},{12,20},{16,16},{20,12},{24,8},{28,4},{1,1},{5... | collective-permute-start | bytes 49160 | tf_op jit(solution)/shard_map/ppermute | solution.py:617
  286.0 26.9 %copy-start.7 = (f32[8,32768]{1,0:T(8,128)S(1)}, f32[8,32768]{1,0:T(8,128)}, u32[]{:S(2)}) copy-start(f32[8,32768]{1,0:T(8,128)} %get-tuple-element.66) | copy-start | bytes 3145732

commit v12 on v11

--- a/solution.py
+++ b/solution.py
@@ -685,9 +685,10 @@
     rows = [to_group(piece, slot) for slot, piece in zip(nearest_last(groups), pieces)]
     _, first[1], edge, far, second = lax.optimization_barrier((pieces, first[1], own, far, second))
     profile = join_call(second, 1, 0, local_len, None)
-    late = swap(first[1])
     line_gram = lines_gram(base, near, across(far), edge_of(edge), own[:, -LANES:])
     profile = join_call(early, 0, 0, local_len, profile)
+    profile, first[1] = lax.optimization_barrier((profile, first[1]))
+    late = swap(first[1])
     late, line_gram = lax.optimization_barrier((late, line_gram))
     profile = join_call(late, 0, 1, local_len, profile)
     profile, line_gram, rows = lax.optimization_barrier((profile, line_gram, rows))

time: 347 us -> 358 us (1.032)
  waiting for transfers between devices: 136 us -> 147 us
    ppermute x6, waiting for transfers between devices: 28.1 us -> 39.1 us  [to_group(): lax.ppermute(piece, 'mem', [(z, z ^ slot) for z in range(groups)])]
  transfers between devices with their start and end apart: 13 -> 13, of which waited for: 6 -> 6; matrix products, arithmetic and copies ran while one was open for 6% -> 5% of each run, Pallas kernels for 31% -> 30%
where the time goes in v12:
time: 358 us; the launch traced here: 356 us
  waiting for transfers between devices  147 us (41%)
  Pallas kernels  122 us (34%)
  starting transfers between devices  34.2 us (10%)
  blocking collectives  22.2 us (6%)
  matrix products  11.6 us (3%)
  other arithmetic  9.46 us (3%)
  local copies, waits for them, and re-layouts  8.57 us (2%)
    all_to_all x5, waiting for transfers between devices, swap(): return lax.all_to_all(piece, 'len', split_axis=0, concat_axis=0, tiled=True)  79.8 us
    pallas_call x2, Pallas kernels, outer_call(): pl.pallas_call(functools.partial(outer_kernel, track), grid=(tiles // som...  44.7 us
    ppermute x6, waiting for transfers between devices, to_group(): lax.ppermute(piece, 'mem', [(z, z ^ slot) for z in range(groups)])  39.1 us
    ppermute x1, waiting for transfers between devices, across(): lax.ppermute(far, 'len', [(d, shards - 1 - d) for d in range(shards)])  28.3 us
    all_to_all x5, starting transfers between devices, swap(): return lax.all_to_all(piece, 'len', split_axis=0, concat_axis=0, tiled=True)  23.2 us
    all_gather x2, blocking collectives, summed(): value = jnp.sum(lax.all_gather(value, axis), axis=0)  22.2 us
    pallas_call x2, Pallas kernels, inner_call(): pl.pallas_call(inner_kernel, grid=(OUTER // WIDE,), in_specs=[pl.BlockSpe...  18.9 us
    pallas_call x1, Pallas kernels, mirror_call(): pl.pallas_call(mirror_kernel, in_specs=[pl.BlockSpec(memory_space=pltpu.S...  16.6 us
  transfers between devices with their start and end apart: 13, of which 6 were waited for; matrix products, arithmetic and copies ran while one was open for 5% of the time, Pallas kernels for 30%

profile of v12, /device:TPU:0, one launch (start us, length us, event | category | flops | bytes accessed | tf_op | source)
XLA Modules:
  0.0 356.2 jit_solution(13642597073275309630)
XLA Ops:
  0.6 6.8 %shard_map.95 = f32[8,8,128,128]{3,2,1,0:T(8,128)} custom-call(f32[8,131072]{1,0:T(8,128)} %in_ref.2), custom_call_target="tpu_custom_call" | custom-call | bytes 8388608 | tf_op jit(solution)/shard_map/pallas_call | solution.py:435
  7.5 5.2 %all-to-all-start = ((f32[8,8,128,128]{3,2,1,0:T(8,128)}), f32[8,8,128,128]{3,2,1,0:T(8,128)}, u32[]{:S(2)}, u32[]{:S(2)}) async-start(f32[8,8,128,128]{3,2,1,0:T(8,128)} %shard_map.95), calls=%async_computation | async-start | bytes 8388608 | tf_op jit(solution)/shard_map/all_to_all | solution.py:660
  12.6 0.0 copy-start.6
  12.7 6.9 %shard_map.96 = f32[8,8,128,128]{3,2,1,0:T(8,128)} custom-call(f32[8,131072]{1,0:T(8,128)} %in_ref.3), custom_call_target="tpu_custom_call" | custom-call | bytes 8388608 | tf_op jit(solution)/shard_map/pallas_call | solution.py:435
  19.8 3.4 constant_dynamic-slice_fusion.1
  23.2 0.9 constant_dynamic-slice_fusion
  24.2 0.1 pad_maximum_fusion.4
  24.3 2.5 collective-permute-start.2
  26.9 1.1 pad_maximum_fusion.3
  27.9 2.6 collective-permute-start.1
  30.6 1.1 pad_maximum_fusion.2
  31.7 0.0 collective-permute-start
  31.7 0.2 fusion.38.params_ref
  31.9 0.1 pad_add_fusion.base_ref
  32.0 29.9 %all-to-all-done.phase_ref = f32[8,8,128,128]{3,2,1,0:T(8,128)} async-done(((f32[8,8,128,128]{3,2,1,0:T(8,128)}), f32[8,8,128,128]{3,2,1,0:T(8,128)}, u32[]{:S(2)}, u32[]{:S(2)}) %all-to-all-start) | async-done | bytes 4194336 | tf_op jit(solution)/shard_map/all_to_all | solution.py:660
  61.9 4.6 %all-to-all-start.1 = ((f32[8,8,128,128]{3,2,1,0:T(8,128)}), f32[8,8,128,128]{3,2,1,0:T(8,128)}, u32[]{:S(2)}, u32[]{:S(2)}) async-start(f32[8,8,128,128]{3,2,1,0:T(8,128)} %shard_map.96), calls=%async_computation.1 | async-start | bytes 8388608 | tf_op jit(solution)/shard_map/all_to_all | solution.py:660
  66.5 5.3 %collective-permute-done.2 = f32[2,8,16512]{2,1,0:T(8,128)S(1)} collective-permute-done((f32[2,8,16512]{2,1,0:T(8,128)S(1)}, f32[2,8,16512]{2,1,0:T(8,128)S(1)}, u32[]{:S(2)}, u32[]{:S(2)}) %collective-permute-start.2) | collective-permute-done | bytes 1056800 | tf_op jit(solution)/shard_map/ppermute | solution.py:573
  71.8 0.1 slice_bitcast_fusion.6
  71.9 0.0 copy-start
  71.9 24.2 %shard_map.97 = (f32[8,2,1024,128]{3,2,1,0:T(8,128)}, f32[8,8,128,128]{3,2,1,0:T(8,128)}, f32[8,8,128,128]{3,2,1,0:T(8,128)}, f32[8,8,128,128]{3,2,1,0:T(8,128)}) custom-call(f32[3]{0:T(128)S(1)} %fusion.38.params_ref, f32[8,8,128,128]{3,2,1,0:T(8,128)} %all-to-all-done.phase_ref, bf16[2,4,512,512]{3,2,1,0:T(8,128)(2,1)} %constant.166.clone.refs_0_.refs_3_, ...), custom_call_target="tpu_custom_call" | custom-call | flops 6442450944 | bytes 33554432 | tf_op jit(solution)/shard_map/pallas_call | solution.py:497
  96.0 9.5 %shard_map.98 = (f32[8,8,64,128]{3,2,1,0:T(8,128)}, f32[8,8,64,128]{3,2,1,0:T(8,128)}) custom-call(f32[8,2,1024,128]{3,2,1,0:T(8,128)} %get-tuple-element.41.mid_ref, bf16[2,4,256,512]{3,2,1,0:T(8,128)(2,1)S(1)} %copy-done), custom_call_target="tpu_custom_call" | custom-call | flops 3221225472 | bytes 12582912 | tf_op jit(solution)/shard_map/pallas_call | solution.py:520
  105.5 10.1 %all-to-all-done.1.phase_ref = f32[8,8,128,128]{3,2,1,0:T(8,128)} async-done(((f32[8,8,128,128]{3,2,1,0:T(8,128)}), f32[8,8,128,128]{3,2,1,0:T(8,128)}, u32[]{:S(2)}, u32[]{:S(2)}) %all-to-all-start.1) | async-done | bytes 4194336 | tf_op jit(solution)/shard_map/all_to_all | solution.py:660
  115.6 4.4 %all-to-all-start.2 = ((f32[8,8,64,128]{3,2,1,0:T(8,128)}), f32[8,8,64,128]{3,2,1,0:T(8,128)}, u32[]{:S(2)}, u32[]{:S(2)}) async-start(f32[8,8,64,128]{3,2,1,0:T(8,128)} %get-tuple-element.44), calls=%async_computation.2 | async-start | bytes 4194304 | tf_op jit(solution)/shard_map/all_to_all | solution.py:660
  120.0 0.0 collective-permute-done.1
  120.0 2.3 slice_bitcast_fusion.7
  122.3 20.6 %shard_map.99.mid_ref = f32[8,2,1024,128]{3,2,1,0:T(8,128)} custom-call(f32[3]{0:T(128)S(1)} %fusion.38.params_ref, f32[8,8,128,128]{3,2,1,0:T(8,128)} %all-to-all-done.1.phase_ref, f32[8,8,128,128]{3,2,1,0:T(8,128)} %get-tuple-element.46.refs_0_, f32[8,8,128,128]{3,2,1,0:T(8,128)} %get-tuple-element.47.refs_1_, ...), custom_call_target="tpu_custom_call" | custom-call | flops 6442450944 | bytes 33554432 | tf_op jit(solution)/shard_map/pallas_call | solution.py:497
  142.8 9.4 %shard_map.100 = f32[8,8,128,128]{3,2,1,0:T(8,128)} custom-call(f32[8,2,1024,128]{3,2,1,0:T(8,128)} %shard_map.99.mid_ref, bf16[2,4,256,512]{3,2,1,0:T(8,128)(2,1)S(1)} %copy-done), custom_call_target="tpu_custom_call" | custom-call | flops 3221225472 | bytes 12582912 | tf_op jit(solution)/shard_map/pallas_call | solution.py:520
  152.3 0.0 all-to-all-done.2.in_ref
  152.3 4.6 %all-to-all-start.3 = ((f32[8,8,128,128]{3,2,1,0:T(8,128)}), f32[8,8,128,128]{3,2,1,0:T(8,128)}, u32[]{:S(2)}, u32[]{:S(2)}) async-start(f32[8,8,128,128]{3,2,1,0:T(8,128)} %shard_map.100), calls=%async_computation.3 | async-start | bytes 8388608 | tf_op jit(solution)/shard_map/all_to_all | solution.py:660
  156.9 1.4 slice_bitcast_fusion.8
  158.3 0.0 copy-done.2
  158.4 0.2 copy-done.3
  158.5 0.2 copy-done.4
  158.7 1.7 pad_maximum_fusion
  160.4 5.7 %shard_map.101.near_ref = f32[2,32,16512]{2,1,0:T(8,128)} custom-call(s32[3]{0:T(128)S(1)} %pad_add_fusion.base_ref, f32[32,16512]{1,0:T(8,128)S(1)} %get-tuple-element.64.own_ref), custom_call_target="tpu_custom_call" | custom-call | flops 52838400 | bytes 6340608 | tf_op jit(solution)/shard_map/pallas_call | solution.py:539
  166.1 39.9 %all-to-all-done.3.in_ref = f32[8,8,128,128]{3,2,1,0:T(8,128)} async-done(((f32[8,8,128,128]{3,2,1,0:T(8,128)}), f32[8,8,128,128]{3,2,1,0:T(8,128)}, u32[]{:S(2)}, u32[]{:S(2)}) %all-to-all-start.3) | async-done | bytes 4194336 | tf_op jit(solution)/shard_map/all_to_all | solution.py:660
  206.0 7.2 %shard_map.102 = (f32[8,32768]{1,0:T(8,128)}, f32[8,32768]{1,0:T(8,128)}, f32[8,32768]{1,0:T(8,128)}, f32[8,32768]{1,0:T(8,128)}) custom-call(s32[1]{0:T(128)} %bitcast.3.group_ref, f32[8,8,128,128]{3,2,1,0:T(8,128)} %all-to-all-done.3.in_ref), custom_call_target="tpu_custom_call" | custom-call | bytes 8388608 | tf_op jit(solution)/shard_map/pallas_call | solution.py:477
  213.2 6.9 %shard_map.103.refs_0_ = f32[2,8,131072]{2,1,0:T(8,128)} custom-call(f32[8,8,128,128]{3,2,1,0:T(8,128)} %all-to-all-done.3.in_ref), custom_call_target="tpu_custom_call" | custom-call | bytes 8388608 | tf_op jit(solution)/shard_map/pallas_call | solution.py:451
  220.1 3.9 %shard_map.104.refs_0_ = f32[2,8,131072]{2,1,0:T(8,128)} custom-call(f32[8,8,64,128]{3,2,1,0:T(8,128)} %all-to-all-done.2.in_ref, f32[2,8,131072]{2,1,0:T(8,128)} %shard_map.103.refs_0_), custom_call_target="tpu_custom_call", output_to_operand_aliasing={{}: (1, {})} | custom-call | bytes 4194304 | tf_op jit(solution)/shard_map/pallas_call | solution.py:451
  224.0 4.5 %all-to-all-start.4 = ((f32[8,8,64,128]{3,2,1,0:T(8,128)}), f32[8,8,64,128]{3,2,1,0:T(8,128)}, u32[]{:S(2)}, u32[]{:S(2)}) async-start(f32[8,8,64,128]{3,2,1,0:T(8,128)} %get-tuple-element.61), calls=%async_computation.4 | async-start | bytes 4194304 | tf_op jit(solution)/shard_map/all_to_all | solution.py:660
  228.5 4.4 %collective-permute-start.5 = (f32[8,32768]{1,0:T(8,128)}, f32[8,32768]{1,0:T(8,128)}, u32[]{:S(2)}, u32[]{:S(2)}) collective-permute-start(f32[8,32768]{1,0:T(8,128)} %get-tuple-element.54), channel_id=1, source_target_pairs={{0,3},{1,2},{2,1},{3,0},{4,7},{5,6},{6,5},{7,4},{8,11},{9,10},{10,... | collective-permute-start | bytes 3145736 | tf_op jit(solution)/shard_map/ppermute | solution.py:573
  232.9 0.0 collective-permute-start.6
  232.9 0.7 collective-permute-start.7
  233.6 0.8 collective-permute-start.4
  234.5 0.0 collective-permute-done.4.edge_ref
  234.5 28.3 %collective-permute-done.3.far_ref = f32[32,16512]{1,0:T(8,128)} collective-permute-done((f32[32,16512]{1,0:T(8,128)}, f32[32,16512]{1,0:T(8,128)}, u32[]{:S(2)}, u32[]{:S(2)}) %collective-permute-start.3) | collective-permute-done | bytes 2113568 | tf_op jit(solution)/shard_map/ppermute | solution.py:622
  262.8 16.6 %shard_map.105 = f32[2,32,16512]{2,1,0:T(8,128)} custom-call(s32[3]{0:T(128)S(1)} %pad_add_fusion.base_ref, f32[2,32,16512]{2,1,0:T(8,128)} %shard_map.101.near_ref, f32[32,16512]{1,0:T(8,128)} %collective-permute-done.3.far_ref, f32[32,128]{1,0:T(8,128)S(1)} %collective-permute-done.4.edge_ref, f32[32,128]{1,0:T(8,128)S(1)} %slice.52.beyond_ref), custom_call_target="tpu_custom_call" | custom-call | flops 52838400 | bytes 10567680 | tf_op jit(solution)/shard_map/pallas_call | solution.py:553
  279.4 3.2 fusion.8
  282.7 3.3 fusion.10
  286.0 0.0 all-to-all-done.4.in_ref
  286.0 4.0 %shard_map.106 = f32[2,8,131072]{2,1,0:T(8,128)} custom-call(f32[8,8,64,128]{3,2,1,0:T(8,128)} %all-to-all-done.4.in_ref, f32[2,8,131072]{2,1,0:T(8,128)} %shard_map.104.refs_0_), custom_call_target="tpu_custom_call", output_to_operand_aliasing={{}: (1, {})} | custom-call | bytes 4194304 | tf_op jit(solution)/shard_map/pallas_call | solution.py:451
  290.0 0.0 collective-permute-done.5
  290.0 33.8 %collective-permute-done.6 = f32[8,32768]{1,0:T(8,128)} collective-permute-done((f32[8,32768]{1,0:T(8,128)}, f32[8,32768]{1,0:T(8,128)}, u32[]{:S(2)}, u32[]{:S(2)}) %collective-permute-start.6) | collective-permute-done | bytes 1048608 | tf_op jit(solution)/shard_map/ppermute | solution.py:573
  323.8 0.0 collective-permute-done.7
  323.8 4.7 %fusion.11 = f32[32,32]{1,0:T(8,128)S(1)} fusion(f32[8,32768]{1,0:T(8,128)} %collective-permute-done.7, f32[8,32768]{1,0:T(8,128)} %collective-permute-done.6, f32[8,32768]{1,0:T(8,128)} %collective-permute-done.5, f32[8,32768]{1,0:T(8,128)S(1)} %copy-done.7), kind=kOutput, calls=%fused_computation.18 | convolution fusion | flops 204473344 | bytes 4198400 | tf_op jit(solution)/shard_map/dot_general | solution.py:577
  328.5 0.2 fusion.18
  328.7 0.2 fusion.42
  328.9 9.1 %all-gather = f32[256,32]{1,0:T(8,128)S(1)} all-gather(f32[32,32]{1,0:T(8,128)S(1)} %fusion.42), channel_id=2, replica_groups=mesh['len'=8,'mem'=4] {'len'}, dimensions={0}, use_global_device_ids=true | all-gather | bytes 36864 | tf_op jit(solution)/shard_map/all_gather | solution.py:650
  338.1 13.1 %all-gather.1 = f32[128,32]{1,0:T(8,128)S(1)} all-gather(f32[32,32]{1,0:T(8,128)S(1)} %reduce_sum.18), channel_id=3, replica_groups=mesh['len'=8,'mem'=4] {'mem'}, dimensions={0}, use_global_device_ids=true | all-gather | bytes 20480 | tf_op jit(solution)/shard_map/all_gather | solution.py:650
  351.2 0.1 copy.16
  351.3 2.9 cholesky.18
  354.3 0.6 compare_reduce_fusion
  354.9 0.6 select_bitcast_fusion
  355.6 0.7 copy.17
  (37 shorter events, 0.4 us)
Async XLA Ops:
  7.5 54.4 %all-to-all-start = ((f32[8,8,128,128]{3,2,1,0:T(8,128)}), f32[8,8,128,128]{3,2,1,0:T(8,128)}, u32[]{:S(2)}, u32[]{:S(2)}) async-start(f32[8,8,128,128]{3,2,1,0:T(8,128)} %shard_map.95), calls=%async_computation | async-start | bytes 8388608 | tf_op jit(solution)/shard_map/all_to_all | solution.py:660
  12.6 7.0 %copy-start.5 = (f32[8]{0:T(128)S(1)}, f32[8]{0:T(128)}, u32[]{:S(2)}) copy-start(f32[8]{0:T(128)} %param.11) | copy-start | bytes 100
  12.6 7.0 %copy-start.6 = (f32[8]{0:T(128)S(1)}, f32[8]{0:T(128)}, u32[]{:S(2)}) copy-start(f32[8]{0:T(128)} %param.10) | copy-start | bytes 100
  24.3 47.5 %collective-permute-start.2 = (f32[2,8,16512]{2,1,0:T(8,128)S(1)}, f32[2,8,16512]{2,1,0:T(8,128)S(1)}, u32[]{:S(2)}, u32[]{:S(2)}) collective-permute-start(f32[2,8,16512]{2,1,0:T(8,128)S(1)} %pad_maximum_fusion.4), channel_id=1, source_target_pairs={{0,1},{1,0},{2,3},{3,2},{4,5},{5,4},{6,7},{7,6},{8,9},{9,8},{10,11... | collective-permute-start | bytes 3170312 | tf_op jit(solution)/shard_map/ppermute | solution.py:573
  27.9 92.0 %collective-permute-start.1 = (f32[2,8,16512]{2,1,0:T(8,128)}, f32[2,8,16512]{2,1,0:T(8,128)}, u32[]{:S(2)}, u32[]{:S(2)}) collective-permute-start(f32[2,8,16512]{2,1,0:T(8,128)} %pad_maximum_fusion.3), channel_id=1, source_target_pairs={{0,2},{1,3},{2,0},{3,1},{4,6},{5,7},{6,4},{7,5},{8,10},{9,11},{10,... | collective-permute-start | bytes 3170312 | tf_op jit(solution)/shard_map/ppermute | solution.py:573
  30.5 1.2 copy-start.9
  31.7 125.2 %collective-permute-start = (f32[2,8,16512]{2,1,0:T(8,128)}, f32[2,8,16512]{2,1,0:T(8,128)}, u32[]{:S(2)}, u32[]{:S(2)}) collective-permute-start(f32[2,8,16512]{2,1,0:T(8,128)} %pad_maximum_fusion.2), channel_id=1, source_target_pairs={{0,3},{1,2},{2,1},{3,0},{4,7},{5,6},{6,5},{7,4},{8,11},{9,10},{10,... | collective-permute-start | bytes 3170312 | tf_op jit(solution)/shard_map/ppermute | solution.py:573
  61.9 53.7 %all-to-all-start.1 = ((f32[8,8,128,128]{3,2,1,0:T(8,128)}), f32[8,8,128,128]{3,2,1,0:T(8,128)}, u32[]{:S(2)}, u32[]{:S(2)}) async-start(f32[8,8,128,128]{3,2,1,0:T(8,128)} %shard_map.96), calls=%async_computation.1 | async-start | bytes 8388608 | tf_op jit(solution)/shard_map/all_to_all | solution.py:660
  71.9 24.2 %copy-start = (bf16[2,4,256,512]{3,2,1,0:T(8,128)(2,1)S(1)}, bf16[2,4,256,512]{3,2,1,0:T(8,128)(2,1)}, u32[]{:S(2)}) copy-start(bf16[2,4,256,512]{3,2,1,0:T(8,128)(2,1)} %constant.167.clone.matrix_ref) | copy-start | bytes 6291460
  115.6 36.6 %all-to-all-start.2 = ((f32[8,8,64,128]{3,2,1,0:T(8,128)}), f32[8,8,64,128]{3,2,1,0:T(8,128)}, u32[]{:S(2)}, u32[]{:S(2)}) async-start(f32[8,8,64,128]{3,2,1,0:T(8,128)} %get-tuple-element.44), calls=%async_computation.2 | async-start | bytes 4194304 | tf_op jit(solution)/shard_map/all_to_all | solution.py:660
  152.3 53.7 %all-to-all-start.3 = ((f32[8,8,128,128]{3,2,1,0:T(8,128)}), f32[8,8,128,128]{3,2,1,0:T(8,128)}, u32[]{:S(2)}, u32[]{:S(2)}) async-start(f32[8,8,128,128]{3,2,1,0:T(8,128)} %shard_map.100), calls=%async_computation.3 | async-start | bytes 8388608 | tf_op jit(solution)/shard_map/all_to_all | solution.py:660
  156.8 1.5 copy-start.1
  156.9 1.5 copy-start.2
  156.9 1.7 copy-start.3
  156.9 1.8 copy-start.4
  213.2 49.6 %collective-permute-start.3 = (f32[32,16512]{1,0:T(8,128)}, f32[32,16512]{1,0:T(8,128)}, u32[]{:S(2)}, u32[]{:S(2)}) collective-permute-start(f32[32,16512]{1,0:T(8,128)} %get-tuple-element.63), channel_id=1, source_target_pairs={{0,28},{4,24},{8,20},{12,16},{16,12},{20,8},{24,4},{28,0},{1,29},{... | collective-permute-start | bytes 6340616 | tf_op jit(solution)/shard_map/ppermute | solution.py:622
  224.0 8.9 %copy-start.8 = (f32[8,32768]{1,0:T(8,128)S(1)}, f32[8,32768]{1,0:T(8,128)}, u32[]{:S(2)}) copy-start(f32[8,32768]{1,0:T(8,128)} %get-tuple-element.56) | copy-start | bytes 3145732
  224.0 61.9 %all-to-all-start.4 = ((f32[8,8,64,128]{3,2,1,0:T(8,128)}), f32[8,8,64,128]{3,2,1,0:T(8,128)}, u32[]{:S(2)}, u32[]{:S(2)}) async-start(f32[8,8,64,128]{3,2,1,0:T(8,128)} %get-tuple-element.61), calls=%async_computation.4 | async-start | bytes 4194304 | tf_op jit(solution)/shard_map/all_to_all | solution.py:660
  228.5 61.5 %collective-permute-start.5 = (f32[8,32768]{1,0:T(8,128)}, f32[8,32768]{1,0:T(8,128)}, u32[]{:S(2)}, u32[]{:S(2)}) collective-permute-start(f32[8,32768]{1,0:T(8,128)} %get-tuple-element.54), channel_id=1, source_target_pairs={{0,3},{1,2},{2,1},{3,0},{4,7},{5,6},{6,5},{7,4},{8,11},{9,10},{10,... | collective-permute-start | bytes 3145736 | tf_op jit(solution)/shard_map/ppermute | solution.py:573
  232.9 90.8 %collective-permute-start.6 = (f32[8,32768]{1,0:T(8,128)}, f32[8,32768]{1,0:T(8,128)}, u32[]{:S(2)}, u32[]{:S(2)}) collective-permute-start(f32[8,32768]{1,0:T(8,128)} %get-tuple-element.55), channel_id=1, source_target_pairs={{0,2},{1,3},{2,0},{3,1},{4,6},{5,7},{6,4},{7,5},{8,10},{9,11},{10,... | collective-permute-start | bytes 3145736 | tf_op jit(solution)/shard_map/ppermute | solution.py:573
  232.9 90.8 %collective-permute-start.7 = (f32[8,32768]{1,0:T(8,128)S(1)}, f32[8,32768]{1,0:T(8,128)}, u32[]{:S(2)}, u32[]{:S(2)}) collective-permute-start(f32[8,32768]{1,0:T(8,128)S(1)} %copy-done.8), channel_id=1, source_target_pairs={{0,1},{1,0},{2,3},{3,2},{4,5},{5,4},{6,7},{7,6},{8,9},{9,8},{10,11... | collective-permute-start | bytes 3145736 | tf_op jit(solution)/shard_map/ppermute | solution.py:573
  233.6 0.9 collective-permute-start.4
  286.0 37.8 %copy-start.7 = (f32[8,32768]{1,0:T(8,128)S(1)}, f32[8,32768]{1,0:T(8,128)}, u32[]{:S(2)}) copy-start(f32[8,32768]{1,0:T(8,128)} %get-tuple-element.70) | copy-start | bytes 3145732

commit v13 on v11

--- a/solution.py
+++ b/solution.py
@@ -18,7 +18,7 @@
 STEP = 16
 SUBLANES = 8
 WIDE = 256
-BLOCK_ROWS = 16
+BLOCK_ROWS = 8
 OUTER_TILES = 2
 VMEM_LIMIT = 48 * 1024 * 1024
 SIN_HALF = (0.49999999785787, -0.02083332246218, 2.604078316692e-4, -1.547581723527e-6, 5.088214043e-9)

time: 347 us -> 356 us (1.026)
  Pallas kernels: 122 us -> 139 us
  waiting for transfers between devices: 136 us -> 126 us
    all_to_all x5, waiting for transfers between devices: 79.8 us -> 72.7 us  [swap(): return lax.all_to_all(piece, 'len', split_axis=0, concat_axis=0, tiled=True)]
    pallas_call x3, Pallas kernels: 14.9 us -> 21.9 us  [join_call(): pl.pallas_call(join_kernel, grid=(steps,), in_specs=[pl.BlockSpec((member...]
    pallas_call x2, Pallas kernels: 13.8 us -> 20.8 us  [part_call(): pl.pallas_call(part_kernel, grid=(rows // BLOCK_ROWS,), in_specs=[pl.Bloc...]
    ppermute x1, waiting for transfers between devices: 28.3 us -> 23.1 us  [across(): lax.ppermute(far, 'len', [(d, shards - 1 - d) for d in range(shards)])]
  transfers between devices with their start and end apart: 13 -> 13, of which waited for: 6 -> 6; matrix products, arithmetic and copies ran while one was open for 6% -> 5% of each run, Pallas kernels for 31% -> 33%
where the time goes in v13:
time: 356 us; the launch traced here: 354 us
  Pallas kernels  139 us (39%)
  waiting for transfers between devices  126 us (35%)
  starting transfers between devices  34.2 us (10%)
  blocking collectives  23.9 us (7%)
  matrix products  11.6 us (3%)
  other arithmetic  9.46 us (3%)
  local copies, waits for them, and re-layouts  8.57 us (2%)
    all_to_all x5, waiting for transfers between devices, swap(): return lax.all_to_all(piece, 'len', split_axis=0, concat_axis=0, tiled=True)  72.7 us
    pallas_call x2, Pallas kernels, outer_call(): pl.pallas_call(functools.partial(outer_kernel, track), grid=(tiles // som...  44.7 us
    ppermute x6, waiting for transfers between devices, to_group(): lax.ppermute(piece, 'mem', [(z, z ^ slot) for z in range(groups)])  29.9 us
    all_gather x2, blocking collectives, summed(): value = jnp.sum(lax.all_gather(value, axis), axis=0)  23.9 us
    all_to_all x5, starting transfers between devices, swap(): return lax.all_to_all(piece, 'len', split_axis=0, concat_axis=0, tiled=True)  23.2 us
    ppermute x1, waiting for transfers between devices, across(): lax.ppermute(far, 'len', [(d, shards - 1 - d) for d in range(shards)])  23.1 us
    pallas_call x3, Pallas kernels, join_call(): pl.pallas_call(join_kernel, grid=(steps,), in_specs=[pl.BlockSpec((member...  21.9 us
    pallas_call x2, Pallas kernels, part_call(): pl.pallas_call(part_kernel, grid=(rows // BLOCK_ROWS,), in_specs=[pl.Bloc...  20.8 us
  transfers between devices with their start and end apart: 13, of which 6 were waited for; matrix products, arithmetic and copies ran while one was open for 5% of the time, Pallas kernels for 33%

profile of v13, /device:TPU:0, one launch (start us, length us, event | category | flops | bytes accessed | tf_op | source)
XLA Modules:
  0.0 353.8 jit_solution(15007981261742978951)
XLA Ops:
  0.6 10.3 %shard_map.95 = f32[8,8,128,128]{3,2,1,0:T(8,128)} custom-call(f32[8,131072]{1,0:T(8,128)} %in_ref.2), custom_call_target="tpu_custom_call" | custom-call | bytes 8388608 | tf_op jit(solution)/shard_map/pallas_call | solution.py:435
  11.0 5.2 %all-to-all-start = ((f32[8,8,128,128]{3,2,1,0:T(8,128)}), f32[8,8,128,128]{3,2,1,0:T(8,128)}, u32[]{:S(2)}, u32[]{:S(2)}) async-start(f32[8,8,128,128]{3,2,1,0:T(8,128)} %shard_map.95), calls=%async_computation | async-start | bytes 8388608 | tf_op jit(solution)/shard_map/all_to_all | solution.py:660
  16.1 0.0 copy-start.6
  16.1 10.5 %shard_map.96 = f32[8,8,128,128]{3,2,1,0:T(8,128)} custom-call(f32[8,131072]{1,0:T(8,128)} %in_ref.3), custom_call_target="tpu_custom_call" | custom-call | bytes 8388608 | tf_op jit(solution)/shard_map/pallas_call | solution.py:435
  26.8 3.4 constant_dynamic-slice_fusion.1
  30.3 0.9 constant_dynamic-slice_fusion
  31.2 0.1 pad_maximum_fusion.4
  31.3 2.5 collective-permute-start.2
  33.9 1.1 pad_maximum_fusion.3
  35.0 2.6 collective-permute-start.1
  37.7 1.1 pad_maximum_fusion.2
  38.8 0.0 collective-permute-start
  38.8 0.2 fusion.38.params_ref
  39.0 0.1 pad_add_fusion.base_ref
  39.1 26.3 %all-to-all-done.phase_ref = f32[8,8,128,128]{3,2,1,0:T(8,128)} async-done(((f32[8,8,128,128]{3,2,1,0:T(8,128)}), f32[8,8,128,128]{3,2,1,0:T(8,128)}, u32[]{:S(2)}, u32[]{:S(2)}) %all-to-all-start) | async-done | bytes 4194336 | tf_op jit(solution)/shard_map/all_to_all | solution.py:660
  65.4 4.6 %all-to-all-start.1 = ((f32[8,8,128,128]{3,2,1,0:T(8,128)}), f32[8,8,128,128]{3,2,1,0:T(8,128)}, u32[]{:S(2)}, u32[]{:S(2)}) async-start(f32[8,8,128,128]{3,2,1,0:T(8,128)} %shard_map.96), calls=%async_computation.1 | async-start | bytes 8388608 | tf_op jit(solution)/shard_map/all_to_all | solution.py:660
  70.0 8.9 %collective-permute-done.2 = f32[2,8,16512]{2,1,0:T(8,128)S(1)} collective-permute-done((f32[2,8,16512]{2,1,0:T(8,128)S(1)}, f32[2,8,16512]{2,1,0:T(8,128)S(1)}, u32[]{:S(2)}, u32[]{:S(2)}) %collective-permute-start.2) | collective-permute-done | bytes 1056800 | tf_op jit(solution)/shard_map/ppermute | solution.py:573
  78.8 0.1 slice_bitcast_fusion.6
  78.9 0.0 copy-start
  78.9 24.2 %shard_map.97 = (f32[8,2,1024,128]{3,2,1,0:T(8,128)}, f32[8,8,128,128]{3,2,1,0:T(8,128)}, f32[8,8,128,128]{3,2,1,0:T(8,128)}, f32[8,8,128,128]{3,2,1,0:T(8,128)}) custom-call(f32[3]{0:T(128)S(1)} %fusion.38.params_ref, f32[8,8,128,128]{3,2,1,0:T(8,128)} %all-to-all-done.phase_ref, bf16[2,4,512,512]{3,2,1,0:T(8,128)(2,1)} %constant.166.clone.refs_0_.refs_3_, ...), custom_call_target="tpu_custom_call" | custom-call | flops 6442450944 | bytes 33554432 | tf_op jit(solution)/shard_map/pallas_call | solution.py:497
  103.1 9.5 %shard_map.98 = (f32[8,8,64,128]{3,2,1,0:T(8,128)}, f32[8,8,64,128]{3,2,1,0:T(8,128)}) custom-call(f32[8,2,1024,128]{3,2,1,0:T(8,128)} %get-tuple-element.39.mid_ref, bf16[2,4,256,512]{3,2,1,0:T(8,128)(2,1)S(1)} %copy-done), custom_call_target="tpu_custom_call" | custom-call | flops 3221225472 | bytes 12582912 | tf_op jit(solution)/shard_map/pallas_call | solution.py:520
  112.6 6.5 %all-to-all-done.1.phase_ref = f32[8,8,128,128]{3,2,1,0:T(8,128)} async-done(((f32[8,8,128,128]{3,2,1,0:T(8,128)}), f32[8,8,128,128]{3,2,1,0:T(8,128)}, u32[]{:S(2)}, u32[]{:S(2)}) %all-to-all-start.1) | async-done | bytes 4194336 | tf_op jit(solution)/shard_map/all_to_all | solution.py:660
  119.1 4.4 %all-to-all-start.2 = ((f32[8,8,64,128]{3,2,1,0:T(8,128)}), f32[8,8,64,128]{3,2,1,0:T(8,128)}, u32[]{:S(2)}, u32[]{:S(2)}) async-start(f32[8,8,64,128]{3,2,1,0:T(8,128)} %get-tuple-element.42), calls=%async_computation.2 | async-start | bytes 4194304 | tf_op jit(solution)/shard_map/all_to_all | solution.py:660
  123.5 0.0 collective-permute-done.1
  123.5 2.3 slice_bitcast_fusion.7
  125.8 20.6 %shard_map.99.mid_ref = f32[8,2,1024,128]{3,2,1,0:T(8,128)} custom-call(f32[3]{0:T(128)S(1)} %fusion.38.params_ref, f32[8,8,128,128]{3,2,1,0:T(8,128)} %all-to-all-done.1.phase_ref, f32[8,8,128,128]{3,2,1,0:T(8,128)} %get-tuple-element.44.refs_0_, f32[8,8,128,128]{3,2,1,0:T(8,128)} %get-tuple-element.45.refs_1_, ...), custom_call_target="tpu_custom_call" | custom-call | flops 6442450944 | bytes 33554432 | tf_op jit(solution)/shard_map/pallas_call | solution.py:497
  146.3 9.4 %shard_map.100 = f32[8,8,128,128]{3,2,1,0:T(8,128)} custom-call(f32[8,2,1024,128]{3,2,1,0:T(8,128)} %shard_map.99.mid_ref, bf16[2,4,256,512]{3,2,1,0:T(8,128)(2,1)S(1)} %copy-done), custom_call_target="tpu_custom_call" | custom-call | flops 3221225472 | bytes 12582912 | tf_op jit(solution)/shard_map/pallas_call | solution.py:520
  155.8 4.6 %all-to-all-start.3 = ((f32[8,8,128,128]{3,2,1,0:T(8,128)}), f32[8,8,128,128]{3,2,1,0:T(8,128)}, u32[]{:S(2)}, u32[]{:S(2)}) async-start(f32[8,8,128,128]{3,2,1,0:T(8,128)} %shard_map.100), calls=%async_computation.3 | async-start | bytes 8388608 | tf_op jit(solution)/shard_map/all_to_all | solution.py:660
  160.4 0.0 collective-permute-done
  160.4 1.4 slice_bitcast_fusion.8
  161.8 0.0 copy-done.2
  161.9 0.2 copy-done.3
  162.0 0.2 copy-done.4
  162.2 1.7 pad_maximum_fusion
  163.9 5.7 %shard_map.101.near_ref = f32[2,32,16512]{2,1,0:T(8,128)} custom-call(s32[3]{0:T(128)S(1)} %pad_add_fusion.base_ref, f32[32,16512]{1,0:T(8,128)S(1)} %get-tuple-element.59.own_ref), custom_call_target="tpu_custom_call" | custom-call | flops 52838400 | bytes 6340608 | tf_op jit(solution)/shard_map/pallas_call | solution.py:539
  169.6 39.9 %all-to-all-done.3.in_ref = f32[8,8,128,128]{3,2,1,0:T(8,128)} async-done(((f32[8,8,128,128]{3,2,1,0:T(8,128)}), f32[8,8,128,128]{3,2,1,0:T(8,128)}, u32[]{:S(2)}, u32[]{:S(2)}) %all-to-all-start.3) | async-done | bytes 4194336 | tf_op jit(solution)/shard_map/all_to_all | solution.py:660
  209.5 10.6 %shard_map.102 = (f32[8,32768]{1,0:T(8,128)}, f32[8,32768]{1,0:T(8,128)}, f32[8,32768]{1,0:T(8,128)}, f32[8,32768]{1,0:T(8,128)}) custom-call(s32[1]{0:T(128)} %bitcast.group_ref, f32[8,8,128,128]{3,2,1,0:T(8,128)} %all-to-all-done.3.in_ref), custom_call_target="tpu_custom_call" | custom-call | bytes 8388608 | tf_op jit(solution)/shard_map/pallas_call | solution.py:477
  220.1 4.5 %all-to-all-start.4 = ((f32[8,8,64,128]{3,2,1,0:T(8,128)}), f32[8,8,64,128]{3,2,1,0:T(8,128)}, u32[]{:S(2)}, u32[]{:S(2)}) async-start(f32[8,8,64,128]{3,2,1,0:T(8,128)} %get-tuple-element.56), calls=%async_computation.4 | async-start | bytes 4194304 | tf_op jit(solution)/shard_map/all_to_all | solution.py:660
  224.6 4.4 %collective-permute-start.5 = (f32[8,32768]{1,0:T(8,128)}, f32[8,32768]{1,0:T(8,128)}, u32[]{:S(2)}, u32[]{:S(2)}) collective-permute-start(f32[8,32768]{1,0:T(8,128)} %get-tuple-element.51), channel_id=1, source_target_pairs={{0,3},{1,2},{2,1},{3,0},{4,7},{5,6},{6,5},{7,4},{8,11},{9,10},{10,... | collective-permute-start | bytes 3145736 | tf_op jit(solution)/shard_map/ppermute | solution.py:573
  229.0 0.0 collective-permute-start.6
  229.0 0.6 collective-permute-start.7
  229.6 0.8 collective-permute-start.4
  230.5 10.3 %shard_map.104.refs_0_ = f32[2,8,131072]{2,1,0:T(8,128)} custom-call(f32[8,8,128,128]{3,2,1,0:T(8,128)} %all-to-all-done.3.in_ref), custom_call_target="tpu_custom_call" | custom-call | bytes 8388608 | tf_op jit(solution)/shard_map/pallas_call | solution.py:451
  240.8 5.8 %shard_map.105.refs_0_ = f32[2,8,131072]{2,1,0:T(8,128)} custom-call(f32[8,8,64,128]{3,2,1,0:T(8,128)} %all-to-all-done.2.in_ref, f32[2,8,131072]{2,1,0:T(8,128)} %shard_map.104.refs_0_), custom_call_target="tpu_custom_call", output_to_operand_aliasing={{}: (1, {})} | custom-call | bytes 4194304 | tf_op jit(solution)/shard_map/pallas_call | solution.py:451
  246.6 0.0 collective-permute-done.4.edge_ref
  246.6 23.1 %collective-permute-done.3.far_ref = f32[32,16512]{1,0:T(8,128)} collective-permute-done((f32[32,16512]{1,0:T(8,128)}, f32[32,16512]{1,0:T(8,128)}, u32[]{:S(2)}, u32[]{:S(2)}) %collective-permute-start.3) | collective-permute-done | bytes 2113568 | tf_op jit(solution)/shard_map/ppermute | solution.py:622
  269.7 16.6 %shard_map.103 = f32[2,32,16512]{2,1,0:T(8,128)} custom-call(s32[3]{0:T(128)S(1)} %pad_add_fusion.base_ref, f32[2,32,16512]{2,1,0:T(8,128)} %shard_map.101.near_ref, f32[32,16512]{1,0:T(8,128)} %collective-permute-done.3.far_ref, f32[32,128]{1,0:T(8,128)S(1)} %collective-permute-done.4.edge_ref, f32[32,128]{1,0:T(8,128)S(1)} %slice.52.beyond_ref), custom_call_target="tpu_custom_call" | custom-call | flops 52838400 | bytes 10567680 | tf_op jit(solution)/shard_map/pallas_call | solution.py:553
  286.3 3.2 fusion.8
  289.5 3.3 fusion.10
  292.8 0.0 all-to-all-done.4.in_ref
  292.8 5.9 %shard_map.106 = f32[2,8,131072]{2,1,0:T(8,128)} custom-call(f32[8,8,64,128]{3,2,1,0:T(8,128)} %all-to-all-done.4.in_ref, f32[2,8,131072]{2,1,0:T(8,128)} %shard_map.105.refs_0_), custom_call_target="tpu_custom_call", output_to_operand_aliasing={{}: (1, {})} | custom-call | bytes 4194304 | tf_op jit(solution)/shard_map/pallas_call | solution.py:451
  298.7 0.0 collective-permute-done.5
  298.7 21.0 %collective-permute-done.6 = f32[8,32768]{1,0:T(8,128)} collective-permute-done((f32[8,32768]{1,0:T(8,128)}, f32[8,32768]{1,0:T(8,128)}, u32[]{:S(2)}, u32[]{:S(2)}) %collective-permute-start.6) | collective-permute-done | bytes 1048608 | tf_op jit(solution)/shard_map/ppermute | solution.py:573
  319.7 0.0 collective-permute-done.7
  319.7 4.7 %fusion.11 = f32[32,32]{1,0:T(8,128)S(1)} fusion(f32[8,32768]{1,0:T(8,128)} %collective-permute-done.7, f32[8,32768]{1,0:T(8,128)} %collective-permute-done.6, f32[8,32768]{1,0:T(8,128)} %collective-permute-done.5, f32[8,32768]{1,0:T(8,128)S(1)} %copy-done.7), kind=kOutput, calls=%fused_computation.18 | convolution fusion | flops 204473344 | bytes 4198400 | tf_op jit(solution)/shard_map/dot_general | solution.py:577
  324.4 0.2 fusion.18
  324.6 0.2 fusion.42
  324.8 9.8 %all-gather = f32[256,32]{1,0:T(8,128)S(1)} all-gather(f32[32,32]{1,0:T(8,128)S(1)} %fusion.42), channel_id=2, replica_groups=mesh['len'=8,'mem'=4] {'len'}, dimensions={0}, use_global_device_ids=true | all-gather | bytes 36864 | tf_op jit(solution)/shard_map/all_gather | solution.py:650
  334.7 14.1 %all-gather.1 = f32[128,32]{1,0:T(8,128)S(1)} all-gather(f32[32,32]{1,0:T(8,128)S(1)} %reduce_sum.18), channel_id=3, replica_groups=mesh['len'=8,'mem'=4] {'mem'}, dimensions={0}, use_global_device_ids=true | all-gather | bytes 20480 | tf_op jit(solution)/shard_map/all_gather | solution.py:650
  348.8 0.1 copy.16
  348.8 2.9 cholesky.18
  351.8 0.6 compare_reduce_fusion
  352.4 0.6 select_bitcast_fusion
  353.1 0.7 copy.17
  (37 shorter events, 0.4 us)
Async XLA Ops:
  11.0 54.4 %all-to-all-start = ((f32[8,8,128,128]{3,2,1,0:T(8,128)}), f32[8,8,128,128]{3,2,1,0:T(8,128)}, u32[]{:S(2)}, u32[]{:S(2)}) async-start(f32[8,8,128,128]{3,2,1,0:T(8,128)} %shard_map.95), calls=%async_computation | async-start | bytes 8388608 | tf_op jit(solution)/shard_map/all_to_all | solution.py:660
  16.1 10.6 %copy-start.5 = (f32[8]{0:T(128)S(1)}, f32[8]{0:T(128)}, u32[]{:S(2)}) copy-start(f32[8]{0:T(128)} %param.11) | copy-start | bytes 100
  16.1 10.6 %copy-start.6 = (f32[8]{0:T(128)S(1)}, f32[8]{0:T(128)}, u32[]{:S(2)}) copy-start(f32[8]{0:T(128)} %param.10) | copy-start | bytes 100
  31.3 47.5 %collective-permute-start.2 = (f32[2,8,16512]{2,1,0:T(8,128)S(1)}, f32[2,8,16512]{2,1,0:T(8,128)S(1)}, u32[]{:S(2)}, u32[]{:S(2)}) collective-permute-start(f32[2,8,16512]{2,1,0:T(8,128)S(1)} %pad_maximum_fusion.4), channel_id=1, source_target_pairs={{0,1},{1,0},{2,3},{3,2},{4,5},{5,4},{6,7},{7,6},{8,9},{9,8},{10,11... | collective-permute-start | bytes 3170312 | tf_op jit(solution)/shard_map/ppermute | solution.py:573
  35.0 88.5 %collective-permute-start.1 = (f32[2,8,16512]{2,1,0:T(8,128)}, f32[2,8,16512]{2,1,0:T(8,128)}, u32[]{:S(2)}, u32[]{:S(2)}) collective-permute-start(f32[2,8,16512]{2,1,0:T(8,128)} %pad_maximum_fusion.3), channel_id=1, source_target_pairs={{0,2},{1,3},{2,0},{3,1},{4,6},{5,7},{6,4},{7,5},{8,10},{9,11},{10,... | collective-permute-start | bytes 3170312 | tf_op jit(solution)/shard_map/ppermute | solution.py:573
  37.6 1.2 copy-start.9
  38.8 121.6 %collective-permute-start = (f32[2,8,16512]{2,1,0:T(8,128)}, f32[2,8,16512]{2,1,0:T(8,128)}, u32[]{:S(2)}, u32[]{:S(2)}) collective-permute-start(f32[2,8,16512]{2,1,0:T(8,128)} %pad_maximum_fusion.2), channel_id=1, source_target_pairs={{0,3},{1,2},{2,1},{3,0},{4,7},{5,6},{6,5},{7,4},{8,11},{9,10},{10,... | collective-permute-start | bytes 3170312 | tf_op jit(solution)/shard_map/ppermute | solution.py:573
  65.4 53.7 %all-to-all-start.1 = ((f32[8,8,128,128]{3,2,1,0:T(8,128)}), f32[8,8,128,128]{3,2,1,0:T(8,128)}, u32[]{:S(2)}, u32[]{:S(2)}) async-start(f32[8,8,128,128]{3,2,1,0:T(8,128)} %shard_map.96), calls=%async_computation.1 | async-start | bytes 8388608 | tf_op jit(solution)/shard_map/all_to_all | solution.py:660
  78.9 24.2 %copy-start = (bf16[2,4,256,512]{3,2,1,0:T(8,128)(2,1)S(1)}, bf16[2,4,256,512]{3,2,1,0:T(8,128)(2,1)}, u32[]{:S(2)}) copy-start(bf16[2,4,256,512]{3,2,1,0:T(8,128)(2,1)} %constant.167.clone.matrix_ref) | copy-start | bytes 6291460
  119.1 36.7 %all-to-all-start.2 = ((f32[8,8,64,128]{3,2,1,0:T(8,128)}), f32[8,8,64,128]{3,2,1,0:T(8,128)}, u32[]{:S(2)}, u32[]{:S(2)}) async-start(f32[8,8,64,128]{3,2,1,0:T(8,128)} %get-tuple-element.42), calls=%async_computation.2 | async-start | bytes 4194304 | tf_op jit(solution)/shard_map/all_to_all | solution.py:660
  155.8 53.7 %all-to-all-start.3 = ((f32[8,8,128,128]{3,2,1,0:T(8,128)}), f32[8,8,128,128]{3,2,1,0:T(8,128)}, u32[]{:S(2)}, u32[]{:S(2)}) async-start(f32[8,8,128,128]{3,2,1,0:T(8,128)} %shard_map.100), calls=%async_computation.3 | async-start | bytes 8388608 | tf_op jit(solution)/shard_map/all_to_all | solution.py:660
  160.3 1.5 copy-start.1
  160.3 1.5 copy-start.2
  160.4 1.7 copy-start.3
  160.4 1.8 copy-start.4
  220.0 8.9 %copy-start.8 = (f32[8,32768]{1,0:T(8,128)S(1)}, f32[8,32768]{1,0:T(8,128)}, u32[]{:S(2)}) copy-start(f32[8,32768]{1,0:T(8,128)} %get-tuple-element.53) | copy-start | bytes 3145732
  220.1 49.6 %collective-permute-start.3 = (f32[32,16512]{1,0:T(8,128)}, f32[32,16512]{1,0:T(8,128)}, u32[]{:S(2)}, u32[]{:S(2)}) collective-permute-start(f32[32,16512]{1,0:T(8,128)} %get-tuple-element.58), channel_id=1, source_target_pairs={{0,28},{4,24},{8,20},{12,16},{16,12},{20,8},{24,4},{28,0},{1,29},{... | collective-permute-start | bytes 6340616 | tf_op jit(solution)/shard_map/ppermute | solution.py:622
  220.1 72.8 %all-to-all-start.4 = ((f32[8,8,64,128]{3,2,1,0:T(8,128)}), f32[8,8,64,128]{3,2,1,0:T(8,128)}, u32[]{:S(2)}, u32[]{:S(2)}) async-start(f32[8,8,64,128]{3,2,1,0:T(8,128)} %get-tuple-element.56), calls=%async_computation.4 | async-start | bytes 4194304 | tf_op jit(solution)/shard_map/all_to_all | solution.py:660
  224.6 74.1 %collective-permute-start.5 = (f32[8,32768]{1,0:T(8,128)}, f32[8,32768]{1,0:T(8,128)}, u32[]{:S(2)}, u32[]{:S(2)}) collective-permute-start(f32[8,32768]{1,0:T(8,128)} %get-tuple-element.51), channel_id=1, source_target_pairs={{0,3},{1,2},{2,1},{3,0},{4,7},{5,6},{6,5},{7,4},{8,11},{9,10},{10,... | collective-permute-start | bytes 3145736 | tf_op jit(solution)/shard_map/ppermute | solution.py:573
  229.0 90.7 %collective-permute-start.6 = (f32[8,32768]{1,0:T(8,128)}, f32[8,32768]{1,0:T(8,128)}, u32[]{:S(2)}, u32[]{:S(2)}) collective-permute-start(f32[8,32768]{1,0:T(8,128)} %get-tuple-element.52), channel_id=1, source_target_pairs={{0,2},{1,3},{2,0},{3,1},{4,6},{5,7},{6,4},{7,5},{8,10},{9,11},{10,... | collective-permute-start | bytes 3145736 | tf_op jit(solution)/shard_map/ppermute | solution.py:573
  229.0 90.7 %collective-permute-start.7 = (f32[8,32768]{1,0:T(8,128)S(1)}, f32[8,32768]{1,0:T(8,128)}, u32[]{:S(2)}, u32[]{:S(2)}) collective-permute-start(f32[8,32768]{1,0:T(8,128)S(1)} %copy-done.8), channel_id=1, source_target_pairs={{0,1},{1,0},{2,3},{3,2},{4,5},{5,4},{6,7},{7,6},{8,9},{9,8},{10,11... | collective-permute-start | bytes 3145736 | tf_op jit(solution)/shard_map/ppermute | solution.py:573
  229.6 17.0 %collective-permute-start.4 = (f32[32,128]{1,0:T(8,128)S(1)}, f32[32,128]{1,0:T(8,128)S(1)}, u32[]{:S(2)}, u32[]{:S(2)}) collective-permute-start(f32[32,128]{1,0:T(8,128)S(1)} %slice.42), channel_id=1, source_target_pairs={{0,0},{4,28},{8,24},{12,20},{16,16},{20,12},{24,8},{28,4},{1,1},{5... | collective-permute-start | bytes 49160 | tf_op jit(solution)/shard_map/ppermute | solution.py:617
  292.8 26.9 %copy-start.7 = (f32[8,32768]{1,0:T(8,128)S(1)}, f32[8,32768]{1,0:T(8,128)}, u32[]{:S(2)}) copy-start(f32[8,32768]{1,0:T(8,128)} %get-tuple-element.66) | copy-start | bytes 3145732
